TPU v7x, 32 devices: a whole 2x2x4 slice. The times are simulated.
32 devices in a mesh: chaos: 4 (over z), space: 8 (over y, x, core).
Axes of the slice: x: 2, y: 2, z: 4, core: 2. Of those that a mesh axis runs over, the one named last changes fastest.
Arguments:
- panels: bfloat16 [212, 24, 2304], P('chaos', 'space'), may hold values from -6 to 6
- mean_field: float32 [24, 2304], P('space'), may hold values from 0.5 to 2
- fluctuations: float32 [6, 24, 2304], P(None, 'space'), may hold values from -1.5 to 1.5
- products: float32 [1218], replicated, may hold values from -4 to 4
- triples: int32 [1218, 3], replicated, may hold values from 0 to 209, as said below
- owner_slot: int32 [210], replicated, may hold values from 0 to 211, as said below
Outputs:
- first_apply: bfloat16 [212, 24, 2304], P('chaos', 'space')
- second_apply: bfloat16 [212, 24, 2304], P('chaos', 'space')
Inputs may be any that keep to these rules, and one draw needn't show every extreme that they name: `triples`: each row (i, j, k) names a nonzero of G_k; i and j are below 210, k below 7; repeated rows add; every chaos coefficient is some row's i and some row's j. `owner_slot`: distinct slots; slot s belongs to the group s // 53 along chaos.
All inputs are finite; a program needn't handle non-finite values.
Results may differ from a plain program's by a relative error of at most 0.007.
Values may be sent and summed in bfloat16 or wider, within the bound.
No kernel may reach another device: no remote copies, remote signals or barrier semaphores. Data moves between devices by JAX's collectives and lax.ppermute only.
A program may use at most 128 MiB of HBM per device.

v0:
```python
import jax
import jax.numpy as jnp
from jax import lax
from jax.sharding import PartitionSpec as P

NXY = 48


scale_factor = 0.15


def padded(block, sides, width):
    for axis, dim in sides:
        count = lax.axis_size(axis)
        forward = [(i, i + 1) for i in range(count - 1)]
        backward = [(target, source) for source, target in forward]
        low = lax.ppermute(
            lax.slice_in_dim(block, block.shape[dim] - width, None, axis=dim), axis, forward
        )
        high = lax.ppermute(lax.slice_in_dim(block, 0, width, axis=dim), axis, backward)
        block = jnp.concatenate([low, block, high], axis=dim)
    return block


def shifted(source, offset, inside):
    length_last = source.shape[-1]
    padding = [(0, 0)] * (source.ndim - 1)
    if offset > 0:
        moved_values = jnp.pad(source[..., offset:], padding + [(0, offset)])
    else:
        moved_values = jnp.pad(source[..., : length_last + offset], padding + [(-offset, 0)])
    return jnp.where(inside, moved_values, jnp.zeros_like(moved_values))


def diffusion(extended, conductance_ext, side_cells):
    center = extended[..., 1:-1, :]
    conduct = conductance_ext[1:-1]
    flux_sum = 0.5 * (conduct + conductance_ext[2:]) * (center - extended[..., 2:, :])
    flux_sum = flux_sum + 0.5 * (conduct + conductance_ext[:-2]) * (center - extended[..., :-2, :])
    column = lax.iota(jnp.int32, center.shape[-1]) % side_cells
    everywhere = column >= 0
    for offset, inside in (
        (1, column < side_cells - 1),
        (-1, column > 0),
        (side_cells, everywhere),
        (-side_cells, everywhere),
    ):
        flux_sum = flux_sum + 0.5 * (conduct + shifted(conduct, offset, inside)) * (
            center - shifted(center, offset, inside)
        )
    return flux_sum


def shards(panels, mean_field, fluctuations, products, triples, owner_slot):
    own_count = panels.shape[0]
    slot_count = own_count * lax.axis_size("chaos")
    coefficients = jnp.concatenate([mean_field[None], fluctuations], axis=0)
    field_count = coefficients.shape[0]
    padded_coef = padded(coefficients, (("space", 1),), 1)
    row_slot = owner_slot[triples[:, 0]]
    column_slot = owner_slot[triples[:, 1]]
    tables = (
        jnp.zeros((field_count, slot_count, slot_count), jnp.float32)
        .at[triples[:, 2], row_slot, column_slot]
        .add(products)
    )
    tables = tables.astype(jnp.bfloat16)
    own_tables = lax.dynamic_slice_in_dim(tables, lax.axis_index("chaos") * own_count, own_count, 1)

    def combine(own_panels):
        summed = jnp.einsum(
            "krc,cpv->krpv",
            own_tables,
            lax.all_gather(own_panels, "chaos", axis=0, tiled=True),
            preferred_element_type=jnp.float32,
        )
        return summed.astype(jnp.bfloat16)

    def galerkin_apply(own_panels):
        combined = padded(combine(own_panels), (("space", 2),), 1)
        combined = lax.optimization_barrier(combined)
        result = jnp.zeros(own_panels.shape, jnp.float32)
        for field_index in range(field_count):
            result = result + diffusion(
                combined[field_index].astype(jnp.float32), padded_coef[field_index], NXY
            )
        return (scale_factor * result).astype(jnp.bfloat16)

    first_values = galerkin_apply(panels)
    second_values = galerkin_apply(first_values)
    return (first_values, second_values)


def solution(mesh):
    in_specs = (P("chaos", "space", None), P("space", None), P(None, "space", None), P(), P(), P())
    out_specs = (P("chaos", "space", None), P("chaos", "space", None))
    return jax.shard_map(shards, mesh=mesh, in_specs=in_specs, out_specs=out_specs, check_vma=False)
```

profile of v0, /device:TPU:1, one launch (start us, length us, event | category | flops | bytes accessed | tf_op | source)
XLA Modules:
  0.0 437.1 jit_solution(7484814226707966239)
XLA Ops:
  10.4 4.5 %collective-permute-start.3 = (f32[7,1,2304]{2,1,0:T(1,128)S(1)}, f32[7,1,2304]{2,1,0:T(1,128)S(1)}, u32[]{:S(2)}, u32[]{:S(2)}) collective-permute-start(f32[7,1,2304]{2,1,0:T(1,128)S(1)} %get-tuple-element.95), channel_id=1, source_target_pairs={{0,1},{1,2},{2,3},{3,4},{4,5},{5,6},{6,7},{8,9},{9,10},{10,11},{11... | collective-permute-start | bytes 193544 | tf_op jit(solution)/shard_map/ppermute | solution.py:17
  14.9 2.5 copy.8
  18.9 8.0 %gather_fusion.1 = s32[1218]{0:T(1024)S(1)} fusion(s32[210]{0:T(256)S(1)} %copy-done, s32[2048]{0:T(1024)S(1)} %get-tuple-element.162), kind=kCustom, calls=%fused_computation.1 | custom fusion | bytes 14616 | tf_op jit(solution)/shard_map/gather | solution.py:61
  27.0 8.0 %gather_fusion = s32[1218]{0:T(1024)S(1)} fusion(s32[210]{0:T(256)S(1)} %copy-done, s32[2048]{0:T(1024)S(1)} %get-tuple-element.163), kind=kCustom, calls=%fused_computation | custom fusion | bytes 14616 | tf_op jit(solution)/shard_map/gather | solution.py:60
  35.2 7.7 %scatter_custom_fusion = f32[314608]{0:T(1024)S(1)} fusion(s32[1218]{0:T(1024)S(1)} %broadcast_select_fusion, f32[1218]{0:T(1024)} %param.9, f32[]{:T(128)} %constant.69.clone.1), kind=kCustom, calls=%fused_computation.181 | custom fusion | flops 1218 | bytes 1258944
  48.6 45.6 %all-gather.3.cloned.1.call-done = bf16[212,3,2304]{2,1,0:T(4,128)(2,1)} async-done(((bf16[53,3,2304]{2,1,0:T(4,128)(2,1)}), bf16[212,3,2304]{2,1,0:T(4,128)(2,1)}) %all-gather.3.cloned.1.call-update) | async-done | bytes 2930704 | tf_op jit(solution)/shard_map/all_gather | solution.py:74
  94.2 3.7 convolution_convert_fusion.1
  100.3 3.7 collective-permute-start.1
  104.0 2.4 collective-permute-start.2
  108.3 15.6 %collective-permute-done.1 = bf16[7,53,1,2304]{3,1,2,0:T(8,128)(2,1)S(1)} collective-permute-done((bf16[7,53,1,2304]{3,1,2,0:T(8,128)(2,1)S(1)}, bf16[7,53,1,2304]{3,1,2,0:T(8,128)(2,1)S(1)}, u32[]{:S(2)}, u32[]{:S(2)}) %collective-permute-start.1) | collective-permute-done | bytes 1709600 | tf_op jit(solution)/shard_map/ppermute | solution.py:17
  123.9 21.1 %collective-permute-done.2 = bf16[7,53,1,2304]{3,1,2,0:T(8,128)(2,1)} collective-permute-done((bf16[7,53,1,2304]{3,1,2,0:T(8,128)(2,1)S(1)}, bf16[7,53,1,2304]{3,1,2,0:T(8,128)(2,1)}, u32[]{:S(2)}, u32[]{:S(2)}) %collective-permute-start.2) | collective-permute-done | bytes 1709600 | tf_op jit(solution)/shard_map/ppermute | solution.py:20
  144.9 7.8 %pad_maximum_fusion = bf16[7,53,5,2304]{3,1,2,0:T(8,128)(2,1)} fusion(bf16[7,53,1,2304]{3,1,2,0:T(8,128)(2,1)} %collective-permute-done.2, bf16[7,53,3,2304]{3,1,2,0:T(8,128)(2,1)} %copy-done.14, bf16[7,53,1,2304]{3,1,2,0:T(8,128)(2,1)S(1)} %collective-permute-done.1), kind=kLoop, calls=%fused_computation.3 | loop fusion | flops 8547840 | bytes 17095680 | tf_op jit(solution)/shard_map/concatenate | solution.py:21
  152.7 9.2 %fusion.131 = (f32[53,5,2304]{2,0,1:T(8,128)S(1)}, f32[53,5,2304]{2,0,1:T(8,128)}, f32[53,5,2304]{2,0,1:T(8,128)}, f32[53,5,2304]{2,0,1:T(8,128)}, f32[53,5,2304...) fusion(bf16[7,53,5,2304]{3,1,2,0:T(8,128)(2,1)} %pad_maximum_fusion), kind=kLoop, calls=%fused_computation.180 | loop fusion | flops 4273920 | bytes 25643520 | tf_op jit(solution)/shard_map/convert_element_type | solution.py:85
  161.9 2.1 fusion.192
  164.0 2.1 fusion.193
  166.4 2.2 fusion.204
  171.0 2.2 fusion.202
  173.2 2.2 fusion.203
  175.6 2.2 fusion.200
  177.8 2.1 fusion.201
  180.2 2.1 fusion.198
  182.3 2.2 fusion.199
  184.7 2.2 fusion.196
  189.2 2.1 fusion.194
  191.4 2.1 fusion.195
  193.5 30.6 %fusion.69 = bf16[53,3,2304]{2,0,1:T(8,128)(2,1)S(1)} fusion(f32[53,5,2304]{2,0,1:T(8,128)} %get-tuple-element.12, f32[53,5,2304]{2,0,1:T(8,128)} %get-tuple-element.13, f32[53,5,2304]{2,0,1:T(8,128)} %get-tuple-element.14, f32[53,5,2304]{2,0,1:T(8,128)} %get-tuple-element.15, f32[53,5,2304]{2,0,1:T(8,128)} %get-tuple-element.16, ...), kind=kLoop, calls=%fused_computation.91 | loop fusion | flops 56782080 | bytes 73266360 | tf_op jit(solution)/shard_map/convert_element_type | solution.py:87
  225.5 73.3 %all-gather.5.cloned.1.call-done = bf16[212,3,2304]{2,1,0:T(4,128)(2,1)} async-done(((bf16[53,3,2304]{2,1,0:T(4,128)(2,1)}), bf16[212,3,2304]{2,1,0:T(4,128)(2,1)}) %all-gather.5.cloned.1.call-update) | async-done | bytes 2930704 | tf_op jit(solution)/shard_map/all_gather | solution.py:74
  298.8 3.9 convolution_convert_fusion
  302.9 2.1 copy-done.15
  305.0 3.7 collective-permute-start.4
  308.7 2.1 collective-permute-start.5
  310.8 17.7 %collective-permute-done.4 = bf16[7,53,1,2304]{3,1,2,0:T(8,128)(2,1)S(1)} collective-permute-done((bf16[7,53,1,2304]{3,1,2,0:T(8,128)(2,1)S(1)}, bf16[7,53,1,2304]{3,1,2,0:T(8,128)(2,1)S(1)}, u32[]{:S(2)}, u32[]{:S(2)}) %collective-permute-start.4) | collective-permute-done | bytes 1709600 | tf_op jit(solution)/shard_map/ppermute | solution.py:17
  328.5 21.1 %collective-permute-done.5 = bf16[7,53,1,2304]{3,1,2,0:T(8,128)(2,1)} collective-permute-done((bf16[7,53,1,2304]{3,1,2,0:T(8,128)(2,1)S(1)}, bf16[7,53,1,2304]{3,1,2,0:T(8,128)(2,1)}, u32[]{:S(2)}, u32[]{:S(2)}) %collective-permute-start.5) | collective-permute-done | bytes 1709600 | tf_op jit(solution)/shard_map/ppermute | solution.py:20
  349.6 7.8 %pad_maximum_fusion.1 = bf16[7,53,5,2304]{3,1,2,0:T(8,128)(2,1)} fusion(bf16[7,53,1,2304]{3,1,2,0:T(8,128)(2,1)} %collective-permute-done.5, bf16[7,53,3,2304]{3,1,2,0:T(8,128)(2,1)} %copy-done.15, bf16[7,53,1,2304]{3,1,2,0:T(8,128)(2,1)S(1)} %collective-permute-done.4), kind=kLoop, calls=%fused_computation.4 | loop fusion | flops 8547840 | bytes 17095680 | tf_op jit(solution)/shard_map/concatenate | solution.py:21
  357.4 9.2 %fusion.124 = (f32[53,5,2304]{2,0,1:T(8,128)S(1)}, f32[53,5,2304]{2,0,1:T(8,128)}, f32[53,5,2304]{2,0,1:T(8,128)}, f32[53,5,2304]{2,0,1:T(8,128)}, f32[53,5,2304...) fusion(bf16[7,53,5,2304]{3,1,2,0:T(8,128)(2,1)} %pad_maximum_fusion.1), kind=kLoop, calls=%fused_computation.166 | loop fusion | flops 4273920 | bytes 25643520 | tf_op jit(solution)/shard_map/convert_element_type | solution.py:85
  366.6 2.1 fusion.178
  368.7 2.1 fusion.179
  371.1 2.2 fusion.190
  375.7 2.2 fusion.188
  377.9 2.2 fusion.189
  380.3 2.2 fusion.186
  382.5 2.1 fusion.187
  384.9 2.1 fusion.184
  387.0 2.2 fusion.185
  389.4 2.2 fusion.182
  393.9 2.1 fusion.180
  396.3 2.1 fusion.181
  398.6 31.3 %fusion.12 = bf16[53,3,2304]{2,0,1:T(8,128)(2,1)} fusion(f32[53,5,2304]{2,0,1:T(8,128)} %get-tuple-element.5, f32[53,5,2304]{2,0,1:T(8,128)} %get-tuple-element.6, f32[53,5,2304]{2,0,1:T(8,128)} %get-tuple-element.7, f32[53,5,2304]{2,0,1:T(8,128)} %get-tuple-element.8, f32[53,5,2304]{2,0,1:T(8,128)} %get-tuple-element.9, ...), kind=kLoop, calls=%fused_computation.20 | loop fusion | flops 56782080 | bytes 73266360 | tf_op jit(solution)/shard_map/convert_element_type | solution.py:87
  (136 shorter events, 27.7 us)
Async XLA Ops:
  7.2 11.8 %copy-start = (s32[210]{0:T(256)S(1)}, s32[210]{0:T(256)}, u32[]{:S(2)}) copy-start(s32[210]{0:T(256)} %param.11) | copy-start | bytes 2524
  7.2 87.0 %all-gather.3.cloned.1.call-start = ((), (), s32[]{:S(2)}) async-start(), calls=%async_computation | async-start | bytes 4884480 | tf_op jit(solution)/shard_map/all_gather | solution.py:74
  7.2 10.2 %copy-start.18 = (f32[3,2304]{1,0:T(4,128)S(1)}, f32[3,2304]{1,0:T(4,128)}, u32[]{:S(2)}) copy-start(f32[3,2304]{1,0:T(4,128)} %param.7) | copy-start | bytes 82948
  8.4 10.4 %copy-start.45 = (s32[1218,3]{0,1:T(4,128)S(1)}, s32[1218,3]{0,1:T(4,128)}, u32[]{:S(2)}) copy-start(s32[1218,3]{0,1:T(4,128)} %param.10) | copy-start | bytes 43852
  8.4 36.2 %collective-permute-start = (f32[7,1,2304]{2,1,0:T(1,128)S(1)}, f32[7,1,2304]{2,1,0:T(1,128)S(1)}, u32[]{:S(2)}, u32[]{:S(2)}) collective-permute-start(f32[7,1,2304]{2,1,0:T(1,128)S(1)} %get-tuple-element.94), channel_id=1, source_target_pairs={{1,0},{2,1},{3,2},{4,3},{5,4},{6,5},{7,6},{9,8},{10,9},{11,10},{12... | collective-permute-start | bytes 193544 | tf_op jit(solution)/shard_map/ppermute | solution.py:20
  10.4 34.3 %collective-permute-start.3 = (f32[7,1,2304]{2,1,0:T(1,128)S(1)}, f32[7,1,2304]{2,1,0:T(1,128)S(1)}, u32[]{:S(2)}, u32[]{:S(2)}) collective-permute-start(f32[7,1,2304]{2,1,0:T(1,128)S(1)} %get-tuple-element.95), channel_id=1, source_target_pairs={{0,1},{1,2},{2,3},{3,4},{4,5},{5,6},{6,7},{8,9},{9,10},{10,11},{11... | collective-permute-start | bytes 193544 | tf_op jit(solution)/shard_map/ppermute | solution.py:17
  17.4 281.4 %all-gather.5.cloned.1.call-start = ((), (), s32[]{:S(2)}) async-start(), calls=%async_computation.1 | async-start | bytes 4884480 | tf_op jit(solution)/shard_map/all_gather | solution.py:74
  26.9 8.0 %copy-start.47 = (s32[3]{0:T(128)S(1)}, s32[3]{0:T(128)}, u32[]{:S(2)}) copy-start(s32[3]{0:T(128)} %constant.253) | copy-start | bytes 40
  27.0 8.1 %copy-start.46 = (s32[3]{0:T(128)S(1)}, s32[3]{0:T(128)}, u32[]{:S(2)}) copy-start(s32[3]{0:T(128)} %constant.250) | copy-start | bytes 40
  44.6 49.6 %copy-start.19 = (bf16[7,212,212]{2,1,0:T(8,128)(2,1)}, bf16[7,212,212]{2,1,0:T(8,128)(2,1)S(1)}, u32[]{:S(2)}) copy-start(bf16[7,212,212]{2,1,0:T(8,128)(2,1)S(1)} %reshape.112) | copy-start | bytes 1887652
  97.9 2.4 copy-start.14
  97.9 8.6 %copy-start.41 = (f32[3,2303]{1,0:T(4,128)S(1)}, f32[3,2303]{1,0:T(4,128)}, u32[]{:S(2)}) copy-start(f32[3,2303]{1,0:T(4,128)} %get-tuple-element.129) | copy-start | bytes 82912
  98.0 8.6 %copy-start.42 = (f32[3,2303]{1,0:T(4,128)S(1)}, f32[3,2303]{1,0:T(4,128)}, u32[]{:S(2)}) copy-start(f32[3,2303]{1,0:T(4,128)} %get-tuple-element.130) | copy-start | bytes 82912
  98.0 8.6 %copy-start.43 = (f32[3,2256]{1,0:T(4,128)S(1)}, f32[3,2256]{1,0:T(4,128)}, u32[]{:S(2)}) copy-start(f32[3,2256]{1,0:T(4,128)} %get-tuple-element.132) | copy-start | bytes 81220
  98.0 8.6 %copy-start.44 = (f32[3,2256]{1,0:T(4,128)S(1)}, f32[3,2256]{1,0:T(4,128)}, u32[]{:S(2)}) copy-start(f32[3,2256]{1,0:T(4,128)} %get-tuple-element.133) | copy-start | bytes 81220
  100.3 23.5 %collective-permute-start.1 = (bf16[7,53,1,2304]{3,1,2,0:T(8,128)(2,1)S(1)}, bf16[7,53,1,2304]{3,1,2,0:T(8,128)(2,1)S(1)}, u32[]{:S(2)}, u32[]{:S(2)}) collective-permute-start(bf16[7,53,1,2304]{3,1,2,0:T(8,128)(2,1)S(1)} %get-tuple-element.20), channel_id=1, source_target_pairs={{0,1},{1,2},{2,3},{3,4},{4,5},{5,6},{6,7},{8,9},{9,10},{10,11},{11... | collective-permute-start | bytes 5128712 | tf_op jit(solution)/shard_map/ppermute | solution.py:17
  104.0 40.9 %collective-permute-start.2 = (bf16[7,53,1,2304]{3,1,2,0:T(8,128)(2,1)S(1)}, bf16[7,53,1,2304]{3,1,2,0:T(8,128)(2,1)}, u32[]{:S(2)}, u32[]{:S(2)}) collective-permute-start(bf16[7,53,1,2304]{3,1,2,0:T(8,128)(2,1)S(1)} %get-tuple-element.21), channel_id=1, source_target_pairs={{1,0},{2,1},{3,2},{4,3},{5,4},{6,5},{7,6},{9,8},{10,9},{11,10},{12... | collective-permute-start | bytes 5128712 | tf_op jit(solution)/shard_map/ppermute | solution.py:20
  164.0 2.4 copy-start.8
  168.6 2.4 copy-start.9
  173.2 2.4 copy-start.10
  177.8 2.4 copy-start.11
  182.3 2.4 copy-start.12
  186.8 2.4 copy-start.13
  224.1 78.5 %copy-start.17 = (bf16[53,3,2304]{2,0,1:T(8,128)(2,1)}, bf16[53,3,2304]{2,0,1:T(8,128)(2,1)S(1)}, u32[]{:S(2)}) copy-start(bf16[53,3,2304]{2,0,1:T(8,128)(2,1)S(1)} %fusion.69) | copy-start | bytes 2198020
  302.6 2.4 copy-start.15
  305.0 23.5 %collective-permute-start.4 = (bf16[7,53,1,2304]{3,1,2,0:T(8,128)(2,1)S(1)}, bf16[7,53,1,2304]{3,1,2,0:T(8,128)(2,1)S(1)}, u32[]{:S(2)}, u32[]{:S(2)}) collective-permute-start(bf16[7,53,1,2304]{3,1,2,0:T(8,128)(2,1)S(1)} %get-tuple-element.18), channel_id=1, source_target_pairs={{0,1},{1,2},{2,3},{3,4},{4,5},{5,6},{6,7},{8,9},{9,10},{10,11},{11... | collective-permute-start | bytes 5128712 | tf_op jit(solution)/shard_map/ppermute | solution.py:17
  308.7 40.9 %collective-permute-start.5 = (bf16[7,53,1,2304]{3,1,2,0:T(8,128)(2,1)S(1)}, bf16[7,53,1,2304]{3,1,2,0:T(8,128)(2,1)}, u32[]{:S(2)}, u32[]{:S(2)}) collective-permute-start(bf16[7,53,1,2304]{3,1,2,0:T(8,128)(2,1)S(1)} %get-tuple-element.19), channel_id=1, source_target_pairs={{1,0},{2,1},{3,2},{4,3},{5,4},{6,5},{7,6},{9,8},{10,9},{11,10},{12... | collective-permute-start | bytes 5128712 | tf_op jit(solution)/shard_map/ppermute | solution.py:20
  368.7 2.4 copy-start.2
  373.3 2.4 copy-start.3
  377.9 2.4 copy-start.4
  382.5 2.4 copy-start.5
  387.0 2.4 copy-start.6
  391.5 2.4 copy-start.7
  396.1 2.3 copy-start.24
  396.1 2.3 copy-start.25
  396.1 2.3 copy-start.26
  396.1 2.3 copy-start.27
  396.1 2.3 copy-start.28
  396.1 2.3 copy-start.29
  396.2 2.3 copy-start.30
  396.2 2.3 copy-start.31
  396.2 2.3 copy-start.32
  396.2 2.3 copy-start.33
  396.2 2.3 copy-start.34
  396.2 2.3 copy-start.35
  396.2 2.3 copy-start.36
  396.2 2.3 copy-start.37
  398.6 31.4 %copy-start.1 = (s32[210]{0:T(256)S(1)}, s32[210]{0:T(256)}, u32[]{:S(2)}) copy-start(s32[210]{0:T(256)} %param.11) | copy-start | bytes 2524
  (8 other events, 18.0 us)
Sparse Core Ops, SparseCore 0:
  17.5 76.6 all-gather.2
  225.6 73.1 all-gather.4
where the time goes:
time: 444 us; the launch traced here: 437 us
  waiting for transfers between devices  194 us (44%)
  other arithmetic  110 us (25%)
  local copies, waits for them, and re-layouts  91.4 us (21%)
  starting transfers between devices  18.4 us (4%)
  between operations  15.1 us (3%)
  matrix products  7.58 us (2%)
    all_gather x2, waiting for transfers between devices, combine(): lax.all_gather(own_panels, 'chaos', axis=0, tiled=True)  119 us
    slice x36, local copies, waits for them, and re-layouts, shifted(): moved_values = jnp.pad(source[..., offset:], padding + [(0, offset)])  62.3 us
    convert_element_type x2, other arithmetic, galerkin_apply(): return (scale_factor * result).astype(jnp.bfloat16)  61.9 us
    ppermute x3, waiting for transfers between devices, padded(): lax.ppermute(lax.slice_in_dim(block, 0, width, axis=dim), axis, backward)  42.2 us
    ppermute x3, waiting for transfers between devices, padded(): lax.ppermute(lax.slice_in_dim(block, block.shape[dim] - width, None, axis...  33.3 us
    convert_element_type x2, other arithmetic, galerkin_apply(): combined[field_index].astype(jnp.float32)  18.4 us
    concatenate x3, other arithmetic, padded(): block = jnp.concatenate([low, block, high], axis=dim)  15.8 us
    ppermute x3, starting transfers between devices, padded(): lax.ppermute(lax.slice_in_dim(block, block.shape[dim] - width, None, axis...  11.8 us
  transfers between devices with their start and end apart: 8, of which 6 were waited for; matrix products, arithmetic and copies ran while one was open for 8% of the time, Pallas kernels for 0%

commit v1 on v0

v1 whole, which is shorter than its diff:
```python
import functools

import jax
import jax.numpy as jnp
from jax import lax
from jax.experimental import pallas as pl
from jax.experimental.pallas import tpu as pltpu
from jax.sharding import PartitionSpec as P

NXY = 48
SCALE = 0.15
LANES = 128
REACH = 2
BLOCK = 32
VMEM = pltpu.VMEM
F32, BF16 = jnp.float32, jnp.bfloat16


def up(value, step):
    return -(-value // step) * step


def params(megabytes):
    return pltpu.CompilerParams(vmem_limit_bytes=megabytes << 20)


def whole(count):
    return [pl.BlockSpec(memory_space=VMEM)] * count


def cut_kernel(count, chunk, me_ref, x_ref, *refs):
    *out_refs, held = refs
    planes, own, cells = x_ref.shape
    padded, width = out_refs[0].shape[1:]
    halo = REACH * NXY
    me = me_ref[0]
    held[...] = jnp.zeros_like(held)
    lane = lax.broadcasted_iota(jnp.int32, (padded, LANES), 1)
    for plane in range(planes):
        held[0:own, :] = x_ref[plane].astype(F32)
        values = held[...]
        for target in range(count):
            turned = values if target == 0 else pltpu.roll(values, cells - target * chunk, 1)
            body = turned[:, : up(chunk + halo, LANES)]
            column = lax.broadcasted_iota(jnp.int32, body.shape, 1)
            end = chunk if target == count - 1 else chunk + halo
            body = jnp.where(column < end, body, 0.0)
            if body.shape[1] < width:
                body = jnp.concatenate([body, jnp.zeros((padded, width - body.shape[1]), F32)], axis=1)
            before = turned[:, cells - LANES :]
            if target == 0:
                before = jnp.zeros_like(before)
            last = jnp.where(lane < LANES - halo, body[:, width - LANES :], before)
            window = jnp.concatenate([body[:, : width - LANES], last], axis=1).astype(BF16)
            for step in range(count):

                @pl.when(lax.bitwise_xor(me, target) == step)
                def _():
                    out_refs[step][plane] = window


def tables_kernel(fields, entries_ref, products_ref, slots_ref, out_ref, by_column):
    rows = by_column.shape[1]
    total = entries_ref.shape[1]
    names = slots_ref.shape[1]
    slots = slots_ref[...].astype(BF16)

    def placed(which):
        name = lax.broadcasted_iota(jnp.int32, (names, total), 0)
        chosen = jnp.where(name == entries_ref[which : which + 1, :], 1.0, 0.0).astype(BF16)
        return jnp.dot(slots, chosen, preferred_element_type=F32)[0:1].astype(jnp.int32)

    row, column = placed(0), placed(1)
    field = entries_ref[2:3, :]
    place = (row // BLOCK) * (fields * BLOCK) + field * BLOCK + row % BLOCK
    rest = products_ref[0:1, :]
    here = lax.broadcasted_iota(jnp.int32, (rows, total), 0) == column
    for part in range(3):
        piece = rest.astype(BF16).astype(F32)
        rest = rest - piece
        by_column[part] = jnp.where(here, piece, 0.0).astype(BF16)
    size = fields * BLOCK

    @pl.loop(0, rows // BLOCK)
    def _(block):
        index = lax.broadcasted_iota(jnp.int32, (size, total), 0) + block * size
        chosen = jnp.where(index == place, 1.0, 0.0).astype(BF16)
        acc = jnp.zeros((size, rows), F32)
        for part in range(3):
            acc += lax.dot_general(
                chosen, by_column[part], (((1,), (1,)), ((), ())), preferred_element_type=F32
            )
        out_ref[pl.ds(pl.multiple_of(block * size, size), size), :] = acc.astype(BF16)


def load_planes(piece_refs, before_ref, after_ref, store):
    planes = piece_refs[0].shape[0]

    def joined(parts):
        return jnp.concatenate([p.astype(F32) for p in parts], axis=0).astype(BF16)

    store[0] = joined([before_ref[i] for i in range(len(piece_refs))])
    for plane in range(planes):
        store[plane + 1] = joined([piece[plane] for piece in piece_refs])
    store[planes + 1] = joined([after_ref[i] for i in range(len(piece_refs))])


def apply_kernel(count, final, *refs):
    piece_refs = refs[:count]
    before_ref, after_ref, tables_ref, weights_ref, masks_ref = refs[count : count + 5]
    if final:
        out_refs = refs[count + 5 : 2 * count + 5]
        held, mixed, weights, result = refs[2 * count + 5 :]
    else:
        out_refs = refs[count + 5 : 2 * count + 5]
        own_refs = refs[2 * count + 5 : 3 * count + 5]
        edge_refs = refs[3 * count + 5 : 3 * count + 7]
        held, mixed, weights, result = refs[3 * count + 7 :]
    planes, padded, width = piece_refs[0].shape
    rows = count * padded
    fields = weights_ref.shape[1]
    load_planes(piece_refs, before_ref, after_ref, held)
    for plane in range(weights_ref.shape[0]):
        for field in range(fields):
            for way in range(6):
                weights[plane, field, way] = jnp.broadcast_to(
                    weights_ref[plane, field, way : way + 1, :], (8, width)
                )
    result[...] = jnp.zeros_like(result)
    size = fields * BLOCK

    def spread(value):
        return jnp.broadcast_to(value[None], (BLOCK // 8, 8, width)).reshape(BLOCK, width)

    for plane in range(planes + 2):
        mixed[...] = jnp.dot(tables_ref[...], held[plane], preferred_element_type=F32).astype(BF16)

        @pl.loop(0, rows // BLOCK)
        def _(block):
            start = pl.multiple_of(block * BLOCK, BLOCK)
            base = pl.multiple_of(block * size, size)

            def sums(ways):
                totals = [jnp.zeros((BLOCK, width), F32) for _ in ways]
                for field in range(fields):
                    values = mixed[pl.ds(base + field * BLOCK, BLOCK), :].astype(F32)
                    for i, way in enumerate(ways):
                        totals[i] += spread(weights[plane, field, way]) * values
                return totals

            here = pl.ds(start, BLOCK)
            if 0 < plane < planes + 1:
                ahead, behind = sums((0, 1))
                flux = ahead + behind - pltpu.roll(behind, width - NXY, 1) - pltpu.roll(ahead, NXY, 1)
                ahead, behind = sums((2, 3))
                flux += ahead + behind
                flux -= spread(masks_ref[0]) * pltpu.roll(behind, width - 1, 1)
                flux -= spread(masks_ref[1]) * pltpu.roll(ahead, 1, 1)
                ahead, behind = sums((4, 5))
                result[plane - 1, here, :] += flux + ahead + behind
                if plane < planes:
                    result[plane, here, :] -= ahead
                if plane > 1:
                    result[plane - 2, here, :] -= behind
            elif plane == 0:
                (ahead,) = sums((4,))
                result[0, here, :] -= ahead
            else:
                (behind,) = sums((5,))
                result[planes - 1, here, :] -= behind

    chunk = out_refs[0].shape[2]
    for plane in range(planes):
        values = SCALE * result[plane]
        if not final:
            values = values * jnp.broadcast_to(masks_ref[2][None], (rows // 8, 8, width)).reshape(rows, width)
        for step in range(count):
            part = values[step * padded : (step + 1) * padded]
            out_refs[step][plane] = part[:, :chunk].astype(BF16)
            if not final:
                own_refs[step][plane] = part.astype(BF16)
                if plane == 0:
                    edge_refs[0][step] = part.astype(BF16)
                if plane == planes - 1:
                    edge_refs[1][step] = part.astype(BF16)


def join_kernel(count, me_ref, *refs):
    piece_refs, (out_ref, held) = refs[:count], refs[count:]
    planes, own, cells = out_ref.shape
    chunk = piece_refs[0].shape[2]
    me = me_ref[0]
    for step in range(count):
        held[lax.bitwise_xor(me, step)] = piece_refs[step][...].astype(F32)
    for plane in range(planes):
        line = jnp.concatenate([held[source, plane][:, :chunk] for source in range(count)], axis=1)
        out_ref[plane] = line[:own].astype(BF16)


def shards(panels, mean_field, fluctuations, products, triples, owner_slot):
    count, slabs = lax.axis_size("chaos"), lax.axis_size("space")
    me = lax.axis_index("chaos")
    own, planes, cells = panels.shape
    chunk, halo = cells // count, REACH * NXY
    width = up(chunk + 2 * halo, LANES)
    padded = up(own, 8)
    rows = count * padded
    fields = 1 + fluctuations.shape[0]
    me_array = me.astype(jnp.int32).reshape(1)
    smem = pl.BlockSpec(memory_space=pltpu.SMEM)

    def exchange(block, step):
        return lax.ppermute(block, "chaos", [(i, i ^ step) for i in range(count)])

    def neighbours(first_plane, last_plane):
        upward = [(i, i + 1) for i in range(slabs - 1)]
        downward = [(target, source) for source, target in upward]
        return lax.ppermute(last_plane, "space", upward), lax.ppermute(first_plane, "space", downward)

    piece = jax.ShapeDtypeStruct((planes, padded, width), BF16)
    cut = pl.pallas_call(
        functools.partial(cut_kernel, count, chunk),
        out_shape=[piece] * count,
        in_specs=[smem] + whole(1),
        out_specs=whole(count),
        scratch_shapes=[VMEM((padded, cells), F32)],
        compiler_params=params(32),
        name="cut",
    )(me_array, jnp.transpose(panels, (1, 0, 2)))
    pieces = [cut[0]] + [exchange(cut[step], step) for step in range(1, count)]

    coefficients = jnp.concatenate([mean_field[None], fluctuations], axis=0)
    before, after = neighbours(coefficients[:, 0], coefficients[:, -1])
    coefficients = jnp.concatenate([before[:, None], coefficients, after[:, None]], axis=1)

    def window(array):
        array = jnp.pad(array, ((0, 0),) * (array.ndim - 1) + ((halo, halo),))
        array = lax.dynamic_slice_in_dim(array, me * chunk, chunk + 2 * halo, array.ndim - 1)
        gap = jnp.zeros(array.shape[:-1] + (width - chunk - 2 * halo,), array.dtype)
        return jnp.concatenate([array[..., halo:], gap, array[..., :halo]], axis=-1)

    conduct = window(coefficients)
    lane_grid = window(jnp.where(jnp.arange(cells) >= 0, jnp.arange(cells) % NXY, 0) + 1)
    not_last = jnp.where(lane_grid == NXY, 0.0, 1.0)
    not_first = jnp.where(lane_grid == 1, 0.0, 1.0)
    inside = jnp.where(lane_grid > 0, 1.0, 0.0)
    masks = jnp.broadcast_to(jnp.stack([not_last, not_first, inside])[:, None], (3, 8, width))
    middle = conduct[:, 1:-1]
    ways = [
        jnp.roll(middle, -NXY, -1),
        jnp.roll(middle, NXY, -1),
        jnp.roll(middle, -1, -1) * not_last,
        jnp.roll(middle, 1, -1) * not_first,
    ]
    zeros = jnp.zeros_like(middle[:, :1])
    faces = [jnp.pad(0.5 * (middle + way), ((0, 0), (1, 1), (0, 0))) for way in ways]
    rising = 0.5 * (conduct[:, :-1] + conduct[:, 1:])
    faces += [jnp.concatenate([rising, zeros], axis=1), jnp.concatenate([zeros, rising], axis=1)]
    weights = jnp.stack(faces, axis=0).transpose(2, 1, 0, 3)

    total = up(products.shape[0], 2 * LANES)
    names = up(owner_slot.shape[0], LANES)
    entries = jnp.pad(triples.T, ((0, 5), (0, total - products.shape[0])), constant_values=-1)
    values = jnp.pad(products, (0, total - products.shape[0]))[None]
    group = owner_slot // own
    slots = lax.bitwise_xor(group, me) * padded + owner_slot - group * own
    slots = jnp.broadcast_to(jnp.pad(slots, (0, names - slots.shape[0])).astype(F32)[None], (16, names))
    tables = pl.pallas_call(
        functools.partial(tables_kernel, fields),
        out_shape=jax.ShapeDtypeStruct((fields * rows, rows), BF16),
        in_specs=whole(3),
        out_specs=whole(1)[0],
        scratch_shapes=[VMEM((3, rows, total), BF16)],
        compiler_params=params(32),
        name="tables",
    )(entries, values, slots)

    def apply(parts, first_halo, last_halo, final):
        short = jax.ShapeDtypeStruct((planes, padded, chunk), BF16)
        out_shape = [short] * count
        if not final:
            edge = jax.ShapeDtypeStruct((count, padded, width), BF16)
            out_shape += [piece] * count + [edge, edge]
        return pl.pallas_call(
            functools.partial(apply_kernel, count, final),
            out_shape=out_shape,
            in_specs=whole(count + 5),
            out_specs=whole(len(out_shape)),
            scratch_shapes=[
                VMEM((planes + 2, rows, width), BF16),
                VMEM((fields * rows, width), BF16),
                VMEM((planes + 2, fields, 6, 8, width), F32),
                VMEM((planes, rows, width), F32),
            ],
            compiler_params=params(48),
            name="second" if final else "first",
        )(*parts, first_halo, last_halo, tables, weights, masks)

    def join(parts):
        joined = pl.pallas_call(
            functools.partial(join_kernel, count),
            out_shape=jax.ShapeDtypeStruct((planes, own, cells), BF16),
            in_specs=[smem] + whole(count),
            out_specs=whole(1)[0],
            scratch_shapes=[VMEM((count, planes, padded, chunk), F32)],
            compiler_params=params(32),
            name="join",
        )(me_array, *parts)
        return jnp.transpose(joined, (1, 0, 2))

    def back(parts):
        return [parts[0]] + [exchange(parts[step], step) for step in range(1, count)]

    low, high = neighbours(jnp.stack([p[0] for p in pieces]), jnp.stack([p[-1] for p in pieces]))
    first = apply(pieces, low, high, False)
    low, high = neighbours(first[-2], first[-1])
    second = apply(first[count : 2 * count], low, high, True)
    return join(back(first[:count])), join(back(second))


def solution(mesh):
    in_specs = (P("chaos", "space", None), P("space", None), P(None, "space", None), P(), P(), P())
    out_specs = (P("chaos", "space", None), P("chaos", "space", None))
    return jax.shard_map(shards, mesh=mesh, in_specs=in_specs, out_specs=out_specs, check_vma=False)
```

time: 444 us -> 117 us (0.26)
  the two profiles are of different devices: /device:TPU:1 before, /device:TPU:11 now
where the time goes in v1:
time: 117 us; the launch traced here: 116 us
  Pallas kernels  39.2 us (34%)
  waiting for transfers between devices  37.1 us (32%)
  starting transfers between devices  25 us (21%)
  local copies, waits for them, and re-layouts  11.7 us (10%)
  other arithmetic  2.41 us (2%)
    pallas_call x2, Pallas kernels, apply(): pl.pallas_call(functools.partial(apply_kernel, count, final), out_shape=o...  30.8 us
    ppermute x9, waiting for transfers between devices, exchange(): return lax.ppermute(block, 'chaos', [(i, i ^ step) for i in range(count)])  30.7 us
    ppermute x3, starting transfers between devices, neighbours(): lax.ppermute(last_plane, 'space', upward)  10.2 us
    ppermute x9, starting transfers between devices, exchange(): return lax.ppermute(block, 'chaos', [(i, i ^ step) for i in range(count)])  8.25 us
    another operation x10, local copies, waits for them, and re-layouts, shards(): weights = jnp.stack(faces, axis=0).transpose(2, 1, 0, 3)  7.24 us
    ppermute x3, starting transfers between devices, neighbours(): lax.ppermute(first_plane, 'space', downward)  6.59 us
    ppermute x3, waiting for transfers between devices, neighbours(): lax.ppermute(first_plane, 'space', downward)  5.2 us
    pallas_call x1, Pallas kernels, shards(): pl.pallas_call(functools.partial(tables_kernel, fields), out_shape=jax.Sh...  5.14 us
  transfers between devices with their start and end apart: 15, of which 8 were waited for; matrix products, arithmetic and copies ran while one was open for 8% of the time, Pallas kernels for 19%

profile of v1, /device:TPU:11, one launch (start us, length us, event | category | flops | bytes accessed | tf_op | source)
XLA Modules:
  0.0 116.4 jit_solution(14668243840928976850)
XLA Ops:
  0.6 0.9 broadcast_in_dim.47
  1.5 1.0 copy.8
  2.5 0.7 copy-done.1
  3.2 2.6 %collective-permute-start.6 = (f32[7,2304]{1,0:T(8,128)S(1)}, f32[7,2304]{1,0:T(8,128)S(1)}, u32[]{:S(2)}, u32[]{:S(2)}) collective-permute-start(f32[7,2304]{1,0:T(8,128)S(1)} %get-tuple-element.50), channel_id=1, source_target_pairs={{1,0},{2,1},{3,2},{4,3},{5,4},{6,5},{7,6},{9,8},{10,9},{11,10},{12... | collective-permute-start | bytes 193544 | tf_op jit(solution)/shard_map/ppermute | solution.py:218
  5.8 3.9 %collective-permute-start.5 = (f32[7,2304]{1,0:T(8,128)S(1)}, f32[7,2304]{1,0:T(8,128)S(1)}, u32[]{:S(2)}, u32[]{:S(2)}) collective-permute-start(f32[7,2304]{1,0:T(8,128)S(1)} %get-tuple-element.51), channel_id=1, source_target_pairs={{0,1},{1,2},{2,3},{3,4},{4,5},{5,6},{6,7},{8,9},{9,10},{10,11},{11... | collective-permute-start | bytes 193544 | tf_op jit(solution)/shard_map/ppermute | solution.py:218
  9.7 0.8 cut.1
  10.6 0.2 collective-permute-start
  10.8 2.3 %collective-permute-start.1 = (bf16[3,56,768]{2,1,0:T(8,128)(2,1)S(1)}, bf16[3,56,768]{2,1,0:T(8,128)(2,1)S(1)}, u32[]{:S(2)}, u32[]{:S(2)}) collective-permute-start(bf16[3,56,768]{2,1,0:T(8,128)(2,1)S(1)} %get-tuple-element.22), channel_id=1, source_target_pairs={{0,16},{8,24},{16,0},{24,8},{1,17},{9,25},{17,1},{25,9},{2,18},{10... | collective-permute-start | bytes 774152 | tf_op jit(solution)/shard_map/ppermute | solution.py:213
  13.1 0.2 collective-permute-start.2
  13.3 0.1 pad_dynamic-slice_fusion.4
  13.4 0.6 copy-done.6
  14.3 0.7 copy-done.4
  15.0 5.1 %tables.1.refs_6_ = bf16[1568,224]{1,0:T(8,128)(2,1)S(1)} custom-call(s32[8,1280]{1,0:T(8,128)S(1)} %pad.35.entries_ref, f32[1,1280]{1,0:T(1,128)S(1)} %broadcast_in_dim.45.products_ref, f32[16,256]{1,0:T(8,128)S(1)} %broadcast_in_dim.46.slots_ref), custom_call_target="tpu_custom_call" | custom-call | tf_op jit(solution)/shard_map/tables/pallas_call | solution.py:268
  20.2 0.1 fusion.3
  20.5 0.1 slice.130
  20.7 0.1 fusion.16
  20.8 0.1 fusion.15
  20.9 0.1 fusion.24
  21.0 0.1 fusion.22
  21.2 0.7 stack.40
  21.9 0.7 copy.13
  22.6 7.6 %collective-permute-done.1.refs_2_ = bf16[3,56,768]{2,1,0:T(8,128)(2,1)S(1)} collective-permute-done((bf16[3,56,768]{2,1,0:T(8,128)(2,1)S(1)}, bf16[3,56,768]{2,1,0:T(8,128)(2,1)S(1)}, u32[]{:S(2)}, u32[]{:S(2)}) %collective-permute-start.1) | collective-permute-done | bytes 258080 | tf_op jit(solution)/shard_map/ppermute | solution.py:213
  30.2 5.5 %collective-permute-done.2.refs_3_ = bf16[3,56,768]{2,1,0:T(8,128)(2,1)S(1)} collective-permute-done((bf16[3,56,768]{2,1,0:T(8,128)(2,1)S(1)}, bf16[3,56,768]{2,1,0:T(8,128)(2,1)S(1)}, u32[]{:S(2)}, u32[]{:S(2)}) %collective-permute-start.2) | collective-permute-done | bytes 258080 | tf_op jit(solution)/shard_map/ppermute | solution.py:213
  35.7 0.8 pad_maximum_fusion
  36.5 3.5 %collective-permute-start.3 = (bf16[4,56,768]{2,1,0:T(8,128)(2,1)}, bf16[4,56,768]{2,1,0:T(8,128)(2,1)S(1)}, u32[]{:S(2)}, u32[]{:S(2)}) collective-permute-start(bf16[4,56,768]{2,1,0:T(8,128)(2,1)} %pad_maximum_fusion), channel_id=1, source_target_pairs={{0,1},{1,2},{2,3},{3,4},{4,5},{5,6},{6,7},{8,9},{9,10},{10,11},{11... | collective-permute-start | bytes 1032200 | tf_op jit(solution)/shard_map/ppermute | solution.py:218
  40.0 0.8 pad_maximum_fusion.1
  40.8 1.9 %collective-permute-start.4 = (bf16[4,56,768]{2,1,0:T(8,128)(2,1)}, bf16[4,56,768]{2,1,0:T(8,128)(2,1)S(1)}, u32[]{:S(2)}, u32[]{:S(2)}) collective-permute-start(bf16[4,56,768]{2,1,0:T(8,128)(2,1)} %pad_maximum_fusion.1), channel_id=1, source_target_pairs={{1,0},{2,1},{3,2},{4,3},{5,4},{6,5},{7,6},{9,8},{10,9},{11,10},{12... | collective-permute-start | bytes 1032200 | tf_op jit(solution)/shard_map/ppermute | solution.py:218
  42.7 0.8 copy.12
  43.5 0.8 copy.11
  44.3 0.8 copy.10
  45.0 0.8 copy.9
  45.8 0.1 copy-done.3
  45.9 2.7 %stack.41 = f32[6,7,5,768]{3,0,1,2:T(8,128)S(1)} concatenate(f32[1,7,5,768]{3,0,1,2:T(1,128)} %copy.9, f32[1,7,5,768]{3,0,1,2:T(1,128)} %copy.10, f32[1,7,5,768]{3,0,1,2:T(1,128)} %copy.11, f32[1,7,5,768]{3,0,1,2:T(1,128)} %copy.12, f32[1,7,5,768]{3,0,1,2:T(1,128)} %copy.13, f32[1,7,5,768]{3,0,1,2:T(1,128)S(1)} %copy-done.3), dimensions={0} | concatenate | bytes 1290240 | tf_op jit(solution)/shard_map/stack | solution.py:259
  48.7 1.8 %collective-permute-done.4.refs_5_ = bf16[4,56,768]{2,1,0:T(8,128)(2,1)S(1)} collective-permute-done((bf16[4,56,768]{2,1,0:T(8,128)(2,1)}, bf16[4,56,768]{2,1,0:T(8,128)(2,1)S(1)}, u32[]{:S(2)}, u32[]{:S(2)}) %collective-permute-start.4) | collective-permute-done | bytes 344096 | tf_op jit(solution)/shard_map/ppermute | solution.py:218
  50.5 15.5 %first.1 = (bf16[3,56,576]{2,1,0:T(8,128)(2,1)S(1)}, bf16[3,56,576]{2,1,0:T(8,128)(2,1)S(1)}, bf16[3,56,576]{2,1,0:T(8,128)(2,1)S(1)}, bf16[3,56,576]{2,1,0:T(8,...) custom-call(bf16[3,56,768]{2,1,0:T(8,128)(2,1)S(1)} %get-tuple-eleme, ...), custom_call_target="tpu_custom_call" | custom-call | tf_op jit(solution)/shard_map/first/pallas_call | solution.py:284
  65.9 2.8 %collective-permute-start.10 = (bf16[4,56,768]{2,1,0:T(8,128)(2,1)S(1)}, bf16[4,56,768]{2,1,0:T(8,128)(2,1)S(1)}, u32[]{:S(2)}, u32[]{:S(2)}) collective-permute-start(bf16[4,56,768]{2,1,0:T(8,128)(2,1)S(1)} %get-tuple-element.32), channel_id=1, source_target_pairs={{0,1},{1,2},{2,3},{3,4},{4,5},{5,6},{6,7},{8,9},{9,10},{10,11},{11... | collective-permute-start | bytes 1032200 | tf_op jit(solution)/shard_map/ppermute | solution.py:218
  68.7 2.1 %collective-permute-start.11 = (bf16[4,56,768]{2,1,0:T(8,128)(2,1)S(1)}, bf16[4,56,768]{2,1,0:T(8,128)(2,1)S(1)}, u32[]{:S(2)}, u32[]{:S(2)}) collective-permute-start(bf16[4,56,768]{2,1,0:T(8,128)(2,1)S(1)} %get-tuple-element.33), channel_id=1, source_target_pairs={{1,0},{2,1},{3,2},{4,3},{5,4},{6,5},{7,6},{9,8},{10,9},{11,10},{12... | collective-permute-start | bytes 1032200 | tf_op jit(solution)/shard_map/ppermute | solution.py:218
  70.9 2.5 %collective-permute-start.8 = (bf16[3,56,576]{2,1,0:T(8,128)(2,1)S(1)}, bf16[3,56,576]{2,1,0:T(8,128)(2,1)S(1)}, u32[]{:S(2)}, u32[]{:S(2)}) collective-permute-start(bf16[3,56,576]{2,1,0:T(8,128)(2,1)S(1)} %get-tuple-element.26), channel_id=1, source_target_pairs={{0,16},{8,24},{16,0},{24,8},{1,17},{9,25},{17,1},{25,9},{2,18},{10... | collective-permute-start | bytes 580616 | tf_op jit(solution)/shard_map/ppermute | solution.py:213
  73.4 0.2 collective-permute-start.9
  73.5 1.2 %collective-permute-done.10.refs_4_ = bf16[4,56,768]{2,1,0:T(8,128)(2,1)S(1)} collective-permute-done((bf16[4,56,768]{2,1,0:T(8,128)(2,1)S(1)}, bf16[4,56,768]{2,1,0:T(8,128)(2,1)S(1)}, u32[]{:S(2)}, u32[]{:S(2)}) %collective-permute-start.10) | collective-permute-done | bytes 344096 | tf_op jit(solution)/shard_map/ppermute | solution.py:218
  74.8 3.4 %collective-permute-done.11.refs_5_ = bf16[4,56,768]{2,1,0:T(8,128)(2,1)S(1)} collective-permute-done((bf16[4,56,768]{2,1,0:T(8,128)(2,1)S(1)}, bf16[4,56,768]{2,1,0:T(8,128)(2,1)S(1)}, u32[]{:S(2)}, u32[]{:S(2)}) %collective-permute-start.11) | collective-permute-done | bytes 344096 | tf_op jit(solution)/shard_map/ppermute | solution.py:218
  78.2 15.4 %second.1 = (bf16[3,56,576]{2,1,0:T(8,128)(2,1)S(1)}, bf16[3,56,576]{2,1,0:T(8,128)(2,1)S(1)}, bf16[3,56,576]{2,1,0:T(8,128)(2,1)S(1)}, bf16[3,56,576]{2,1,0:T(8,128)(2,1)S(1)}) custom-call(bf16[3,56,768]{2,1,0:T(8,128)(2,1)S(1)} %get-tuple-element.28.refs_0_, bf16[3,56,768]{2,1,0:T(8,128)(2,1)S(1)} %get-tuple-element.29.refs_1_, ...), custom_call_target="tpu_custom_call" | custom-call | tf_op jit(solution)/shard_map/second/pallas_call | solution.py:284
  93.7 2.8 %collective-permute-start.13 = (bf16[3,56,576]{2,1,0:T(8,128)(2,1)S(1)}, bf16[3,56,576]{2,1,0:T(8,128)(2,1)S(1)}, u32[]{:S(2)}, u32[]{:S(2)}) collective-permute-start(bf16[3,56,576]{2,1,0:T(8,128)(2,1)S(1)} %get-tuple-element.36), channel_id=1, source_target_pairs={{0,16},{8,24},{16,0},{24,8},{1,17},{9,25},{17,1},{25,9},{2,18},{10... | collective-permute-start | bytes 580616 | tf_op jit(solution)/shard_map/ppermute | solution.py:213
  96.4 1.2 %join.2 = bf16[3,53,2304]{2,1,0:T(8,128)(2,1)} custom-call(s32[1]{0:T(128)} %bitcast.me_ref, bf16[3,56,576]{2,1,0:T(8,128)(2,1)S(1)} %get-tuple-element.24.refs_0_, bf16[3,56,576]{2,1,0:T(8,128)(2,1)S(1)} %collective-permute-done.7.refs_1_, bf16[3,56,576]{2,1,0:T(8,128)(2,1)S(1)} %collective-permute-done.8.refs_2_, ...), custom_call_target="tpu_custom_call" | custom-call | tf_op jit(solution)/shard_map/join/pallas_call | solution.py:300
  97.6 4.3 %collective-permute-done.12.refs_1_ = bf16[3,56,576]{2,1,0:T(8,128)(2,1)S(1)} collective-permute-done((bf16[3,56,576]{2,1,0:T(8,128)(2,1)S(1)}, bf16[3,56,576]{2,1,0:T(8,128)(2,1)S(1)}, u32[]{:S(2)}, u32[]{:S(2)}) %collective-permute-start.12) | collective-permute-done | bytes 193568 | tf_op jit(solution)/shard_map/ppermute | solution.py:213
  101.9 8.8 %collective-permute-done.13.refs_2_ = bf16[3,56,576]{2,1,0:T(8,128)(2,1)S(1)} collective-permute-done((bf16[3,56,576]{2,1,0:T(8,128)(2,1)S(1)}, bf16[3,56,576]{2,1,0:T(8,128)(2,1)S(1)}, u32[]{:S(2)}, u32[]{:S(2)}) %collective-permute-start.13) | collective-permute-done | bytes 193568 | tf_op jit(solution)/shard_map/ppermute | solution.py:213
  110.8 4.5 %collective-permute-done.14.refs_3_ = bf16[3,56,576]{2,1,0:T(8,128)(2,1)S(1)} collective-permute-done((bf16[3,56,576]{2,1,0:T(8,128)(2,1)S(1)}, bf16[3,56,576]{2,1,0:T(8,128)(2,1)S(1)}, u32[]{:S(2)}, u32[]{:S(2)}) %collective-permute-start.14) | collective-permute-done | bytes 193568 | tf_op jit(solution)/shard_map/ppermute | solution.py:213
  115.2 1.2 %join.3 = bf16[3,53,2304]{2,1,0:T(8,128)(2,1)} custom-call(s32[1]{0:T(128)} %bitcast.me_ref, bf16[3,56,576]{2,1,0:T(8,128)(2,1)S(1)} %get-tuple-element.34.refs_0_, bf16[3,56,576]{2,1,0:T(8,128)(2,1)S(1)} %collective-permute-done.12.refs_1_, bf16[3,56,576]{2,1,0:T(8,128)(2,1)S(1)} %collective-permute-done.13.refs_2_, ...), custom_call_target="tpu_custom_call" | custom-call | tf_op jit(solution)/shard_map/join/pallas_call | solution.py:300
  (48 shorter events, 0.9 us)
Async XLA Ops:
  0.6 9.1 %copy-start = (bf16[53,3,2304]{2,0,1:T(8,128)(2,1)S(1)}, bf16[53,3,2304]{2,0,1:T(8,128)(2,1)}, u32[]{:S(2)}) copy-start(bf16[53,3,2304]{2,0,1:T(8,128)(2,1)} %param.6) | copy-start | bytes 2198020
  2.5 0.7 copy-start.1
  3.2 17.0 %collective-permute-start.6 = (f32[7,2304]{1,0:T(8,128)S(1)}, f32[7,2304]{1,0:T(8,128)S(1)}, u32[]{:S(2)}, u32[]{:S(2)}) collective-permute-start(f32[7,2304]{1,0:T(8,128)S(1)} %get-tuple-element.50), channel_id=1, source_target_pairs={{1,0},{2,1},{3,2},{4,3},{5,4},{6,5},{7,6},{9,8},{10,9},{11,10},{12... | collective-permute-start | bytes 193544 | tf_op jit(solution)/shard_map/ppermute | solution.py:218
  5.8 14.4 %collective-permute-start.5 = (f32[7,2304]{1,0:T(8,128)S(1)}, f32[7,2304]{1,0:T(8,128)S(1)}, u32[]{:S(2)}, u32[]{:S(2)}) collective-permute-start(f32[7,2304]{1,0:T(8,128)S(1)} %get-tuple-element.51), channel_id=1, source_target_pairs={{0,1},{1,2},{2,3},{3,4},{4,5},{5,6},{6,7},{8,9},{9,10},{10,11},{11... | collective-permute-start | bytes 193544 | tf_op jit(solution)/shard_map/ppermute | solution.py:218
  10.6 12.1 %collective-permute-start = (bf16[3,56,768]{2,1,0:T(8,128)(2,1)S(1)}, bf16[3,56,768]{2,1,0:T(8,128)(2,1)S(1)}, u32[]{:S(2)}, u32[]{:S(2)}) collective-permute-start(bf16[3,56,768]{2,1,0:T(8,128)(2,1)S(1)} %get-tuple-element.21), channel_id=1, source_target_pairs={{0,8},{8,0},{16,24},{24,16},{1,9},{9,1},{17,25},{25,17},{2,10},{10... | collective-permute-start | bytes 774152 | tf_op jit(solution)/shard_map/ppermute | solution.py:213
  10.8 19.4 %collective-permute-start.1 = (bf16[3,56,768]{2,1,0:T(8,128)(2,1)S(1)}, bf16[3,56,768]{2,1,0:T(8,128)(2,1)S(1)}, u32[]{:S(2)}, u32[]{:S(2)}) collective-permute-start(bf16[3,56,768]{2,1,0:T(8,128)(2,1)S(1)} %get-tuple-element.22), channel_id=1, source_target_pairs={{0,16},{8,24},{16,0},{24,8},{1,17},{9,25},{17,1},{25,9},{2,18},{10... | collective-permute-start | bytes 774152 | tf_op jit(solution)/shard_map/ppermute | solution.py:213
  13.1 22.6 %collective-permute-start.2 = (bf16[3,56,768]{2,1,0:T(8,128)(2,1)S(1)}, bf16[3,56,768]{2,1,0:T(8,128)(2,1)S(1)}, u32[]{:S(2)}, u32[]{:S(2)}) collective-permute-start(bf16[3,56,768]{2,1,0:T(8,128)(2,1)S(1)} %get-tuple-element.23), channel_id=1, source_target_pairs={{0,24},{8,16},{16,8},{24,0},{1,25},{9,17},{17,9},{25,1},{2,26},{10... | collective-permute-start | bytes 774152 | tf_op jit(solution)/shard_map/ppermute | solution.py:213
  13.4 0.7 copy-start.5
  13.4 0.7 copy-start.6
  14.2 0.7 copy-start.4
  15.0 5.2 %copy-start.2 = (f32[6,3,2304]{2,0,1:T(8,128)S(1)}, f32[6,3,2304]{2,0,1:T(8,128)}, u32[]{:S(2)}) copy-start(f32[6,3,2304]{2,0,1:T(8,128)} %copy-done.1) | copy-start | bytes 497668
  36.5 12.2 %collective-permute-start.3 = (bf16[4,56,768]{2,1,0:T(8,128)(2,1)}, bf16[4,56,768]{2,1,0:T(8,128)(2,1)S(1)}, u32[]{:S(2)}, u32[]{:S(2)}) collective-permute-start(bf16[4,56,768]{2,1,0:T(8,128)(2,1)} %pad_maximum_fusion), channel_id=1, source_target_pairs={{0,1},{1,2},{2,3},{3,4},{4,5},{5,6},{6,7},{8,9},{9,10},{10,11},{11... | collective-permute-start | bytes 1032200 | tf_op jit(solution)/shard_map/ppermute | solution.py:218
  40.8 9.7 %collective-permute-start.4 = (bf16[4,56,768]{2,1,0:T(8,128)(2,1)}, bf16[4,56,768]{2,1,0:T(8,128)(2,1)S(1)}, u32[]{:S(2)}, u32[]{:S(2)}) collective-permute-start(bf16[4,56,768]{2,1,0:T(8,128)(2,1)} %pad_maximum_fusion.1), channel_id=1, source_target_pairs={{1,0},{2,1},{3,2},{4,3},{5,4},{6,5},{7,6},{9,8},{10,9},{11,10},{12... | collective-permute-start | bytes 1032200 | tf_op jit(solution)/shard_map/ppermute | solution.py:218
  45.0 0.9 copy-start.3
  65.9 8.8 %collective-permute-start.10 = (bf16[4,56,768]{2,1,0:T(8,128)(2,1)S(1)}, bf16[4,56,768]{2,1,0:T(8,128)(2,1)S(1)}, u32[]{:S(2)}, u32[]{:S(2)}) collective-permute-start(bf16[4,56,768]{2,1,0:T(8,128)(2,1)S(1)} %get-tuple-element.32), channel_id=1, source_target_pairs={{0,1},{1,2},{2,3},{3,4},{4,5},{5,6},{6,7},{8,9},{9,10},{10,11},{11... | collective-permute-start | bytes 1032200 | tf_op jit(solution)/shard_map/ppermute | solution.py:218
  68.7 9.5 %collective-permute-start.11 = (bf16[4,56,768]{2,1,0:T(8,128)(2,1)S(1)}, bf16[4,56,768]{2,1,0:T(8,128)(2,1)S(1)}, u32[]{:S(2)}, u32[]{:S(2)}) collective-permute-start(bf16[4,56,768]{2,1,0:T(8,128)(2,1)S(1)} %get-tuple-element.33), channel_id=1, source_target_pairs={{1,0},{2,1},{3,2},{4,3},{5,4},{6,5},{7,6},{9,8},{10,9},{11,10},{12... | collective-permute-start | bytes 1032200 | tf_op jit(solution)/shard_map/ppermute | solution.py:218
  70.8 25.6 %collective-permute-start.7 = (bf16[3,56,576]{2,1,0:T(8,128)(2,1)S(1)}, bf16[3,56,576]{2,1,0:T(8,128)(2,1)S(1)}, u32[]{:S(2)}, u32[]{:S(2)}) collective-permute-start(bf16[3,56,576]{2,1,0:T(8,128)(2,1)S(1)} %get-tuple-element.25), channel_id=1, source_target_pairs={{0,8},{8,0},{16,24},{24,16},{1,9},{9,1},{17,25},{25,17},{2,10},{10... | collective-permute-start | bytes 580616 | tf_op jit(solution)/shard_map/ppermute | solution.py:213
  70.9 25.5 %collective-permute-start.8 = (bf16[3,56,576]{2,1,0:T(8,128)(2,1)S(1)}, bf16[3,56,576]{2,1,0:T(8,128)(2,1)S(1)}, u32[]{:S(2)}, u32[]{:S(2)}) collective-permute-start(bf16[3,56,576]{2,1,0:T(8,128)(2,1)S(1)} %get-tuple-element.26), channel_id=1, source_target_pairs={{0,16},{8,24},{16,0},{24,8},{1,17},{9,25},{17,1},{25,9},{2,18},{10... | collective-permute-start | bytes 580616 | tf_op jit(solution)/shard_map/ppermute | solution.py:213
  73.4 23.1 %collective-permute-start.9 = (bf16[3,56,576]{2,1,0:T(8,128)(2,1)S(1)}, bf16[3,56,576]{2,1,0:T(8,128)(2,1)S(1)}, u32[]{:S(2)}, u32[]{:S(2)}) collective-permute-start(bf16[3,56,576]{2,1,0:T(8,128)(2,1)S(1)} %get-tuple-element.27), channel_id=1, source_target_pairs={{0,24},{8,16},{16,8},{24,0},{1,25},{9,17},{17,9},{25,1},{2,26},{10... | collective-permute-start | bytes 580616 | tf_op jit(solution)/shard_map/ppermute | solution.py:213
  93.6 8.4 %collective-permute-start.12 = (bf16[3,56,576]{2,1,0:T(8,128)(2,1)S(1)}, bf16[3,56,576]{2,1,0:T(8,128)(2,1)S(1)}, u32[]{:S(2)}, u32[]{:S(2)}) collective-permute-start(bf16[3,56,576]{2,1,0:T(8,128)(2,1)S(1)} %get-tuple-element.35), channel_id=1, source_target_pairs={{0,8},{8,0},{16,24},{24,16},{1,9},{9,1},{17,25},{25,17},{2,10},{10... | collective-permute-start | bytes 580616 | tf_op jit(solution)/shard_map/ppermute | solution.py:213
  93.7 17.1 %collective-permute-start.13 = (bf16[3,56,576]{2,1,0:T(8,128)(2,1)S(1)}, bf16[3,56,576]{2,1,0:T(8,128)(2,1)S(1)}, u32[]{:S(2)}, u32[]{:S(2)}) collective-permute-start(bf16[3,56,576]{2,1,0:T(8,128)(2,1)S(1)} %get-tuple-element.36), channel_id=1, source_target_pairs={{0,16},{8,24},{16,0},{24,8},{1,17},{9,25},{17,1},{25,9},{2,18},{10... | collective-permute-start | bytes 580616 | tf_op jit(solution)/shard_map/ppermute | solution.py:213
  96.4 18.8 %collective-permute-start.14 = (bf16[3,56,576]{2,1,0:T(8,128)(2,1)S(1)}, bf16[3,56,576]{2,1,0:T(8,128)(2,1)S(1)}, u32[]{:S(2)}, u32[]{:S(2)}) collective-permute-start(bf16[3,56,576]{2,1,0:T(8,128)(2,1)S(1)} %get-tuple-element.37), channel_id=1, source_target_pairs={{0,24},{8,16},{16,8},{24,0},{1,25},{9,17},{17,9},{25,1},{2,26},{10... | collective-permute-start | bytes 580616 | tf_op jit(solution)/shard_map/ppermute | solution.py:213

commit v2 on v0

v2 whole, which is shorter than its diff:
```python
import functools

import jax
import jax.numpy as jnp
from jax import lax
from jax.experimental import pallas as pl
from jax.experimental.pallas import tpu as pltpu
from jax.sharding import PartitionSpec as P

NXY = 48
SCALE = 0.15
LANES = 128
REACH = 2
BLOCK = 32
VMEM = pltpu.VMEM
F32, BF16 = jnp.float32, jnp.bfloat16
NEXT_X, LAST_X, NEXT_Y, LAST_Y, NEXT_Z, LAST_Z, ALL = range(7)


def up(value, step):
    return -(-value // step) * step


def call(kernel, name, out_shape, args, scratch=(), scalars=0, unread=0):
    in_specs = [pl.BlockSpec(memory_space=pltpu.SMEM)] * scalars
    in_specs += [pl.BlockSpec(memory_space=VMEM)] * (len(args) - scalars - unread)
    in_specs += [pl.BlockSpec(memory_space=pl.ANY)] * unread
    return pl.pallas_call(
        kernel,
        out_shape=out_shape,
        in_specs=in_specs,
        out_specs=[pl.BlockSpec(memory_space=VMEM)] * len(out_shape),
        scratch_shapes=scratch,
        compiler_params=pltpu.CompilerParams(vmem_limit_bytes=40 << 20),
        name=name,
    )(*args)


def cut_kernel(count, chunk, me_ref, x_ref, mean_ref, other_ref, *refs):
    edge_refs, middle_refs = refs[:count], refs[count : 2 * count]
    low_ref, high_ref, held = refs[2 * count :]
    planes, own, cells = x_ref.shape
    _, padded, width = edge_refs[0].shape
    halo = REACH * NXY
    me = me_ref[0]
    for out_ref, plane in ((low_ref, 0), (high_ref, planes - 1)):
        out_ref[0:1, :] = mean_ref[plane : plane + 1, :]
        for field in range(other_ref.shape[0]):
            out_ref[field + 1 : field + 2, :] = other_ref[field, plane : plane + 1, :]
    held[...] = jnp.zeros_like(held)
    lane = lax.broadcasted_iota(jnp.int32, (padded, LANES), 1)
    for plane in range(planes):
        held[0:own, :] = x_ref[plane].astype(F32)
        values = held[...]
        for target in range(count):
            turned = values if target == 0 else pltpu.roll(values, cells - target * chunk, 1)
            body = turned[:, : up(chunk + halo, LANES)]
            column = lax.broadcasted_iota(jnp.int32, body.shape, 1)
            end = chunk if target == count - 1 else chunk + halo
            body = jnp.where(column < end, body, 0.0)
            if body.shape[1] < width:
                body = jnp.concatenate([body, jnp.zeros((padded, width - body.shape[1]), F32)], axis=1)
            before = turned[:, cells - LANES :]
            if target == 0:
                before = jnp.zeros_like(before)
            last = jnp.where(lane < LANES - halo, body[:, width - LANES :], before)
            window = jnp.concatenate([body[:, : width - LANES], last], axis=1).astype(BF16)
            for step in range(count):

                @pl.when(lax.bitwise_xor(me, target) == step)
                def _():
                    if plane == 0:
                        edge_refs[step][0] = window
                    elif plane == planes - 1:
                        edge_refs[step][1] = window
                    else:
                        middle_refs[step][...] = window


def tables_kernel(fields, entries_ref, products_ref, slots_ref, out_ref, by_column):
    rows = by_column.shape[1]
    total = entries_ref.shape[1]
    names = slots_ref.shape[1]
    slots = slots_ref[...].astype(BF16)

    def placed(which):
        name = lax.broadcasted_iota(jnp.int32, (names, total), 0)
        chosen = jnp.where(name == entries_ref[which : which + 1, :], 1.0, 0.0).astype(BF16)
        return jnp.dot(slots, chosen, preferred_element_type=F32)[0:1].astype(jnp.int32)

    row, column = placed(0), placed(1)
    field = entries_ref[2:3, :]
    place = (row // BLOCK) * (fields * BLOCK) + field * BLOCK + row % BLOCK
    rest = products_ref[0:1, :]
    here = lax.broadcasted_iota(jnp.int32, (rows, total), 0) == column
    for part in range(3):
        piece = rest.astype(BF16).astype(F32)
        rest = rest - piece
        by_column[part] = jnp.where(here, piece, 0.0).astype(BF16)
    size = fields * BLOCK

    @pl.loop(0, rows // BLOCK)
    def _(block):
        index = lax.broadcasted_iota(jnp.int32, (size, total), 0) + block * size
        chosen = jnp.where(index == place, 1.0, 0.0).astype(BF16)
        acc = jnp.zeros((size, rows), F32)
        for part in range(3):
            acc += lax.dot_general(
                chosen, by_column[part], (((1,), (1,)), ((), ())), preferred_element_type=F32
            )
        out_ref[pl.ds(pl.multiple_of(block * size, size), size), :] = acc.astype(BF16)


def weights_kernel(conduct_ref, masks_ref, out_ref):
    planes, fields, _, tiles = out_ref.shape[:4]
    width = tiles * LANES

    def mask(which):
        return jnp.concatenate([masks_ref[which, tile, 0:1, :] for tile in range(tiles)], axis=1)

    for plane in range(planes):
        own = conduct_ref[plane + 1]
        others = (
            pltpu.roll(own, width - NXY, 1),
            pltpu.roll(own, NXY, 1),
            pltpu.roll(own, width - 1, 1) * mask(0),
            pltpu.roll(own, 1, 1) * mask(1),
            conduct_ref[plane + 2],
            conduct_ref[plane],
        )
        for way, other in enumerate(others):
            face = 0.5 * (own + other)
            for field in range(fields):
                for tile in range(tiles):
                    out_ref[plane, field, way, tile] = jnp.broadcast_to(
                        face[field : field + 1, tile * LANES : (tile + 1) * LANES], (8, LANES)
                    )


def joined(parts):
    return jnp.concatenate([part.astype(F32) for part in parts], axis=0).astype(BF16)


def edges_kernel(count, *refs):
    parts, (low_ref, high_ref) = refs[:count], refs[-2:]
    low_ref[...] = joined([part[0] for part in parts])
    high_ref[...] = joined([part[1] for part in parts])


def spread(value):
    return jnp.broadcast_to(value[None], (BLOCK // 8, 8, LANES)).reshape(BLOCK, LANES)


def mix(tables_ref, values, mixed):
    result = jnp.dot(tables_ref[...], values, preferred_element_type=F32).astype(BF16)
    for tile in range(values.shape[1] // LANES):
        mixed[tile] = result[:, tile * LANES : (tile + 1) * LANES]


def weigh(mixed, weights_ref, plane, ways, sums):
    _, tiles, rows, _ = sums.shape
    fields = weights_ref.shape[1]

    @pl.loop(0, rows // BLOCK * tiles)
    def _(index):
        block, tile = index // tiles, index % tiles
        here = pl.ds(pl.multiple_of(block * BLOCK, BLOCK), BLOCK)
        base = pl.multiple_of(block * (fields * BLOCK), fields * BLOCK)
        totals = [jnp.zeros((BLOCK, LANES), F32) for _ in ways]
        for field in range(fields):
            values = mixed[tile, pl.ds(base + field * BLOCK, BLOCK), :].astype(F32)
            for i, way in enumerate(ways):
                totals[i] += spread(weights_ref[plane, field, way, tile]) * values
        for i, way in enumerate(ways):
            sums[way, tile, here, :] = totals[i]
        if len(ways) == 6:
            sums[ALL, tile, here, :] = functools.reduce(jnp.add, totals)


def settle(sums, masks_ref, write):
    _, tiles, rows, _ = sums.shape
    lane = lax.broadcasted_iota(jnp.int32, (BLOCK, LANES), 1)
    for block in range(rows // BLOCK):
        here = slice(block * BLOCK, (block + 1) * BLOCK)

        def ahead(way, shift):
            turned = [pltpu.roll(sums[way, tile, here, :], LANES - shift, 1) for tile in range(tiles)]
            return [jnp.where(lane < LANES - shift, turned[t], turned[(t + 1) % tiles]) for t in range(tiles)]

        def behind(way, shift):
            turned = [pltpu.roll(sums[way, tile, here, :], shift, 1) for tile in range(tiles)]
            return [jnp.where(lane >= shift, turned[t], turned[(t - 1) % tiles]) for t in range(tiles)]

        shares = zip(ahead(LAST_X, NXY), behind(NEXT_X, NXY), ahead(LAST_Y, 1), behind(NEXT_Y, 1))
        for tile, (a, b, c, d) in enumerate(shares):
            value = sums[ALL, tile, here, :] - a - b
            value = value - spread(masks_ref[0, tile]) * c - spread(masks_ref[1, tile]) * d
            write(tile, here, value)


def outer(low, high, tables_ref, weights_ref, masks_ref, low_out, high_out, middle_out, mixed, sums):
    last = weights_ref.shape[0] - 1
    for plane, values, out_ref, way in ((0, low, low_out, NEXT_Z), (last, high, high_out, LAST_Z)):
        mix(tables_ref, values, mixed)
        weigh(mixed, weights_ref, plane, range(6), sums)

        def write(tile, here, value):
            out_ref[tile, here, :] = value
            given = sums[way, tile, here, :]
            middle_out[tile, here, :] = -given if plane == 0 else middle_out[tile, here, :] - given

        settle(sums, masks_ref, write)


def inner(values, low_in, high_in, middle_in, tables_ref, weights_ref, masks_ref, low_out, high_out, out, mixed, sums):
    mix(tables_ref, values, mixed)
    weigh(mixed, weights_ref, 1, range(6), sums)

    def write(tile, here, value):
        out[tile, here, :] = SCALE * (value + middle_in[tile, here, :])
        low_out[tile, here, :] = low_in[tile, here, :] - sums[LAST_Z, tile, here, :]
        high_out[tile, here, :] = high_in[tile, here, :] - sums[NEXT_Z, tile, here, :]

    settle(sums, masks_ref, write)


def emit(result, masks_ref, whole_ref, piece_refs, plane):
    tiles, rows, _ = result.shape
    if whole_ref is not None:
        for tile in range(tiles):
            inside = jnp.broadcast_to(masks_ref[2, tile][None], (rows // 8, 8, LANES)).reshape(rows, LANES)
            whole_ref[:, tile * LANES : (tile + 1) * LANES] = (result[tile] * inside).astype(BF16)
    padded, chunk = piece_refs[0].shape[-2:]
    for step, piece_ref in enumerate(piece_refs):
        for tile in range(up(chunk, LANES) // LANES):
            lanes = min(LANES, chunk - tile * LANES)
            part = result[tile, step * padded : (step + 1) * padded, :][:, :lanes].astype(BF16)
            if plane is None:
                piece_ref[:, tile * LANES : tile * LANES + lanes] = part
            else:
                piece_ref[plane, :, tile * LANES : tile * LANES + lanes] = part


def outer_kernel(low_ref, high_ref, tables_ref, weights_ref, masks_ref, low_out, high_out, middle_out, mixed, sums):
    outer(
        low_ref[...], high_ref[...], tables_ref, weights_ref, masks_ref, low_out, high_out, middle_out, mixed, sums
    )


def inner_kernel(count, *refs):
    parts = refs[:count]
    low_in, high_in, middle_in, tables_ref, weights_ref, masks_ref = refs[count : count + 6]
    low_out, high_out, whole_ref, *pieces = refs[count + 6 : 2 * count + 9]
    mixed, sums, result = refs[2 * count + 9 :]
    values = joined([part[...] for part in parts])
    inner(
        values, low_in, high_in, middle_in, tables_ref, weights_ref, masks_ref, low_out, high_out, result, mixed, sums
    )
    emit(result, masks_ref, whole_ref, pieces, None)


def own_kernel(low_ref, values_ref, high_ref, tables_ref, weights_ref, masks_ref, low_out, high_out, *refs):
    *pieces, mixed, sums, result, middle, low, high = refs
    outer(low_ref[...], high_ref[...], tables_ref, weights_ref, masks_ref, low, high, middle, mixed, sums)
    inner(
        values_ref[...], low, high, middle, tables_ref, weights_ref, masks_ref, low_out, high_out, result, mixed, sums
    )
    emit(result, masks_ref, None, pieces, None)


def fix_kernel(count, first, before_ref, after_ref, low_in, high_in, tables_ref, weights_ref, masks_ref, *refs):
    if first:
        wholes, nears, refs = refs[:2], refs[2:4], refs[4:]
    pieces, (mixed, sums, result) = refs[:count], refs[count:]
    last = weights_ref.shape[0] - 1
    sides = ((before_ref, low_in, 0, LAST_Z), (after_ref, high_in, last, NEXT_Z))
    for side, (halo_ref, share_ref, plane, way) in enumerate(sides):
        mix(tables_ref, halo_ref[...], mixed)
        weigh(mixed, weights_ref, plane, (way,), sums)
        for tile in range(sums.shape[1]):
            result[tile] = SCALE * (share_ref[tile] - sums[way, tile])
        emit(result, masks_ref, wholes[side] if first else None, pieces, side)
        if first:
            nears[side][...] = wholes[side][:, : nears[side].shape[1]]


def join_kernel(count, me_ref, *refs):
    edge_refs, middle_refs, (out_ref, held) = refs[:count], refs[count : 2 * count], refs[2 * count :]
    planes, own, cells = out_ref.shape
    me = me_ref[0]
    for step in range(count):
        source = lax.bitwise_xor(me, step)
        held[source, 0] = edge_refs[step][0].astype(F32)
        held[source, 1] = middle_refs[step][...].astype(F32)
        held[source, 2] = edge_refs[step][1].astype(F32)
    for plane in range(planes):
        line = jnp.concatenate([held[source, plane] for source in range(count)], axis=1)
        out_ref[plane] = line[:own].astype(BF16)


def shards(panels, mean_field, fluctuations, products, triples, owner_slot):
    count, slabs = lax.axis_size("chaos"), lax.axis_size("space")
    me = lax.axis_index("chaos")
    own, planes, cells = panels.shape
    assert planes == 3
    chunk, halo = cells // count, REACH * NXY
    width = up(chunk + 2 * halo, LANES)
    near = up(chunk, LANES)
    padded = up(own, 8)
    rows = count * padded
    fields = 1 + fluctuations.shape[0]
    me_array = me.astype(jnp.int32).reshape(1)
    tiles = width // LANES

    def exchange(block, step):
        return lax.ppermute(block, "chaos", [(i, i ^ step) for i in range(count)])

    def exchanged(blocks):
        return [blocks[0]] + [exchange(blocks[step], step) for step in range(1, count)]

    def neighbours(first_plane, last_plane):
        upward = [(i, i + 1) for i in range(slabs - 1)]
        downward = [(target, source) for source, target in upward]
        return lax.ppermute(last_plane, "space", upward), lax.ppermute(first_plane, "space", downward)

    def shape(*dims, dtype=BF16):
        return jax.ShapeDtypeStruct(dims, dtype)

    cut = call(
        functools.partial(cut_kernel, count, chunk),
        "cut",
        [shape(2, padded, width)] * count + [shape(padded, width)] * count + [shape(fields, cells, dtype=F32)] * 2,
        (me_array, jnp.transpose(panels, (1, 0, 2)), mean_field, fluctuations),
        [VMEM((padded, cells), F32)],
        scalars=1,
    )
    edges, middles = exchanged(cut[:count]), exchanged(cut[count : 2 * count])

    total = up(products.shape[0], 2 * LANES)
    names = up(owner_slot.shape[0], LANES)
    entries = jnp.pad(triples.T, ((0, 5), (0, total - products.shape[0])), constant_values=-1)
    values = jnp.pad(products, (0, total - products.shape[0]))[None]
    group = owner_slot // own
    slots = lax.bitwise_xor(group, me) * padded + owner_slot - group * own
    slots = jnp.broadcast_to(jnp.pad(slots, (0, names - slots.shape[0])).astype(F32)[None], (16, names))
    (tables,) = call(
        functools.partial(tables_kernel, fields),
        "tables",
        [shape(fields * rows, rows)],
        (entries, values, slots),
        [VMEM((3, rows, total), BF16)],
    )

    before, after = neighbours(*cut[2 * count :])
    conduct = jnp.concatenate([mean_field[:, None], fluctuations.transpose(1, 0, 2)], axis=1)
    conduct = jnp.concatenate([before[None], conduct, after[None]], axis=0)
    conduct = jnp.pad(conduct, ((0, 0), (0, 0), (halo, halo)))
    conduct = lax.dynamic_slice_in_dim(conduct, me * chunk, chunk + 2 * halo, 2)
    gap = jnp.zeros(conduct.shape[:-1] + (width - chunk - 2 * halo,), F32)
    conduct = jnp.concatenate([conduct[..., halo:], gap, conduct[..., :halo]], axis=-1)

    lane = jnp.arange(width)
    place = jnp.where(lane < width - halo, lane, lane - width) + halo
    row = place // NXY - REACH + me * (chunk // NXY)
    inside = (row >= 0) & (row < NXY) & ((lane < chunk + halo) | (lane >= width - halo))
    masks = jnp.stack([place % NXY < NXY - 1, place % NXY > 0, inside]).astype(F32)
    masks = jnp.broadcast_to(masks.reshape(3, tiles, 1, LANES), (3, tiles, 8, LANES))
    (weights,) = call(
        weights_kernel, "weights", [shape(planes, fields, 6, tiles, 8, LANES, dtype=F32)], (conduct, masks)
    )

    common = (tables, weights, masks)
    plane_whole = shape(rows, width)
    share = shape(tiles, rows, LANES, dtype=F32)
    piece, pair = shape(padded, chunk), shape(2, padded, chunk)
    mixed = VMEM((tiles, fields * rows, LANES), BF16)
    sums = VMEM((7, tiles, rows, LANES), F32)
    result = VMEM((tiles, rows, LANES), F32)

    low, high = call(
        functools.partial(edges_kernel, count), "edges", [plane_whole] * 2, (*edges, tables, weights), unread=2
    )
    before, after = neighbours(low, high)
    low, high, middle = call(outer_kernel, "outer", [share] * 3, (low, high, *common), [mixed, sums])
    low, high, middle, *first_middles = call(
        functools.partial(inner_kernel, count),
        "inner",
        [share] * 2 + [plane_whole] + [piece] * count,
        (*middles, low, high, middle, *common),
        [mixed, sums, result],
    )
    first_middles = exchanged(first_middles)
    low, high, low_near, high_near, *first_edges = call(
        functools.partial(fix_kernel, count, True),
        "fix",
        [plane_whole] * 2 + [shape(rows, near)] * 2 + [pair] * count,
        (before, after, low, high, *common),
        [mixed, sums, result],
    )
    before, after = neighbours(low_near, high_near)
    first_edges = exchanged(first_edges)
    low, high, *second_middles = call(
        own_kernel,
        "own",
        [share] * 2 + [piece] * count,
        (low, middle, high, *common),
        [mixed, sums] + [result] * 4,
    )
    second_middles = exchanged(second_middles)
    near_tiles = near // LANES
    second_edges = exchanged(
        call(
            functools.partial(fix_kernel, count, False),
            "last",
            [pair] * count,
            (before, after, low, high, *common),
            [
                VMEM((near_tiles, fields * rows, LANES), BF16),
                VMEM((7, near_tiles, rows, LANES), F32),
                VMEM((near_tiles, rows, LANES), F32),
            ],
        )
    )

    def join(edge_parts, middle_parts):
        (result,) = call(
            functools.partial(join_kernel, count),
            "join",
            [shape(planes, own, cells)],
            (me_array, *edge_parts, *middle_parts),
            [VMEM((count, planes, padded, chunk), F32)],
            scalars=1,
        )
        return jnp.transpose(result, (1, 0, 2))

    return join(first_edges, first_middles), join(second_edges, second_middles)


def solution(mesh):
    in_specs = (P("chaos", "space", None), P("space", None), P(None, "space", None), P(), P(), P())
    out_specs = (P("chaos", "space", None), P("chaos", "space", None))
    return jax.shard_map(shards, mesh=mesh, in_specs=in_specs, out_specs=out_specs, check_vma=False)
```

time: 444 us -> 116 us (0.26)
  the two profiles are of different devices: /device:TPU:1 before, /device:TPU:0 now
where the time goes in v2:
time: 116 us; the launch traced here: 114 us
  starting transfers between devices  43.7 us (38%)
  Pallas kernels  42.7 us (37%)
  waiting for transfers between devices  20.9 us (18%)
  local copies, waits for them, and re-layouts  4.43 us (4%)
    pallas_call x11, Pallas kernels, call(): pl.pallas_call(kernel, out_shape=out_shape, in_specs=in_specs, out_specs=...  42.7 us
    ppermute x18, starting transfers between devices, exchange(): return lax.ppermute(block, 'chaos', [(i, i ^ step) for i in range(count)])  27.6 us
    ppermute x18, waiting for transfers between devices, exchange(): return lax.ppermute(block, 'chaos', [(i, i ^ step) for i in range(count)])  20.9 us
    ppermute x3, starting transfers between devices, neighbours(): lax.ppermute(last_plane, 'space', upward)  12 us
    ppermute x3, starting transfers between devices, neighbours(): lax.ppermute(first_plane, 'space', downward)  4.06 us
    unnamed x7, local copies, waits for them, and re-layouts  2.87 us
  transfers between devices with their start and end apart: 24, of which 3 were waited for; matrix products, arithmetic and copies ran while one was open for 2% of the time, Pallas kernels for 32%

profile of v2, /device:TPU:0, one launch (start us, length us, event | category | flops | bytes accessed | tf_op | source)
XLA Modules:
  0.0 113.7 jit_solution(4483890998383436949)
XLA Ops:
  0.6 0.9 copy-done
  1.6 1.1 copy-done.1
  2.7 0.8 copy-done.2
  3.5 0.9 cut.1
  4.3 2.4 %collective-permute-start.3 = (f32[7,2304]{1,0:T(8,128)S(1)}, f32[7,2304]{1,0:T(8,128)S(1)}, u32[]{:S(2)}, u32[]{:S(2)}) collective-permute-start(f32[7,2304]{1,0:T(8,128)S(1)} %get-tuple-element.46), channel_id=1, source_target_pairs={{0,1},{1,2},{2,3},{3,4},{4,5},{5,6},{6,7},{8,9},{9,10},{10,11},{11... | collective-permute-start | bytes 193544 | tf_op jit(solution)/shard_map/ppermute | solution.py:324
  6.7 1.3 %collective-permute-start.4 = (f32[7,2304]{1,0:T(8,128)S(1)}, f32[7,2304]{1,0:T(8,128)S(1)}, u32[]{:S(2)}, u32[]{:S(2)}) collective-permute-start(f32[7,2304]{1,0:T(8,128)S(1)} %get-tuple-element.47), channel_id=1, source_target_pairs={{1,0},{2,1},{3,2},{4,3},{5,4},{6,5},{7,6},{9,8},{10,9},{11,10},{12... | collective-permute-start | bytes 193544 | tf_op jit(solution)/shard_map/ppermute | solution.py:324
  8.0 2.5 %collective-permute-start = (bf16[2,56,768]{2,1,0:T(8,128)(2,1)S(1)}, bf16[2,56,768]{2,1,0:T(8,128)(2,1)S(1)}, u32[]{:S(2)}, u32[]{:S(2)}) collective-permute-start(bf16[2,56,768]{2,1,0:T(8,128)(2,1)S(1)} %get-tuple-element.43), channel_id=1, source_target_pairs={{0,8},{8,0},{16,24},{24,16},{1,9},{9,1},{17,25},{25,17},{2,10},{10... | collective-permute-start | bytes 516104 | tf_op jit(solution)/shard_map/ppermute | solution.py:316
  10.5 2.6 %collective-permute-start.1 = (bf16[2,56,768]{2,1,0:T(8,128)(2,1)S(1)}, bf16[2,56,768]{2,1,0:T(8,128)(2,1)S(1)}, u32[]{:S(2)}, u32[]{:S(2)}) collective-permute-start(bf16[2,56,768]{2,1,0:T(8,128)(2,1)S(1)} %get-tuple-element.44), channel_id=1, source_target_pairs={{0,16},{8,24},{16,0},{24,8},{1,17},{9,25},{17,1},{25,9},{2,18},{10... | collective-permute-start | bytes 516104 | tf_op jit(solution)/shard_map/ppermute | solution.py:316
  13.1 0.0 collective-permute-start.2
  13.2 0.7 multiply_subtract_fusion
  13.9 0.7 pad.17
  14.6 0.7 pad.16.entries_ref
  15.4 5.1 %tables.1.refs_4_.tables_ref.refs_7_ = bf16[1568,224]{1,0:T(8,128)(2,1)S(1)} custom-call(s32[8,1280]{1,0:T(8,128)S(1)} %pad.16.entries_ref, f32[1,1280]{1,0:T(1,128)S(1)} %broadcast_in_dim.23.products_ref, f32[16,256]{1,0:T(8,128)S(1)} %broadcast_in_dim.24.slots_ref), custom_call_target="tpu_custom_call" | custom-call | tf_op jit(solution)/shard_map/tables/pallas_call | solution.py:28
  20.5 0.0 collective-permute-done.4
  20.5 0.1 fusion.3
  20.7 0.1 slice.8
  20.8 0.1 pad_maximum_fusion.conduct_ref
  20.9 0.3 weights.1.refs_5_.weights_ref.refs_8_
  21.2 0.0 collective-permute-done.1.refs_2_
  21.2 3.0 %collective-permute-done.2.refs_3_ = bf16[2,56,768]{2,1,0:T(8,128)(2,1)S(1)} collective-permute-done((bf16[2,56,768]{2,1,0:T(8,128)(2,1)S(1)}, bf16[2,56,768]{2,1,0:T(8,128)(2,1)S(1)}, u32[]{:S(2)}, u32[]{:S(2)}) %collective-permute-start.2) | collective-permute-done | bytes 172064 | tf_op jit(solution)/shard_map/ppermute | solution.py:316
  24.2 4.8 %collective-permute-start.5 = (bf16[224,768]{1,0:T(8,128)(2,1)S(1)}, bf16[224,768]{1,0:T(8,128)(2,1)S(1)}, u32[]{:S(2)}, u32[]{:S(2)}) collective-permute-start(bf16[224,768]{1,0:T(8,128)(2,1)S(1)} %get-tuple-element.48.high_ref), channel_id=1, source_target_pairs={{0,1},{1,2},{2,3},{3,4},{4,5},{5,6},{6,7},{8,9},{9,10},{10,11},{11... | collective-permute-start | bytes 1032200 | tf_op jit(solution)/shard_map/ppermute | solution.py:324
  29.0 1.3 %collective-permute-start.6 = (bf16[224,768]{1,0:T(8,128)(2,1)S(1)}, bf16[224,768]{1,0:T(8,128)(2,1)S(1)}, u32[]{:S(2)}, u32[]{:S(2)}) collective-permute-start(bf16[224,768]{1,0:T(8,128)(2,1)S(1)} %get-tuple-element.49.low_ref), channel_id=1, source_target_pairs={{1,0},{2,1},{3,2},{4,3},{5,4},{6,5},{7,6},{9,8},{10,9},{11,10},{12... | collective-permute-start | bytes 1032200 | tf_op jit(solution)/shard_map/ppermute | solution.py:324
  30.3 3.2 %collective-permute-start.7 = (bf16[56,768]{1,0:T(8,128)(2,1)S(1)}, bf16[56,768]{1,0:T(8,128)(2,1)S(1)}, u32[]{:S(2)}, u32[]{:S(2)}) collective-permute-start(bf16[56,768]{1,0:T(8,128)(2,1)S(1)} %get-tuple-element.51), channel_id=1, source_target_pairs={{0,8},{8,0},{16,24},{24,16},{1,9},{9,1},{17,25},{25,17},{2,10},{10... | collective-permute-start | bytes 258056 | tf_op jit(solution)/shard_map/ppermute | solution.py:316
  33.5 1.1 collective-permute-start.8
  34.6 1.4 %collective-permute-start.9 = (bf16[56,768]{1,0:T(8,128)(2,1)S(1)}, bf16[56,768]{1,0:T(8,128)(2,1)S(1)}, u32[]{:S(2)}, u32[]{:S(2)}) collective-permute-start(bf16[56,768]{1,0:T(8,128)(2,1)S(1)} %get-tuple-element.53), channel_id=1, source_target_pairs={{0,24},{8,16},{16,8},{24,0},{1,25},{9,17},{17,9},{25,1},{2,26},{10... | collective-permute-start | bytes 258056 | tf_op jit(solution)/shard_map/ppermute | solution.py:316
  35.9 8.4 %outer.1 = (f32[6,224,128]{2,1,0:T(8,128)S(1)}, f32[6,224,128]{2,1,0:T(8,128)S(1)}, f32[6,224,128]{2,1,0:T(8,128)S(1)}) custom-call(bf16[224,768]{1,0:T(8,128)(2,1)S(1)} %get-tuple-element.49.low_ref, bf16[224,768]{1,0:T(8,128)(2,1)S(1)} %get-tuple-element.48.high_ref, bf16[1568,224]{1,0:T(8,128)(2,1)S(1)} %tables.1.refs_4_.tables_ref.refs_7_, ...), custom_call_target="tpu_custom_call" | custom-call | tf_op jit(solution)/shard_map/outer/pallas_call | solution.py:28
  44.4 0.0 collective-permute-done.8.refs_2_
  44.4 4.5 %inner.1 = (f32[6,224,128]{2,1,0:T(8,128)S(1)}, f32[6,224,128]{2,1,0:T(8,128)S(1)}, bf16[224,768]{1,0:T(8,128)(2,1)S(1)}, bf16[56,576]{1,0:T(8,128)(2,1)S(1)}, b...) custom-call(bf16[56,768]{1,0:T(8,128)(2,1)S(1)} %get-tuple-element.50.refs_0_, ...), custom_call_target="tpu_custom_call" | custom-call | tf_op jit(solution)/shard_map/inner/pallas_call | solution.py:28
  49.0 4.8 %fix.1 = (bf16[224,768]{1,0:T(8,128)(2,1)S(1)}, bf16[224,768]{1,0:T(8,128)(2,1)S(1)}, bf16[224,640]{1,0:T(8,128)(2,1)S(1)}, bf16[224,640]{1,0:T(8,128)(2,1)S(1)}...) custom-call(bf16[224,768]{1,0:T(8,128)(2,1)S(1)} %collective-permute, ...), custom_call_target="tpu_custom_call" | custom-call | tf_op jit(solution)/shard_map/fix/pallas_call | solution.py:28
  53.8 4.9 %collective-permute-start.16 = (bf16[224,640]{1,0:T(8,128)(2,1)S(1)}, bf16[224,640]{1,0:T(8,128)(2,1)S(1)}, u32[]{:S(2)}, u32[]{:S(2)}) collective-permute-start(bf16[224,640]{1,0:T(8,128)(2,1)S(1)} %get-tuple-element.67), channel_id=1, source_target_pairs={{0,1},{1,2},{2,3},{3,4},{4,5},{5,6},{6,7},{8,9},{9,10},{10,11},{11... | collective-permute-start | bytes 860168 | tf_op jit(solution)/shard_map/ppermute | solution.py:324
  58.7 1.5 %collective-permute-start.17 = (bf16[224,640]{1,0:T(8,128)(2,1)S(1)}, bf16[224,640]{1,0:T(8,128)(2,1)S(1)}, u32[]{:S(2)}, u32[]{:S(2)}) collective-permute-start(bf16[224,640]{1,0:T(8,128)(2,1)S(1)} %get-tuple-element.68), channel_id=1, source_target_pairs={{1,0},{2,1},{3,2},{4,3},{5,4},{6,5},{7,6},{9,8},{10,9},{11,10},{12... | collective-permute-start | bytes 860168 | tf_op jit(solution)/shard_map/ppermute | solution.py:324
  60.2 0.8 collective-permute-start.13
  61.0 2.3 %collective-permute-start.14 = (bf16[56,576]{1,0:T(8,128)(2,1)S(1)}, bf16[56,576]{1,0:T(8,128)(2,1)S(1)}, u32[]{:S(2)}, u32[]{:S(2)}) collective-permute-start(bf16[56,576]{1,0:T(8,128)(2,1)S(1)} %get-tuple-element.65), channel_id=1, source_target_pairs={{0,16},{8,24},{16,0},{24,8},{1,17},{9,25},{17,1},{25,9},{2,18},{10... | collective-permute-start | bytes 193544 | tf_op jit(solution)/shard_map/ppermute | solution.py:316
  63.2 0.8 collective-permute-start.10
  64.0 12.2 %own.1 = (f32[6,224,128]{2,1,0:T(8,128)S(1)}, f32[6,224,128]{2,1,0:T(8,128)S(1)}, bf16[56,576]{1,0:T(8,128)(2,1)S(1)}, bf16[56,576]{1,0:T(8,128)(2,1)S(1)}, bf16...) custom-call(bf16[224,768]{1,0:T(8,128)(2,1)S(1)} %get-tuple-element.69.low_ref, ...), custom_call_target="tpu_custom_call" | custom-call | tf_op jit(solution)/shard_map/own/pallas_call | solution.py:28
  76.2 1.4 %collective-permute-start.15 = (bf16[56,576]{1,0:T(8,128)(2,1)S(1)}, bf16[56,576]{1,0:T(8,128)(2,1)S(1)}, u32[]{:S(2)}, u32[]{:S(2)}) collective-permute-start(bf16[56,576]{1,0:T(8,128)(2,1)S(1)} %get-tuple-element.66), channel_id=1, source_target_pairs={{0,24},{8,16},{16,8},{24,0},{1,25},{9,17},{17,9},{25,1},{2,26},{10... | collective-permute-start | bytes 193544 | tf_op jit(solution)/shard_map/ppermute | solution.py:316
  77.6 1.4 %collective-permute-start.11 = (bf16[2,56,576]{2,1,0:T(8,128)(2,1)S(1)}, bf16[2,56,576]{2,1,0:T(8,128)(2,1)S(1)}, u32[]{:S(2)}, u32[]{:S(2)}) collective-permute-start(bf16[2,56,576]{2,1,0:T(8,128)(2,1)S(1)} %get-tuple-element.61), channel_id=1, source_target_pairs={{0,16},{8,24},{16,0},{24,8},{1,17},{9,25},{17,1},{25,9},{2,18},{10... | collective-permute-start | bytes 387080 | tf_op jit(solution)/shard_map/ppermute | solution.py:316
  79.0 1.4 %collective-permute-start.12 = (bf16[2,56,576]{2,1,0:T(8,128)(2,1)S(1)}, bf16[2,56,576]{2,1,0:T(8,128)(2,1)S(1)}, u32[]{:S(2)}, u32[]{:S(2)}) collective-permute-start(bf16[2,56,576]{2,1,0:T(8,128)(2,1)S(1)} %get-tuple-element.62), channel_id=1, source_target_pairs={{0,24},{8,16},{16,8},{24,0},{1,25},{9,17},{17,9},{25,1},{2,26},{10... | collective-permute-start | bytes 387080 | tf_op jit(solution)/shard_map/ppermute | solution.py:316
  80.4 0.7 collective-permute-start.21
  81.1 4.1 %last.1 = (bf16[2,56,576]{2,1,0:T(8,128)(2,1)S(1)}, bf16[2,56,576]{2,1,0:T(8,128)(2,1)S(1)}, bf16[2,56,576]{2,1,0:T(8,128)(2,1)S(1)}, bf16[2,56,576]{2,1,0:T(8,128)(2,1)S(1)}) custom-call(bf16[224,640]{1,0:T(8,128)(2,1)S(1)} %collective-permute-done.16.before_ref, bf16[224,640]{1,0:T(8,128)(2,1)S(1)} %collective-permute-done.17.after_ref, ...), custom_call_target="tpu_custom_call" | custom-call | tf_op jit(solution)/shard_map/last/pallas_call | solution.py:28
  85.3 1.3 %collective-permute-start.18 = (bf16[2,56,576]{2,1,0:T(8,128)(2,1)S(1)}, bf16[2,56,576]{2,1,0:T(8,128)(2,1)S(1)}, u32[]{:S(2)}, u32[]{:S(2)}) collective-permute-start(bf16[2,56,576]{2,1,0:T(8,128)(2,1)S(1)} %get-tuple-element.75), channel_id=1, source_target_pairs={{0,8},{8,0},{16,24},{24,16},{1,9},{9,1},{17,25},{25,17},{2,10},{10... | collective-permute-start | bytes 387080 | tf_op jit(solution)/shard_map/ppermute | solution.py:316
  86.6 1.2 %collective-permute-done.21.refs_5_ = bf16[56,576]{1,0:T(8,128)(2,1)S(1)} collective-permute-done((bf16[56,576]{1,0:T(8,128)(2,1)S(1)}, bf16[56,576]{1,0:T(8,128)(2,1)S(1)}, u32[]{:S(2)}, u32[]{:S(2)}) %collective-permute-start.21) | collective-permute-done | bytes 64544 | tf_op jit(solution)/shard_map/ppermute | solution.py:316
  87.8 2.3 %collective-permute-start.19 = (bf16[2,56,576]{2,1,0:T(8,128)(2,1)S(1)}, bf16[2,56,576]{2,1,0:T(8,128)(2,1)S(1)}, u32[]{:S(2)}, u32[]{:S(2)}) collective-permute-start(bf16[2,56,576]{2,1,0:T(8,128)(2,1)S(1)} %get-tuple-element.76), channel_id=1, source_target_pairs={{0,16},{8,24},{16,0},{24,8},{1,17},{9,25},{17,1},{25,9},{2,18},{10... | collective-permute-start | bytes 387080 | tf_op jit(solution)/shard_map/ppermute | solution.py:316
  90.1 2.6 %collective-permute-start.20 = (bf16[2,56,576]{2,1,0:T(8,128)(2,1)S(1)}, bf16[2,56,576]{2,1,0:T(8,128)(2,1)S(1)}, u32[]{:S(2)}, u32[]{:S(2)}) collective-permute-start(bf16[2,56,576]{2,1,0:T(8,128)(2,1)S(1)} %get-tuple-element.77), channel_id=1, source_target_pairs={{0,24},{8,16},{16,8},{24,0},{1,25},{9,17},{17,9},{25,1},{2,26},{10... | collective-permute-start | bytes 387080 | tf_op jit(solution)/shard_map/ppermute | solution.py:316
  92.7 2.0 %collective-permute-start.23 = (bf16[56,576]{1,0:T(8,128)(2,1)S(1)}, bf16[56,576]{1,0:T(8,128)(2,1)S(1)}, u32[]{:S(2)}, u32[]{:S(2)}) collective-permute-start(bf16[56,576]{1,0:T(8,128)(2,1)S(1)} %get-tuple-element.81), channel_id=1, source_target_pairs={{0,24},{8,16},{16,8},{24,0},{1,25},{9,17},{17,9},{25,1},{2,26},{10... | collective-permute-start | bytes 193544 | tf_op jit(solution)/shard_map/ppermute | solution.py:316
  94.6 1.2 %join.2 = bf16[3,53,2304]{2,1,0:T(8,128)(2,1)} custom-call(s32[1]{0:T(128)} %bitcast.me_ref, bf16[2,56,576]{2,1,0:T(8,128)(2,1)S(1)} %get-tuple-element.59.refs_0_, bf16[2,56,576]{2,1,0:T(8,128)(2,1)S(1)} %collective-permute-done.10.refs_1_, bf16[2,56,576]{2,1,0:T(8,128)(2,1)S(1)} %collective-permute-done.11.refs_2_, ...), custom_call_target="tpu_custom_call" | custom-call | tf_op jit(solution)/shard_map/join/pallas_call | solution.py:28
  95.8 16.7 %collective-permute-done.22.refs_6_ = bf16[56,576]{1,0:T(8,128)(2,1)S(1)} collective-permute-done((bf16[56,576]{1,0:T(8,128)(2,1)S(1)}, bf16[56,576]{1,0:T(8,128)(2,1)S(1)}, u32[]{:S(2)}, u32[]{:S(2)}) %collective-permute-start.22) | collective-permute-done | bytes 64544 | tf_op jit(solution)/shard_map/ppermute | solution.py:316
  112.5 1.2 %join.3 = bf16[3,53,2304]{2,1,0:T(8,128)(2,1)} custom-call(s32[1]{0:T(128)} %bitcast.me_ref, bf16[2,56,576]{2,1,0:T(8,128)(2,1)S(1)} %get-tuple-element.74.refs_0_, bf16[2,56,576]{2,1,0:T(8,128)(2,1)S(1)} %collective-permute-done.18.refs_1_, bf16[2,56,576]{2,1,0:T(8,128)(2,1)S(1)} %collective-permute-done.19.refs_2_, ...), custom_call_target="tpu_custom_call" | custom-call | tf_op jit(solution)/shard_map/join/pallas_call | solution.py:28
  (33 shorter events, 0.2 us)
Async XLA Ops:
  0.6 0.9 copy-start
  1.6 1.1 copy-start.1
  2.7 0.8 copy-start.2
  4.3 16.2 %collective-permute-start.3 = (f32[7,2304]{1,0:T(8,128)S(1)}, f32[7,2304]{1,0:T(8,128)S(1)}, u32[]{:S(2)}, u32[]{:S(2)}) collective-permute-start(f32[7,2304]{1,0:T(8,128)S(1)} %get-tuple-element.46), channel_id=1, source_target_pairs={{0,1},{1,2},{2,3},{3,4},{4,5},{5,6},{6,7},{8,9},{9,10},{10,11},{11... | collective-permute-start | bytes 193544 | tf_op jit(solution)/shard_map/ppermute | solution.py:324
  6.7 13.8 %collective-permute-start.4 = (f32[7,2304]{1,0:T(8,128)S(1)}, f32[7,2304]{1,0:T(8,128)S(1)}, u32[]{:S(2)}, u32[]{:S(2)}) collective-permute-start(f32[7,2304]{1,0:T(8,128)S(1)} %get-tuple-element.47), channel_id=1, source_target_pairs={{1,0},{2,1},{3,2},{4,3},{5,4},{6,5},{7,6},{9,8},{10,9},{11,10},{12... | collective-permute-start | bytes 193544 | tf_op jit(solution)/shard_map/ppermute | solution.py:324
  8.0 13.1 %collective-permute-start = (bf16[2,56,768]{2,1,0:T(8,128)(2,1)S(1)}, bf16[2,56,768]{2,1,0:T(8,128)(2,1)S(1)}, u32[]{:S(2)}, u32[]{:S(2)}) collective-permute-start(bf16[2,56,768]{2,1,0:T(8,128)(2,1)S(1)} %get-tuple-element.43), channel_id=1, source_target_pairs={{0,8},{8,0},{16,24},{24,16},{1,9},{9,1},{17,25},{25,17},{2,10},{10... | collective-permute-start | bytes 516104 | tf_op jit(solution)/shard_map/ppermute | solution.py:316
  10.5 10.7 %collective-permute-start.1 = (bf16[2,56,768]{2,1,0:T(8,128)(2,1)S(1)}, bf16[2,56,768]{2,1,0:T(8,128)(2,1)S(1)}, u32[]{:S(2)}, u32[]{:S(2)}) collective-permute-start(bf16[2,56,768]{2,1,0:T(8,128)(2,1)S(1)} %get-tuple-element.44), channel_id=1, source_target_pairs={{0,16},{8,24},{16,0},{24,8},{1,17},{9,25},{17,1},{25,9},{2,18},{10... | collective-permute-start | bytes 516104 | tf_op jit(solution)/shard_map/ppermute | solution.py:316
  13.1 11.1 %collective-permute-start.2 = (bf16[2,56,768]{2,1,0:T(8,128)(2,1)S(1)}, bf16[2,56,768]{2,1,0:T(8,128)(2,1)S(1)}, u32[]{:S(2)}, u32[]{:S(2)}) collective-permute-start(bf16[2,56,768]{2,1,0:T(8,128)(2,1)S(1)} %get-tuple-element.45), channel_id=1, source_target_pairs={{0,24},{8,16},{16,8},{24,0},{1,25},{9,17},{17,9},{25,1},{2,26},{10... | collective-permute-start | bytes 516104 | tf_op jit(solution)/shard_map/ppermute | solution.py:316
  24.2 24.8 %collective-permute-start.5 = (bf16[224,768]{1,0:T(8,128)(2,1)S(1)}, bf16[224,768]{1,0:T(8,128)(2,1)S(1)}, u32[]{:S(2)}, u32[]{:S(2)}) collective-permute-start(bf16[224,768]{1,0:T(8,128)(2,1)S(1)} %get-tuple-element.48.high_ref), channel_id=1, source_target_pairs={{0,1},{1,2},{2,3},{3,4},{4,5},{5,6},{6,7},{8,9},{9,10},{10,11},{11... | collective-permute-start | bytes 1032200 | tf_op jit(solution)/shard_map/ppermute | solution.py:324
  29.0 20.0 %collective-permute-start.6 = (bf16[224,768]{1,0:T(8,128)(2,1)S(1)}, bf16[224,768]{1,0:T(8,128)(2,1)S(1)}, u32[]{:S(2)}, u32[]{:S(2)}) collective-permute-start(bf16[224,768]{1,0:T(8,128)(2,1)S(1)} %get-tuple-element.49.low_ref), channel_id=1, source_target_pairs={{1,0},{2,1},{3,2},{4,3},{5,4},{6,5},{7,6},{9,8},{10,9},{11,10},{12... | collective-permute-start | bytes 1032200 | tf_op jit(solution)/shard_map/ppermute | solution.py:324
  30.3 14.1 %collective-permute-start.7 = (bf16[56,768]{1,0:T(8,128)(2,1)S(1)}, bf16[56,768]{1,0:T(8,128)(2,1)S(1)}, u32[]{:S(2)}, u32[]{:S(2)}) collective-permute-start(bf16[56,768]{1,0:T(8,128)(2,1)S(1)} %get-tuple-element.51), channel_id=1, source_target_pairs={{0,8},{8,0},{16,24},{24,16},{1,9},{9,1},{17,25},{25,17},{2,10},{10... | collective-permute-start | bytes 258056 | tf_op jit(solution)/shard_map/ppermute | solution.py:316
  33.5 10.9 %collective-permute-start.8 = (bf16[56,768]{1,0:T(8,128)(2,1)S(1)}, bf16[56,768]{1,0:T(8,128)(2,1)S(1)}, u32[]{:S(2)}, u32[]{:S(2)}) collective-permute-start(bf16[56,768]{1,0:T(8,128)(2,1)S(1)} %get-tuple-element.52), channel_id=1, source_target_pairs={{0,16},{8,24},{16,0},{24,8},{1,17},{9,25},{17,1},{25,9},{2,18},{10... | collective-permute-start | bytes 258056 | tf_op jit(solution)/shard_map/ppermute | solution.py:316
  34.6 9.9 %collective-permute-start.9 = (bf16[56,768]{1,0:T(8,128)(2,1)S(1)}, bf16[56,768]{1,0:T(8,128)(2,1)S(1)}, u32[]{:S(2)}, u32[]{:S(2)}) collective-permute-start(bf16[56,768]{1,0:T(8,128)(2,1)S(1)} %get-tuple-element.53), channel_id=1, source_target_pairs={{0,24},{8,16},{16,8},{24,0},{1,25},{9,17},{17,9},{25,1},{2,26},{10... | collective-permute-start | bytes 258056 | tf_op jit(solution)/shard_map/ppermute | solution.py:316
  53.8 25.2 %collective-permute-start.16 = (bf16[224,640]{1,0:T(8,128)(2,1)S(1)}, bf16[224,640]{1,0:T(8,128)(2,1)S(1)}, u32[]{:S(2)}, u32[]{:S(2)}) collective-permute-start(bf16[224,640]{1,0:T(8,128)(2,1)S(1)} %get-tuple-element.67), channel_id=1, source_target_pairs={{0,1},{1,2},{2,3},{3,4},{4,5},{5,6},{6,7},{8,9},{9,10},{10,11},{11... | collective-permute-start | bytes 860168 | tf_op jit(solution)/shard_map/ppermute | solution.py:324
  58.7 21.7 %collective-permute-start.17 = (bf16[224,640]{1,0:T(8,128)(2,1)S(1)}, bf16[224,640]{1,0:T(8,128)(2,1)S(1)}, u32[]{:S(2)}, u32[]{:S(2)}) collective-permute-start(bf16[224,640]{1,0:T(8,128)(2,1)S(1)} %get-tuple-element.68), channel_id=1, source_target_pairs={{1,0},{2,1},{3,2},{4,3},{5,4},{6,5},{7,6},{9,8},{10,9},{11,10},{12... | collective-permute-start | bytes 860168 | tf_op jit(solution)/shard_map/ppermute | solution.py:324
  60.2 16.0 %collective-permute-start.13 = (bf16[56,576]{1,0:T(8,128)(2,1)S(1)}, bf16[56,576]{1,0:T(8,128)(2,1)S(1)}, u32[]{:S(2)}, u32[]{:S(2)}) collective-permute-start(bf16[56,576]{1,0:T(8,128)(2,1)S(1)} %get-tuple-element.64), channel_id=1, source_target_pairs={{0,8},{8,0},{16,24},{24,16},{1,9},{9,1},{17,25},{25,17},{2,10},{10... | collective-permute-start | bytes 193544 | tf_op jit(solution)/shard_map/ppermute | solution.py:316
  61.0 16.7 %collective-permute-start.14 = (bf16[56,576]{1,0:T(8,128)(2,1)S(1)}, bf16[56,576]{1,0:T(8,128)(2,1)S(1)}, u32[]{:S(2)}, u32[]{:S(2)}) collective-permute-start(bf16[56,576]{1,0:T(8,128)(2,1)S(1)} %get-tuple-element.65), channel_id=1, source_target_pairs={{0,16},{8,24},{16,0},{24,8},{1,17},{9,25},{17,1},{25,9},{2,18},{10... | collective-permute-start | bytes 193544 | tf_op jit(solution)/shard_map/ppermute | solution.py:316
  63.2 26.9 %collective-permute-start.10 = (bf16[2,56,576]{2,1,0:T(8,128)(2,1)S(1)}, bf16[2,56,576]{2,1,0:T(8,128)(2,1)S(1)}, u32[]{:S(2)}, u32[]{:S(2)}) collective-permute-start(bf16[2,56,576]{2,1,0:T(8,128)(2,1)S(1)} %get-tuple-element.60), channel_id=1, source_target_pairs={{0,8},{8,0},{16,24},{24,16},{1,9},{9,1},{17,25},{25,17},{2,10},{10... | collective-permute-start | bytes 387080 | tf_op jit(solution)/shard_map/ppermute | solution.py:316
  76.2 9.1 %collective-permute-start.15 = (bf16[56,576]{1,0:T(8,128)(2,1)S(1)}, bf16[56,576]{1,0:T(8,128)(2,1)S(1)}, u32[]{:S(2)}, u32[]{:S(2)}) collective-permute-start(bf16[56,576]{1,0:T(8,128)(2,1)S(1)} %get-tuple-element.66), channel_id=1, source_target_pairs={{0,24},{8,16},{16,8},{24,0},{1,25},{9,17},{17,9},{25,1},{2,26},{10... | collective-permute-start | bytes 193544 | tf_op jit(solution)/shard_map/ppermute | solution.py:316
  77.6 15.0 %collective-permute-start.11 = (bf16[2,56,576]{2,1,0:T(8,128)(2,1)S(1)}, bf16[2,56,576]{2,1,0:T(8,128)(2,1)S(1)}, u32[]{:S(2)}, u32[]{:S(2)}) collective-permute-start(bf16[2,56,576]{2,1,0:T(8,128)(2,1)S(1)} %get-tuple-element.61), channel_id=1, source_target_pairs={{0,16},{8,24},{16,0},{24,8},{1,17},{9,25},{17,1},{25,9},{2,18},{10... | collective-permute-start | bytes 387080 | tf_op jit(solution)/shard_map/ppermute | solution.py:316
  79.0 13.7 %collective-permute-start.12 = (bf16[2,56,576]{2,1,0:T(8,128)(2,1)S(1)}, bf16[2,56,576]{2,1,0:T(8,128)(2,1)S(1)}, u32[]{:S(2)}, u32[]{:S(2)}) collective-permute-start(bf16[2,56,576]{2,1,0:T(8,128)(2,1)S(1)} %get-tuple-element.62), channel_id=1, source_target_pairs={{0,24},{8,16},{16,8},{24,0},{1,25},{9,17},{17,9},{25,1},{2,26},{10... | collective-permute-start | bytes 387080 | tf_op jit(solution)/shard_map/ppermute | solution.py:316
  80.4 7.4 %collective-permute-start.21 = (bf16[56,576]{1,0:T(8,128)(2,1)S(1)}, bf16[56,576]{1,0:T(8,128)(2,1)S(1)}, u32[]{:S(2)}, u32[]{:S(2)}) collective-permute-start(bf16[56,576]{1,0:T(8,128)(2,1)S(1)} %get-tuple-element.79), channel_id=1, source_target_pairs={{0,8},{8,0},{16,24},{24,16},{1,9},{9,1},{17,25},{25,17},{2,10},{10... | collective-permute-start | bytes 193544 | tf_op jit(solution)/shard_map/ppermute | solution.py:316
  85.3 27.2 %collective-permute-start.18 = (bf16[2,56,576]{2,1,0:T(8,128)(2,1)S(1)}, bf16[2,56,576]{2,1,0:T(8,128)(2,1)S(1)}, u32[]{:S(2)}, u32[]{:S(2)}) collective-permute-start(bf16[2,56,576]{2,1,0:T(8,128)(2,1)S(1)} %get-tuple-element.75), channel_id=1, source_target_pairs={{0,8},{8,0},{16,24},{24,16},{1,9},{9,1},{17,25},{25,17},{2,10},{10... | collective-permute-start | bytes 387080 | tf_op jit(solution)/shard_map/ppermute | solution.py:316
  87.8 24.7 %collective-permute-start.19 = (bf16[2,56,576]{2,1,0:T(8,128)(2,1)S(1)}, bf16[2,56,576]{2,1,0:T(8,128)(2,1)S(1)}, u32[]{:S(2)}, u32[]{:S(2)}) collective-permute-start(bf16[2,56,576]{2,1,0:T(8,128)(2,1)S(1)} %get-tuple-element.76), channel_id=1, source_target_pairs={{0,16},{8,24},{16,0},{24,8},{1,17},{9,25},{17,1},{25,9},{2,18},{10... | collective-permute-start | bytes 387080 | tf_op jit(solution)/shard_map/ppermute | solution.py:316
  90.1 22.4 %collective-permute-start.20 = (bf16[2,56,576]{2,1,0:T(8,128)(2,1)S(1)}, bf16[2,56,576]{2,1,0:T(8,128)(2,1)S(1)}, u32[]{:S(2)}, u32[]{:S(2)}) collective-permute-start(bf16[2,56,576]{2,1,0:T(8,128)(2,1)S(1)} %get-tuple-element.77), channel_id=1, source_target_pairs={{0,24},{8,16},{16,8},{24,0},{1,25},{9,17},{17,9},{25,1},{2,26},{10... | collective-permute-start | bytes 387080 | tf_op jit(solution)/shard_map/ppermute | solution.py:316
  92.6 19.8 %collective-permute-start.22 = (bf16[56,576]{1,0:T(8,128)(2,1)S(1)}, bf16[56,576]{1,0:T(8,128)(2,1)S(1)}, u32[]{:S(2)}, u32[]{:S(2)}) collective-permute-start(bf16[56,576]{1,0:T(8,128)(2,1)S(1)} %get-tuple-element.80), channel_id=1, source_target_pairs={{0,16},{8,24},{16,0},{24,8},{1,17},{9,25},{17,1},{25,9},{2,18},{10... | collective-permute-start | bytes 193544 | tf_op jit(solution)/shard_map/ppermute | solution.py:316
  92.7 19.8 %collective-permute-start.23 = (bf16[56,576]{1,0:T(8,128)(2,1)S(1)}, bf16[56,576]{1,0:T(8,128)(2,1)S(1)}, u32[]{:S(2)}, u32[]{:S(2)}) collective-permute-start(bf16[56,576]{1,0:T(8,128)(2,1)S(1)} %get-tuple-element.81), channel_id=1, source_target_pairs={{0,24},{8,16},{16,8},{24,0},{1,25},{9,17},{17,9},{25,1},{2,26},{10... | collective-permute-start | bytes 193544 | tf_op jit(solution)/shard_map/ppermute | solution.py:316

commit v3 on v2

--- a/solution.py
+++ b/solution.py
@@ -21,7 +21,7 @@
     return -(-value // step) * step
 
 
-def call(kernel, name, out_shape, args, scratch=(), scalars=0, unread=0):
+def call(kernel, name, micros, out_shape, args, scratch=(), scalars=0, unread=0):
     in_specs = [pl.BlockSpec(memory_space=pltpu.SMEM)] * scalars
     in_specs += [pl.BlockSpec(memory_space=VMEM)] * (len(args) - scalars - unread)
     in_specs += [pl.BlockSpec(memory_space=pl.ANY)] * unread
@@ -32,21 +32,18 @@
         out_specs=[pl.BlockSpec(memory_space=VMEM)] * len(out_shape),
         scratch_shapes=scratch,
         compiler_params=pltpu.CompilerParams(vmem_limit_bytes=40 << 20),
+        cost_estimate=pl.CostEstimate(flops=0, bytes_accessed=int(micros * 3.6e6), transcendentals=0),
         name=name,
     )(*args)
 
 
-def cut_kernel(count, chunk, me_ref, x_ref, mean_ref, other_ref, *refs):
+def cut_kernel(count, chunk, me_ref, x_ref, *refs):
     edge_refs, middle_refs = refs[:count], refs[count : 2 * count]
-    low_ref, high_ref, held = refs[2 * count :]
+    held = refs[2 * count]
     planes, own, cells = x_ref.shape
     _, padded, width = edge_refs[0].shape
     halo = REACH * NXY
     me = me_ref[0]
-    for out_ref, plane in ((low_ref, 0), (high_ref, planes - 1)):
-        out_ref[0:1, :] = mean_ref[plane : plane + 1, :]
-        for field in range(other_ref.shape[0]):
-            out_ref[field + 1 : field + 2, :] = other_ref[field, plane : plane + 1, :]
     held[...] = jnp.zeros_like(held)
     lane = lax.broadcasted_iota(jnp.int32, (padded, LANES), 1)
     for plane in range(planes):
@@ -77,7 +74,14 @@
                         middle_refs[step][...] = window
 
 
-def tables_kernel(fields, entries_ref, products_ref, slots_ref, out_ref, by_column):
+def sides_kernel(mean_ref, other_ref, _, low_ref, high_ref):
+    for out_ref, plane in ((low_ref, 0), (high_ref, mean_ref.shape[0] - 1)):
+        out_ref[0:1, :] = mean_ref[plane : plane + 1, :]
+        for field in range(other_ref.shape[0]):
+            out_ref[field + 1 : field + 2, :] = other_ref[field, plane : plane + 1, :]
+
+
+def tables_kernel(fields, entries_ref, products_ref, slots_ref, _, out_ref, by_column):
     rows = by_column.shape[1]
     total = entries_ref.shape[1]
     names = slots_ref.shape[1]
@@ -160,21 +164,20 @@
 def weigh(mixed, weights_ref, plane, ways, sums):
     _, tiles, rows, _ = sums.shape
     fields = weights_ref.shape[1]
-
-    @pl.loop(0, rows // BLOCK * tiles)
-    def _(index):
-        block, tile = index // tiles, index % tiles
-        here = pl.ds(pl.multiple_of(block * BLOCK, BLOCK), BLOCK)
-        base = pl.multiple_of(block * (fields * BLOCK), fields * BLOCK)
-        totals = [jnp.zeros((BLOCK, LANES), F32) for _ in ways]
-        for field in range(fields):
-            values = mixed[tile, pl.ds(base + field * BLOCK, BLOCK), :].astype(F32)
+    for tile in range(tiles):
+        for block in range(rows // BLOCK):
+            totals = [None] * len(ways)
+            for field in range(fields):
+                start = (block * fields + field) * BLOCK
+                values = mixed[tile, start : start + BLOCK, :].astype(F32)
+                for i, way in enumerate(ways):
+                    term = spread(weights_ref[plane, field, way, tile]) * values
+                    totals[i] = term if field == 0 else totals[i] + term
+            here = slice(block * BLOCK, (block + 1) * BLOCK)
             for i, way in enumerate(ways):
-                totals[i] += spread(weights_ref[plane, field, way, tile]) * values
-        for i, way in enumerate(ways):
-            sums[way, tile, here, :] = totals[i]
-        if len(ways) == 6:
-            sums[ALL, tile, here, :] = functools.reduce(jnp.add, totals)
+                sums[way, tile, here, :] = totals[i]
+            if len(ways) == 6:
+                sums[ALL, tile, here, :] = functools.reduce(jnp.add, totals)
 
 
 def settle(sums, masks_ref, write):
@@ -224,24 +227,38 @@
     settle(sums, masks_ref, write)
 
 
-def emit(result, masks_ref, whole_ref, piece_refs, plane):
+def fill(result, masks_ref, out_ref):
     tiles, rows, _ = result.shape
-    if whole_ref is not None:
-        for tile in range(tiles):
-            inside = jnp.broadcast_to(masks_ref[2, tile][None], (rows // 8, 8, LANES)).reshape(rows, LANES)
-            whole_ref[:, tile * LANES : (tile + 1) * LANES] = (result[tile] * inside).astype(BF16)
-    padded, chunk = piece_refs[0].shape[-2:]
+    for tile in range(tiles):
+        inside = jnp.broadcast_to(masks_ref[2, tile][None], (rows // 8, 8, LANES)).reshape(rows, LANES)
+        out_ref[:, tile * LANES : (tile + 1) * LANES] = (result[tile] * inside).astype(BF16)
+
+
+def packing(planes, chunk):
+    full, odd = divmod(chunk, LANES)
+    beside = LANES // odd if odd else 0
+    return full, odd, beside, planes * full + (-(-planes // beside) if odd else 0)
+
+
+def emit(results, chunk, piece_refs):
+    full, odd, beside, _ = packing(len(results), chunk)
+    padded = piece_refs[0].shape[1]
+    lane = lax.broadcasted_iota(jnp.int32, (padded, LANES), 1)
     for step, piece_ref in enumerate(piece_refs):
-        for tile in range(up(chunk, LANES) // LANES):
-            lanes = min(LANES, chunk - tile * LANES)
-            part = result[tile, step * padded : (step + 1) * padded, :][:, :lanes].astype(BF16)
-            if plane is None:
-                piece_ref[:, tile * LANES : tile * LANES + lanes] = part
-            else:
-                piece_ref[plane, :, tile * LANES : tile * LANES + lanes] = part
-
-
-def outer_kernel(low_ref, high_ref, tables_ref, weights_ref, masks_ref, low_out, high_out, middle_out, mixed, sums):
+        here = slice(step * padded, (step + 1) * padded)
+        for plane, result in enumerate(results):
+            for tile in range(full):
+                piece_ref[plane * full + tile] = result[tile, here, :].astype(BF16)
+        for first in range(0, len(results) if odd else 0, beside or 1):
+            packed = results[first][full, here, :]
+            for place in range(1, min(beside, len(results) - first)):
+                turned = pltpu.roll(results[first + place][full, here, :], place * odd, 1)
+                packed = jnp.where(lane < place * odd, packed, turned)
+            piece_ref[len(results) * full + first // beside] = packed.astype(BF16)
+
+
+def outer_kernel(low_ref, high_ref, tables_ref, weights_ref, masks_ref, *refs):
+    low_out, high_out, middle_out, mixed, sums = refs[-5:]
     outer(
         low_ref[...], high_ref[...], tables_ref, weights_ref, masks_ref, low_out, high_out, middle_out, mixed, sums
     )
@@ -250,52 +267,57 @@
 def inner_kernel(count, *refs):
     parts = refs[:count]
     low_in, high_in, middle_in, tables_ref, weights_ref, masks_ref = refs[count : count + 6]
-    low_out, high_out, whole_ref, *pieces = refs[count + 6 : 2 * count + 9]
-    mixed, sums, result = refs[2 * count + 9 :]
+    low_out, high_out, middle_out, whole_ref, mixed, sums = refs[count + 6 :]
     values = joined([part[...] for part in parts])
     inner(
-        values, low_in, high_in, middle_in, tables_ref, weights_ref, masks_ref, low_out, high_out, result, mixed, sums
-    )
-    emit(result, masks_ref, whole_ref, pieces, None)
-
-
-def own_kernel(low_ref, values_ref, high_ref, tables_ref, weights_ref, masks_ref, low_out, high_out, *refs):
-    *pieces, mixed, sums, result, middle, low, high = refs
+        values, low_in, high_in, middle_in, tables_ref, weights_ref, masks_ref, low_out, high_out, middle_out, mixed, sums
+    )
+    fill(middle_out, masks_ref, whole_ref)
+
+
+def own_kernel(
+    low_ref, values_ref, high_ref, tables_ref, weights_ref, masks_ref, low_out, high_out, middle_out, mixed, sums, *held
+):
+    low, high, middle = held
     outer(low_ref[...], high_ref[...], tables_ref, weights_ref, masks_ref, low, high, middle, mixed, sums)
     inner(
-        values_ref[...], low, high, middle, tables_ref, weights_ref, masks_ref, low_out, high_out, result, mixed, sums
-    )
-    emit(result, masks_ref, None, pieces, None)
-
-
-def fix_kernel(count, first, before_ref, after_ref, low_in, high_in, tables_ref, weights_ref, masks_ref, *refs):
+        values_ref[...], low, high, middle, tables_ref, weights_ref, masks_ref, low_out, high_out, middle_out, mixed, sums
+    )
+
+
+def fix_kernel(count, chunk, first, before_ref, after_ref, low_in, high_in, middle_in, *refs):
+    tables_ref, weights_ref, masks_ref, *refs = refs
     if first:
         wholes, nears, refs = refs[:2], refs[2:4], refs[4:]
-    pieces, (mixed, sums, result) = refs[:count], refs[count:]
+    pieces, (mixed, sums, low, high) = refs[:count], refs[count:]
     last = weights_ref.shape[0] - 1
-    sides = ((before_ref, low_in, 0, LAST_Z), (after_ref, high_in, last, NEXT_Z))
-    for side, (halo_ref, share_ref, plane, way) in enumerate(sides):
+    sides = ((before_ref, low_in, low, 0, LAST_Z), (after_ref, high_in, high, last, NEXT_Z))
+    for side, (halo_ref, share_ref, result, plane, way) in enumerate(sides):
         mix(tables_ref, halo_ref[...], mixed)
         weigh(mixed, weights_ref, plane, (way,), sums)
         for tile in range(sums.shape[1]):
             result[tile] = SCALE * (share_ref[tile] - sums[way, tile])
-        emit(result, masks_ref, wholes[side] if first else None, pieces, side)
         if first:
+            fill(result, masks_ref, wholes[side])
             nears[side][...] = wholes[side][:, : nears[side].shape[1]]
-
-
-def join_kernel(count, me_ref, *refs):
-    edge_refs, middle_refs, (out_ref, held) = refs[:count], refs[count : 2 * count], refs[2 * count :]
-    planes, own, cells = out_ref.shape
+    emit((low, middle_in, high), chunk, pieces)
+
+
+def join_kernel(count, chunk, me_ref, *refs):
+    piece_refs, (out_ref, held) = refs[:count], refs[count:]
+    planes, own, _ = out_ref.shape
+    full, odd, beside, _ = packing(planes, chunk)
     me = me_ref[0]
     for step in range(count):
-        source = lax.bitwise_xor(me, step)
-        held[source, 0] = edge_refs[step][0].astype(F32)
-        held[source, 1] = middle_refs[step][...].astype(F32)
-        held[source, 2] = edge_refs[step][1].astype(F32)
+        held[lax.bitwise_xor(me, step)] = piece_refs[step][...].astype(F32)
     for plane in range(planes):
-        line = jnp.concatenate([held[source, plane] for source in range(count)], axis=1)
-        out_ref[plane] = line[:own].astype(BF16)
+        parts = []
+        for source in range(count):
+            parts += [held[source, plane * full + tile] for tile in range(full)]
+            if odd:
+                tile, place = planes * full + plane // beside, plane % beside
+                parts.append(held[source, tile][:, place * odd : (place + 1) * odd])
+        out_ref[plane] = jnp.concatenate(parts, axis=1)[:own].astype(BF16)
 
 
 def shards(panels, mean_field, fluctuations, products, triples, owner_slot):
@@ -329,8 +351,9 @@
     cut = call(
         functools.partial(cut_kernel, count, chunk),
         "cut",
-        [shape(2, padded, width)] * count + [shape(padded, width)] * count + [shape(fields, cells, dtype=F32)] * 2,
-        (me_array, jnp.transpose(panels, (1, 0, 2)), mean_field, fluctuations),
+        1,
+        [shape(2, padded, width)] * count + [shape(padded, width)] * count,
+        (me_array, jnp.transpose(panels, (1, 0, 2))),
         [VMEM((padded, cells), F32)],
         scalars=1,
     )
@@ -346,12 +369,22 @@
     (tables,) = call(
         functools.partial(tables_kernel, fields),
         "tables",
+        5,
         [shape(fields * rows, rows)],
-        (entries, values, slots),
+        (entries, values, slots, cut[0]),
         [VMEM((3, rows, total), BF16)],
-    )
-
-    before, after = neighbours(*cut[2 * count :])
+        unread=1,
+    )
+
+    sides = call(
+        sides_kernel,
+        "sides",
+        0.2,
+        [shape(fields, cells, dtype=F32)] * 2,
+        (mean_field, fluctuations, tables),
+        unread=1,
+    )
+    before, after = neighbours(*sides)
     conduct = jnp.concatenate([mean_field[:, None], fluctuations.transpose(1, 0, 2)], axis=1)
     conduct = jnp.concatenate([before[None], conduct, after[None]], axis=0)
     conduct = jnp.pad(conduct, ((0, 0), (0, 0), (halo, halo)))
@@ -366,74 +399,76 @@
     masks = jnp.stack([place % NXY < NXY - 1, place % NXY > 0, inside]).astype(F32)
     masks = jnp.broadcast_to(masks.reshape(3, tiles, 1, LANES), (3, tiles, 8, LANES))
     (weights,) = call(
-        weights_kernel, "weights", [shape(planes, fields, 6, tiles, 8, LANES, dtype=F32)], (conduct, masks)
+        weights_kernel, "weights", 0.3, [shape(planes, fields, 6, tiles, 8, LANES, dtype=F32)], (conduct, masks)
     )
 
     common = (tables, weights, masks)
     plane_whole = shape(rows, width)
     share = shape(tiles, rows, LANES, dtype=F32)
-    piece, pair = shape(padded, chunk), shape(2, padded, chunk)
-    mixed = VMEM((tiles, fields * rows, LANES), BF16)
-    sums = VMEM((7, tiles, rows, LANES), F32)
-    result = VMEM((tiles, rows, LANES), F32)
+    pieces = [shape(packing(planes, chunk)[-1], padded, LANES)] * count
+    near_tiles = near // LANES
+
+    def scratch(tiles, held):
+        held = [VMEM((tiles, rows, LANES), F32)] * held
+        return [VMEM((tiles, fields * rows, LANES), BF16), VMEM((7, tiles, rows, LANES), F32)] + held
 
     low, high = call(
-        functools.partial(edges_kernel, count), "edges", [plane_whole] * 2, (*edges, tables, weights), unread=2
+        functools.partial(edges_kernel, count), "edges", 0.5, [plane_whole] * 2, (*edges, tables, weights), unread=2
     )
     before, after = neighbours(low, high)
-    low, high, middle = call(outer_kernel, "outer", [share] * 3, (low, high, *common), [mixed, sums])
-    low, high, middle, *first_middles = call(
+    low, high, middle = call(
+        outer_kernel,
+        "outer",
+        6,
+        [share] * 3,
+        (low, high, *common, *middles[1:]),
+        scratch(tiles, 0),
+        unread=count - 1,
+    )
+    low, high, middle, middle_whole = call(
         functools.partial(inner_kernel, count),
         "inner",
-        [share] * 2 + [plane_whole] + [piece] * count,
+        3,
+        [share] * 3 + [plane_whole],
         (*middles, low, high, middle, *common),
-        [mixed, sums, result],
-    )
-    first_middles = exchanged(first_middles)
-    low, high, low_near, high_near, *first_edges = call(
-        functools.partial(fix_kernel, count, True),
+        scratch(tiles, 0),
+    )
+    low, high, low_near, high_near, *first = call(
+        functools.partial(fix_kernel, count, chunk, True),
         "fix",
-        [plane_whole] * 2 + [shape(rows, near)] * 2 + [pair] * count,
-        (before, after, low, high, *common),
-        [mixed, sums, result],
+        3,
+        [plane_whole] * 2 + [shape(rows, near)] * 2 + pieces,
+        (before, after, low, high, middle, *common),
+        scratch(tiles, 2),
     )
     before, after = neighbours(low_near, high_near)
-    first_edges = exchanged(first_edges)
-    low, high, *second_middles = call(
-        own_kernel,
-        "own",
-        [share] * 2 + [piece] * count,
-        (low, middle, high, *common),
-        [mixed, sums] + [result] * 4,
-    )
-    second_middles = exchanged(second_middles)
-    near_tiles = near // LANES
-    second_edges = exchanged(
-        call(
-            functools.partial(fix_kernel, count, False),
-            "last",
-            [pair] * count,
-            (before, after, low, high, *common),
-            [
-                VMEM((near_tiles, fields * rows, LANES), BF16),
-                VMEM((7, near_tiles, rows, LANES), F32),
-                VMEM((near_tiles, rows, LANES), F32),
-            ],
-        )
-    )
-
-    def join(edge_parts, middle_parts):
+    first = exchanged(first)
+    low, high, middle = call(
+        own_kernel, "own", 9, [share] * 3, (low, middle_whole, high, *common), scratch(tiles, 3)
+    )
+    second = call(
+        functools.partial(fix_kernel, count, chunk, False),
+        "last",
+        3,
+        pieces,
+        (before, after, low, high, middle, *common),
+        scratch(near_tiles, 2),
+    )
+    second = exchanged(second)
+
+    def join(parts):
         (result,) = call(
-            functools.partial(join_kernel, count),
+            functools.partial(join_kernel, count, chunk),
             "join",
+            1,
             [shape(planes, own, cells)],
-            (me_array, *edge_parts, *middle_parts),
-            [VMEM((count, planes, padded, chunk), F32)],
+            (me_array, *parts),
+            [VMEM((count,) + pieces[0].shape, F32)],
             scalars=1,
         )
         return jnp.transpose(result, (1, 0, 2))
 
-    return join(first_edges, first_middles), join(second_edges, second_middles)
+    return join(first), join(second)
 
 
 def solution(mesh):

time: 116 us -> 98.6 us (0.85)
  the two profiles are of different devices: /device:TPU:0 before, /device:TPU:10 now
where the time goes in v3:
time: 98.6 us; the launch traced here: 98.1 us
  starting transfers between devices  32.7 us (33%)
  Pallas kernels  31.2 us (32%)
  waiting for transfers between devices  28 us (28%)
  local copies, waits for them, and re-layouts  4.43 us (4%)
    pallas_call x12, Pallas kernels, call(): pl.pallas_call(kernel, out_shape=out_shape, in_specs=in_specs, out_specs=...  31.2 us
    ppermute x12, waiting for transfers between devices, exchange(): return lax.ppermute(block, 'chaos', [(i, i ^ step) for i in range(count)])  26.2 us
    ppermute x12, starting transfers between devices, exchange(): return lax.ppermute(block, 'chaos', [(i, i ^ step) for i in range(count)])  14.8 us
    ppermute x3, starting transfers between devices, neighbours(): lax.ppermute(first_plane, 'space', downward)  9.61 us
    ppermute x3, starting transfers between devices, neighbours(): lax.ppermute(last_plane, 'space', upward)  8.31 us
    unnamed x7, local copies, waits for them, and re-layouts  2.87 us
  transfers between devices with their start and end apart: 18, of which 7 were waited for; matrix products, arithmetic and copies ran while one was open for 3% of the time, Pallas kernels for 28%

profile of v3, /device:TPU:10, one launch (start us, length us, event | category | flops | bytes accessed | tf_op | source)
XLA Modules:
  0.0 98.1 jit_solution(660775503850075918)
XLA Ops:
  0.6 1.1 %copy-done.1 = bf16[53,3,2304]{2,0,1:T(8,128)(2,1)S(1)} copy-done((bf16[53,3,2304]{2,0,1:T(8,128)(2,1)S(1)}, bf16[53,3,2304]{2,0,1:T(8,128)(2,1)}, u32[]{:S(2)}) %copy-start.1) | copy-done | bytes 732696
  1.8 0.8 cut.1
  2.6 0.5 collective-permute-start
  3.1 2.6 %collective-permute-start.1 = (bf16[2,56,768]{2,1,0:T(8,128)(2,1)S(1)}, bf16[2,56,768]{2,1,0:T(8,128)(2,1)S(1)}, u32[]{:S(2)}, u32[]{:S(2)}) collective-permute-start(bf16[2,56,768]{2,1,0:T(8,128)(2,1)S(1)} %get-tuple-element.38), channel_id=1, source_target_pairs={{0,16},{8,24},{16,0},{24,8},{1,17},{9,25},{17,1},{25,9},{2,18},{10... | collective-permute-start | bytes 516104 | tf_op jit(solution)/shard_map/ppermute | solution.py:338
  5.7 0.5 collective-permute-start.2
  6.2 0.7 multiply_subtract_fusion
  6.9 0.7 pad.17
  7.6 0.7 pad.16.entries_ref
  8.3 5.1 %tables.1._.refs_4_.tables_ref.refs_7_.refs_0_ = bf16[1568,224]{1,0:T(8,128)(2,1)S(1)} custom-call(s32[8,1280]{1,0:T(8,128)S(1)} %pad.16.entries_ref, f32[1,1280]{1,0:T(1,128)S(1)} %broadcast_in_dim.23.products_ref, f32[16,256]{1,0:T(8,128)S(1)} %broadcast_in_dim.24.slots_ref, bf16[2,56,768]{2,1,0:T(8,128)(2,1)S(1)} %get-tuple-element.36._.refs_0_), custom_call_target="tpu_custom_call" | custom-call | bytes 18000000 | tf_op jit(solution)/shard_map/tables/pallas_call | solution.py:28
  13.5 0.0 copy-start
  13.5 0.9 copy-done
  14.4 0.8 copy-done.2
  15.2 1.9 %collective-permute-start.3 = (f32[7,2304]{1,0:T(8,128)S(1)}, f32[7,2304]{1,0:T(8,128)S(1)}, u32[]{:S(2)}, u32[]{:S(2)}) collective-permute-start(f32[7,2304]{1,0:T(8,128)S(1)} %get-tuple-element.40), channel_id=1, source_target_pairs={{0,1},{1,2},{2,3},{3,4},{4,5},{5,6},{6,7},{8,9},{9,10},{10,11},{11... | collective-permute-start | bytes 193544 | tf_op jit(solution)/shard_map/ppermute | solution.py:346
  17.1 3.6 %collective-permute-start.4 = (f32[7,2304]{1,0:T(8,128)S(1)}, f32[7,2304]{1,0:T(8,128)S(1)}, u32[]{:S(2)}, u32[]{:S(2)}) collective-permute-start(f32[7,2304]{1,0:T(8,128)S(1)} %get-tuple-element.41), channel_id=1, source_target_pairs={{1,0},{2,1},{3,2},{4,3},{5,4},{6,5},{7,6},{9,8},{10,9},{11,10},{12... | collective-permute-start | bytes 193544 | tf_op jit(solution)/shard_map/ppermute | solution.py:346
  20.9 0.0 collective-permute-done.3
  20.9 1.8 %collective-permute-done.4 = f32[7,2304]{1,0:T(8,128)S(1)} collective-permute-done((f32[7,2304]{1,0:T(8,128)S(1)}, f32[7,2304]{1,0:T(8,128)S(1)}, u32[]{:S(2)}, u32[]{:S(2)}) %collective-permute-start.4) | collective-permute-done | bytes 64544 | tf_op jit(solution)/shard_map/ppermute | solution.py:346
  22.7 0.1 fusion.3
  22.9 0.1 slice.8
  23.0 0.1 pad_maximum_fusion.conduct_ref
  23.1 0.3 weights.1.refs_5_.weights_ref.refs_8_.refs_1_
  23.4 0.0 collective-permute-done.refs_1_
  23.4 4.5 %collective-permute-start.5 = (bf16[224,768]{1,0:T(8,128)(2,1)S(1)}, bf16[224,768]{1,0:T(8,128)(2,1)S(1)}, u32[]{:S(2)}, u32[]{:S(2)}) collective-permute-start(bf16[224,768]{1,0:T(8,128)(2,1)S(1)} %get-tuple-element.42.high_ref), channel_id=1, source_target_pairs={{0,1},{1,2},{2,3},{3,4},{4,5},{5,6},{6,7},{8,9},{9,10},{10,11},{11... | collective-permute-start | bytes 1032200 | tf_op jit(solution)/shard_map/ppermute | solution.py:346
  27.9 2.1 %collective-permute-start.6 = (bf16[224,768]{1,0:T(8,128)(2,1)S(1)}, bf16[224,768]{1,0:T(8,128)(2,1)S(1)}, u32[]{:S(2)}, u32[]{:S(2)}) collective-permute-start(bf16[224,768]{1,0:T(8,128)(2,1)S(1)} %get-tuple-element.43.low_ref), channel_id=1, source_target_pairs={{1,0},{2,1},{3,2},{4,3},{5,4},{6,5},{7,6},{9,8},{10,9},{11,10},{12... | collective-permute-start | bytes 1032200 | tf_op jit(solution)/shard_map/ppermute | solution.py:346
  30.0 1.4 %collective-permute-start.7 = (bf16[56,768]{1,0:T(8,128)(2,1)S(1)}, bf16[56,768]{1,0:T(8,128)(2,1)S(1)}, u32[]{:S(2)}, u32[]{:S(2)}) collective-permute-start(bf16[56,768]{1,0:T(8,128)(2,1)S(1)} %get-tuple-element.45), channel_id=1, source_target_pairs={{0,8},{8,0},{16,24},{24,16},{1,9},{9,1},{17,25},{25,17},{2,10},{10... | collective-permute-start | bytes 258056 | tf_op jit(solution)/shard_map/ppermute | solution.py:338
  31.4 2.2 %collective-permute-start.8 = (bf16[56,768]{1,0:T(8,128)(2,1)S(1)}, bf16[56,768]{1,0:T(8,128)(2,1)S(1)}, u32[]{:S(2)}, u32[]{:S(2)}) collective-permute-start(bf16[56,768]{1,0:T(8,128)(2,1)S(1)} %get-tuple-element.46), channel_id=1, source_target_pairs={{0,16},{8,24},{16,0},{24,8},{1,17},{9,25},{17,1},{25,9},{2,18},{10... | collective-permute-start | bytes 258056 | tf_op jit(solution)/shard_map/ppermute | solution.py:338
  33.7 0.5 collective-permute-start.9
  34.1 0.9 collective-permute-done.7.refs_0_.refs_1_
  35.0 5.2 %collective-permute-done.8.refs_1_.refs_2_ = bf16[56,768]{1,0:T(8,128)(2,1)S(1)} collective-permute-done((bf16[56,768]{1,0:T(8,128)(2,1)S(1)}, bf16[56,768]{1,0:T(8,128)(2,1)S(1)}, u32[]{:S(2)}, u32[]{:S(2)}) %collective-permute-start.8) | collective-permute-done | bytes 86048 | tf_op jit(solution)/shard_map/ppermute | solution.py:338
  40.2 2.3 %collective-permute-done.9.refs_2_.refs_3_ = bf16[56,768]{1,0:T(8,128)(2,1)S(1)} collective-permute-done((bf16[56,768]{1,0:T(8,128)(2,1)S(1)}, bf16[56,768]{1,0:T(8,128)(2,1)S(1)}, u32[]{:S(2)}, u32[]{:S(2)}) %collective-permute-start.9) | collective-permute-done | bytes 86048 | tf_op jit(solution)/shard_map/ppermute | solution.py:338
  42.6 6.2 %outer.1 = (f32[6,224,128]{2,1,0:T(8,128)S(1)}, f32[6,224,128]{2,1,0:T(8,128)S(1)}, f32[6,224,128]{2,1,0:T(8,128)S(1)}) custom-call(bf16[224,768]{1,0:T(8,128)(2,1)S(1)} %get-tuple-element.43.low_ref, bf16[224,768]{1,0:T(8,128)(2,1)S(1)} %get-tuple-element.42.high_ref, bf16[1568,224]{1,0:T(8,128)(2,1)S(1)} %tables.1._.refs_4_.tables_ref.refs_7_.refs_0_, ...), custom_call_target="tpu_custom_call" | custom-call | bytes 21600000 | tf_op jit(solution)/shard_map/outer/pallas_call | solution.py:28
  48.8 3.4 %inner.1 = (f32[6,224,128]{2,1,0:T(8,128)S(1)}, f32[6,224,128]{2,1,0:T(8,128)S(1)}, f32[6,224,128]{2,1,0:T(8,128)S(1)}, bf16[224,768]{1,0:T(8,128)(2,1)S(1)}) custom-call(bf16[56,768]{1,0:T(8,128)(2,1)S(1)} %get-tuple-element.44.refs_0_, bf16[56,768]{1,0:T(8,128)(2,1)S(1)} %collective-permute-done.7.refs_0_.refs_1_, ...), custom_call_target="tpu_custom_call" | custom-call | bytes 10800000 | tf_op jit(solution)/shard_map/inner/pallas_call | solution.py:28
  52.2 0.0 collective-permute-done.5.before_ref
  52.2 1.7 %fix.1 = (bf16[224,768]{1,0:T(8,128)(2,1)S(1)}, bf16[224,768]{1,0:T(8,128)(2,1)S(1)}, bf16[224,640]{1,0:T(8,128)(2,1)S(1)}, bf16[224,640]{1,0:T(8,128)(2,1)S(1)}...) custom-call(bf16[224,768]{1,0:T(8,128)(2,1)S(1)} %collective-permute, ...), custom_call_target="tpu_custom_call" | custom-call | bytes 10800000 | tf_op jit(solution)/shard_map/fix/pallas_call | solution.py:28
  53.9 1.9 %collective-permute-start.13 = (bf16[224,640]{1,0:T(8,128)(2,1)S(1)}, bf16[224,640]{1,0:T(8,128)(2,1)S(1)}, u32[]{:S(2)}, u32[]{:S(2)}) collective-permute-start(bf16[224,640]{1,0:T(8,128)(2,1)S(1)} %get-tuple-element.58), channel_id=1, source_target_pairs={{0,1},{1,2},{2,3},{3,4},{4,5},{5,6},{6,7},{8,9},{9,10},{10,11},{11... | collective-permute-start | bytes 860168 | tf_op jit(solution)/shard_map/ppermute | solution.py:346
  55.8 3.9 %collective-permute-start.14 = (bf16[224,640]{1,0:T(8,128)(2,1)S(1)}, bf16[224,640]{1,0:T(8,128)(2,1)S(1)}, u32[]{:S(2)}, u32[]{:S(2)}) collective-permute-start(bf16[224,640]{1,0:T(8,128)(2,1)S(1)} %get-tuple-element.59), channel_id=1, source_target_pairs={{1,0},{2,1},{3,2},{4,3},{5,4},{6,5},{7,6},{9,8},{10,9},{11,10},{12... | collective-permute-start | bytes 860168 | tf_op jit(solution)/shard_map/ppermute | solution.py:346
  59.7 0.1 collective-permute-start.10
  59.8 3.0 %collective-permute-start.11 = (bf16[14,56,128]{2,1,0:T(8,128)(2,1)S(1)}, bf16[14,56,128]{2,1,0:T(8,128)(2,1)S(1)}, u32[]{:S(2)}, u32[]{:S(2)}) collective-permute-start(bf16[14,56,128]{2,1,0:T(8,128)(2,1)S(1)} %get-tuple-element.56), channel_id=1, source_target_pairs={{0,16},{8,24},{16,0},{24,8},{1,17},{9,25},{17,1},{25,9},{2,18},{10... | collective-permute-start | bytes 602120 | tf_op jit(solution)/shard_map/ppermute | solution.py:338
  62.8 0.4 collective-permute-start.12
  63.3 9.7 %own.1 = (f32[6,224,128]{2,1,0:T(8,128)S(1)}, f32[6,224,128]{2,1,0:T(8,128)S(1)}, f32[6,224,128]{2,1,0:T(8,128)S(1)}) custom-call(bf16[224,768]{1,0:T(8,128)(2,1)S(1)} %get-tuple-element.60.low_ref, bf16[224,768]{1,0:T(8,128)(2,1)S(1)} %get-tuple-element.61.values_ref, bf16[224,768]{1,0:T(8,128)(2,1)S(1)} %get-tuple-element.62.high_ref, ...), custom_call_target="tpu_custom_call" | custom-call | bytes 32400000 | tf_op jit(solution)/shard_map/own/pallas_call | solution.py:28
  73.0 1.5 %last.1 = (bf16[14,56,128]{2,1,0:T(8,128)(2,1)S(1)}, bf16[14,56,128]{2,1,0:T(8,128)(2,1)S(1)}, bf16[14,56,128]{2,1,0:T(8,128)(2,1)S(1)}, bf16[14,56,128]{2,1,0:T(8,128)(2,1)S(1)}) custom-call(bf16[224,640]{1,0:T(8,128)(2,1)S(1)} %collective-permute-done.13.before_ref, bf16[224,640]{1,0:T(8,128)(2,1)S(1)} %collective-permute-done.14.after_ref, ...), custom_call_target="tpu_custom_call" | custom-call | bytes 10800000 | tf_op jit(solution)/shard_map/last/pallas_call | solution.py:28
  74.5 1.1 %collective-permute-start.15 = (bf16[14,56,128]{2,1,0:T(8,128)(2,1)S(1)}, bf16[14,56,128]{2,1,0:T(8,128)(2,1)S(1)}, u32[]{:S(2)}, u32[]{:S(2)}) collective-permute-start(bf16[14,56,128]{2,1,0:T(8,128)(2,1)S(1)} %get-tuple-element.67), channel_id=1, source_target_pairs={{0,8},{8,0},{16,24},{24,16},{1,9},{9,1},{17,25},{25,17},{2,10},{10... | collective-permute-start | bytes 602120 | tf_op jit(solution)/shard_map/ppermute | solution.py:338
  75.6 2.0 %collective-permute-start.16 = (bf16[14,56,128]{2,1,0:T(8,128)(2,1)S(1)}, bf16[14,56,128]{2,1,0:T(8,128)(2,1)S(1)}, u32[]{:S(2)}, u32[]{:S(2)}) collective-permute-start(bf16[14,56,128]{2,1,0:T(8,128)(2,1)S(1)} %get-tuple-element.68), channel_id=1, source_target_pairs={{0,16},{8,24},{16,0},{24,8},{1,17},{9,25},{17,1},{25,9},{2,18},{10... | collective-permute-start | bytes 602120 | tf_op jit(solution)/shard_map/ppermute | solution.py:338
  77.6 0.4 collective-permute-start.17
  78.1 12.4 %collective-permute-done.12.refs_3_ = bf16[14,56,128]{2,1,0:T(8,128)(2,1)S(1)} collective-permute-done((bf16[14,56,128]{2,1,0:T(8,128)(2,1)S(1)}, bf16[14,56,128]{2,1,0:T(8,128)(2,1)S(1)}, u32[]{:S(2)}, u32[]{:S(2)}) %collective-permute-start.12) | collective-permute-done | bytes 200736 | tf_op jit(solution)/shard_map/ppermute | solution.py:338
  90.5 1.2 %join.2 = bf16[3,53,2304]{2,1,0:T(8,128)(2,1)} custom-call(s32[1]{0:T(128)} %bitcast.me_ref, bf16[14,56,128]{2,1,0:T(8,128)(2,1)S(1)} %get-tuple-element.54.refs_0_, bf16[14,56,128]{2,1,0:T(8,128)(2,1)S(1)} %collective-permute-done.10.refs_1_, bf16[14,56,128]{2,1,0:T(8,128)(2,1)S(1)} %collective-permute-done.11.refs_2_, ...), custom_call_target="tpu_custom_call" | custom-call | bytes 3600000 | tf_op jit(solution)/shard_map/join/pallas_call | solution.py:28
  91.7 1.7 %collective-permute-done.16.refs_2_ = bf16[14,56,128]{2,1,0:T(8,128)(2,1)S(1)} collective-permute-done((bf16[14,56,128]{2,1,0:T(8,128)(2,1)S(1)}, bf16[14,56,128]{2,1,0:T(8,128)(2,1)S(1)}, u32[]{:S(2)}, u32[]{:S(2)}) %collective-permute-start.16) | collective-permute-done | bytes 200736 | tf_op jit(solution)/shard_map/ppermute | solution.py:338
  93.4 3.6 %collective-permute-done.17.refs_3_ = bf16[14,56,128]{2,1,0:T(8,128)(2,1)S(1)} collective-permute-done((bf16[14,56,128]{2,1,0:T(8,128)(2,1)S(1)}, bf16[14,56,128]{2,1,0:T(8,128)(2,1)S(1)}, u32[]{:S(2)}, u32[]{:S(2)}) %collective-permute-start.17) | collective-permute-done | bytes 200736 | tf_op jit(solution)/shard_map/ppermute | solution.py:338
  97.0 1.2 %join.3 = bf16[3,53,2304]{2,1,0:T(8,128)(2,1)} custom-call(s32[1]{0:T(128)} %bitcast.me_ref, bf16[14,56,128]{2,1,0:T(8,128)(2,1)S(1)} %get-tuple-element.66.refs_0_, bf16[14,56,128]{2,1,0:T(8,128)(2,1)S(1)} %collective-permute-done.15.refs_1_, bf16[14,56,128]{2,1,0:T(8,128)(2,1)S(1)} %collective-permute-done.16.refs_2_, ...), custom_call_target="tpu_custom_call" | custom-call | bytes 3600000 | tf_op jit(solution)/shard_map/join/pallas_call | solution.py:28
  (22 shorter events, 0.2 us)
Async XLA Ops:
  0.6 1.1 %copy-start.1 = (bf16[53,3,2304]{2,0,1:T(8,128)(2,1)S(1)}, bf16[53,3,2304]{2,0,1:T(8,128)(2,1)}, u32[]{:S(2)}) copy-start(bf16[53,3,2304]{2,0,1:T(8,128)(2,1)} %param.6) | copy-start | bytes 2198020
  2.6 20.7 %collective-permute-start = (bf16[2,56,768]{2,1,0:T(8,128)(2,1)S(1)}, bf16[2,56,768]{2,1,0:T(8,128)(2,1)S(1)}, u32[]{:S(2)}, u32[]{:S(2)}) collective-permute-start(bf16[2,56,768]{2,1,0:T(8,128)(2,1)S(1)} %get-tuple-element.37), channel_id=1, source_target_pairs={{0,8},{8,0},{16,24},{24,16},{1,9},{9,1},{17,25},{25,17},{2,10},{10... | collective-permute-start | bytes 516104 | tf_op jit(solution)/shard_map/ppermute | solution.py:338
  3.1 20.2 %collective-permute-start.1 = (bf16[2,56,768]{2,1,0:T(8,128)(2,1)S(1)}, bf16[2,56,768]{2,1,0:T(8,128)(2,1)S(1)}, u32[]{:S(2)}, u32[]{:S(2)}) collective-permute-start(bf16[2,56,768]{2,1,0:T(8,128)(2,1)S(1)} %get-tuple-element.38), channel_id=1, source_target_pairs={{0,16},{8,24},{16,0},{24,8},{1,17},{9,25},{17,1},{25,9},{2,18},{10... | collective-permute-start | bytes 516104 | tf_op jit(solution)/shard_map/ppermute | solution.py:338
  5.7 17.7 %collective-permute-start.2 = (bf16[2,56,768]{2,1,0:T(8,128)(2,1)S(1)}, bf16[2,56,768]{2,1,0:T(8,128)(2,1)S(1)}, u32[]{:S(2)}, u32[]{:S(2)}) collective-permute-start(bf16[2,56,768]{2,1,0:T(8,128)(2,1)S(1)} %get-tuple-element.39), channel_id=1, source_target_pairs={{0,24},{8,16},{16,8},{24,0},{1,25},{9,17},{17,9},{25,1},{2,26},{10... | collective-permute-start | bytes 516104 | tf_op jit(solution)/shard_map/ppermute | solution.py:338
  13.5 0.9 copy-start
  14.4 0.8 copy-start.2
  15.2 5.7 %collective-permute-start.3 = (f32[7,2304]{1,0:T(8,128)S(1)}, f32[7,2304]{1,0:T(8,128)S(1)}, u32[]{:S(2)}, u32[]{:S(2)}) collective-permute-start(f32[7,2304]{1,0:T(8,128)S(1)} %get-tuple-element.40), channel_id=1, source_target_pairs={{0,1},{1,2},{2,3},{3,4},{4,5},{5,6},{6,7},{8,9},{9,10},{10,11},{11... | collective-permute-start | bytes 193544 | tf_op jit(solution)/shard_map/ppermute | solution.py:346
  17.1 5.6 %collective-permute-start.4 = (f32[7,2304]{1,0:T(8,128)S(1)}, f32[7,2304]{1,0:T(8,128)S(1)}, u32[]{:S(2)}, u32[]{:S(2)}) collective-permute-start(f32[7,2304]{1,0:T(8,128)S(1)} %get-tuple-element.41), channel_id=1, source_target_pairs={{1,0},{2,1},{3,2},{4,3},{5,4},{6,5},{7,6},{9,8},{10,9},{11,10},{12... | collective-permute-start | bytes 193544 | tf_op jit(solution)/shard_map/ppermute | solution.py:346
  23.4 28.8 %collective-permute-start.5 = (bf16[224,768]{1,0:T(8,128)(2,1)S(1)}, bf16[224,768]{1,0:T(8,128)(2,1)S(1)}, u32[]{:S(2)}, u32[]{:S(2)}) collective-permute-start(bf16[224,768]{1,0:T(8,128)(2,1)S(1)} %get-tuple-element.42.high_ref), channel_id=1, source_target_pairs={{0,1},{1,2},{2,3},{3,4},{4,5},{5,6},{6,7},{8,9},{9,10},{10,11},{11... | collective-permute-start | bytes 1032200 | tf_op jit(solution)/shard_map/ppermute | solution.py:346
  27.9 24.3 %collective-permute-start.6 = (bf16[224,768]{1,0:T(8,128)(2,1)S(1)}, bf16[224,768]{1,0:T(8,128)(2,1)S(1)}, u32[]{:S(2)}, u32[]{:S(2)}) collective-permute-start(bf16[224,768]{1,0:T(8,128)(2,1)S(1)} %get-tuple-element.43.low_ref), channel_id=1, source_target_pairs={{1,0},{2,1},{3,2},{4,3},{5,4},{6,5},{7,6},{9,8},{10,9},{11,10},{12... | collective-permute-start | bytes 1032200 | tf_op jit(solution)/shard_map/ppermute | solution.py:346
  30.0 5.0 %collective-permute-start.7 = (bf16[56,768]{1,0:T(8,128)(2,1)S(1)}, bf16[56,768]{1,0:T(8,128)(2,1)S(1)}, u32[]{:S(2)}, u32[]{:S(2)}) collective-permute-start(bf16[56,768]{1,0:T(8,128)(2,1)S(1)} %get-tuple-element.45), channel_id=1, source_target_pairs={{0,8},{8,0},{16,24},{24,16},{1,9},{9,1},{17,25},{25,17},{2,10},{10... | collective-permute-start | bytes 258056 | tf_op jit(solution)/shard_map/ppermute | solution.py:338
  31.4 8.8 %collective-permute-start.8 = (bf16[56,768]{1,0:T(8,128)(2,1)S(1)}, bf16[56,768]{1,0:T(8,128)(2,1)S(1)}, u32[]{:S(2)}, u32[]{:S(2)}) collective-permute-start(bf16[56,768]{1,0:T(8,128)(2,1)S(1)} %get-tuple-element.46), channel_id=1, source_target_pairs={{0,16},{8,24},{16,0},{24,8},{1,17},{9,25},{17,1},{25,9},{2,18},{10... | collective-permute-start | bytes 258056 | tf_op jit(solution)/shard_map/ppermute | solution.py:338
  33.7 8.9 %collective-permute-start.9 = (bf16[56,768]{1,0:T(8,128)(2,1)S(1)}, bf16[56,768]{1,0:T(8,128)(2,1)S(1)}, u32[]{:S(2)}, u32[]{:S(2)}) collective-permute-start(bf16[56,768]{1,0:T(8,128)(2,1)S(1)} %get-tuple-element.47), channel_id=1, source_target_pairs={{0,24},{8,16},{16,8},{24,0},{1,25},{9,17},{17,9},{25,1},{2,26},{10... | collective-permute-start | bytes 258056 | tf_op jit(solution)/shard_map/ppermute | solution.py:338
  53.9 19.1 %collective-permute-start.13 = (bf16[224,640]{1,0:T(8,128)(2,1)S(1)}, bf16[224,640]{1,0:T(8,128)(2,1)S(1)}, u32[]{:S(2)}, u32[]{:S(2)}) collective-permute-start(bf16[224,640]{1,0:T(8,128)(2,1)S(1)} %get-tuple-element.58), channel_id=1, source_target_pairs={{0,1},{1,2},{2,3},{3,4},{4,5},{5,6},{6,7},{8,9},{9,10},{10,11},{11... | collective-permute-start | bytes 860168 | tf_op jit(solution)/shard_map/ppermute | solution.py:346
  55.8 17.2 %collective-permute-start.14 = (bf16[224,640]{1,0:T(8,128)(2,1)S(1)}, bf16[224,640]{1,0:T(8,128)(2,1)S(1)}, u32[]{:S(2)}, u32[]{:S(2)}) collective-permute-start(bf16[224,640]{1,0:T(8,128)(2,1)S(1)} %get-tuple-element.59), channel_id=1, source_target_pairs={{1,0},{2,1},{3,2},{4,3},{5,4},{6,5},{7,6},{9,8},{10,9},{11,10},{12... | collective-permute-start | bytes 860168 | tf_op jit(solution)/shard_map/ppermute | solution.py:346
  59.7 17.9 %collective-permute-start.10 = (bf16[14,56,128]{2,1,0:T(8,128)(2,1)S(1)}, bf16[14,56,128]{2,1,0:T(8,128)(2,1)S(1)}, u32[]{:S(2)}, u32[]{:S(2)}) collective-permute-start(bf16[14,56,128]{2,1,0:T(8,128)(2,1)S(1)} %get-tuple-element.55), channel_id=1, source_target_pairs={{0,8},{8,0},{16,24},{24,16},{1,9},{9,1},{17,25},{25,17},{2,10},{10... | collective-permute-start | bytes 602120 | tf_op jit(solution)/shard_map/ppermute | solution.py:338
  59.8 18.3 %collective-permute-start.11 = (bf16[14,56,128]{2,1,0:T(8,128)(2,1)S(1)}, bf16[14,56,128]{2,1,0:T(8,128)(2,1)S(1)}, u32[]{:S(2)}, u32[]{:S(2)}) collective-permute-start(bf16[14,56,128]{2,1,0:T(8,128)(2,1)S(1)} %get-tuple-element.56), channel_id=1, source_target_pairs={{0,16},{8,24},{16,0},{24,8},{1,17},{9,25},{17,1},{25,9},{2,18},{10... | collective-permute-start | bytes 602120 | tf_op jit(solution)/shard_map/ppermute | solution.py:338
  62.8 27.7 %collective-permute-start.12 = (bf16[14,56,128]{2,1,0:T(8,128)(2,1)S(1)}, bf16[14,56,128]{2,1,0:T(8,128)(2,1)S(1)}, u32[]{:S(2)}, u32[]{:S(2)}) collective-permute-start(bf16[14,56,128]{2,1,0:T(8,128)(2,1)S(1)} %get-tuple-element.57), channel_id=1, source_target_pairs={{0,24},{8,16},{16,8},{24,0},{1,25},{9,17},{17,9},{25,1},{2,26},{10... | collective-permute-start | bytes 602120 | tf_op jit(solution)/shard_map/ppermute | solution.py:338
  74.5 17.2 %collective-permute-start.15 = (bf16[14,56,128]{2,1,0:T(8,128)(2,1)S(1)}, bf16[14,56,128]{2,1,0:T(8,128)(2,1)S(1)}, u32[]{:S(2)}, u32[]{:S(2)}) collective-permute-start(bf16[14,56,128]{2,1,0:T(8,128)(2,1)S(1)} %get-tuple-element.67), channel_id=1, source_target_pairs={{0,8},{8,0},{16,24},{24,16},{1,9},{9,1},{17,25},{25,17},{2,10},{10... | collective-permute-start | bytes 602120 | tf_op jit(solution)/shard_map/ppermute | solution.py:338
  75.6 17.8 %collective-permute-start.16 = (bf16[14,56,128]{2,1,0:T(8,128)(2,1)S(1)}, bf16[14,56,128]{2,1,0:T(8,128)(2,1)S(1)}, u32[]{:S(2)}, u32[]{:S(2)}) collective-permute-start(bf16[14,56,128]{2,1,0:T(8,128)(2,1)S(1)} %get-tuple-element.68), channel_id=1, source_target_pairs={{0,16},{8,24},{16,0},{24,8},{1,17},{9,25},{17,1},{25,9},{2,18},{10... | collective-permute-start | bytes 602120 | tf_op jit(solution)/shard_map/ppermute | solution.py:338
  77.6 19.3 %collective-permute-start.17 = (bf16[14,56,128]{2,1,0:T(8,128)(2,1)S(1)}, bf16[14,56,128]{2,1,0:T(8,128)(2,1)S(1)}, u32[]{:S(2)}, u32[]{:S(2)}) collective-permute-start(bf16[14,56,128]{2,1,0:T(8,128)(2,1)S(1)} %get-tuple-element.69), channel_id=1, source_target_pairs={{0,24},{8,16},{16,8},{24,0},{1,25},{9,17},{17,9},{25,1},{2,26},{10... | collective-permute-start | bytes 602120 | tf_op jit(solution)/shard_map/ppermute | solution.py:338

commit v4 on v3

--- a/solution.py
+++ b/solution.py
@@ -37,13 +37,12 @@
     )(*args)
 
 
-def cut_kernel(count, chunk, me_ref, x_ref, *refs):
-    edge_refs, middle_refs = refs[:count], refs[count : 2 * count]
-    held = refs[2 * count]
+def cut_kernel(count, chunk, place_ref, x_ref, *refs):
+    *out_refs, held = refs
     planes, own, cells = x_ref.shape
-    _, padded, width = edge_refs[0].shape
+    _, padded, width = out_refs[0].shape
     halo = REACH * NXY
-    me = me_ref[0]
+    me, turn = place_ref[0], place_ref[1]
     held[...] = jnp.zeros_like(held)
     lane = lax.broadcasted_iota(jnp.int32, (padded, LANES), 1)
     for plane in range(planes):
@@ -66,36 +65,46 @@
 
                 @pl.when(lax.bitwise_xor(me, target) == step)
                 def _():
-                    if plane == 0:
-                        edge_refs[step][0] = window
-                    elif plane == planes - 1:
-                        edge_refs[step][1] = window
-                    else:
-                        middle_refs[step][...] = window
-
-
-def sides_kernel(mean_ref, other_ref, _, low_ref, high_ref):
-    for out_ref, plane in ((low_ref, 0), (high_ref, mean_ref.shape[0] - 1)):
-        out_ref[0:1, :] = mean_ref[plane : plane + 1, :]
+                    out_refs[step][plane + turn * (planes - 1 - 2 * plane)] = window
+
+
+def sides_kernel(place_ref, mean_ref, other_ref, _, low_ref, high_ref):
+    turn = place_ref[1]
+    last = mean_ref.shape[0] - 1
+    for plane, turned, out_ref in ((0, last, low_ref), (last, 0, high_ref)):
+
+        def facing(ref):
+            return jnp.where(turn > 0, ref[turned : turned + 1, :], ref[plane : plane + 1, :])
+
+        out_ref[0:1, :] = facing(mean_ref)
         for field in range(other_ref.shape[0]):
-            out_ref[field + 1 : field + 2, :] = other_ref[field, plane : plane + 1, :]
-
-
-def tables_kernel(fields, entries_ref, products_ref, slots_ref, _, out_ref, by_column):
-    rows = by_column.shape[1]
-    total = entries_ref.shape[1]
-    names = slots_ref.shape[1]
-    slots = slots_ref[...].astype(BF16)
+            out_ref[field + 1 : field + 2, :] = facing(other_ref.at[field])
+
+
+def tables_kernel(fields, own, place_ref, triples_ref, products_ref, owners_ref, _, out_ref, held, by_column):
+    rows, total = by_column.shape[1:]
+    entries, factors = triples_ref.shape[1], products_ref.shape[1]
+    named = owners_ref.shape[1]
+    names = up(named, LANES)
+    padded = up(own, 8)
+    held[...] = jnp.zeros_like(held)
+    held[0:3, :entries] = triples_ref[...].astype(F32)
+    held[3:4, :factors] = products_ref[...]
+    held[4:5, :named] = owners_ref[...].astype(F32)
+    owners = held[4:5, :names].astype(jnp.int32)
+    group = owners // own
+    slots = lax.bitwise_xor(group, place_ref[0]) * padded + owners - group * own
+    slots = jnp.broadcast_to(slots.astype(F32), (16, names)).astype(BF16)
 
     def placed(which):
         name = lax.broadcasted_iota(jnp.int32, (names, total), 0)
-        chosen = jnp.where(name == entries_ref[which : which + 1, :], 1.0, 0.0).astype(BF16)
+        chosen = jnp.where(name == held[which : which + 1, :].astype(jnp.int32), 1.0, 0.0).astype(BF16)
         return jnp.dot(slots, chosen, preferred_element_type=F32)[0:1].astype(jnp.int32)
 
     row, column = placed(0), placed(1)
-    field = entries_ref[2:3, :]
+    field = held[2:3, :].astype(jnp.int32)
     place = (row // BLOCK) * (fields * BLOCK) + field * BLOCK + row % BLOCK
-    rest = products_ref[0:1, :]
+    rest = held[3:4, :]
     here = lax.broadcasted_iota(jnp.int32, (rows, total), 0) == column
     for part in range(3):
         piece = rest.astype(BF16).astype(F32)
@@ -145,10 +154,10 @@
     return jnp.concatenate([part.astype(F32) for part in parts], axis=0).astype(BF16)
 
 
-def edges_kernel(count, *refs):
-    parts, (low_ref, high_ref) = refs[:count], refs[-2:]
-    low_ref[...] = joined([part[0] for part in parts])
-    high_ref[...] = joined([part[1] for part in parts])
+def gather_kernel(count, *refs):
+    parts, out_refs = refs[:count], refs[-refs[0].shape[0] :]
+    for plane, out_ref in enumerate(out_refs):
+        out_ref[...] = joined([part[plane] for part in parts])
 
 
 def spread(value):
@@ -161,10 +170,10 @@
         mixed[tile] = result[:, tile * LANES : (tile + 1) * LANES]
 
 
-def weigh(mixed, weights_ref, plane, ways, sums):
-    _, tiles, rows, _ = sums.shape
+def weigh(mixed, weights_ref, plane, ways, sums, tiles):
+    rows = sums.shape[2]
     fields = weights_ref.shape[1]
-    for tile in range(tiles):
+    for tile in tiles:
         for block in range(rows // BLOCK):
             totals = [None] * len(ways)
             for field in range(fields):
@@ -180,51 +189,65 @@
                 sums[ALL, tile, here, :] = functools.reduce(jnp.add, totals)
 
 
-def settle(sums, masks_ref, write):
-    _, tiles, rows, _ = sums.shape
+def settle(sums, masks_ref, tiles, write):
+    every, rows = sums.shape[1], sums.shape[2]
     lane = lax.broadcasted_iota(jnp.int32, (BLOCK, LANES), 1)
     for block in range(rows // BLOCK):
         here = slice(block * BLOCK, (block + 1) * BLOCK)
 
         def ahead(way, shift):
             turned = [pltpu.roll(sums[way, tile, here, :], LANES - shift, 1) for tile in range(tiles)]
-            return [jnp.where(lane < LANES - shift, turned[t], turned[(t + 1) % tiles]) for t in range(tiles)]
-
-        def behind(way, shift):
+            following = turned[1:] + turned[: 1 if tiles == every else 0]
+            following += turned[-1:] * (tiles - len(following))
+            return [jnp.where(lane < LANES - shift, turned[t], following[t]) for t in range(tiles)]
+
+        def behind(way, shift, ring):
             turned = [pltpu.roll(sums[way, tile, here, :], shift, 1) for tile in range(tiles)]
-            return [jnp.where(lane >= shift, turned[t], turned[(t - 1) % tiles]) for t in range(tiles)]
-
-        shares = zip(ahead(LAST_X, NXY), behind(NEXT_X, NXY), ahead(LAST_Y, 1), behind(NEXT_Y, 1))
+            before = turned[0]
+            if ring:
+                before = turned[-1] if tiles == every else pltpu.roll(sums[way, every - 1, here, :], shift, 1)
+            previous = [before] + turned[:-1]
+            return [jnp.where(lane >= shift, turned[t], previous[t]) for t in range(tiles)]
+
+        shares = zip(
+            ahead(LAST_X, NXY), behind(NEXT_X, NXY, True), ahead(LAST_Y, 1), behind(NEXT_Y, 1, False)
+        )
         for tile, (a, b, c, d) in enumerate(shares):
             value = sums[ALL, tile, here, :] - a - b
             value = value - spread(masks_ref[0, tile]) * c - spread(masks_ref[1, tile]) * d
             write(tile, here, value)
 
 
-def outer(low, high, tables_ref, weights_ref, masks_ref, low_out, high_out, middle_out, mixed, sums):
+def measure_plane(values, plane, tables_ref, weights_ref, mixed, sums, tiles):
+    mix(tables_ref, values, mixed)
+    weigh(mixed, weights_ref, plane, range(6), sums, range(tiles))
+    weigh(mixed, weights_ref, plane, (NEXT_X,), sums, range(tiles, sums.shape[1]))
+
+
+def outer(low, high, tables_ref, weights_ref, masks_ref, low_out, high_out, middle_out, mixed, sums, tiles):
     last = weights_ref.shape[0] - 1
     for plane, values, out_ref, way in ((0, low, low_out, NEXT_Z), (last, high, high_out, LAST_Z)):
-        mix(tables_ref, values, mixed)
-        weigh(mixed, weights_ref, plane, range(6), sums)
+        measure_plane(values, plane, tables_ref, weights_ref, mixed.at[min(plane, 1)], sums, tiles)
 
         def write(tile, here, value):
             out_ref[tile, here, :] = value
             given = sums[way, tile, here, :]
             middle_out[tile, here, :] = -given if plane == 0 else middle_out[tile, here, :] - given
 
-        settle(sums, masks_ref, write)
-
-
-def inner(values, low_in, high_in, middle_in, tables_ref, weights_ref, masks_ref, low_out, high_out, out, mixed, sums):
-    mix(tables_ref, values, mixed)
-    weigh(mixed, weights_ref, 1, range(6), sums)
+        settle(sums, masks_ref, tiles, write)
+
+
+def inner(
+    values, low_in, high_in, middle_in, tables_ref, weights_ref, masks_ref, low_out, high_out, out, mixed, sums, tiles
+):
+    measure_plane(values, 1, tables_ref, weights_ref, mixed.at[0], sums, tiles)
 
     def write(tile, here, value):
         out[tile, here, :] = SCALE * (value + middle_in[tile, here, :])
         low_out[tile, here, :] = low_in[tile, here, :] - sums[LAST_Z, tile, here, :]
         high_out[tile, here, :] = high_in[tile, here, :] - sums[NEXT_Z, tile, here, :]
 
-    settle(sums, masks_ref, write)
+    settle(sums, masks_ref, tiles, write)
 
 
 def fill(result, masks_ref, out_ref):
@@ -257,32 +280,13 @@
             piece_ref[len(results) * full + first // beside] = packed.astype(BF16)
 
 
-def outer_kernel(low_ref, high_ref, tables_ref, weights_ref, masks_ref, *refs):
-    low_out, high_out, middle_out, mixed, sums = refs[-5:]
-    outer(
-        low_ref[...], high_ref[...], tables_ref, weights_ref, masks_ref, low_out, high_out, middle_out, mixed, sums
-    )
-
-
-def inner_kernel(count, *refs):
-    parts = refs[:count]
-    low_in, high_in, middle_in, tables_ref, weights_ref, masks_ref = refs[count : count + 6]
-    low_out, high_out, middle_out, whole_ref, mixed, sums = refs[count + 6 :]
-    values = joined([part[...] for part in parts])
-    inner(
-        values, low_in, high_in, middle_in, tables_ref, weights_ref, masks_ref, low_out, high_out, middle_out, mixed, sums
-    )
-    fill(middle_out, masks_ref, whole_ref)
-
-
-def own_kernel(
-    low_ref, values_ref, high_ref, tables_ref, weights_ref, masks_ref, low_out, high_out, middle_out, mixed, sums, *held
-):
-    low, high, middle = held
-    outer(low_ref[...], high_ref[...], tables_ref, weights_ref, masks_ref, low, high, middle, mixed, sums)
-    inner(
-        values_ref[...], low, high, middle, tables_ref, weights_ref, masks_ref, low_out, high_out, middle_out, mixed, sums
-    )
+def own_kernel(tiles, first, low_ref, values_ref, high_ref, tables_ref, weights_ref, masks_ref, *refs):
+    low_out, high_out, middle_out, *whole_ref, mixed, sums, low, high, middle = refs
+    shared = (tables_ref, weights_ref, masks_ref)
+    outer(low_ref[...], high_ref[...], *shared, low, high, middle, mixed, sums, tiles)
+    inner(values_ref[...], low, high, middle, *shared, low_out, high_out, middle_out, mixed, sums, tiles)
+    if first:
+        fill(middle_out, masks_ref, whole_ref[0])
 
 
 def fix_kernel(count, chunk, first, before_ref, after_ref, low_in, high_in, middle_in, *refs):
@@ -293,8 +297,8 @@
     last = weights_ref.shape[0] - 1
     sides = ((before_ref, low_in, low, 0, LAST_Z), (after_ref, high_in, high, last, NEXT_Z))
     for side, (halo_ref, share_ref, result, plane, way) in enumerate(sides):
-        mix(tables_ref, halo_ref[...], mixed)
-        weigh(mixed, weights_ref, plane, (way,), sums)
+        mix(tables_ref, halo_ref[...], mixed.at[side])
+        weigh(mixed.at[side], weights_ref, plane, (way,), sums, range(sums.shape[1]))
         for tile in range(sums.shape[1]):
             result[tile] = SCALE * (share_ref[tile] - sums[way, tile])
         if first:
@@ -303,11 +307,11 @@
     emit((low, middle_in, high), chunk, pieces)
 
 
-def join_kernel(count, chunk, me_ref, *refs):
+def join_kernel(count, chunk, place_ref, *refs):
     piece_refs, (out_ref, held) = refs[:count], refs[count:]
     planes, own, _ = out_ref.shape
     full, odd, beside, _ = packing(planes, chunk)
-    me = me_ref[0]
+    me, turn = place_ref[0], place_ref[1]
     for step in range(count):
         held[lax.bitwise_xor(me, step)] = piece_refs[step][...].astype(F32)
     for plane in range(planes):
@@ -317,7 +321,7 @@
             if odd:
                 tile, place = planes * full + plane // beside, plane % beside
                 parts.append(held[source, tile][:, place * odd : (place + 1) * odd])
-        out_ref[plane] = jnp.concatenate(parts, axis=1)[:own].astype(BF16)
+        out_ref[plane + turn * (planes - 1 - 2 * plane)] = jnp.concatenate(parts, axis=1)[:own].astype(BF16)
 
 
 def shards(panels, mean_field, fluctuations, products, triples, owner_slot):
@@ -331,7 +335,8 @@
     padded = up(own, 8)
     rows = count * padded
     fields = 1 + fluctuations.shape[0]
-    me_array = me.astype(jnp.int32).reshape(1)
+    turn = lax.axis_index("space") % 2
+    place = jnp.stack([me, turn]).astype(jnp.int32)
     tiles = width // LANES
 
     def exchange(block, step):
@@ -341,9 +346,10 @@
         return [blocks[0]] + [exchange(blocks[step], step) for step in range(1, count)]
 
     def neighbours(first_plane, last_plane):
-        upward = [(i, i + 1) for i in range(slabs - 1)]
-        downward = [(target, source) for source, target in upward]
-        return lax.ppermute(last_plane, "space", upward), lax.ppermute(first_plane, "space", downward)
+        pairs = [(i, i ^ 1) for i in range(slabs)]
+        others = [(i, i - 1 if i % 2 == 0 else i + 1) for i in range(1, slabs - 1)]
+        after = lax.ppermute(last_plane, "space", pairs)
+        return lax.ppermute(first_plane, "space", others), after
 
     def shape(*dims, dtype=BF16):
         return jax.ShapeDtypeStruct(dims, dtype)
@@ -352,27 +358,21 @@
         functools.partial(cut_kernel, count, chunk),
         "cut",
         1,
-        [shape(2, padded, width)] * count + [shape(padded, width)] * count,
-        (me_array, jnp.transpose(panels, (1, 0, 2))),
+        [shape(planes, padded, width)] * count,
+        (place, jnp.transpose(panels, (1, 0, 2))),
         [VMEM((padded, cells), F32)],
         scalars=1,
     )
-    edges, middles = exchanged(cut[:count]), exchanged(cut[count : 2 * count])
-
-    total = up(products.shape[0], 2 * LANES)
-    names = up(owner_slot.shape[0], LANES)
-    entries = jnp.pad(triples.T, ((0, 5), (0, total - products.shape[0])), constant_values=-1)
-    values = jnp.pad(products, (0, total - products.shape[0]))[None]
-    group = owner_slot // own
-    slots = lax.bitwise_xor(group, me) * padded + owner_slot - group * own
-    slots = jnp.broadcast_to(jnp.pad(slots, (0, names - slots.shape[0])).astype(F32)[None], (16, names))
+    parts = exchanged(cut)
+
     (tables,) = call(
-        functools.partial(tables_kernel, fields),
+        functools.partial(tables_kernel, fields, own),
         "tables",
         5,
         [shape(fields * rows, rows)],
-        (entries, values, slots, cut[0]),
-        [VMEM((3, rows, total), BF16)],
+        (place, triples.T, products[None], owner_slot[None], cut[0]),
+        [VMEM((8, up(products.shape[0], 2 * LANES)), F32), VMEM((3, rows, up(products.shape[0], 2 * LANES)), BF16)],
+        scalars=1,
         unread=1,
     )
 
@@ -381,11 +381,13 @@
         "sides",
         0.2,
         [shape(fields, cells, dtype=F32)] * 2,
-        (mean_field, fluctuations, tables),
+        (place, mean_field, fluctuations, tables),
+        scalars=1,
         unread=1,
     )
     before, after = neighbours(*sides)
     conduct = jnp.concatenate([mean_field[:, None], fluctuations.transpose(1, 0, 2)], axis=1)
+    conduct = jnp.where(turn > 0, conduct[::-1], conduct)
     conduct = jnp.concatenate([before[None], conduct, after[None]], axis=0)
     conduct = jnp.pad(conduct, ((0, 0), (0, 0), (halo, halo)))
     conduct = lax.dynamic_slice_in_dim(conduct, me * chunk, chunk + 2 * halo, 2)
@@ -393,10 +395,10 @@
     conduct = jnp.concatenate([conduct[..., halo:], gap, conduct[..., :halo]], axis=-1)
 
     lane = jnp.arange(width)
-    place = jnp.where(lane < width - halo, lane, lane - width) + halo
-    row = place // NXY - REACH + me * (chunk // NXY)
+    cell = jnp.where(lane < width - halo, lane, lane - width) + halo
+    row = cell // NXY - REACH + me * (chunk // NXY)
     inside = (row >= 0) & (row < NXY) & ((lane < chunk + halo) | (lane >= width - halo))
-    masks = jnp.stack([place % NXY < NXY - 1, place % NXY > 0, inside]).astype(F32)
+    masks = jnp.stack([cell % NXY < NXY - 1, cell % NXY > 0, inside]).astype(F32)
     masks = jnp.broadcast_to(masks.reshape(3, tiles, 1, LANES), (3, tiles, 8, LANES))
     (weights,) = call(
         weights_kernel, "weights", 0.3, [shape(planes, fields, 6, tiles, 8, LANES, dtype=F32)], (conduct, masks)
@@ -410,30 +412,21 @@
 
     def scratch(tiles, held):
         held = [VMEM((tiles, rows, LANES), F32)] * held
-        return [VMEM((tiles, fields * rows, LANES), BF16), VMEM((7, tiles, rows, LANES), F32)] + held
-
-    low, high = call(
-        functools.partial(edges_kernel, count), "edges", 0.5, [plane_whole] * 2, (*edges, tables, weights), unread=2
+        return [VMEM((2, tiles, fields * rows, LANES), BF16), VMEM((7, tiles, rows, LANES), F32)] + held
+
+    low, middle_whole, high = call(
+        functools.partial(gather_kernel, count), "gather", 0.5, [plane_whole] * planes, (*parts, tables, weights), unread=2
     )
     before, after = neighbours(low, high)
-    low, high, middle = call(
-        outer_kernel,
-        "outer",
-        6,
-        [share] * 3,
-        (low, high, *common, *middles[1:]),
-        scratch(tiles, 0),
-        unread=count - 1,
-    )
     low, high, middle, middle_whole = call(
-        functools.partial(inner_kernel, count),
-        "inner",
-        3,
+        functools.partial(own_kernel, tiles, True),
+        "first",
+        9,
         [share] * 3 + [plane_whole],
-        (*middles, low, high, middle, *common),
-        scratch(tiles, 0),
-    )
-    low, high, low_near, high_near, *first = call(
+        (low, middle_whole, high, *common),
+        scratch(tiles, 3),
+    )
+    low, high, low_near, high_near, *sent = call(
         functools.partial(fix_kernel, count, chunk, True),
         "fix",
         3,
@@ -442,9 +435,14 @@
         scratch(tiles, 2),
     )
     before, after = neighbours(low_near, high_near)
-    first = exchanged(first)
+    sent = exchanged(sent)
     low, high, middle = call(
-        own_kernel, "own", 9, [share] * 3, (low, middle_whole, high, *common), scratch(tiles, 3)
+        functools.partial(own_kernel, near_tiles, False),
+        "second",
+        8,
+        [share] * 3,
+        (low, middle_whole, high, *common),
+        scratch(tiles, 3),
     )
     second = call(
         functools.partial(fix_kernel, count, chunk, False),
@@ -462,13 +460,13 @@
             "join",
             1,
             [shape(planes, own, cells)],
-            (me_array, *parts),
+            (place, *parts),
             [VMEM((count,) + pieces[0].shape, F32)],
             scalars=1,
         )
         return jnp.transpose(result, (1, 0, 2))
 
-    return join(first), join(second)
+    return join(sent), join(second)
 
 
 def solution(mesh):

time: 98.6 us -> 87.4 us (0.89)
  the two profiles are of different devices: /device:TPU:10 before, /device:TPU:0 now
where the time goes in v4:
time: 87.4 us; the launch traced here: 85.9 us
  Pallas kernels  29.6 us (34%)
  starting transfers between devices  28.6 us (33%)
  waiting for transfers between devices  20.5 us (23%)
  local copies, waits for them, and re-layouts  5.9 us (7%)
  between operations  0.89 us (1%)
    pallas_call x11, Pallas kernels, call(): pl.pallas_call(kernel, out_shape=out_shape, in_specs=in_specs, out_specs=...  29.6 us
    ppermute x9, waiting for transfers between devices, exchange(): return lax.ppermute(block, 'chaos', [(i, i ^ step) for i in range(count)])  20.5 us
    ppermute x9, starting transfers between devices, exchange(): return lax.ppermute(block, 'chaos', [(i, i ^ step) for i in range(count)])  17.3 us
    ppermute x3, starting transfers between devices, neighbours(): after = lax.ppermute(last_plane, 'space', pairs)  8.92 us
    unnamed x13, local copies, waits for them, and re-layouts  4.31 us
    ppermute x3, starting transfers between devices, neighbours(): return (lax.ppermute(first_plane, 'space', others), after)  2.43 us
  transfers between devices with their start and end apart: 15, of which 4 were waited for; matrix products, arithmetic and copies ran while one was open for 2% of the time, Pallas kernels for 29%

profile of v4, /device:TPU:0, one launch (start us, length us, event | category | flops | bytes accessed | tf_op | source)
XLA Modules:
  0.0 85.9 jit_solution(3096101758216772290)
XLA Ops:
  0.6 0.0 copy-start.1
  0.7 0.1 pad_add_fusion.place_ref
  0.7 1.2 %copy-done.2 = bf16[53,3,2304]{2,0,1:T(8,128)(2,1)S(1)} copy-done((bf16[53,3,2304]{2,0,1:T(8,128)(2,1)S(1)}, bf16[53,3,2304]{2,0,1:T(8,128)(2,1)}, u32[]{:S(2)}) %copy-start.2) | copy-done | bytes 732696
  1.9 1.4 %cut.1 = (bf16[3,56,768]{2,1,0:T(8,128)(2,1)S(1)}, bf16[3,56,768]{2,1,0:T(8,128)(2,1)S(1)}, bf16[3,56,768]{2,1,0:T(8,128)(2,1)S(1)}, bf16[3,56,768]{2,1,0:T(8,128)(2,1)S(1)}) custom-call(s32[2]{0:T(128)S(1)} %pad_add_fusion.place_ref, bf16[3,53,2304]{2,1,0:T(8,128)(2,1)S(1)} %bitcast.12), custom_call_target="tpu_custom_call" | custom-call | bytes 3600000 | tf_op jit(solution)/shard_map/cut/pallas_call | solution.py:28
  3.3 3.1 %collective-permute-start = (bf16[3,56,768]{2,1,0:T(8,128)(2,1)S(1)}, bf16[3,56,768]{2,1,0:T(8,128)(2,1)S(1)}, u32[]{:S(2)}, u32[]{:S(2)}) collective-permute-start(bf16[3,56,768]{2,1,0:T(8,128)(2,1)S(1)} %get-tuple-element.31), channel_id=1, source_target_pairs={{0,8},{8,0},{16,24},{24,16},{1,9},{9,1},{17,25},{25,17},{2,10},{10... | collective-permute-start | bytes 774152 | tf_op jit(solution)/shard_map/ppermute | solution.py:343
  6.4 2.6 %collective-permute-start.1 = (bf16[3,56,768]{2,1,0:T(8,128)(2,1)S(1)}, bf16[3,56,768]{2,1,0:T(8,128)(2,1)S(1)}, u32[]{:S(2)}, u32[]{:S(2)}) collective-permute-start(bf16[3,56,768]{2,1,0:T(8,128)(2,1)S(1)} %get-tuple-element.32), channel_id=1, source_target_pairs={{0,16},{8,24},{16,0},{24,8},{1,17},{9,25},{17,1},{25,9},{2,18},{10... | collective-permute-start | bytes 774152 | tf_op jit(solution)/shard_map/ppermute | solution.py:343
  9.0 0.0 collective-permute-start.2
  9.0 0.7 broadcast_in_dim.20.products_ref
  9.7 0.7 copy-done.4
  10.4 0.7 copy-done.5
  11.1 5.7 %tables.1._.refs_4_.tables_ref.refs_0_ = bf16[1568,224]{1,0:T(8,128)(2,1)S(1)} custom-call(s32[2]{0:T(128)S(1)} %pad_add_fusion.place_ref, s32[3,1218]{1,0:T(4,128)S(1)} %bitcast.13, f32[1,1218]{1,0:T(1,128)S(1)} %broadcast_in_dim.20.products_ref, s32[1,210]{1,0:T(1,128)S(1)} %bitcast.14, bf16[3,56,768]{2,1,0:T(8,128)(2,1)S(1)} %get-tuple-element.30._.refs_0_), custom_call_target="tpu_custom_call" | custom-call | bytes 18000000 | tf_op jit(solution)/shard_map/tables/pallas_call | solution.py:28
  16.8 0.0 copy-start
  16.8 0.9 %copy-done = f32[6,3,2304]{2,1,0:T(4,128)S(1)} copy-done((f32[6,3,2304]{2,1,0:T(4,128)S(1)}, f32[6,3,2304]{2,1,0:T(4,128)}, u32[]{:S(2)}) %copy-start) | copy-done | bytes 165912
  17.7 0.8 copy-done.3
  18.5 0.6 sides.1
  19.1 0.7 collective-permute-start.3
  19.7 3.1 %collective-permute-start.4 = (f32[7,2304]{1,0:T(8,128)S(1)}, f32[7,2304]{1,0:T(8,128)S(1)}, u32[]{:S(2)}, u32[]{:S(2)}) collective-permute-start(f32[7,2304]{1,0:T(8,128)S(1)} %get-tuple-element.35), channel_id=1, source_target_pairs={{0,1},{1,0},{2,3},{3,2},{4,5},{5,4},{6,7},{7,6},{8,9},{9,8},{10,11... | collective-permute-start | bytes 193544 | tf_op jit(solution)/shard_map/ppermute | solution.py:351
  22.9 0.8 broadcast_in_dim.23
  23.8 0.1 pad_maximum_fusion
  23.9 0.0 collective-permute-done.4
  23.9 0.1 fusion.2
  24.0 0.1 slice.8
  24.1 0.1 pad_maximum_fusion.1.conduct_ref
  24.2 0.3 weights.1.refs_5_.weights_ref.refs_1_
  24.5 0.0 collective-permute-done.refs_1_
  24.5 3.0 %collective-permute-done.1.refs_2_ = bf16[3,56,768]{2,1,0:T(8,128)(2,1)S(1)} collective-permute-done((bf16[3,56,768]{2,1,0:T(8,128)(2,1)S(1)}, bf16[3,56,768]{2,1,0:T(8,128)(2,1)S(1)}, u32[]{:S(2)}, u32[]{:S(2)}) %collective-permute-start.1) | collective-permute-done | bytes 258080 | tf_op jit(solution)/shard_map/ppermute | solution.py:343
  27.5 0.1 gather.1
  27.6 0.9 %collective-permute-start.5 = (bf16[224,768]{1,0:T(8,128)(2,1)S(1)}, bf16[224,768]{1,0:T(8,128)(2,1)S(1)}, u32[]{:S(2)}, u32[]{:S(2)}) collective-permute-start(bf16[224,768]{1,0:T(8,128)(2,1)S(1)} %get-tuple-element.36.low_ref), channel_id=1, source_target_pairs={{1,2},{2,1},{3,4},{4,3},{5,6},{6,5},{9,10},{10,9},{11,12},{12,11},... | collective-permute-start | bytes 1032200 | tf_op jit(solution)/shard_map/ppermute | solution.py:352
  28.4 2.9 %collective-permute-start.6 = (bf16[224,768]{1,0:T(8,128)(2,1)S(1)}, bf16[224,768]{1,0:T(8,128)(2,1)S(1)}, u32[]{:S(2)}, u32[]{:S(2)}) collective-permute-start(bf16[224,768]{1,0:T(8,128)(2,1)S(1)} %get-tuple-element.37.high_ref), channel_id=1, source_target_pairs={{0,1},{1,0},{2,3},{3,2},{4,5},{5,4},{6,7},{7,6},{8,9},{9,8},{10,11... | collective-permute-start | bytes 1032200 | tf_op jit(solution)/shard_map/ppermute | solution.py:351
  31.3 8.1 %first.1 = (f32[6,224,128]{2,1,0:T(8,128)S(1)}, f32[6,224,128]{2,1,0:T(8,128)S(1)}, f32[6,224,128]{2,1,0:T(8,128)S(1)}, bf16[224,768]{1,0:T(8,128)(2,1)S(1)}) custom-call(bf16[224,768]{1,0:T(8,128)(2,1)S(1)} %get-tuple-element.36.low_ref, bf16[224,768]{1,0:T(8,128)(2,1)S(1)} %get-tuple-element.38.values_ref, ...), custom_call_target="tpu_custom_call" | custom-call | bytes 32400000 | tf_op jit(solution)/shard_map/first/pallas_call | solution.py:28
  39.4 0.0 collective-permute-done.5.before_ref
  39.5 0.0 collective-permute-done.6.after_ref
  39.5 1.6 %fix.1 = (bf16[224,768]{1,0:T(8,128)(2,1)S(1)}, bf16[224,768]{1,0:T(8,128)(2,1)S(1)}, bf16[224,640]{1,0:T(8,128)(2,1)S(1)}, bf16[224,640]{1,0:T(8,128)(2,1)S(1)}...) custom-call(bf16[224,768]{1,0:T(8,128)(2,1)S(1)} %collective-permute, ...), custom_call_target="tpu_custom_call" | custom-call | bytes 10800000 | tf_op jit(solution)/shard_map/fix/pallas_call | solution.py:28
  41.1 0.9 %collective-permute-start.10 = (bf16[224,640]{1,0:T(8,128)(2,1)S(1)}, bf16[224,640]{1,0:T(8,128)(2,1)S(1)}, u32[]{:S(2)}, u32[]{:S(2)}) collective-permute-start(bf16[224,640]{1,0:T(8,128)(2,1)S(1)} %get-tuple-element.46), channel_id=1, source_target_pairs={{1,2},{2,1},{3,4},{4,3},{5,6},{6,5},{9,10},{10,9},{11,12},{12,11},... | collective-permute-start | bytes 860168 | tf_op jit(solution)/shard_map/ppermute | solution.py:352
  42.0 2.9 %collective-permute-start.11 = (bf16[224,640]{1,0:T(8,128)(2,1)S(1)}, bf16[224,640]{1,0:T(8,128)(2,1)S(1)}, u32[]{:S(2)}, u32[]{:S(2)}) collective-permute-start(bf16[224,640]{1,0:T(8,128)(2,1)S(1)} %get-tuple-element.47), channel_id=1, source_target_pairs={{0,1},{1,0},{2,3},{3,2},{4,5},{5,4},{6,7},{7,6},{8,9},{9,8},{10,11... | collective-permute-start | bytes 860168 | tf_op jit(solution)/shard_map/ppermute | solution.py:351
  44.9 4.7 %collective-permute-start.7 = (bf16[14,56,128]{2,1,0:T(8,128)(2,1)S(1)}, bf16[14,56,128]{2,1,0:T(8,128)(2,1)S(1)}, u32[]{:S(2)}, u32[]{:S(2)}) collective-permute-start(bf16[14,56,128]{2,1,0:T(8,128)(2,1)S(1)} %get-tuple-element.43), channel_id=1, source_target_pairs={{0,8},{8,0},{16,24},{24,16},{1,9},{9,1},{17,25},{25,17},{2,10},{10... | collective-permute-start | bytes 602120 | tf_op jit(solution)/shard_map/ppermute | solution.py:343
  49.5 1.0 %collective-permute-start.8 = (bf16[14,56,128]{2,1,0:T(8,128)(2,1)S(1)}, bf16[14,56,128]{2,1,0:T(8,128)(2,1)S(1)}, u32[]{:S(2)}, u32[]{:S(2)}) collective-permute-start(bf16[14,56,128]{2,1,0:T(8,128)(2,1)S(1)} %get-tuple-element.44), channel_id=1, source_target_pairs={{0,16},{8,24},{16,0},{24,8},{1,17},{9,25},{17,1},{25,9},{2,18},{10... | collective-permute-start | bytes 602120 | tf_op jit(solution)/shard_map/ppermute | solution.py:343
  50.5 1.5 %collective-permute-start.9 = (bf16[14,56,128]{2,1,0:T(8,128)(2,1)S(1)}, bf16[14,56,128]{2,1,0:T(8,128)(2,1)S(1)}, u32[]{:S(2)}, u32[]{:S(2)}) collective-permute-start(bf16[14,56,128]{2,1,0:T(8,128)(2,1)S(1)} %get-tuple-element.45), channel_id=1, source_target_pairs={{0,24},{8,16},{16,8},{24,0},{1,25},{9,17},{17,9},{25,1},{2,26},{10... | collective-permute-start | bytes 602120 | tf_op jit(solution)/shard_map/ppermute | solution.py:343
  52.0 7.0 %second.1 = (f32[6,224,128]{2,1,0:T(8,128)S(1)}, f32[6,224,128]{2,1,0:T(8,128)S(1)}, f32[6,224,128]{2,1,0:T(8,128)S(1)}) custom-call(bf16[224,768]{1,0:T(8,128)(2,1)S(1)} %get-tuple-element.48.low_ref, bf16[224,768]{1,0:T(8,128)(2,1)S(1)} %get-tuple-element.49.values_ref, bf16[224,768]{1,0:T(8,128)(2,1)S(1)} %get-tuple-element.50.high_ref, ...), custom_call_target="tpu_custom_call" | custom-call | bytes 28800000 | tf_op jit(solution)/shard_map/second/pallas_call | solution.py:28
  59.1 1.4 %last.1 = (bf16[14,56,128]{2,1,0:T(8,128)(2,1)S(1)}, bf16[14,56,128]{2,1,0:T(8,128)(2,1)S(1)}, bf16[14,56,128]{2,1,0:T(8,128)(2,1)S(1)}, bf16[14,56,128]{2,1,0:T(8,128)(2,1)S(1)}) custom-call(bf16[224,640]{1,0:T(8,128)(2,1)S(1)} %collective-permute-done.10.before_ref, bf16[224,640]{1,0:T(8,128)(2,1)S(1)} %collective-permute-done.11.after_ref, ...), custom_call_target="tpu_custom_call" | custom-call | bytes 10800000 | tf_op jit(solution)/shard_map/last/pallas_call | solution.py:28
  60.5 1.1 %collective-permute-start.12 = (bf16[14,56,128]{2,1,0:T(8,128)(2,1)S(1)}, bf16[14,56,128]{2,1,0:T(8,128)(2,1)S(1)}, u32[]{:S(2)}, u32[]{:S(2)}) collective-permute-start(bf16[14,56,128]{2,1,0:T(8,128)(2,1)S(1)} %get-tuple-element.55), channel_id=1, source_target_pairs={{0,8},{8,0},{16,24},{24,16},{1,9},{9,1},{17,25},{25,17},{2,10},{10... | collective-permute-start | bytes 602120 | tf_op jit(solution)/shard_map/ppermute | solution.py:343
  61.6 1.9 %collective-permute-start.13 = (bf16[14,56,128]{2,1,0:T(8,128)(2,1)S(1)}, bf16[14,56,128]{2,1,0:T(8,128)(2,1)S(1)}, u32[]{:S(2)}, u32[]{:S(2)}) collective-permute-start(bf16[14,56,128]{2,1,0:T(8,128)(2,1)S(1)} %get-tuple-element.56), channel_id=1, source_target_pairs={{0,16},{8,24},{16,0},{24,8},{1,17},{9,25},{17,1},{25,9},{2,18},{10... | collective-permute-start | bytes 602120 | tf_op jit(solution)/shard_map/ppermute | solution.py:343
  63.5 1.5 %collective-permute-start.14 = (bf16[14,56,128]{2,1,0:T(8,128)(2,1)S(1)}, bf16[14,56,128]{2,1,0:T(8,128)(2,1)S(1)}, u32[]{:S(2)}, u32[]{:S(2)}) collective-permute-start(bf16[14,56,128]{2,1,0:T(8,128)(2,1)S(1)} %get-tuple-element.57), channel_id=1, source_target_pairs={{0,24},{8,16},{16,8},{24,0},{1,25},{9,17},{17,9},{25,1},{2,26},{10... | collective-permute-start | bytes 602120 | tf_op jit(solution)/shard_map/ppermute | solution.py:343
  65.0 2.0 %collective-permute-done.8.refs_2_ = bf16[14,56,128]{2,1,0:T(8,128)(2,1)S(1)} collective-permute-done((bf16[14,56,128]{2,1,0:T(8,128)(2,1)S(1)}, bf16[14,56,128]{2,1,0:T(8,128)(2,1)S(1)}, u32[]{:S(2)}, u32[]{:S(2)}) %collective-permute-start.8) | collective-permute-done | bytes 200736 | tf_op jit(solution)/shard_map/ppermute | solution.py:343
  67.0 1.7 %join.2 = bf16[3,53,2304]{2,1,0:T(8,128)(2,1)} custom-call(s32[2]{0:T(128)S(1)} %pad_add_fusion.place_ref, bf16[14,56,128]{2,1,0:T(8,128)(2,1)S(1)} %get-tuple-element.42.refs_0_, bf16[14,56,128]{2,1,0:T(8,128)(2,1)S(1)} %collective-permute-done.7.refs_1_, bf16[14,56,128]{2,1,0:T(8,128)(2,1)S(1)} %collective-permute-done.8.refs_2_, ...), custom_call_target="tpu_custom_call" | custom-call | bytes 3600000 | tf_op jit(solution)/shard_map/join/pallas_call | solution.py:28
  68.7 2.4 %collective-permute-done.12.refs_1_ = bf16[14,56,128]{2,1,0:T(8,128)(2,1)S(1)} collective-permute-done((bf16[14,56,128]{2,1,0:T(8,128)(2,1)S(1)}, bf16[14,56,128]{2,1,0:T(8,128)(2,1)S(1)}, u32[]{:S(2)}, u32[]{:S(2)}) %collective-permute-start.12) | collective-permute-done | bytes 200736 | tf_op jit(solution)/shard_map/ppermute | solution.py:343
  71.1 13.1 %collective-permute-done.13.refs_2_ = bf16[14,56,128]{2,1,0:T(8,128)(2,1)S(1)} collective-permute-done((bf16[14,56,128]{2,1,0:T(8,128)(2,1)S(1)}, bf16[14,56,128]{2,1,0:T(8,128)(2,1)S(1)}, u32[]{:S(2)}, u32[]{:S(2)}) %collective-permute-start.13) | collective-permute-done | bytes 200736 | tf_op jit(solution)/shard_map/ppermute | solution.py:343
  84.2 1.7 %join.3 = bf16[3,53,2304]{2,1,0:T(8,128)(2,1)} custom-call(s32[2]{0:T(128)S(1)} %pad_add_fusion.place_ref, bf16[14,56,128]{2,1,0:T(8,128)(2,1)S(1)} %get-tuple-element.54.refs_0_, bf16[14,56,128]{2,1,0:T(8,128)(2,1)S(1)} %collective-permute-done.12.refs_1_, bf16[14,56,128]{2,1,0:T(8,128)(2,1)S(1)} %collective-permute-done.13.refs_2_, ...), custom_call_target="tpu_custom_call" | custom-call | bytes 3600000 | tf_op jit(solution)/shard_map/join/pallas_call | solution.py:28
  (19 shorter events, 0.2 us)
Async XLA Ops:
  0.6 23.1 %copy-start.1 = (f32[6,3,2304]{2,1,0:T(4,128)S(1)}, f32[6,3,2304]{2,1,0:T(4,128)}, u32[]{:S(2)}) copy-start(f32[6,3,2304]{2,1,0:T(4,128)} %other_ref.1) | copy-start | bytes 497668
  0.7 1.2 %copy-start.2 = (bf16[53,3,2304]{2,0,1:T(8,128)(2,1)S(1)}, bf16[53,3,2304]{2,0,1:T(8,128)(2,1)}, u32[]{:S(2)}) copy-start(bf16[53,3,2304]{2,0,1:T(8,128)(2,1)} %param.6) | copy-start | bytes 2198020
  3.3 21.2 %collective-permute-start = (bf16[3,56,768]{2,1,0:T(8,128)(2,1)S(1)}, bf16[3,56,768]{2,1,0:T(8,128)(2,1)S(1)}, u32[]{:S(2)}, u32[]{:S(2)}) collective-permute-start(bf16[3,56,768]{2,1,0:T(8,128)(2,1)S(1)} %get-tuple-element.31), channel_id=1, source_target_pairs={{0,8},{8,0},{16,24},{24,16},{1,9},{9,1},{17,25},{25,17},{2,10},{10... | collective-permute-start | bytes 774152 | tf_op jit(solution)/shard_map/ppermute | solution.py:343
  6.4 21.1 %collective-permute-start.1 = (bf16[3,56,768]{2,1,0:T(8,128)(2,1)S(1)}, bf16[3,56,768]{2,1,0:T(8,128)(2,1)S(1)}, u32[]{:S(2)}, u32[]{:S(2)}) collective-permute-start(bf16[3,56,768]{2,1,0:T(8,128)(2,1)S(1)} %get-tuple-element.32), channel_id=1, source_target_pairs={{0,16},{8,24},{16,0},{24,8},{1,17},{9,25},{17,1},{25,9},{2,18},{10... | collective-permute-start | bytes 774152 | tf_op jit(solution)/shard_map/ppermute | solution.py:343
  9.0 18.5 %collective-permute-start.2 = (bf16[3,56,768]{2,1,0:T(8,128)(2,1)S(1)}, bf16[3,56,768]{2,1,0:T(8,128)(2,1)S(1)}, u32[]{:S(2)}, u32[]{:S(2)}) collective-permute-start(bf16[3,56,768]{2,1,0:T(8,128)(2,1)S(1)} %get-tuple-element.33), channel_id=1, source_target_pairs={{0,24},{8,16},{16,8},{24,0},{1,25},{9,17},{17,9},{25,1},{2,26},{10... | collective-permute-start | bytes 774152 | tf_op jit(solution)/shard_map/ppermute | solution.py:343
  9.7 0.7 copy-start.4
  10.4 0.7 copy-start.5
  16.8 0.9 %copy-start = (f32[6,3,2304]{2,1,0:T(4,128)S(1)}, f32[6,3,2304]{2,1,0:T(4,128)}, u32[]{:S(2)}) copy-start(f32[6,3,2304]{2,1,0:T(4,128)} %other_ref.1) | copy-start | bytes 497668
  17.7 0.8 copy-start.3
  19.1 4.8 %collective-permute-start.3 = (f32[7,2304]{1,0:T(8,128)S(1)}, f32[7,2304]{1,0:T(8,128)S(1)}, u32[]{:S(2)}, u32[]{:S(2)}) collective-permute-start(f32[7,2304]{1,0:T(8,128)S(1)} %get-tuple-element.34), channel_id=1, source_target_pairs={{1,2},{2,1},{3,4},{4,3},{5,6},{6,5},{9,10},{10,9},{11,12},{12,11},... | collective-permute-start | bytes 193544 | tf_op jit(solution)/shard_map/ppermute | solution.py:352
  19.7 4.2 %collective-permute-start.4 = (f32[7,2304]{1,0:T(8,128)S(1)}, f32[7,2304]{1,0:T(8,128)S(1)}, u32[]{:S(2)}, u32[]{:S(2)}) collective-permute-start(f32[7,2304]{1,0:T(8,128)S(1)} %get-tuple-element.35), channel_id=1, source_target_pairs={{0,1},{1,0},{2,3},{3,2},{4,5},{5,4},{6,7},{7,6},{8,9},{9,8},{10,11... | collective-permute-start | bytes 193544 | tf_op jit(solution)/shard_map/ppermute | solution.py:351
  27.6 11.9 %collective-permute-start.5 = (bf16[224,768]{1,0:T(8,128)(2,1)S(1)}, bf16[224,768]{1,0:T(8,128)(2,1)S(1)}, u32[]{:S(2)}, u32[]{:S(2)}) collective-permute-start(bf16[224,768]{1,0:T(8,128)(2,1)S(1)} %get-tuple-element.36.low_ref), channel_id=1, source_target_pairs={{1,2},{2,1},{3,4},{4,3},{5,6},{6,5},{9,10},{10,9},{11,12},{12,11},... | collective-permute-start | bytes 1032200 | tf_op jit(solution)/shard_map/ppermute | solution.py:352
  28.4 11.0 %collective-permute-start.6 = (bf16[224,768]{1,0:T(8,128)(2,1)S(1)}, bf16[224,768]{1,0:T(8,128)(2,1)S(1)}, u32[]{:S(2)}, u32[]{:S(2)}) collective-permute-start(bf16[224,768]{1,0:T(8,128)(2,1)S(1)} %get-tuple-element.37.high_ref), channel_id=1, source_target_pairs={{0,1},{1,0},{2,3},{3,2},{4,5},{5,4},{6,7},{7,6},{8,9},{9,8},{10,11... | collective-permute-start | bytes 1032200 | tf_op jit(solution)/shard_map/ppermute | solution.py:351
  41.1 18.0 %collective-permute-start.10 = (bf16[224,640]{1,0:T(8,128)(2,1)S(1)}, bf16[224,640]{1,0:T(8,128)(2,1)S(1)}, u32[]{:S(2)}, u32[]{:S(2)}) collective-permute-start(bf16[224,640]{1,0:T(8,128)(2,1)S(1)} %get-tuple-element.46), channel_id=1, source_target_pairs={{1,2},{2,1},{3,4},{4,3},{5,6},{6,5},{9,10},{10,9},{11,12},{12,11},... | collective-permute-start | bytes 860168 | tf_op jit(solution)/shard_map/ppermute | solution.py:352
  42.0 17.1 %collective-permute-start.11 = (bf16[224,640]{1,0:T(8,128)(2,1)S(1)}, bf16[224,640]{1,0:T(8,128)(2,1)S(1)}, u32[]{:S(2)}, u32[]{:S(2)}) collective-permute-start(bf16[224,640]{1,0:T(8,128)(2,1)S(1)} %get-tuple-element.47), channel_id=1, source_target_pairs={{0,1},{1,0},{2,3},{3,2},{4,5},{5,4},{6,7},{7,6},{8,9},{9,8},{10,11... | collective-permute-start | bytes 860168 | tf_op jit(solution)/shard_map/ppermute | solution.py:351
  44.9 18.6 %collective-permute-start.7 = (bf16[14,56,128]{2,1,0:T(8,128)(2,1)S(1)}, bf16[14,56,128]{2,1,0:T(8,128)(2,1)S(1)}, u32[]{:S(2)}, u32[]{:S(2)}) collective-permute-start(bf16[14,56,128]{2,1,0:T(8,128)(2,1)S(1)} %get-tuple-element.43), channel_id=1, source_target_pairs={{0,8},{8,0},{16,24},{24,16},{1,9},{9,1},{17,25},{25,17},{2,10},{10... | collective-permute-start | bytes 602120 | tf_op jit(solution)/shard_map/ppermute | solution.py:343
  49.5 17.4 %collective-permute-start.8 = (bf16[14,56,128]{2,1,0:T(8,128)(2,1)S(1)}, bf16[14,56,128]{2,1,0:T(8,128)(2,1)S(1)}, u32[]{:S(2)}, u32[]{:S(2)}) collective-permute-start(bf16[14,56,128]{2,1,0:T(8,128)(2,1)S(1)} %get-tuple-element.44), channel_id=1, source_target_pairs={{0,16},{8,24},{16,0},{24,8},{1,17},{9,25},{17,1},{25,9},{2,18},{10... | collective-permute-start | bytes 602120 | tf_op jit(solution)/shard_map/ppermute | solution.py:343
  50.5 16.4 %collective-permute-start.9 = (bf16[14,56,128]{2,1,0:T(8,128)(2,1)S(1)}, bf16[14,56,128]{2,1,0:T(8,128)(2,1)S(1)}, u32[]{:S(2)}, u32[]{:S(2)}) collective-permute-start(bf16[14,56,128]{2,1,0:T(8,128)(2,1)S(1)} %get-tuple-element.45), channel_id=1, source_target_pairs={{0,24},{8,16},{16,8},{24,0},{1,25},{9,17},{17,9},{25,1},{2,26},{10... | collective-permute-start | bytes 602120 | tf_op jit(solution)/shard_map/ppermute | solution.py:343
  60.5 10.6 %collective-permute-start.12 = (bf16[14,56,128]{2,1,0:T(8,128)(2,1)S(1)}, bf16[14,56,128]{2,1,0:T(8,128)(2,1)S(1)}, u32[]{:S(2)}, u32[]{:S(2)}) collective-permute-start(bf16[14,56,128]{2,1,0:T(8,128)(2,1)S(1)} %get-tuple-element.55), channel_id=1, source_target_pairs={{0,8},{8,0},{16,24},{24,16},{1,9},{9,1},{17,25},{25,17},{2,10},{10... | collective-permute-start | bytes 602120 | tf_op jit(solution)/shard_map/ppermute | solution.py:343
  61.6 22.6 %collective-permute-start.13 = (bf16[14,56,128]{2,1,0:T(8,128)(2,1)S(1)}, bf16[14,56,128]{2,1,0:T(8,128)(2,1)S(1)}, u32[]{:S(2)}, u32[]{:S(2)}) collective-permute-start(bf16[14,56,128]{2,1,0:T(8,128)(2,1)S(1)} %get-tuple-element.56), channel_id=1, source_target_pairs={{0,16},{8,24},{16,0},{24,8},{1,17},{9,25},{17,1},{25,9},{2,18},{10... | collective-permute-start | bytes 602120 | tf_op jit(solution)/shard_map/ppermute | solution.py:343
  63.5 20.7 %collective-permute-start.14 = (bf16[14,56,128]{2,1,0:T(8,128)(2,1)S(1)}, bf16[14,56,128]{2,1,0:T(8,128)(2,1)S(1)}, u32[]{:S(2)}, u32[]{:S(2)}) collective-permute-start(bf16[14,56,128]{2,1,0:T(8,128)(2,1)S(1)} %get-tuple-element.57), channel_id=1, source_target_pairs={{0,24},{8,16},{16,8},{24,0},{1,25},{9,17},{17,9},{25,1},{2,26},{10... | collective-permute-start | bytes 602120 | tf_op jit(solution)/shard_map/ppermute | solution.py:343

commit v5 on v4

--- a/solution.py
+++ b/solution.py
@@ -10,6 +10,7 @@
 NXY = 48
 SCALE = 0.15
 LANES = 128
+JOINT = 8
 REACH = 2
 BLOCK = 32
 VMEM = pltpu.VMEM
@@ -32,17 +33,17 @@
         out_specs=[pl.BlockSpec(memory_space=VMEM)] * len(out_shape),
         scratch_shapes=scratch,
         compiler_params=pltpu.CompilerParams(vmem_limit_bytes=40 << 20),
-        cost_estimate=pl.CostEstimate(flops=0, bytes_accessed=int(micros * 3.6e6), transcendentals=0),
+        cost_estimate=pl.CostEstimate(flops=int(micros * 1.1e9), bytes_accessed=int(micros * 3.6e6), transcendentals=0),
         name=name,
     )(*args)
 
 
 def cut_kernel(count, chunk, place_ref, x_ref, *refs):
-    *out_refs, held = refs
+    out_refs, middle_refs, held = refs[:count], refs[count:-1], refs[-1]
     planes, own, cells = x_ref.shape
     _, padded, width = out_refs[0].shape
     halo = REACH * NXY
-    me, turn = place_ref[0], place_ref[1]
+    me = place_ref[0]
     held[...] = jnp.zeros_like(held)
     lane = lax.broadcasted_iota(jnp.int32, (padded, LANES), 1)
     for plane in range(planes):
@@ -65,7 +66,12 @@
 
                 @pl.when(lax.bitwise_xor(me, target) == step)
                 def _():
-                    out_refs[step][plane + turn * (planes - 1 - 2 * plane)] = window
+                    if out_refs[step].shape[0] == planes:
+                        out_refs[step][plane] = window
+                    elif plane == 0 or plane == planes - 1:
+                        out_refs[step][min(plane, 1)] = window
+                    else:
+                        middle_refs[step - JOINT][...] = window
 
 
 def sides_kernel(place_ref, mean_ref, other_ref, _, low_ref, high_ref):
@@ -154,10 +160,11 @@
     return jnp.concatenate([part.astype(F32) for part in parts], axis=0).astype(BF16)
 
 
-def gather_kernel(count, *refs):
-    parts, out_refs = refs[:count], refs[-refs[0].shape[0] :]
-    for plane, out_ref in enumerate(out_refs):
-        out_ref[...] = joined([part[plane] for part in parts])
+def gather_kernel(count, place_ref, *refs):
+    parts, (low_ref, high_ref) = refs[:count], refs[-2:]
+    turn = place_ref[1]
+    low_ref[...] = joined([part[turn * (part.shape[0] - 1)] for part in parts])
+    high_ref[...] = joined([part[(1 - turn) * (part.shape[0] - 1)] for part in parts])
 
 
 def spread(value):
@@ -280,13 +287,24 @@
             piece_ref[len(results) * full + first // beside] = packed.astype(BF16)
 
 
-def own_kernel(tiles, first, low_ref, values_ref, high_ref, tables_ref, weights_ref, masks_ref, *refs):
-    low_out, high_out, middle_out, *whole_ref, mixed, sums, low, high, middle = refs
+def outer_kernel(low_ref, high_ref, tables_ref, weights_ref, masks_ref, *outs):
+    outer(low_ref[...], high_ref[...], tables_ref, weights_ref, masks_ref, *outs, weights_ref.shape[3])
+
+
+def inner_kernel(count, *refs):
+    parts = [part[1] if len(part.shape) == 3 else part[...] for part in refs[:count]]
+    low_in, high_in, middle_in, tables_ref, weights_ref, masks_ref, *outs = refs[count:]
+    low_out, high_out, middle_out, whole_ref, mixed, sums = outs
+    shared = (tables_ref, weights_ref, masks_ref, low_out, high_out, middle_out, mixed, sums)
+    inner(joined(parts), low_in, high_in, middle_in, *shared, weights_ref.shape[3])
+    fill(middle_out, masks_ref, whole_ref)
+
+
+def own_kernel(tiles, low_ref, values_ref, high_ref, tables_ref, weights_ref, masks_ref, *refs):
+    low_out, high_out, middle_out, mixed, sums, low, high, middle = refs
     shared = (tables_ref, weights_ref, masks_ref)
     outer(low_ref[...], high_ref[...], *shared, low, high, middle, mixed, sums, tiles)
     inner(values_ref[...], low, high, middle, *shared, low_out, high_out, middle_out, mixed, sums, tiles)
-    if first:
-        fill(middle_out, masks_ref, whole_ref[0])
 
 
 def fix_kernel(count, chunk, first, before_ref, after_ref, low_in, high_in, middle_in, *refs):
@@ -319,9 +337,14 @@
         for source in range(count):
             parts += [held[source, plane * full + tile] for tile in range(full)]
             if odd:
-                tile, place = planes * full + plane // beside, plane % beside
-                parts.append(held[source, tile][:, place * odd : (place + 1) * odd])
-        out_ref[plane + turn * (planes - 1 - 2 * plane)] = jnp.concatenate(parts, axis=1)[:own].astype(BF16)
+                tile, spot = planes * full + plane // beside, plane % beside
+                parts.append(held[source, tile][:, spot * odd : (spot + 1) * odd])
+        line = jnp.concatenate(parts, axis=1)[:own].astype(BF16)
+        for turned in range(2):
+
+            @pl.when(turn == turned)
+            def _():
+                out_ref[planes - 1 - plane if turned else plane] = line
 
 
 def shards(panels, mean_field, fluctuations, products, triples, owner_slot):
@@ -343,7 +366,8 @@
         return lax.ppermute(block, "chaos", [(i, i ^ step) for i in range(count)])
 
     def exchanged(blocks):
-        return [blocks[0]] + [exchange(blocks[step], step) for step in range(1, count)]
+        arrived = {step: exchange(blocks[step], step) for step in range(count - 1, 0, -1)}
+        return [blocks[0]] + [arrived[step] for step in range(1, count)]
 
     def neighbours(first_plane, last_plane):
         pairs = [(i, i ^ 1) for i in range(slabs)]
@@ -354,16 +378,19 @@
     def shape(*dims, dtype=BF16):
         return jax.ShapeDtypeStruct(dims, dtype)
 
+    joint = min(JOINT, count)
     cut = call(
         functools.partial(cut_kernel, count, chunk),
         "cut",
         1,
-        [shape(planes, padded, width)] * count,
+        [shape(planes if step < joint else 2, padded, width) for step in range(count)]
+        + [shape(padded, width)] * (count - joint),
         (place, jnp.transpose(panels, (1, 0, 2))),
         [VMEM((padded, cells), F32)],
         scalars=1,
     )
-    parts = exchanged(cut)
+    parts = exchanged(cut[:count])
+    middles = parts[:joint] + [exchange(cut[count + step - joint], step) for step in range(joint, count)]
 
     (tables,) = call(
         functools.partial(tables_kernel, fields, own),
@@ -414,17 +441,24 @@
         held = [VMEM((tiles, rows, LANES), F32)] * held
         return [VMEM((2, tiles, fields * rows, LANES), BF16), VMEM((7, tiles, rows, LANES), F32)] + held
 
-    low, middle_whole, high = call(
-        functools.partial(gather_kernel, count), "gather", 0.5, [plane_whole] * planes, (*parts, tables, weights), unread=2
+    low, high = call(
+        functools.partial(gather_kernel, count),
+        "gather",
+        0.5,
+        [plane_whole] * 2,
+        (place, *parts, tables, weights),
+        scalars=1,
+        unread=2,
     )
     before, after = neighbours(low, high)
+    low, high, middle = call(outer_kernel, "outer", 6, [share] * 3, (low, high, *common), scratch(tiles, 0))
     low, high, middle, middle_whole = call(
-        functools.partial(own_kernel, tiles, True),
-        "first",
-        9,
+        functools.partial(inner_kernel, count),
+        "inner",
+        3,
         [share] * 3 + [plane_whole],
-        (low, middle_whole, high, *common),
-        scratch(tiles, 3),
+        (*middles, low, high, middle, *common),
+        scratch(tiles, 0),
     )
     low, high, low_near, high_near, *sent = call(
         functools.partial(fix_kernel, count, chunk, True),
@@ -434,10 +468,10 @@
         (before, after, low, high, middle, *common),
         scratch(tiles, 2),
     )
+    sent = exchanged(sent)
     before, after = neighbours(low_near, high_near)
-    sent = exchanged(sent)
     low, high, middle = call(
-        functools.partial(own_kernel, near_tiles, False),
+        functools.partial(own_kernel, near_tiles),
         "second",
         8,
         [share] * 3,
@@ -461,7 +495,7 @@
             1,
             [shape(planes, own, cells)],
             (place, *parts),
-            [VMEM((count,) + pieces[0].shape, F32)],
+            [VMEM((count,) + parts[0].shape, F32)],
             scalars=1,
         )
         return jnp.transpose(result, (1, 0, 2))

time: 87.4 us -> 85.2 us (0.975)
  local copies, waits for them, and re-layouts: 5.9 us -> 1.32 us
  Pallas kernels: 29.6 us -> 33.3 us
    pallas_call x11 -> x12, Pallas kernels: 29.6 us -> 33.3 us  [call(): pl.pallas_call(kernel, out_shape=out_shape, in_specs=in_specs, out_specs=...]
    unnamed x13, local copies, waits for them, and re-layouts: 4.31 us -> 1.2 us
    ppermute x9, waiting for transfers between devices: 20.5 us -> 19 us  [exchange(): return lax.ppermute(block, 'chaos', [(i, i ^ step) for i in range(count)])]
  transfers between devices with their start and end apart: 15 -> 15, of which waited for: 4 -> 4; matrix products, arithmetic and copies ran while one was open for 2% -> 1% of each run, Pallas kernels for 29% -> 33%
where the time goes in v5:
time: 85.2 us; the launch traced here: 84.3 us
  Pallas kernels  33.3 us (39%)
  starting transfers between devices  28.7 us (34%)
  waiting for transfers between devices  19.7 us (23%)
  local copies, waits for them, and re-layouts  1.32 us (2%)
  between operations  0.95 us (1%)
    pallas_call x12, Pallas kernels, call(): pl.pallas_call(kernel, out_shape=out_shape, in_specs=in_specs, out_specs=...  33.3 us
    ppermute x9, waiting for transfers between devices, exchange(): return lax.ppermute(block, 'chaos', [(i, i ^ step) for i in range(count)])  19 us
    ppermute x9, starting transfers between devices, exchange(): return lax.ppermute(block, 'chaos', [(i, i ^ step) for i in range(count)])  17.3 us
    ppermute x3, starting transfers between devices, neighbours(): after = lax.ppermute(last_plane, 'space', pairs)  8.93 us
    ppermute x3, starting transfers between devices, neighbours(): return (lax.ppermute(first_plane, 'space', others), after)  2.42 us
  transfers between devices with their start and end apart: 15, of which 4 were waited for; matrix products, arithmetic and copies ran while one was open for 1% of the time, Pallas kernels for 33%

profile of v5, /device:TPU:0, one launch (start us, length us, event | category | flops | bytes accessed | tf_op | source)
XLA Modules:
  0.0 84.3 jit_solution(15486998615776107183)
XLA Ops:
  0.7 0.1 pad_add_fusion.place_ref
  0.8 1.1 %copy-done.2 = bf16[53,3,2304]{2,0,1:T(8,128)(2,1)S(1)} copy-done((bf16[53,3,2304]{2,0,1:T(8,128)(2,1)S(1)}, bf16[53,3,2304]{2,0,1:T(8,128)(2,1)}, u32[]{:S(2)}) %copy-start.2) | copy-done | bytes 732696
  1.9 1.4 %cut.1 = (bf16[3,56,768]{2,1,0:T(8,128)(2,1)S(1)}, bf16[3,56,768]{2,1,0:T(8,128)(2,1)S(1)}, bf16[3,56,768]{2,1,0:T(8,128)(2,1)S(1)}, bf16[3,56,768]{2,1,0:T(8,128)(2,1)S(1)}) custom-call(s32[2]{0:T(128)S(1)} %pad_add_fusion.place_ref, bf16[3,53,2304]{2,1,0:T(8,128)(2,1)S(1)} %bitcast.12), custom_call_target="tpu_custom_call" | custom-call | flops 1100000000 | bytes 3600000 | tf_op jit(solution)/shard_map/cut/pallas_call | solution.py:29
  3.3 3.1 %collective-permute-start = (bf16[3,56,768]{2,1,0:T(8,128)(2,1)S(1)}, bf16[3,56,768]{2,1,0:T(8,128)(2,1)S(1)}, u32[]{:S(2)}, u32[]{:S(2)}) collective-permute-start(bf16[3,56,768]{2,1,0:T(8,128)(2,1)S(1)} %get-tuple-element.33), channel_id=1, source_target_pairs={{0,8},{8,0},{16,24},{24,16},{1,9},{9,1},{17,25},{25,17},{2,10},{10... | collective-permute-start | bytes 774152 | tf_op jit(solution)/shard_map/ppermute | solution.py:366
  6.4 2.6 %collective-permute-start.1 = (bf16[3,56,768]{2,1,0:T(8,128)(2,1)S(1)}, bf16[3,56,768]{2,1,0:T(8,128)(2,1)S(1)}, u32[]{:S(2)}, u32[]{:S(2)}) collective-permute-start(bf16[3,56,768]{2,1,0:T(8,128)(2,1)S(1)} %get-tuple-element.34), channel_id=1, source_target_pairs={{0,16},{8,24},{16,0},{24,8},{1,17},{9,25},{17,1},{25,9},{2,18},{10... | collective-permute-start | bytes 774152 | tf_op jit(solution)/shard_map/ppermute | solution.py:366
  8.9 0.0 collective-permute-start.2
  9.0 0.0 copy-start
  9.0 0.0 copy-start.1
  9.0 5.7 %tables.1._.refs_4_.tables_ref.refs_7_.refs_0_ = bf16[1568,224]{1,0:T(8,128)(2,1)S(1)} custom-call(s32[2]{0:T(128)S(1)} %pad_add_fusion.place_ref, s32[3,1218]{1,0:T(4,128)S(1)} %bitcast.13, f32[1,1218]{1,0:T(1,128)S(1)} %broadcast_in_dim.20.products_ref, s32[1,210]{1,0:T(1,128)S(1)} %bitcast.14, bf16[3,56,768]{2,1,0:T(8,128)(2,1)S(1)} %get-tuple-element.32._.refs_0_), custom_call_target="tpu_custom_call" | custom-call | flops 5500000256 | bytes 18000000 | tf_op jit(solution)/shard_map/tables/pallas_call | solution.py:29
  14.7 0.6 sides.1
  15.3 0.7 collective-permute-start.3
  16.0 3.1 %collective-permute-start.4 = (f32[7,2304]{1,0:T(8,128)S(1)}, f32[7,2304]{1,0:T(8,128)S(1)}, u32[]{:S(2)}, u32[]{:S(2)}) collective-permute-start(f32[7,2304]{1,0:T(8,128)S(1)} %get-tuple-element.37), channel_id=1, source_target_pairs={{0,1},{1,0},{2,3},{3,2},{4,5},{5,4},{6,7},{7,6},{8,9},{9,8},{10,11... | collective-permute-start | bytes 193544 | tf_op jit(solution)/shard_map/ppermute | solution.py:375
  19.2 0.1 pad_maximum_fusion
  19.3 0.0 collective-permute-done.3
  19.3 0.7 collective-permute-done.4
  20.0 0.1 fusion.2
  20.1 0.1 slice.8
  20.2 0.1 pad_maximum_fusion.1.conduct_ref
  20.3 0.3 weights.1.refs_5_.weights_ref.refs_8_.refs_1_
  20.6 0.0 collective-permute-done.refs_1_
  20.6 6.8 %collective-permute-done.1.refs_2_ = bf16[3,56,768]{2,1,0:T(8,128)(2,1)S(1)} collective-permute-done((bf16[3,56,768]{2,1,0:T(8,128)(2,1)S(1)}, bf16[3,56,768]{2,1,0:T(8,128)(2,1)S(1)}, u32[]{:S(2)}, u32[]{:S(2)}) %collective-permute-start.1) | collective-permute-done | bytes 258080 | tf_op jit(solution)/shard_map/ppermute | solution.py:366
  27.5 0.0 collective-permute-done.2.refs_3_
  27.5 0.6 gather.1
  28.1 0.9 %collective-permute-start.5 = (bf16[224,768]{1,0:T(8,128)(2,1)S(1)}, bf16[224,768]{1,0:T(8,128)(2,1)S(1)}, u32[]{:S(2)}, u32[]{:S(2)}) collective-permute-start(bf16[224,768]{1,0:T(8,128)(2,1)S(1)} %get-tuple-element.38.low_ref), channel_id=1, source_target_pairs={{1,2},{2,1},{3,4},{4,3},{5,6},{6,5},{9,10},{10,9},{11,12},{12,11},... | collective-permute-start | bytes 1032200 | tf_op jit(solution)/shard_map/ppermute | solution.py:376
  28.9 2.9 %collective-permute-start.6 = (bf16[224,768]{1,0:T(8,128)(2,1)S(1)}, bf16[224,768]{1,0:T(8,128)(2,1)S(1)}, u32[]{:S(2)}, u32[]{:S(2)}) collective-permute-start(bf16[224,768]{1,0:T(8,128)(2,1)S(1)} %get-tuple-element.39.high_ref), channel_id=1, source_target_pairs={{0,1},{1,0},{2,3},{3,2},{4,5},{5,4},{6,7},{7,6},{8,9},{9,8},{10,11... | collective-permute-start | bytes 1032200 | tf_op jit(solution)/shard_map/ppermute | solution.py:375
  31.8 6.2 %outer.1 = (f32[6,224,128]{2,1,0:T(8,128)S(1)}, f32[6,224,128]{2,1,0:T(8,128)S(1)}, f32[6,224,128]{2,1,0:T(8,128)S(1)}) custom-call(bf16[224,768]{1,0:T(8,128)(2,1)S(1)} %get-tuple-element.38.low_ref, bf16[224,768]{1,0:T(8,128)(2,1)S(1)} %get-tuple-element.39.high_ref, bf16[1568,224]{1,0:T(8,128)(2,1)S(1)} %tables.1._.refs_4_.tables_ref.refs_7_.refs_0_, ...), custom_call_target="tpu_custom_call" | custom-call | flops 6600000000 | bytes 21600000 | tf_op jit(solution)/shard_map/outer/pallas_call | solution.py:29
  38.0 3.3 %inner.1 = (f32[6,224,128]{2,1,0:T(8,128)S(1)}, f32[6,224,128]{2,1,0:T(8,128)S(1)}, f32[6,224,128]{2,1,0:T(8,128)S(1)}, bf16[224,768]{1,0:T(8,128)(2,1)S(1)}) custom-call(bf16[3,56,768]{2,1,0:T(8,128)(2,1)S(1)} %get-tuple-element.32._.refs_0_, bf16[3,56,768]{2,1,0:T(8,128)(2,1)S(1)} %collective-permute-done.refs_1_, ...), custom_call_target="tpu_custom_call" | custom-call | flops 3300000000 | bytes 10800000 | tf_op jit(solution)/shard_map/inner/pallas_call | solution.py:29
  41.4 0.0 collective-permute-done.5.before_ref
  41.4 0.0 collective-permute-done.6.after_ref
  41.4 1.7 %fix.1 = (bf16[224,768]{1,0:T(8,128)(2,1)S(1)}, bf16[224,768]{1,0:T(8,128)(2,1)S(1)}, bf16[224,640]{1,0:T(8,128)(2,1)S(1)}, bf16[224,640]{1,0:T(8,128)(2,1)S(1)}...) custom-call(bf16[224,768]{1,0:T(8,128)(2,1)S(1)} %collective-permute, ...), custom_call_target="tpu_custom_call" | custom-call | flops 3300000000 | bytes 10800000 | tf_op jit(solution)/shard_map/fix/pallas_call | solution.py:29
  43.1 4.7 %collective-permute-start.7 = (bf16[14,56,128]{2,1,0:T(8,128)(2,1)S(1)}, bf16[14,56,128]{2,1,0:T(8,128)(2,1)S(1)}, u32[]{:S(2)}, u32[]{:S(2)}) collective-permute-start(bf16[14,56,128]{2,1,0:T(8,128)(2,1)S(1)} %get-tuple-element.47), channel_id=1, source_target_pairs={{0,8},{8,0},{16,24},{24,16},{1,9},{9,1},{17,25},{25,17},{2,10},{10... | collective-permute-start | bytes 602120 | tf_op jit(solution)/shard_map/ppermute | solution.py:366
  47.8 1.1 %collective-permute-start.8 = (bf16[14,56,128]{2,1,0:T(8,128)(2,1)S(1)}, bf16[14,56,128]{2,1,0:T(8,128)(2,1)S(1)}, u32[]{:S(2)}, u32[]{:S(2)}) collective-permute-start(bf16[14,56,128]{2,1,0:T(8,128)(2,1)S(1)} %get-tuple-element.48), channel_id=1, source_target_pairs={{0,16},{8,24},{16,0},{24,8},{1,17},{9,25},{17,1},{25,9},{2,18},{10... | collective-permute-start | bytes 602120 | tf_op jit(solution)/shard_map/ppermute | solution.py:366
  48.9 1.4 %collective-permute-start.9 = (bf16[14,56,128]{2,1,0:T(8,128)(2,1)S(1)}, bf16[14,56,128]{2,1,0:T(8,128)(2,1)S(1)}, u32[]{:S(2)}, u32[]{:S(2)}) collective-permute-start(bf16[14,56,128]{2,1,0:T(8,128)(2,1)S(1)} %get-tuple-element.49), channel_id=1, source_target_pairs={{0,24},{8,16},{16,8},{24,0},{1,25},{9,17},{17,9},{25,1},{2,26},{10... | collective-permute-start | bytes 602120 | tf_op jit(solution)/shard_map/ppermute | solution.py:366
  50.3 0.9 %collective-permute-start.10 = (bf16[224,640]{1,0:T(8,128)(2,1)S(1)}, bf16[224,640]{1,0:T(8,128)(2,1)S(1)}, u32[]{:S(2)}, u32[]{:S(2)}) collective-permute-start(bf16[224,640]{1,0:T(8,128)(2,1)S(1)} %get-tuple-element.50), channel_id=1, source_target_pairs={{1,2},{2,1},{3,4},{4,3},{5,6},{6,5},{9,10},{10,9},{11,12},{12,11},... | collective-permute-start | bytes 860168 | tf_op jit(solution)/shard_map/ppermute | solution.py:376
  51.2 2.9 %collective-permute-start.11 = (bf16[224,640]{1,0:T(8,128)(2,1)S(1)}, bf16[224,640]{1,0:T(8,128)(2,1)S(1)}, u32[]{:S(2)}, u32[]{:S(2)}) collective-permute-start(bf16[224,640]{1,0:T(8,128)(2,1)S(1)} %get-tuple-element.51), channel_id=1, source_target_pairs={{0,1},{1,0},{2,3},{3,2},{4,5},{5,4},{6,7},{7,6},{8,9},{9,8},{10,11... | collective-permute-start | bytes 860168 | tf_op jit(solution)/shard_map/ppermute | solution.py:375
  54.1 8.3 %second.1 = (f32[6,224,128]{2,1,0:T(8,128)S(1)}, f32[6,224,128]{2,1,0:T(8,128)S(1)}, f32[6,224,128]{2,1,0:T(8,128)S(1)}) custom-call(bf16[224,768]{1,0:T(8,128)(2,1)S(1)} %get-tuple-element.52.low_ref, bf16[224,768]{1,0:T(8,128)(2,1)S(1)} %get-tuple-element.53.values_ref, bf16[224,768]{1,0:T(8,128)(2,1)S(1)} %get-tuple-element.54.high_ref, ...), custom_call_target="tpu_custom_call" | custom-call | flops 8800000000 | bytes 28800000 | tf_op jit(solution)/shard_map/second/pallas_call | solution.py:29
  62.4 0.0 collective-permute-done.10.before_ref
  62.4 0.0 collective-permute-done.11.after_ref
  62.4 1.5 %last.1 = (bf16[14,56,128]{2,1,0:T(8,128)(2,1)S(1)}, bf16[14,56,128]{2,1,0:T(8,128)(2,1)S(1)}, bf16[14,56,128]{2,1,0:T(8,128)(2,1)S(1)}, bf16[14,56,128]{2,1,0:T(8,128)(2,1)S(1)}) custom-call(bf16[224,640]{1,0:T(8,128)(2,1)S(1)} %collective-permute-done.10.before_ref, bf16[224,640]{1,0:T(8,128)(2,1)S(1)} %collective-permute-done.11.after_ref, ...), custom_call_target="tpu_custom_call" | custom-call | flops 3300000000 | bytes 10800000 | tf_op jit(solution)/shard_map/last/pallas_call | solution.py:29
  63.9 1.1 %collective-permute-start.12 = (bf16[14,56,128]{2,1,0:T(8,128)(2,1)S(1)}, bf16[14,56,128]{2,1,0:T(8,128)(2,1)S(1)}, u32[]{:S(2)}, u32[]{:S(2)}) collective-permute-start(bf16[14,56,128]{2,1,0:T(8,128)(2,1)S(1)} %get-tuple-element.59), channel_id=1, source_target_pairs={{0,8},{8,0},{16,24},{24,16},{1,9},{9,1},{17,25},{25,17},{2,10},{10... | collective-permute-start | bytes 602120 | tf_op jit(solution)/shard_map/ppermute | solution.py:366
  65.0 2.0 %collective-permute-start.13 = (bf16[14,56,128]{2,1,0:T(8,128)(2,1)S(1)}, bf16[14,56,128]{2,1,0:T(8,128)(2,1)S(1)}, u32[]{:S(2)}, u32[]{:S(2)}) collective-permute-start(bf16[14,56,128]{2,1,0:T(8,128)(2,1)S(1)} %get-tuple-element.60), channel_id=1, source_target_pairs={{0,16},{8,24},{16,0},{24,8},{1,17},{9,25},{17,1},{25,9},{2,18},{10... | collective-permute-start | bytes 602120 | tf_op jit(solution)/shard_map/ppermute | solution.py:366
  67.0 0.0 collective-permute-done.7.refs_1_
  67.0 1.4 %collective-permute-start.14 = (bf16[14,56,128]{2,1,0:T(8,128)(2,1)S(1)}, bf16[14,56,128]{2,1,0:T(8,128)(2,1)S(1)}, u32[]{:S(2)}, u32[]{:S(2)}) collective-permute-start(bf16[14,56,128]{2,1,0:T(8,128)(2,1)S(1)} %get-tuple-element.61), channel_id=1, source_target_pairs={{0,24},{8,16},{16,8},{24,0},{1,25},{9,17},{17,9},{25,1},{2,26},{10... | collective-permute-start | bytes 602120 | tf_op jit(solution)/shard_map/ppermute | solution.py:366
  68.4 0.0 collective-permute-done.8.refs_2_
  68.4 1.9 %join.2 = bf16[3,53,2304]{2,1,0:T(8,128)(2,1)} custom-call(s32[2]{0:T(128)S(1)} %pad_add_fusion.place_ref, bf16[14,56,128]{2,1,0:T(8,128)(2,1)S(1)} %get-tuple-element.46.refs_0_, bf16[14,56,128]{2,1,0:T(8,128)(2,1)S(1)} %collective-permute-done.7.refs_1_, bf16[14,56,128]{2,1,0:T(8,128)(2,1)S(1)} %collective-permute-done.8.refs_2_, ...), custom_call_target="tpu_custom_call" | custom-call | flops 1100000000 | bytes 3600000 | tf_op jit(solution)/shard_map/join/pallas_call | solution.py:29
  70.3 4.2 %collective-permute-done.12.refs_1_ = bf16[14,56,128]{2,1,0:T(8,128)(2,1)S(1)} collective-permute-done((bf16[14,56,128]{2,1,0:T(8,128)(2,1)S(1)}, bf16[14,56,128]{2,1,0:T(8,128)(2,1)S(1)}, u32[]{:S(2)}, u32[]{:S(2)}) %collective-permute-start.12) | collective-permute-done | bytes 200736 | tf_op jit(solution)/shard_map/ppermute | solution.py:366
  74.5 7.9 %collective-permute-done.13.refs_2_ = bf16[14,56,128]{2,1,0:T(8,128)(2,1)S(1)} collective-permute-done((bf16[14,56,128]{2,1,0:T(8,128)(2,1)S(1)}, bf16[14,56,128]{2,1,0:T(8,128)(2,1)S(1)}, u32[]{:S(2)}, u32[]{:S(2)}) %collective-permute-start.13) | collective-permute-done | bytes 200736 | tf_op jit(solution)/shard_map/ppermute | solution.py:366
  82.4 1.9 %join.3 = bf16[3,53,2304]{2,1,0:T(8,128)(2,1)} custom-call(s32[2]{0:T(128)S(1)} %pad_add_fusion.place_ref, bf16[14,56,128]{2,1,0:T(8,128)(2,1)S(1)} %get-tuple-element.58.refs_0_, bf16[14,56,128]{2,1,0:T(8,128)(2,1)S(1)} %collective-permute-done.12.refs_1_, bf16[14,56,128]{2,1,0:T(8,128)(2,1)S(1)} %collective-permute-done.13.refs_2_, ...), custom_call_target="tpu_custom_call" | custom-call | flops 1100000000 | bytes 3600000 | tf_op jit(solution)/shard_map/join/pallas_call | solution.py:29
  (20 shorter events, 0.2 us)
Async XLA Ops:
  0.6 8.3 %copy-start.5 = (f32[1218]{0:T(1024)S(1)}, f32[1218]{0:T(1024)}, u32[]{:S(2)}) copy-start(f32[1218]{0:T(1024)} %param.9) | copy-start | bytes 14620
  0.6 8.3 %copy-start.4 = (s32[210]{0:T(256)S(1)}, s32[210]{0:T(256)}, u32[]{:S(2)}) copy-start(s32[210]{0:T(256)} %param.11) | copy-start | bytes 2524
  0.7 8.3 %copy-start.3 = (s32[1218,3]{0,1:T(4,128)S(1)}, s32[1218,3]{0,1:T(4,128)}, u32[]{:S(2)}) copy-start(s32[1218,3]{0,1:T(4,128)} %param.10) | copy-start | bytes 43852
  0.7 1.1 %copy-start.2 = (bf16[53,3,2304]{2,0,1:T(8,128)(2,1)S(1)}, bf16[53,3,2304]{2,0,1:T(8,128)(2,1)}, u32[]{:S(2)}) copy-start(bf16[53,3,2304]{2,0,1:T(8,128)(2,1)} %param.6) | copy-start | bytes 2198020
  3.3 17.3 %collective-permute-start = (bf16[3,56,768]{2,1,0:T(8,128)(2,1)S(1)}, bf16[3,56,768]{2,1,0:T(8,128)(2,1)S(1)}, u32[]{:S(2)}, u32[]{:S(2)}) collective-permute-start(bf16[3,56,768]{2,1,0:T(8,128)(2,1)S(1)} %get-tuple-element.33), channel_id=1, source_target_pairs={{0,8},{8,0},{16,24},{24,16},{1,9},{9,1},{17,25},{25,17},{2,10},{10... | collective-permute-start | bytes 774152 | tf_op jit(solution)/shard_map/ppermute | solution.py:366
  6.4 21.1 %collective-permute-start.1 = (bf16[3,56,768]{2,1,0:T(8,128)(2,1)S(1)}, bf16[3,56,768]{2,1,0:T(8,128)(2,1)S(1)}, u32[]{:S(2)}, u32[]{:S(2)}) collective-permute-start(bf16[3,56,768]{2,1,0:T(8,128)(2,1)S(1)} %get-tuple-element.34), channel_id=1, source_target_pairs={{0,16},{8,24},{16,0},{24,8},{1,17},{9,25},{17,1},{25,9},{2,18},{10... | collective-permute-start | bytes 774152 | tf_op jit(solution)/shard_map/ppermute | solution.py:366
  8.9 18.5 %collective-permute-start.2 = (bf16[3,56,768]{2,1,0:T(8,128)(2,1)S(1)}, bf16[3,56,768]{2,1,0:T(8,128)(2,1)S(1)}, u32[]{:S(2)}, u32[]{:S(2)}) collective-permute-start(bf16[3,56,768]{2,1,0:T(8,128)(2,1)S(1)} %get-tuple-element.35), channel_id=1, source_target_pairs={{0,24},{8,16},{16,8},{24,0},{1,25},{9,17},{17,9},{25,1},{2,26},{10... | collective-permute-start | bytes 774152 | tf_op jit(solution)/shard_map/ppermute | solution.py:366
  9.0 5.7 %copy-start = (f32[6,3,2304]{2,1,0:T(4,128)S(1)}, f32[6,3,2304]{2,1,0:T(4,128)}, u32[]{:S(2)}) copy-start(f32[6,3,2304]{2,1,0:T(4,128)} %other_ref.1) | copy-start | bytes 497668
  9.0 5.7 %copy-start.1 = (f32[3,2304]{1,0:T(4,128)S(1)}, f32[3,2304]{1,0:T(4,128)}, u32[]{:S(2)}) copy-start(f32[3,2304]{1,0:T(4,128)} %mean_ref.1) | copy-start | bytes 82948
  15.3 4.0 %collective-permute-start.3 = (f32[7,2304]{1,0:T(8,128)S(1)}, f32[7,2304]{1,0:T(8,128)S(1)}, u32[]{:S(2)}, u32[]{:S(2)}) collective-permute-start(f32[7,2304]{1,0:T(8,128)S(1)} %get-tuple-element.36), channel_id=1, source_target_pairs={{1,2},{2,1},{3,4},{4,3},{5,6},{6,5},{9,10},{10,9},{11,12},{12,11},... | collective-permute-start | bytes 193544 | tf_op jit(solution)/shard_map/ppermute | solution.py:376
  16.0 4.0 %collective-permute-start.4 = (f32[7,2304]{1,0:T(8,128)S(1)}, f32[7,2304]{1,0:T(8,128)S(1)}, u32[]{:S(2)}, u32[]{:S(2)}) collective-permute-start(f32[7,2304]{1,0:T(8,128)S(1)} %get-tuple-element.37), channel_id=1, source_target_pairs={{0,1},{1,0},{2,3},{3,2},{4,5},{5,4},{6,7},{7,6},{8,9},{9,8},{10,11... | collective-permute-start | bytes 193544 | tf_op jit(solution)/shard_map/ppermute | solution.py:375
  28.1 13.3 %collective-permute-start.5 = (bf16[224,768]{1,0:T(8,128)(2,1)S(1)}, bf16[224,768]{1,0:T(8,128)(2,1)S(1)}, u32[]{:S(2)}, u32[]{:S(2)}) collective-permute-start(bf16[224,768]{1,0:T(8,128)(2,1)S(1)} %get-tuple-element.38.low_ref), channel_id=1, source_target_pairs={{1,2},{2,1},{3,4},{4,3},{5,6},{6,5},{9,10},{10,9},{11,12},{12,11},... | collective-permute-start | bytes 1032200 | tf_op jit(solution)/shard_map/ppermute | solution.py:376
  28.9 12.4 %collective-permute-start.6 = (bf16[224,768]{1,0:T(8,128)(2,1)S(1)}, bf16[224,768]{1,0:T(8,128)(2,1)S(1)}, u32[]{:S(2)}, u32[]{:S(2)}) collective-permute-start(bf16[224,768]{1,0:T(8,128)(2,1)S(1)} %get-tuple-element.39.high_ref), channel_id=1, source_target_pairs={{0,1},{1,0},{2,3},{3,2},{4,5},{5,4},{6,7},{7,6},{8,9},{9,8},{10,11... | collective-permute-start | bytes 1032200 | tf_op jit(solution)/shard_map/ppermute | solution.py:375
  43.1 23.9 %collective-permute-start.7 = (bf16[14,56,128]{2,1,0:T(8,128)(2,1)S(1)}, bf16[14,56,128]{2,1,0:T(8,128)(2,1)S(1)}, u32[]{:S(2)}, u32[]{:S(2)}) collective-permute-start(bf16[14,56,128]{2,1,0:T(8,128)(2,1)S(1)} %get-tuple-element.47), channel_id=1, source_target_pairs={{0,8},{8,0},{16,24},{24,16},{1,9},{9,1},{17,25},{25,17},{2,10},{10... | collective-permute-start | bytes 602120 | tf_op jit(solution)/shard_map/ppermute | solution.py:366
  47.8 20.6 %collective-permute-start.8 = (bf16[14,56,128]{2,1,0:T(8,128)(2,1)S(1)}, bf16[14,56,128]{2,1,0:T(8,128)(2,1)S(1)}, u32[]{:S(2)}, u32[]{:S(2)}) collective-permute-start(bf16[14,56,128]{2,1,0:T(8,128)(2,1)S(1)} %get-tuple-element.48), channel_id=1, source_target_pairs={{0,16},{8,24},{16,0},{24,8},{1,17},{9,25},{17,1},{25,9},{2,18},{10... | collective-permute-start | bytes 602120 | tf_op jit(solution)/shard_map/ppermute | solution.py:366
  48.9 19.5 %collective-permute-start.9 = (bf16[14,56,128]{2,1,0:T(8,128)(2,1)S(1)}, bf16[14,56,128]{2,1,0:T(8,128)(2,1)S(1)}, u32[]{:S(2)}, u32[]{:S(2)}) collective-permute-start(bf16[14,56,128]{2,1,0:T(8,128)(2,1)S(1)} %get-tuple-element.49), channel_id=1, source_target_pairs={{0,24},{8,16},{16,8},{24,0},{1,25},{9,17},{17,9},{25,1},{2,26},{10... | collective-permute-start | bytes 602120 | tf_op jit(solution)/shard_map/ppermute | solution.py:366
  50.3 12.1 %collective-permute-start.10 = (bf16[224,640]{1,0:T(8,128)(2,1)S(1)}, bf16[224,640]{1,0:T(8,128)(2,1)S(1)}, u32[]{:S(2)}, u32[]{:S(2)}) collective-permute-start(bf16[224,640]{1,0:T(8,128)(2,1)S(1)} %get-tuple-element.50), channel_id=1, source_target_pairs={{1,2},{2,1},{3,4},{4,3},{5,6},{6,5},{9,10},{10,9},{11,12},{12,11},... | collective-permute-start | bytes 860168 | tf_op jit(solution)/shard_map/ppermute | solution.py:376
  51.2 11.2 %collective-permute-start.11 = (bf16[224,640]{1,0:T(8,128)(2,1)S(1)}, bf16[224,640]{1,0:T(8,128)(2,1)S(1)}, u32[]{:S(2)}, u32[]{:S(2)}) collective-permute-start(bf16[224,640]{1,0:T(8,128)(2,1)S(1)} %get-tuple-element.51), channel_id=1, source_target_pairs={{0,1},{1,0},{2,3},{3,2},{4,5},{5,4},{6,7},{7,6},{8,9},{9,8},{10,11... | collective-permute-start | bytes 860168 | tf_op jit(solution)/shard_map/ppermute | solution.py:375
  63.9 10.6 %collective-permute-start.12 = (bf16[14,56,128]{2,1,0:T(8,128)(2,1)S(1)}, bf16[14,56,128]{2,1,0:T(8,128)(2,1)S(1)}, u32[]{:S(2)}, u32[]{:S(2)}) collective-permute-start(bf16[14,56,128]{2,1,0:T(8,128)(2,1)S(1)} %get-tuple-element.59), channel_id=1, source_target_pairs={{0,8},{8,0},{16,24},{24,16},{1,9},{9,1},{17,25},{25,17},{2,10},{10... | collective-permute-start | bytes 602120 | tf_op jit(solution)/shard_map/ppermute | solution.py:366
  65.0 17.4 %collective-permute-start.13 = (bf16[14,56,128]{2,1,0:T(8,128)(2,1)S(1)}, bf16[14,56,128]{2,1,0:T(8,128)(2,1)S(1)}, u32[]{:S(2)}, u32[]{:S(2)}) collective-permute-start(bf16[14,56,128]{2,1,0:T(8,128)(2,1)S(1)} %get-tuple-element.60), channel_id=1, source_target_pairs={{0,16},{8,24},{16,0},{24,8},{1,17},{9,25},{17,1},{25,9},{2,18},{10... | collective-permute-start | bytes 602120 | tf_op jit(solution)/shard_map/ppermute | solution.py:366
  67.0 15.4 %collective-permute-start.14 = (bf16[14,56,128]{2,1,0:T(8,128)(2,1)S(1)}, bf16[14,56,128]{2,1,0:T(8,128)(2,1)S(1)}, u32[]{:S(2)}, u32[]{:S(2)}) collective-permute-start(bf16[14,56,128]{2,1,0:T(8,128)(2,1)S(1)} %get-tuple-element.61), channel_id=1, source_target_pairs={{0,24},{8,16},{16,8},{24,0},{1,25},{9,17},{17,9},{25,1},{2,26},{10... | collective-permute-start | bytes 602120 | tf_op jit(solution)/shard_map/ppermute | solution.py:366

commit v6 on v5

--- a/solution.py
+++ b/solution.py
@@ -10,7 +10,8 @@
 NXY = 48
 SCALE = 0.15
 LANES = 128
-JOINT = 8
+JOINT = 2
+EXTRA = 32
 REACH = 2
 BLOCK = 32
 VMEM = pltpu.VMEM
@@ -38,12 +39,12 @@
     )(*args)
 
 
-def cut_kernel(count, chunk, place_ref, x_ref, *refs):
+def cut_kernel(count, chunk, me_ref, x_ref, *refs):
     out_refs, middle_refs, held = refs[:count], refs[count:-1], refs[-1]
     planes, own, cells = x_ref.shape
     _, padded, width = out_refs[0].shape
     halo = REACH * NXY
-    me = place_ref[0]
+    me = me_ref[0]
     held[...] = jnp.zeros_like(held)
     lane = lax.broadcasted_iota(jnp.int32, (padded, LANES), 1)
     for plane in range(planes):
@@ -74,20 +75,7 @@
                         middle_refs[step - JOINT][...] = window
 
 
-def sides_kernel(place_ref, mean_ref, other_ref, _, low_ref, high_ref):
-    turn = place_ref[1]
-    last = mean_ref.shape[0] - 1
-    for plane, turned, out_ref in ((0, last, low_ref), (last, 0, high_ref)):
-
-        def facing(ref):
-            return jnp.where(turn > 0, ref[turned : turned + 1, :], ref[plane : plane + 1, :])
-
-        out_ref[0:1, :] = facing(mean_ref)
-        for field in range(other_ref.shape[0]):
-            out_ref[field + 1 : field + 2, :] = facing(other_ref.at[field])
-
-
-def tables_kernel(fields, own, place_ref, triples_ref, products_ref, owners_ref, _, out_ref, held, by_column):
+def tables_kernel(fields, own, me_ref, triples_ref, products_ref, owners_ref, _, out_ref, held, by_column):
     rows, total = by_column.shape[1:]
     entries, factors = triples_ref.shape[1], products_ref.shape[1]
     named = owners_ref.shape[1]
@@ -99,7 +87,7 @@
     held[4:5, :named] = owners_ref[...].astype(F32)
     owners = held[4:5, :names].astype(jnp.int32)
     group = owners // own
-    slots = lax.bitwise_xor(group, place_ref[0]) * padded + owners - group * own
+    slots = lax.bitwise_xor(group, me_ref[0]) * padded + owners - group * own
     slots = jnp.broadcast_to(slots.astype(F32), (16, names)).astype(BF16)
 
     def placed(which):
@@ -130,41 +118,54 @@
         out_ref[pl.ds(pl.multiple_of(block * size, size), size), :] = acc.astype(BF16)
 
 
-def weights_kernel(conduct_ref, masks_ref, out_ref):
-    planes, fields, _, tiles = out_ref.shape[:4]
+def spread_face(face, out_ref):
+    for field in range(out_ref.shape[0]):
+        for tile in range(out_ref.shape[1]):
+            out_ref[field, tile] = jnp.broadcast_to(
+                face[field : field + 1, tile * LANES : (tile + 1) * LANES], (8, LANES)
+            )
+
+
+def weights_kernel(conduct_ref, masks_ref, *refs):
+    out_ref = refs[-1 - (len(refs) - 2) // 2]
+    passed, passed_out = refs[: (len(refs) - 2) // 2], refs[len(refs) - (len(refs) - 2) // 2 :]
+    for in_ref, to_ref in zip(passed, passed_out):
+        to_ref[...] = in_ref[...]
+    planes, _, _, tiles = out_ref.shape[:4]
     width = tiles * LANES
 
     def mask(which):
         return jnp.concatenate([masks_ref[which, tile, 0:1, :] for tile in range(tiles)], axis=1)
 
     for plane in range(planes):
-        own = conduct_ref[plane + 1]
+        own = conduct_ref[plane]
         others = (
             pltpu.roll(own, width - NXY, 1),
             pltpu.roll(own, NXY, 1),
             pltpu.roll(own, width - 1, 1) * mask(0),
             pltpu.roll(own, 1, 1) * mask(1),
-            conduct_ref[plane + 2],
-            conduct_ref[plane],
+            conduct_ref[min(plane + 1, planes - 1)],
+            conduct_ref[max(plane - 1, 0)],
         )
         for way, other in enumerate(others):
-            face = 0.5 * (own + other)
-            for field in range(fields):
-                for tile in range(tiles):
-                    out_ref[plane, field, way, tile] = jnp.broadcast_to(
-                        face[field : field + 1, tile * LANES : (tile + 1) * LANES], (8, LANES)
-                    )
+            spread_face(0.5 * (own + other), out_ref.at[plane, way])
 
 
 def joined(parts):
     return jnp.concatenate([part.astype(F32) for part in parts], axis=0).astype(BF16)
 
 
-def gather_kernel(count, place_ref, *refs):
-    parts, (low_ref, high_ref) = refs[:count], refs[-2:]
-    turn = place_ref[1]
-    low_ref[...] = joined([part[turn * (part.shape[0] - 1)] for part in parts])
-    high_ref[...] = joined([part[(1 - turn) * (part.shape[0] - 1)] for part in parts])
+def gather_kernel(count, turn_ref, conduct_ref, *refs):
+    parts, out_refs = refs[:count], refs[-2:]
+    for side, out_ref in enumerate(out_refs):
+        place = lax.bitwise_xor(turn_ref[0], side)
+        rest = conduct_ref[side * (conduct_ref.shape[0] - 1)]
+        pieces = []
+        for _ in range(3):
+            pieces.append(rest.astype(BF16))
+            rest = rest - pieces[-1].astype(F32)
+        pieces.append(jnp.zeros_like(pieces[0]))
+        out_ref[...] = joined([part[place * (part.shape[0] - 1)] for part in parts] + pieces)
 
 
 def spread(value):
@@ -177,22 +178,21 @@
         mixed[tile] = result[:, tile * LANES : (tile + 1) * LANES]
 
 
-def weigh(mixed, weights_ref, plane, ways, sums, tiles):
+def weigh(values_of, face_of, ways, fields, sums, tiles):
     rows = sums.shape[2]
-    fields = weights_ref.shape[1]
     for tile in tiles:
         for block in range(rows // BLOCK):
             totals = [None] * len(ways)
             for field in range(fields):
                 start = (block * fields + field) * BLOCK
-                values = mixed[tile, start : start + BLOCK, :].astype(F32)
+                values = values_of(tile, slice(start, start + BLOCK))
                 for i, way in enumerate(ways):
-                    term = spread(weights_ref[plane, field, way, tile]) * values
+                    term = spread(face_of(way, field, tile)) * values
                     totals[i] = term if field == 0 else totals[i] + term
             here = slice(block * BLOCK, (block + 1) * BLOCK)
             for i, way in enumerate(ways):
                 sums[way, tile, here, :] = totals[i]
-            if len(ways) == 6:
+            if len(ways) > 1:
                 sums[ALL, tile, here, :] = functools.reduce(jnp.add, totals)
 
 
@@ -225,16 +225,28 @@
             write(tile, here, value)
 
 
-def measure_plane(values, plane, tables_ref, weights_ref, mixed, sums, tiles):
+def measure_plane(values, plane, tables_ref, weights_ref, faces_ref, mixed, sums, tiles):
+    planes, _, fields = weights_ref.shape[:3]
+    outside = {0: LAST_Z, planes - 1: NEXT_Z}.get(plane)
+    ways = [way for way in range(6) if way != outside or faces_ref is not None]
+
+    def values_of(tile, rows):
+        return mixed[tile, rows, :].astype(F32)
+
+    def face_of(way, field, tile):
+        if way == outside:
+            return faces_ref[min(plane, 1), field, tile]
+        return weights_ref[plane, way, field, tile]
+
     mix(tables_ref, values, mixed)
-    weigh(mixed, weights_ref, plane, range(6), sums, range(tiles))
-    weigh(mixed, weights_ref, plane, (NEXT_X,), sums, range(tiles, sums.shape[1]))
-
-
-def outer(low, high, tables_ref, weights_ref, masks_ref, low_out, high_out, middle_out, mixed, sums, tiles):
+    weigh(values_of, face_of, ways, fields, sums, range(tiles))
+    weigh(values_of, face_of, (NEXT_X,), fields, sums, range(tiles, sums.shape[1]))
+
+
+def outer(low, high, tables_ref, weights_ref, masks_ref, faces_ref, low_out, high_out, middle_out, mixed, sums, tiles):
     last = weights_ref.shape[0] - 1
     for plane, values, out_ref, way in ((0, low, low_out, NEXT_Z), (last, high, high_out, LAST_Z)):
-        measure_plane(values, plane, tables_ref, weights_ref, mixed.at[min(plane, 1)], sums, tiles)
+        measure_plane(values, plane, tables_ref, weights_ref, faces_ref, mixed.at[min(plane, 1)], sums, tiles)
 
         def write(tile, here, value):
             out_ref[tile, here, :] = value
@@ -247,7 +259,7 @@
 def inner(
     values, low_in, high_in, middle_in, tables_ref, weights_ref, masks_ref, low_out, high_out, out, mixed, sums, tiles
 ):
-    measure_plane(values, 1, tables_ref, weights_ref, mixed.at[0], sums, tiles)
+    measure_plane(values, 1, tables_ref, weights_ref, None, mixed.at[0], sums, tiles)
 
     def write(tile, here, value):
         out[tile, here, :] = SCALE * (value + middle_in[tile, here, :])
@@ -288,7 +300,9 @@
 
 
 def outer_kernel(low_ref, high_ref, tables_ref, weights_ref, masks_ref, *outs):
-    outer(low_ref[...], high_ref[...], tables_ref, weights_ref, masks_ref, *outs, weights_ref.shape[3])
+    rows = tables_ref.shape[1]
+    shared = (tables_ref, weights_ref, masks_ref, None)
+    outer(low_ref[0:rows, :], high_ref[0:rows, :], *shared, *outs, weights_ref.shape[3])
 
 
 def inner_kernel(count, *refs):
@@ -300,36 +314,68 @@
     fill(middle_out, masks_ref, whole_ref)
 
 
-def own_kernel(tiles, low_ref, values_ref, high_ref, tables_ref, weights_ref, masks_ref, *refs):
+def own_kernel(tiles, low_ref, values_ref, high_ref, tables_ref, weights_ref, masks_ref, faces_ref, *refs):
     low_out, high_out, middle_out, mixed, sums, low, high, middle = refs
     shared = (tables_ref, weights_ref, masks_ref)
-    outer(low_ref[...], high_ref[...], *shared, low, high, middle, mixed, sums, tiles)
+    outer(low_ref[...], high_ref[...], *shared, faces_ref, low, high, middle, mixed, sums, tiles)
     inner(values_ref[...], low, high, middle, *shared, low_out, high_out, middle_out, mixed, sums, tiles)
 
 
-def fix_kernel(count, chunk, first, before_ref, after_ref, low_in, high_in, middle_in, *refs):
-    tables_ref, weights_ref, masks_ref, *refs = refs
-    if first:
-        wholes, nears, refs = refs[:2], refs[2:4], refs[4:]
-    pieces, (mixed, sums, low, high) = refs[:count], refs[count:]
-    last = weights_ref.shape[0] - 1
-    sides = ((before_ref, low_in, low, 0, LAST_Z), (after_ref, high_in, high, last, NEXT_Z))
-    for side, (halo_ref, share_ref, result, plane, way) in enumerate(sides):
-        mix(tables_ref, halo_ref[...], mixed.at[side])
-        weigh(mixed.at[side], weights_ref, plane, (way,), sums, range(sums.shape[1]))
-        for tile in range(sums.shape[1]):
-            result[tile] = SCALE * (share_ref[tile] - sums[way, tile])
-        if first:
-            fill(result, masks_ref, wholes[side])
-            nears[side][...] = wholes[side][:, : nears[side].shape[1]]
-    emit((low, middle_in, high), chunk, pieces)
-
-
-def join_kernel(count, chunk, place_ref, *refs):
+def first_fix_kernel(count, chunk, turn_ref, *refs):
+    halo_refs, own_refs, share_refs, (middle_in, tables_ref, masks_ref), refs = (
+        refs[0:2], refs[2:4], refs[4:6], refs[6:9], refs[9:]
+    )
+    wholes, nears, faces_ref, pieces, (mixed, sums, ends) = refs[:2], refs[2:4], refs[4], refs[5:-3], refs[-3:]
+    rows, (_, fields, tiles, _, _) = tables_ref.shape[1], faces_ref.shape
+    for side in range(2):
+        coefficient = 0.0
+        for ref in (own_refs[side], halo_refs[side]):
+            parts = ref[rows : rows + EXTRA, :].astype(F32)
+            coefficient = coefficient + ((parts[16:24] + parts[8:16]) + parts[0:8])
+        spread_face(0.5 * coefficient, faces_ref.at[side])
+        for index, ref in enumerate((own_refs[side], halo_refs[side])):
+            mix(tables_ref, ref[0:rows, :], mixed.at[index])
+
+        def values_of(tile, here):
+            return mixed[0, tile, here, :].astype(F32) - mixed[1, tile, here, :].astype(F32)
+
+        def face_of(way, field, tile):
+            return faces_ref[side, field, tile]
+
+        weigh(values_of, face_of, (0,), fields, sums, range(tiles))
+        result = ends.at[lax.bitwise_xor(turn_ref[0], side)]
+        for tile in range(tiles):
+            result[tile] = SCALE * (share_refs[side][tile] + sums[0, tile])
+        fill(result, masks_ref, wholes[side])
+        nears[side][...] = wholes[side][:, : nears[side].shape[1]]
+    emit((ends.at[0], middle_in, ends.at[1]), chunk, pieces)
+
+
+def last_fix_kernel(count, chunk, turn_ref, *refs):
+    halo_refs, share_refs, (middle_in, tables_ref, faces_ref), refs = refs[0:2], refs[2:4], refs[4:7], refs[7:]
+    pieces, (mixed, sums, ends) = refs[:-3], refs[-3:]
+    fields, tiles = faces_ref.shape[1], sums.shape[1]
+    for side in range(2):
+        mix(tables_ref, halo_refs[side][...], mixed.at[side])
+
+        def values_of(tile, here):
+            return mixed[side, tile, here, :].astype(F32)
+
+        def face_of(way, field, tile):
+            return faces_ref[side, field, tile]
+
+        weigh(values_of, face_of, (0,), fields, sums, range(tiles))
+        result = ends.at[lax.bitwise_xor(turn_ref[0], side)]
+        for tile in range(tiles):
+            result[tile] = SCALE * (share_refs[side][tile] - sums[0, tile])
+    emit((ends.at[0], middle_in, ends.at[1]), chunk, pieces)
+
+
+def join_kernel(count, chunk, me_ref, *refs):
     piece_refs, (out_ref, held) = refs[:count], refs[count:]
     planes, own, _ = out_ref.shape
     full, odd, beside, _ = packing(planes, chunk)
-    me, turn = place_ref[0], place_ref[1]
+    me = me_ref[0]
     for step in range(count):
         held[lax.bitwise_xor(me, step)] = piece_refs[step][...].astype(F32)
     for plane in range(planes):
@@ -339,12 +385,7 @@
             if odd:
                 tile, spot = planes * full + plane // beside, plane % beside
                 parts.append(held[source, tile][:, spot * odd : (spot + 1) * odd])
-        line = jnp.concatenate(parts, axis=1)[:own].astype(BF16)
-        for turned in range(2):
-
-            @pl.when(turn == turned)
-            def _():
-                out_ref[planes - 1 - plane if turned else plane] = line
+        out_ref[plane] = jnp.concatenate(parts, axis=1)[:own].astype(BF16)
 
 
 def shards(panels, mean_field, fluctuations, products, triples, owner_slot):
@@ -358,8 +399,8 @@
     padded = up(own, 8)
     rows = count * padded
     fields = 1 + fluctuations.shape[0]
-    turn = lax.axis_index("space") % 2
-    place = jnp.stack([me, turn]).astype(jnp.int32)
+    turn = lax.bitwise_and(lax.axis_index("space"), 1)
+    me_alone, turn_alone = me.astype(jnp.int32).reshape(1), turn.astype(jnp.int32).reshape(1)
     tiles = width // LANES
 
     def exchange(block, step):
@@ -385,38 +426,26 @@
         1,
         [shape(planes if step < joint else 2, padded, width) for step in range(count)]
         + [shape(padded, width)] * (count - joint),
-        (place, jnp.transpose(panels, (1, 0, 2))),
+        (me_alone, jnp.transpose(panels, (1, 0, 2))),
         [VMEM((padded, cells), F32)],
         scalars=1,
     )
     parts = exchanged(cut[:count])
-    middles = parts[:joint] + [exchange(cut[count + step - joint], step) for step in range(joint, count)]
 
     (tables,) = call(
         functools.partial(tables_kernel, fields, own),
         "tables",
         5,
         [shape(fields * rows, rows)],
-        (place, triples.T, products[None], owner_slot[None], cut[0]),
+        (me_alone, triples.T, products[None], owner_slot[None], cut[0]),
         [VMEM((8, up(products.shape[0], 2 * LANES)), F32), VMEM((3, rows, up(products.shape[0], 2 * LANES)), BF16)],
         scalars=1,
         unread=1,
     )
 
-    sides = call(
-        sides_kernel,
-        "sides",
-        0.2,
-        [shape(fields, cells, dtype=F32)] * 2,
-        (place, mean_field, fluctuations, tables),
-        scalars=1,
-        unread=1,
-    )
-    before, after = neighbours(*sides)
     conduct = jnp.concatenate([mean_field[:, None], fluctuations.transpose(1, 0, 2)], axis=1)
     conduct = jnp.where(turn > 0, conduct[::-1], conduct)
-    conduct = jnp.concatenate([before[None], conduct, after[None]], axis=0)
-    conduct = jnp.pad(conduct, ((0, 0), (0, 0), (halo, halo)))
+    conduct = jnp.pad(conduct, ((0, 0), (0, up(fields, 8) - fields), (halo, halo)))
     conduct = lax.dynamic_slice_in_dim(conduct, me * chunk, chunk + 2 * halo, 2)
     gap = jnp.zeros(conduct.shape[:-1] + (width - chunk - 2 * halo,), F32)
     conduct = jnp.concatenate([conduct[..., halo:], gap, conduct[..., :halo]], axis=-1)
@@ -427,9 +456,15 @@
     inside = (row >= 0) & (row < NXY) & ((lane < chunk + halo) | (lane >= width - halo))
     masks = jnp.stack([cell % NXY < NXY - 1, cell % NXY > 0, inside]).astype(F32)
     masks = jnp.broadcast_to(masks.reshape(3, tiles, 1, LANES), (3, tiles, 8, LANES))
-    (weights,) = call(
-        weights_kernel, "weights", 0.3, [shape(planes, fields, 6, tiles, 8, LANES, dtype=F32)], (conduct, masks)
-    )
+    weights, *middles = call(
+        weights_kernel,
+        "weights",
+        0.5,
+        [shape(planes, 6, fields, tiles, 8, LANES, dtype=F32)] + [shape(padded, width)] * (count - joint),
+        (conduct, masks, *cut[count:], tables),
+        unread=1,
+    )
+    middles = parts[:joint] + [exchange(middles[step - joint], step) for step in range(joint, count)]
 
     common = (tables, weights, masks)
     plane_whole = shape(rows, width)
@@ -437,54 +472,59 @@
     pieces = [shape(packing(planes, chunk)[-1], padded, LANES)] * count
     near_tiles = near // LANES
 
-    def scratch(tiles, held):
-        held = [VMEM((tiles, rows, LANES), F32)] * held
-        return [VMEM((2, tiles, fields * rows, LANES), BF16), VMEM((7, tiles, rows, LANES), F32)] + held
+    def scratch(tiles, kinds=7):
+        return [VMEM((2, tiles, fields * rows, LANES), BF16), VMEM((kinds, tiles, rows, LANES), F32)]
 
     low, high = call(
         functools.partial(gather_kernel, count),
         "gather",
         0.5,
-        [plane_whole] * 2,
-        (place, *parts, tables, weights),
+        [shape(rows + EXTRA, width)] * 2,
+        (turn_alone, conduct, *parts, tables, weights),
         scalars=1,
         unread=2,
     )
-    before, after = neighbours(low, high)
-    low, high, middle = call(outer_kernel, "outer", 6, [share] * 3, (low, high, *common), scratch(tiles, 0))
+    halos = neighbours(low, high)
+    edges = (low, high)
+    low, high, middle = call(outer_kernel, "outer", 6, [share] * 3, (low, high, *common), scratch(tiles))
     low, high, middle, middle_whole = call(
         functools.partial(inner_kernel, count),
         "inner",
         3,
         [share] * 3 + [plane_whole],
         (*middles, low, high, middle, *common),
-        scratch(tiles, 0),
-    )
-    low, high, low_near, high_near, *sent = call(
-        functools.partial(fix_kernel, count, chunk, True),
+        scratch(tiles),
+    )
+    low, high, low_near, high_near, faces, *sent = call(
+        functools.partial(first_fix_kernel, count, chunk),
         "fix",
         3,
-        [plane_whole] * 2 + [shape(rows, near)] * 2 + pieces,
-        (before, after, low, high, middle, *common),
-        scratch(tiles, 2),
+        [plane_whole] * 2
+        + [shape(rows, near)] * 2
+        + [shape(2, fields, tiles, 8, LANES, dtype=F32)]
+        + pieces,
+        (turn_alone, *halos, *edges, low, high, middle, tables, masks),
+        scratch(tiles, 1) + [VMEM((2, tiles, rows, LANES), F32)],
+        scalars=1,
     )
     sent = exchanged(sent)
-    before, after = neighbours(low_near, high_near)
+    halos = neighbours(low_near, high_near)
     low, high, middle = call(
         functools.partial(own_kernel, near_tiles),
         "second",
         8,
         [share] * 3,
-        (low, middle_whole, high, *common),
-        scratch(tiles, 3),
+        (low, middle_whole, high, *common, faces),
+        scratch(tiles) + [VMEM((tiles, rows, LANES), F32)] * 3,
     )
     second = call(
-        functools.partial(fix_kernel, count, chunk, False),
+        functools.partial(last_fix_kernel, count, chunk),
         "last",
         3,
         pieces,
-        (before, after, low, high, middle, *common),
-        scratch(near_tiles, 2),
+        (turn_alone, *halos, low, high, middle, tables, faces),
+        scratch(near_tiles, 1) + [VMEM((2, near_tiles, rows, LANES), F32)],
+        scalars=1,
     )
     second = exchanged(second)
 
@@ -494,7 +534,7 @@
             "join",
             1,
             [shape(planes, own, cells)],
-            (place, *parts),
+            (me_alone, *parts),
             [VMEM((count,) + parts[0].shape, F32)],
             scalars=1,
         )

time: 85.2 us -> 86.6 us (1.016)
  Pallas kernels: 33.3 us -> 30.9 us
  starting transfers between devices: 28.7 us -> 30.6 us
  waiting for transfers between devices: 19.7 us -> 21.3 us
    ppermute x9 -> x11, starting transfers between devices: 17.3 us -> 23 us  [exchange(): return lax.ppermute(block, 'chaos', [(i, i ^ step) for i in range(count)])]
    ppermute x3 -> x2, starting transfers between devices: 8.93 us -> 5.79 us  [neighbours(): after = lax.ppermute(last_plane, 'space', pairs)]
    pallas_call x12 -> x11, Pallas kernels: 33.3 us -> 30.9 us  [call(): pl.pallas_call(kernel, out_shape=out_shape, in_specs=in_specs, out_specs=...]
    ppermute x9 -> x11, waiting for transfers between devices: 19 us -> 21.3 us  [exchange(): return lax.ppermute(block, 'chaos', [(i, i ^ step) for i in range(count)])]
    ppermute x3 -> x2, starting transfers between devices: 2.42 us -> 1.77 us  [neighbours(): return (lax.ppermute(first_plane, 'space', others), after)]
  transfers between devices with their start and end apart: 15 -> 15, of which waited for: 4 -> 4; matrix products, arithmetic and copies ran while one was open for 1% -> 1% of each run, Pallas kernels for 33% -> 30%
where the time goes in v6:
time: 86.6 us; the launch traced here: 85.4 us
  Pallas kernels  30.9 us (36%)
  starting transfers between devices  30.6 us (35%)
  waiting for transfers between devices  21.3 us (25%)
  local copies, waits for them, and re-layouts  1.4 us (2%)
  between operations  0.91 us (1%)
    pallas_call x11, Pallas kernels, call(): pl.pallas_call(kernel, out_shape=out_shape, in_specs=in_specs, out_specs=...  30.9 us
    ppermute x11, starting transfers between devices, exchange(): return lax.ppermute(block, 'chaos', [(i, i ^ step) for i in range(count)])  23 us
    ppermute x11, waiting for transfers between devices, exchange(): return lax.ppermute(block, 'chaos', [(i, i ^ step) for i in range(count)])  21.3 us
    ppermute x2, starting transfers between devices, neighbours(): after = lax.ppermute(last_plane, 'space', pairs)  5.79 us
    ppermute x2, starting transfers between devices, neighbours(): return (lax.ppermute(first_plane, 'space', others), after)  1.77 us
  transfers between devices with their start and end apart: 15, of which 4 were waited for; matrix products, arithmetic and copies ran while one was open for 1% of the time, Pallas kernels for 30%

profile of v6, /device:TPU:0, one launch (start us, length us, event | category | flops | bytes accessed | tf_op | source)
XLA Modules:
  0.0 85.4 jit_solution(18235467385278255343)
XLA Ops:
  0.7 0.0 copy-start
  0.7 1.1 %copy-done = bf16[53,3,2304]{2,0,1:T(8,128)(2,1)S(1)} copy-done((bf16[53,3,2304]{2,0,1:T(8,128)(2,1)S(1)}, bf16[53,3,2304]{2,0,1:T(8,128)(2,1)}, u32[]{:S(2)}) %copy-start) | copy-done | bytes 732696
  1.8 0.8 cut.1
  2.6 3.1 %collective-permute-start = (bf16[3,56,768]{2,1,0:T(8,128)(2,1)S(1)}, bf16[3,56,768]{2,1,0:T(8,128)(2,1)S(1)}, u32[]{:S(2)}, u32[]{:S(2)}) collective-permute-start(bf16[3,56,768]{2,1,0:T(8,128)(2,1)S(1)} %get-tuple-element.37), channel_id=1, source_target_pairs={{0,8},{8,0},{16,24},{24,16},{1,9},{9,1},{17,25},{25,17},{2,10},{10... | collective-permute-start | bytes 774152 | tf_op jit(solution)/shard_map/ppermute | solution.py:407
  5.7 2.6 %collective-permute-start.1 = (bf16[2,56,768]{2,1,0:T(8,128)(2,1)S(1)}, bf16[2,56,768]{2,1,0:T(8,128)(2,1)S(1)}, u32[]{:S(2)}, u32[]{:S(2)}) collective-permute-start(bf16[2,56,768]{2,1,0:T(8,128)(2,1)S(1)} %get-tuple-element.38), channel_id=1, source_target_pairs={{0,16},{8,24},{16,0},{24,8},{1,17},{9,25},{17,1},{25,9},{2,18},{10... | collective-permute-start | bytes 516104 | tf_op jit(solution)/shard_map/ppermute | solution.py:407
  8.3 0.0 collective-permute-start.2
  8.4 0.0 copy-done.4
  8.5 0.1 pad_maximum_fusion
  8.5 0.1 pad_dynamic-slice_fusion.1
  8.6 0.1 pad_dynamic-slice_fusion
  8.8 5.1 %tables.1.refs_2_.refs_4_.tables_ref.refs_7_.refs_5_ = bf16[1568,224]{1,0:T(8,128)(2,1)S(1)} custom-call(s32[1]{0:T(128)} %bitcast.me_ref, s32[3,1218]{1,0:T(4,128)S(1)} %bitcast.11, f32[1,1218]{1,0:T(1,128)S(1)} %broadcast_in_dim.15.products_ref, s32[1,210]{1,0:T(1,128)S(1)} %bitcast.12, bf16[3,56,768]{2,1,0:T(8,128)(2,1)S(1)} %get-tuple-element.36._.refs_0_), custom_call_target="tpu_custom_call" | custom-call | flops 5500000256 | bytes 18000000 | tf_op jit(solution)/shard_map/tables/pallas_call | solution.py:30
  14.0 0.1 pad_maximum_fusion.1.conduct_ref
  14.0 0.2 weights.1
  14.3 2.0 %collective-permute-start.5 = (bf16[56,768]{1,0:T(8,128)(2,1)S(1)}, bf16[56,768]{1,0:T(8,128)(2,1)S(1)}, u32[]{:S(2)}, u32[]{:S(2)}) collective-permute-start(bf16[56,768]{1,0:T(8,128)(2,1)S(1)} %get-tuple-element.45), channel_id=1, source_target_pairs={{0,16},{8,24},{16,0},{24,8},{1,17},{9,25},{17,1},{25,9},{2,18},{10... | collective-permute-start | bytes 258056 | tf_op jit(solution)/shard_map/ppermute | solution.py:407
  16.3 2.0 %collective-permute-start.6 = (bf16[56,768]{1,0:T(8,128)(2,1)S(1)}, bf16[56,768]{1,0:T(8,128)(2,1)S(1)}, u32[]{:S(2)}, u32[]{:S(2)}) collective-permute-start(bf16[56,768]{1,0:T(8,128)(2,1)S(1)} %get-tuple-element.46), channel_id=1, source_target_pairs={{0,24},{8,16},{16,8},{24,0},{1,25},{9,17},{17,9},{25,1},{2,26},{10... | collective-permute-start | bytes 258056 | tf_op jit(solution)/shard_map/ppermute | solution.py:407
  18.3 0.0 collective-permute-done.1.refs_2_
  18.3 4.5 %collective-permute-done.2.refs_3_ = bf16[2,56,768]{2,1,0:T(8,128)(2,1)S(1)} collective-permute-done((bf16[2,56,768]{2,1,0:T(8,128)(2,1)S(1)}, bf16[2,56,768]{2,1,0:T(8,128)(2,1)S(1)}, u32[]{:S(2)}, u32[]{:S(2)}) %collective-permute-start.2) | collective-permute-done | bytes 172064 | tf_op jit(solution)/shard_map/ppermute | solution.py:407
  22.8 0.0 collective-permute-done.refs_1_
  22.8 0.1 gather.1
  22.8 0.9 %collective-permute-start.3 = (bf16[256,768]{1,0:T(8,128)(2,1)S(1)}, bf16[256,768]{1,0:T(8,128)(2,1)S(1)}, u32[]{:S(2)}, u32[]{:S(2)}) collective-permute-start(bf16[256,768]{1,0:T(8,128)(2,1)S(1)} %get-tuple-element.43.low_ref.refs_2_), channel_id=1, source_target_pairs={{1,2},{2,1},{3,4},{4,3},{5,6},{6,5},{9,10},{10,9},{11,12},{12,11},... | collective-permute-start | bytes 1179656 | tf_op jit(solution)/shard_map/ppermute | solution.py:417
  23.7 2.9 %collective-permute-start.4 = (bf16[256,768]{1,0:T(8,128)(2,1)S(1)}, bf16[256,768]{1,0:T(8,128)(2,1)S(1)}, u32[]{:S(2)}, u32[]{:S(2)}) collective-permute-start(bf16[256,768]{1,0:T(8,128)(2,1)S(1)} %get-tuple-element.44.high_ref.refs_3_), channel_id=1, source_target_pairs={{0,1},{1,0},{2,3},{3,2},{4,5},{5,4},{6,7},{7,6},{8,9},{9,8},{10,11... | collective-permute-start | bytes 1179656 | tf_op jit(solution)/shard_map/ppermute | solution.py:416
  26.6 5.8 %outer.1 = (f32[6,224,128]{2,1,0:T(8,128)S(1)}, f32[6,224,128]{2,1,0:T(8,128)S(1)}, f32[6,224,128]{2,1,0:T(8,128)S(1)}) custom-call(bf16[256,768]{1,0:T(8,128)(2,1)S(1)} %get-tuple-element.43.low_ref.refs_2_, bf16[256,768]{1,0:T(8,128)(2,1)S(1)} %get-tuple-element.44.high_ref.refs_3_, bf16[1568,224]{1,0:T(8,128)(2,1)S(1)} %tables.1.refs_2_.refs_4_.tables_ref.refs_7_.refs_5_, ...), custom_call_target="tpu_custom_call" | custom-call | flops 6600000000 | bytes 21600000 | tf_op jit(solution)/shard_map/outer/pallas_call | solution.py:30
  32.4 0.0 collective-permute-done.5.refs_2_
  32.5 0.0 collective-permute-done.6.refs_3_
  32.5 3.3 %inner.1 = (f32[6,224,128]{2,1,0:T(8,128)S(1)}, f32[6,224,128]{2,1,0:T(8,128)S(1)}, f32[6,224,128]{2,1,0:T(8,128)S(1)}, bf16[224,768]{1,0:T(8,128)(2,1)S(1)}) custom-call(bf16[3,56,768]{2,1,0:T(8,128)(2,1)S(1)} %get-tuple-element.36._.refs_0_, bf16[3,56,768]{2,1,0:T(8,128)(2,1)S(1)} %collective-permute-done.refs_1_, ...), custom_call_target="tpu_custom_call" | custom-call | flops 3300000000 | bytes 10800000 | tf_op jit(solution)/shard_map/inner/pallas_call | solution.py:30
  35.8 0.0 collective-permute-done.3.refs_0_
  35.8 0.0 collective-permute-done.4.refs_1_
  35.8 3.5 %fix.1 = (bf16[224,768]{1,0:T(8,128)(2,1)S(1)}, bf16[224,768]{1,0:T(8,128)(2,1)S(1)}, bf16[224,640]{1,0:T(8,128)(2,1)S(1)}, bf16[224,640]{1,0:T(8,128)(2,1)S(1)}...) custom-call(s32[1]{0:T(128)} %bitcast.1.turn_ref, ...), custom_call_target="tpu_custom_call" | custom-call | flops 3300000000 | bytes 10800000 | tf_op jit(solution)/shard_map/fix/pallas_call | solution.py:30
  39.3 0.9 %collective-permute-start.10 = (bf16[224,640]{1,0:T(8,128)(2,1)S(1)}, bf16[224,640]{1,0:T(8,128)(2,1)S(1)}, u32[]{:S(2)}, u32[]{:S(2)}) collective-permute-start(bf16[224,640]{1,0:T(8,128)(2,1)S(1)} %get-tuple-element.57), channel_id=1, source_target_pairs={{1,2},{2,1},{3,4},{4,3},{5,6},{6,5},{9,10},{10,9},{11,12},{12,11},... | collective-permute-start | bytes 860168 | tf_op jit(solution)/shard_map/ppermute | solution.py:417
  40.2 2.9 %collective-permute-start.11 = (bf16[224,640]{1,0:T(8,128)(2,1)S(1)}, bf16[224,640]{1,0:T(8,128)(2,1)S(1)}, u32[]{:S(2)}, u32[]{:S(2)}) collective-permute-start(bf16[224,640]{1,0:T(8,128)(2,1)S(1)} %get-tuple-element.58), channel_id=1, source_target_pairs={{0,1},{1,0},{2,3},{3,2},{4,5},{5,4},{6,7},{7,6},{8,9},{9,8},{10,11... | collective-permute-start | bytes 860168 | tf_op jit(solution)/shard_map/ppermute | solution.py:416
  43.1 6.5 %collective-permute-start.7 = (bf16[14,56,128]{2,1,0:T(8,128)(2,1)S(1)}, bf16[14,56,128]{2,1,0:T(8,128)(2,1)S(1)}, u32[]{:S(2)}, u32[]{:S(2)}) collective-permute-start(bf16[14,56,128]{2,1,0:T(8,128)(2,1)S(1)} %get-tuple-element.54), channel_id=1, source_target_pairs={{0,8},{8,0},{16,24},{24,16},{1,9},{9,1},{17,25},{25,17},{2,10},{10... | collective-permute-start | bytes 602120 | tf_op jit(solution)/shard_map/ppermute | solution.py:407
  49.6 1.0 %collective-permute-start.8 = (bf16[14,56,128]{2,1,0:T(8,128)(2,1)S(1)}, bf16[14,56,128]{2,1,0:T(8,128)(2,1)S(1)}, u32[]{:S(2)}, u32[]{:S(2)}) collective-permute-start(bf16[14,56,128]{2,1,0:T(8,128)(2,1)S(1)} %get-tuple-element.55), channel_id=1, source_target_pairs={{0,16},{8,24},{16,0},{24,8},{1,17},{9,25},{17,1},{25,9},{2,18},{10... | collective-permute-start | bytes 602120 | tf_op jit(solution)/shard_map/ppermute | solution.py:407
  50.6 1.5 %collective-permute-start.9 = (bf16[14,56,128]{2,1,0:T(8,128)(2,1)S(1)}, bf16[14,56,128]{2,1,0:T(8,128)(2,1)S(1)}, u32[]{:S(2)}, u32[]{:S(2)}) collective-permute-start(bf16[14,56,128]{2,1,0:T(8,128)(2,1)S(1)} %get-tuple-element.56), channel_id=1, source_target_pairs={{0,24},{8,16},{16,8},{24,0},{1,25},{9,17},{17,9},{25,1},{2,26},{10... | collective-permute-start | bytes 602120 | tf_op jit(solution)/shard_map/ppermute | solution.py:407
  52.1 8.1 %second.1 = (f32[6,224,128]{2,1,0:T(8,128)S(1)}, f32[6,224,128]{2,1,0:T(8,128)S(1)}, f32[6,224,128]{2,1,0:T(8,128)S(1)}) custom-call(bf16[224,768]{1,0:T(8,128)(2,1)S(1)} %get-tuple-element.59.low_ref, bf16[224,768]{1,0:T(8,128)(2,1)S(1)} %get-tuple-element.60.values_ref, bf16[224,768]{1,0:T(8,128)(2,1)S(1)} %get-tuple-element.61.high_ref, ...), custom_call_target="tpu_custom_call" | custom-call | flops 8800000000 | bytes 28800000 | tf_op jit(solution)/shard_map/second/pallas_call | solution.py:30
  60.2 0.0 collective-permute-done.10.refs_0_
  60.2 0.0 collective-permute-done.11.refs_1_
  60.2 1.5 %last.1 = (bf16[14,56,128]{2,1,0:T(8,128)(2,1)S(1)}, bf16[14,56,128]{2,1,0:T(8,128)(2,1)S(1)}, bf16[14,56,128]{2,1,0:T(8,128)(2,1)S(1)}, bf16[14,56,128]{2,1,0:T(8,128)(2,1)S(1)}) custom-call(s32[1]{0:T(128)} %bitcast.1.turn_ref, bf16[224,640]{1,0:T(8,128)(2,1)S(1)} %collective-permute-done.10.refs_0_, bf16[224,640]{1,0:T(8,128)(2,1)S(1)} %collective-permute-done.11.refs_1_, ...), custom_call_target="tpu_custom_call" | custom-call | flops 3300000000 | bytes 10800000 | tf_op jit(solution)/shard_map/last/pallas_call | solution.py:30
  61.7 1.1 %collective-permute-start.12 = (bf16[14,56,128]{2,1,0:T(8,128)(2,1)S(1)}, bf16[14,56,128]{2,1,0:T(8,128)(2,1)S(1)}, u32[]{:S(2)}, u32[]{:S(2)}) collective-permute-start(bf16[14,56,128]{2,1,0:T(8,128)(2,1)S(1)} %get-tuple-element.67), channel_id=1, source_target_pairs={{0,8},{8,0},{16,24},{24,16},{1,9},{9,1},{17,25},{25,17},{2,10},{10... | collective-permute-start | bytes 602120 | tf_op jit(solution)/shard_map/ppermute | solution.py:407
  62.8 1.9 %collective-permute-start.13 = (bf16[14,56,128]{2,1,0:T(8,128)(2,1)S(1)}, bf16[14,56,128]{2,1,0:T(8,128)(2,1)S(1)}, u32[]{:S(2)}, u32[]{:S(2)}) collective-permute-start(bf16[14,56,128]{2,1,0:T(8,128)(2,1)S(1)} %get-tuple-element.68), channel_id=1, source_target_pairs={{0,16},{8,24},{16,0},{24,8},{1,17},{9,25},{17,1},{25,9},{2,18},{10... | collective-permute-start | bytes 602120 | tf_op jit(solution)/shard_map/ppermute | solution.py:407
  64.7 0.0 collective-permute-done.7.refs_1_
  64.8 1.5 %collective-permute-start.14 = (bf16[14,56,128]{2,1,0:T(8,128)(2,1)S(1)}, bf16[14,56,128]{2,1,0:T(8,128)(2,1)S(1)}, u32[]{:S(2)}, u32[]{:S(2)}) collective-permute-start(bf16[14,56,128]{2,1,0:T(8,128)(2,1)S(1)} %get-tuple-element.69), channel_id=1, source_target_pairs={{0,24},{8,16},{16,8},{24,0},{1,25},{9,17},{17,9},{25,1},{2,26},{10... | collective-permute-start | bytes 602120 | tf_op jit(solution)/shard_map/ppermute | solution.py:407
  66.2 0.8 collective-permute-done.8.refs_2_
  67.0 0.0 collective-permute-done.9.refs_3_
  67.0 1.2 %join.2 = bf16[3,53,2304]{2,1,0:T(8,128)(2,1)} custom-call(s32[1]{0:T(128)} %bitcast.me_ref, bf16[14,56,128]{2,1,0:T(8,128)(2,1)S(1)} %get-tuple-element.53.refs_0_, bf16[14,56,128]{2,1,0:T(8,128)(2,1)S(1)} %collective-permute-done.7.refs_1_, bf16[14,56,128]{2,1,0:T(8,128)(2,1)S(1)} %collective-permute-done.8.refs_2_, ...), custom_call_target="tpu_custom_call" | custom-call | flops 1100000000 | bytes 3600000 | tf_op jit(solution)/shard_map/join/pallas_call | solution.py:30
  68.2 3.0 %collective-permute-done.12.refs_1_ = bf16[14,56,128]{2,1,0:T(8,128)(2,1)S(1)} collective-permute-done((bf16[14,56,128]{2,1,0:T(8,128)(2,1)S(1)}, bf16[14,56,128]{2,1,0:T(8,128)(2,1)S(1)}, u32[]{:S(2)}, u32[]{:S(2)}) %collective-permute-start.12) | collective-permute-done | bytes 200736 | tf_op jit(solution)/shard_map/ppermute | solution.py:407
  71.1 13.1 %collective-permute-done.13.refs_2_ = bf16[14,56,128]{2,1,0:T(8,128)(2,1)S(1)} collective-permute-done((bf16[14,56,128]{2,1,0:T(8,128)(2,1)S(1)}, bf16[14,56,128]{2,1,0:T(8,128)(2,1)S(1)}, u32[]{:S(2)}, u32[]{:S(2)}) %collective-permute-start.13) | collective-permute-done | bytes 200736 | tf_op jit(solution)/shard_map/ppermute | solution.py:407
  84.2 0.0 collective-permute-done.14.refs_3_
  84.2 1.2 %join.3 = bf16[3,53,2304]{2,1,0:T(8,128)(2,1)} custom-call(s32[1]{0:T(128)} %bitcast.me_ref, bf16[14,56,128]{2,1,0:T(8,128)(2,1)S(1)} %get-tuple-element.66.refs_0_, bf16[14,56,128]{2,1,0:T(8,128)(2,1)S(1)} %collective-permute-done.12.refs_1_, bf16[14,56,128]{2,1,0:T(8,128)(2,1)S(1)} %collective-permute-done.13.refs_2_, ...), custom_call_target="tpu_custom_call" | custom-call | flops 1100000000 | bytes 3600000 | tf_op jit(solution)/shard_map/join/pallas_call | solution.py:30
  (17 shorter events, 0.2 us)
Async XLA Ops:
  0.6 8.1 %copy-start.5 = (f32[1218]{0:T(1024)S(1)}, f32[1218]{0:T(1024)}, u32[]{:S(2)}) copy-start(f32[1218]{0:T(1024)} %param.9) | copy-start | bytes 14620
  0.6 8.1 %copy-start.2 = (s32[210]{0:T(256)S(1)}, s32[210]{0:T(256)}, u32[]{:S(2)}) copy-start(s32[210]{0:T(256)} %param.11) | copy-start | bytes 2524
  0.7 1.1 %copy-start = (bf16[53,3,2304]{2,0,1:T(8,128)(2,1)S(1)}, bf16[53,3,2304]{2,0,1:T(8,128)(2,1)}, u32[]{:S(2)}) copy-start(bf16[53,3,2304]{2,0,1:T(8,128)(2,1)} %param.6) | copy-start | bytes 2198020
  1.8 6.6 %copy-start.3 = (f32[6,3,2304]{2,1,0:T(4,128)S(1)}, f32[6,3,2304]{2,1,0:T(4,128)}, u32[]{:S(2)}) copy-start(f32[6,3,2304]{2,1,0:T(4,128)} %param.8) | copy-start | bytes 497668
  1.8 6.6 %copy-start.4 = (f32[3,2304]{1,0:T(4,128)S(1)}, f32[3,2304]{1,0:T(4,128)}, u32[]{:S(2)}) copy-start(f32[3,2304]{1,0:T(4,128)} %param.7) | copy-start | bytes 82948
  1.8 7.0 %copy-start.1 = (s32[1218,3]{0,1:T(4,128)S(1)}, s32[1218,3]{0,1:T(4,128)}, u32[]{:S(2)}) copy-start(s32[1218,3]{0,1:T(4,128)} %param.10) | copy-start | bytes 43852
  2.6 20.1 %collective-permute-start = (bf16[3,56,768]{2,1,0:T(8,128)(2,1)S(1)}, bf16[3,56,768]{2,1,0:T(8,128)(2,1)S(1)}, u32[]{:S(2)}, u32[]{:S(2)}) collective-permute-start(bf16[3,56,768]{2,1,0:T(8,128)(2,1)S(1)} %get-tuple-element.37), channel_id=1, source_target_pairs={{0,8},{8,0},{16,24},{24,16},{1,9},{9,1},{17,25},{25,17},{2,10},{10... | collective-permute-start | bytes 774152 | tf_op jit(solution)/shard_map/ppermute | solution.py:407
  5.7 12.5 %collective-permute-start.1 = (bf16[2,56,768]{2,1,0:T(8,128)(2,1)S(1)}, bf16[2,56,768]{2,1,0:T(8,128)(2,1)S(1)}, u32[]{:S(2)}, u32[]{:S(2)}) collective-permute-start(bf16[2,56,768]{2,1,0:T(8,128)(2,1)S(1)} %get-tuple-element.38), channel_id=1, source_target_pairs={{0,16},{8,24},{16,0},{24,8},{1,17},{9,25},{17,1},{25,9},{2,18},{10... | collective-permute-start | bytes 516104 | tf_op jit(solution)/shard_map/ppermute | solution.py:407
  8.3 14.4 %collective-permute-start.2 = (bf16[2,56,768]{2,1,0:T(8,128)(2,1)S(1)}, bf16[2,56,768]{2,1,0:T(8,128)(2,1)S(1)}, u32[]{:S(2)}, u32[]{:S(2)}) collective-permute-start(bf16[2,56,768]{2,1,0:T(8,128)(2,1)S(1)} %get-tuple-element.39), channel_id=1, source_target_pairs={{0,24},{8,16},{16,8},{24,0},{1,25},{9,17},{17,9},{25,1},{2,26},{10... | collective-permute-start | bytes 516104 | tf_op jit(solution)/shard_map/ppermute | solution.py:407
  14.3 18.2 %collective-permute-start.5 = (bf16[56,768]{1,0:T(8,128)(2,1)S(1)}, bf16[56,768]{1,0:T(8,128)(2,1)S(1)}, u32[]{:S(2)}, u32[]{:S(2)}) collective-permute-start(bf16[56,768]{1,0:T(8,128)(2,1)S(1)} %get-tuple-element.45), channel_id=1, source_target_pairs={{0,16},{8,24},{16,0},{24,8},{1,17},{9,25},{17,1},{25,9},{2,18},{10... | collective-permute-start | bytes 258056 | tf_op jit(solution)/shard_map/ppermute | solution.py:407
  16.3 16.2 %collective-permute-start.6 = (bf16[56,768]{1,0:T(8,128)(2,1)S(1)}, bf16[56,768]{1,0:T(8,128)(2,1)S(1)}, u32[]{:S(2)}, u32[]{:S(2)}) collective-permute-start(bf16[56,768]{1,0:T(8,128)(2,1)S(1)} %get-tuple-element.46), channel_id=1, source_target_pairs={{0,24},{8,16},{16,8},{24,0},{1,25},{9,17},{17,9},{25,1},{2,26},{10... | collective-permute-start | bytes 258056 | tf_op jit(solution)/shard_map/ppermute | solution.py:407
  22.8 12.9 %collective-permute-start.3 = (bf16[256,768]{1,0:T(8,128)(2,1)S(1)}, bf16[256,768]{1,0:T(8,128)(2,1)S(1)}, u32[]{:S(2)}, u32[]{:S(2)}) collective-permute-start(bf16[256,768]{1,0:T(8,128)(2,1)S(1)} %get-tuple-element.43.low_ref.refs_2_), channel_id=1, source_target_pairs={{1,2},{2,1},{3,4},{4,3},{5,6},{6,5},{9,10},{10,9},{11,12},{12,11},... | collective-permute-start | bytes 1179656 | tf_op jit(solution)/shard_map/ppermute | solution.py:417
  23.7 12.1 %collective-permute-start.4 = (bf16[256,768]{1,0:T(8,128)(2,1)S(1)}, bf16[256,768]{1,0:T(8,128)(2,1)S(1)}, u32[]{:S(2)}, u32[]{:S(2)}) collective-permute-start(bf16[256,768]{1,0:T(8,128)(2,1)S(1)} %get-tuple-element.44.high_ref.refs_3_), channel_id=1, source_target_pairs={{0,1},{1,0},{2,3},{3,2},{4,5},{5,4},{6,7},{7,6},{8,9},{9,8},{10,11... | collective-permute-start | bytes 1179656 | tf_op jit(solution)/shard_map/ppermute | solution.py:416
  39.3 20.9 %collective-permute-start.10 = (bf16[224,640]{1,0:T(8,128)(2,1)S(1)}, bf16[224,640]{1,0:T(8,128)(2,1)S(1)}, u32[]{:S(2)}, u32[]{:S(2)}) collective-permute-start(bf16[224,640]{1,0:T(8,128)(2,1)S(1)} %get-tuple-element.57), channel_id=1, source_target_pairs={{1,2},{2,1},{3,4},{4,3},{5,6},{6,5},{9,10},{10,9},{11,12},{12,11},... | collective-permute-start | bytes 860168 | tf_op jit(solution)/shard_map/ppermute | solution.py:417
  40.2 20.0 %collective-permute-start.11 = (bf16[224,640]{1,0:T(8,128)(2,1)S(1)}, bf16[224,640]{1,0:T(8,128)(2,1)S(1)}, u32[]{:S(2)}, u32[]{:S(2)}) collective-permute-start(bf16[224,640]{1,0:T(8,128)(2,1)S(1)} %get-tuple-element.58), channel_id=1, source_target_pairs={{0,1},{1,0},{2,3},{3,2},{4,5},{5,4},{6,7},{7,6},{8,9},{9,8},{10,11... | collective-permute-start | bytes 860168 | tf_op jit(solution)/shard_map/ppermute | solution.py:416
  43.1 21.6 %collective-permute-start.7 = (bf16[14,56,128]{2,1,0:T(8,128)(2,1)S(1)}, bf16[14,56,128]{2,1,0:T(8,128)(2,1)S(1)}, u32[]{:S(2)}, u32[]{:S(2)}) collective-permute-start(bf16[14,56,128]{2,1,0:T(8,128)(2,1)S(1)} %get-tuple-element.54), channel_id=1, source_target_pairs={{0,8},{8,0},{16,24},{24,16},{1,9},{9,1},{17,25},{25,17},{2,10},{10... | collective-permute-start | bytes 602120 | tf_op jit(solution)/shard_map/ppermute | solution.py:407
  49.6 17.4 %collective-permute-start.8 = (bf16[14,56,128]{2,1,0:T(8,128)(2,1)S(1)}, bf16[14,56,128]{2,1,0:T(8,128)(2,1)S(1)}, u32[]{:S(2)}, u32[]{:S(2)}) collective-permute-start(bf16[14,56,128]{2,1,0:T(8,128)(2,1)S(1)} %get-tuple-element.55), channel_id=1, source_target_pairs={{0,16},{8,24},{16,0},{24,8},{1,17},{9,25},{17,1},{25,9},{2,18},{10... | collective-permute-start | bytes 602120 | tf_op jit(solution)/shard_map/ppermute | solution.py:407
  50.6 16.4 %collective-permute-start.9 = (bf16[14,56,128]{2,1,0:T(8,128)(2,1)S(1)}, bf16[14,56,128]{2,1,0:T(8,128)(2,1)S(1)}, u32[]{:S(2)}, u32[]{:S(2)}) collective-permute-start(bf16[14,56,128]{2,1,0:T(8,128)(2,1)S(1)} %get-tuple-element.56), channel_id=1, source_target_pairs={{0,24},{8,16},{16,8},{24,0},{1,25},{9,17},{17,9},{25,1},{2,26},{10... | collective-permute-start | bytes 602120 | tf_op jit(solution)/shard_map/ppermute | solution.py:407
  61.7 9.4 %collective-permute-start.12 = (bf16[14,56,128]{2,1,0:T(8,128)(2,1)S(1)}, bf16[14,56,128]{2,1,0:T(8,128)(2,1)S(1)}, u32[]{:S(2)}, u32[]{:S(2)}) collective-permute-start(bf16[14,56,128]{2,1,0:T(8,128)(2,1)S(1)} %get-tuple-element.67), channel_id=1, source_target_pairs={{0,8},{8,0},{16,24},{24,16},{1,9},{9,1},{17,25},{25,17},{2,10},{10... | collective-permute-start | bytes 602120 | tf_op jit(solution)/shard_map/ppermute | solution.py:407
  62.8 21.3 %collective-permute-start.13 = (bf16[14,56,128]{2,1,0:T(8,128)(2,1)S(1)}, bf16[14,56,128]{2,1,0:T(8,128)(2,1)S(1)}, u32[]{:S(2)}, u32[]{:S(2)}) collective-permute-start(bf16[14,56,128]{2,1,0:T(8,128)(2,1)S(1)} %get-tuple-element.68), channel_id=1, source_target_pairs={{0,16},{8,24},{16,0},{24,8},{1,17},{9,25},{17,1},{25,9},{2,18},{10... | collective-permute-start | bytes 602120 | tf_op jit(solution)/shard_map/ppermute | solution.py:407
  64.8 19.4 %collective-permute-start.14 = (bf16[14,56,128]{2,1,0:T(8,128)(2,1)S(1)}, bf16[14,56,128]{2,1,0:T(8,128)(2,1)S(1)}, u32[]{:S(2)}, u32[]{:S(2)}) collective-permute-start(bf16[14,56,128]{2,1,0:T(8,128)(2,1)S(1)} %get-tuple-element.69), channel_id=1, source_target_pairs={{0,24},{8,16},{16,8},{24,0},{1,25},{9,17},{17,9},{25,1},{2,26},{10... | collective-permute-start | bytes 602120 | tf_op jit(solution)/shard_map/ppermute | solution.py:407

commit v7 on v6

--- a/solution.py
+++ b/solution.py
@@ -127,8 +127,8 @@
 
 
 def weights_kernel(conduct_ref, masks_ref, *refs):
-    out_ref = refs[-1 - (len(refs) - 2) // 2]
-    passed, passed_out = refs[: (len(refs) - 2) // 2], refs[len(refs) - (len(refs) - 2) // 2 :]
+    number = (len(refs) - 3) // 2
+    passed, out_ref, passed_out = refs[:number], refs[number + 2], refs[number + 3 :]
     for in_ref, to_ref in zip(passed, passed_out):
         to_ref[...] = in_ref[...]
     planes, _, _, tiles = out_ref.shape[:4]
@@ -276,27 +276,61 @@
         out_ref[:, tile * LANES : (tile + 1) * LANES] = (result[tile] * inside).astype(BF16)
 
 
-def packing(planes, chunk):
-    full, odd = divmod(chunk, LANES)
-    beside = LANES // odd if odd else 0
-    return full, odd, beside, planes * full + (-(-planes // beside) if odd else 0)
-
-
-def emit(results, chunk, piece_refs):
-    full, odd, beside, _ = packing(len(results), chunk)
-    padded = piece_refs[0].shape[1]
+class Packing:
+    def __init__(self, planes, chunk, own):
+        self.planes, self.own, self.padded = planes, own, up(own, 8)
+        self.full, self.odd = divmod(chunk, LANES)
+        self.beside = LANES // self.odd if self.odd else 1
+        last = planes % self.beside * self.odd if self.odd else 0
+        images = planes * self.full + (-(-planes // self.beside) if self.odd else 0)
+        self.fold = up(-(-self.padded // 2), 8) if 0 < last <= LANES // 2 else 0
+        self.plain = images - 1 if self.fold else images
+        self.main = own // 8 * 8
+        self.rest = own - self.main
+        self.folded = self.plain * self.main
+        self.later = self.folded + self.fold
+        self.rows = up(self.later + self.plain * self.rest + 8, 16)
+
+
+def emit(results, packing, line, piece_refs):
+    full, odd, beside, padded = packing.full, packing.odd, packing.beside, packing.padded
     lane = lax.broadcasted_iota(jnp.int32, (padded, LANES), 1)
+    line[...] = jnp.zeros_like(line)
     for step, piece_ref in enumerate(piece_refs):
         here = slice(step * padded, (step + 1) * padded)
-        for plane, result in enumerate(results):
-            for tile in range(full):
-                piece_ref[plane * full + tile] = result[tile, here, :].astype(BF16)
-        for first in range(0, len(results) if odd else 0, beside or 1):
+        images = [result[tile, here, :] for result in results for tile in range(full)]
+        for first in range(0, len(results) if odd else 0, beside):
             packed = results[first][full, here, :]
-            for place in range(1, min(beside, len(results) - first)):
-                turned = pltpu.roll(results[first + place][full, here, :], place * odd, 1)
-                packed = jnp.where(lane < place * odd, packed, turned)
-            piece_ref[len(results) * full + first // beside] = packed.astype(BF16)
+            for spot in range(1, min(beside, len(results) - first)):
+                turned = pltpu.roll(results[first + spot][full, here, :], spot * odd, 1)
+                packed = jnp.where(lane < spot * odd, packed, turned)
+            images.append(packed)
+        if packing.fold:
+            image = images.pop()
+            later = pltpu.roll(image[padded - packing.fold :], LANES // 2, 1)
+            block = jnp.where(lane[: packing.fold] < LANES // 2, image[: packing.fold], later)
+            line[packing.folded : packing.later, :] = block
+        for index, image in enumerate(images):
+            line[index * packing.main : (index + 1) * packing.main, :] = image[: packing.main]
+            if packing.rest:
+                place = packing.later + index * packing.rest
+                line[place : place + packing.rest, :] = image[packing.main : packing.own]
+        piece_ref[...] = line[...].astype(BF16)
+
+
+def images_of(held, packing):
+    images = []
+    for index in range(packing.plain):
+        image = held[index * packing.main : (index + 1) * packing.main, :]
+        if packing.rest:
+            place = packing.later + index * packing.rest
+            image = jnp.concatenate([image, held[place : place + 8, :]], axis=0)
+        images.append(image)
+    if packing.fold:
+        block = held[packing.folded : packing.later, :]
+        later = pltpu.roll(block, LANES // 2, 1)[2 * packing.fold - packing.padded :]
+        images.append(jnp.concatenate([block, later], axis=0))
+    return images
 
 
 def outer_kernel(low_ref, high_ref, tables_ref, weights_ref, masks_ref, *outs):
@@ -321,11 +355,11 @@
     inner(values_ref[...], low, high, middle, *shared, low_out, high_out, middle_out, mixed, sums, tiles)
 
 
-def first_fix_kernel(count, chunk, turn_ref, *refs):
+def first_fix_kernel(packing, turn_ref, *refs):
     halo_refs, own_refs, share_refs, (middle_in, tables_ref, masks_ref), refs = (
         refs[0:2], refs[2:4], refs[4:6], refs[6:9], refs[9:]
     )
-    wholes, nears, faces_ref, pieces, (mixed, sums, ends) = refs[:2], refs[2:4], refs[4], refs[5:-3], refs[-3:]
+    wholes, nears, faces_ref, pieces, (mixed, sums, ends, line) = refs[:2], refs[2:4], refs[4], refs[5:-4], refs[-4:]
     rows, (_, fields, tiles, _, _) = tables_ref.shape[1], faces_ref.shape
     for side in range(2):
         coefficient = 0.0
@@ -348,12 +382,12 @@
             result[tile] = SCALE * (share_refs[side][tile] + sums[0, tile])
         fill(result, masks_ref, wholes[side])
         nears[side][...] = wholes[side][:, : nears[side].shape[1]]
-    emit((ends.at[0], middle_in, ends.at[1]), chunk, pieces)
-
-
-def last_fix_kernel(count, chunk, turn_ref, *refs):
+    emit((ends.at[0], middle_in, ends.at[1]), packing, line, pieces)
+
+
+def last_fix_kernel(packing, turn_ref, *refs):
     halo_refs, share_refs, (middle_in, tables_ref, faces_ref), refs = refs[0:2], refs[2:4], refs[4:7], refs[7:]
-    pieces, (mixed, sums, ends) = refs[:-3], refs[-3:]
+    pieces, (mixed, sums, ends, line) = refs[:-4], refs[-4:]
     fields, tiles = faces_ref.shape[1], sums.shape[1]
     for side in range(2):
         mix(tables_ref, halo_refs[side][...], mixed.at[side])
@@ -368,24 +402,24 @@
         result = ends.at[lax.bitwise_xor(turn_ref[0], side)]
         for tile in range(tiles):
             result[tile] = SCALE * (share_refs[side][tile] - sums[0, tile])
-    emit((ends.at[0], middle_in, ends.at[1]), chunk, pieces)
-
-
-def join_kernel(count, chunk, me_ref, *refs):
+    emit((ends.at[0], middle_in, ends.at[1]), packing, line, pieces)
+
+
+def join_kernel(count, packing, me_ref, *refs):
     piece_refs, (out_ref, held) = refs[:count], refs[count:]
-    planes, own, _ = out_ref.shape
-    full, odd, beside, _ = packing(planes, chunk)
+    full, odd, beside = packing.full, packing.odd, packing.beside
     me = me_ref[0]
     for step in range(count):
         held[lax.bitwise_xor(me, step)] = piece_refs[step][...].astype(F32)
-    for plane in range(planes):
+    pieces = [images_of(held.at[source], packing) for source in range(count)]
+    for plane in range(packing.planes):
         parts = []
-        for source in range(count):
-            parts += [held[source, plane * full + tile] for tile in range(full)]
+        for images in pieces:
+            parts += images[plane * full : (plane + 1) * full]
             if odd:
-                tile, spot = planes * full + plane // beside, plane % beside
-                parts.append(held[source, tile][:, spot * odd : (spot + 1) * odd])
-        out_ref[plane] = jnp.concatenate(parts, axis=1)[:own].astype(BF16)
+                spot = plane % beside
+                parts.append(images[packing.planes * full + plane // beside][:, spot * odd : (spot + 1) * odd])
+        out_ref[plane] = jnp.concatenate(parts, axis=1)[: packing.own].astype(BF16)
 
 
 def shards(panels, mean_field, fluctuations, products, triples, owner_slot):
@@ -461,15 +495,17 @@
         "weights",
         0.5,
         [shape(planes, 6, fields, tiles, 8, LANES, dtype=F32)] + [shape(padded, width)] * (count - joint),
-        (conduct, masks, *cut[count:], tables),
-        unread=1,
+        (conduct, masks, *cut[count:], tables, parts[-1] if count <= joint else parts[joint]),
+        unread=2,
     )
     middles = parts[:joint] + [exchange(middles[step - joint], step) for step in range(joint, count)]
 
     common = (tables, weights, masks)
     plane_whole = shape(rows, width)
     share = shape(tiles, rows, LANES, dtype=F32)
-    pieces = [shape(packing(planes, chunk)[-1], padded, LANES)] * count
+    packing = Packing(planes, chunk, own)
+    pieces = [shape(packing.rows, LANES)] * count
+    line = VMEM((packing.rows, LANES), F32)
     near_tiles = near // LANES
 
     def scratch(tiles, kinds=7):
@@ -496,7 +532,7 @@
         scratch(tiles),
     )
     low, high, low_near, high_near, faces, *sent = call(
-        functools.partial(first_fix_kernel, count, chunk),
+        functools.partial(first_fix_kernel, packing),
         "fix",
         3,
         [plane_whole] * 2
@@ -504,7 +540,7 @@
         + [shape(2, fields, tiles, 8, LANES, dtype=F32)]
         + pieces,
         (turn_alone, *halos, *edges, low, high, middle, tables, masks),
-        scratch(tiles, 1) + [VMEM((2, tiles, rows, LANES), F32)],
+        scratch(tiles, 1) + [VMEM((2, tiles, rows, LANES), F32), line],
         scalars=1,
     )
     sent = exchanged(sent)
@@ -518,19 +554,19 @@
         scratch(tiles) + [VMEM((tiles, rows, LANES), F32)] * 3,
     )
     second = call(
-        functools.partial(last_fix_kernel, count, chunk),
+        functools.partial(last_fix_kernel, packing),
         "last",
         3,
         pieces,
         (turn_alone, *halos, low, high, middle, tables, faces),
-        scratch(near_tiles, 1) + [VMEM((2, near_tiles, rows, LANES), F32)],
+        scratch(near_tiles, 1) + [VMEM((2, near_tiles, rows, LANES), F32), line],
         scalars=1,
     )
     second = exchanged(second)
 
     def join(parts):
         (result,) = call(
-            functools.partial(join_kernel, count, chunk),
+            functools.partial(join_kernel, count, packing),
             "join",
             1,
             [shape(planes, own, cells)],

time: 86.6 us -> 83.6 us (0.965)
  starting transfers between devices: 30.6 us -> 28.1 us
  waiting for transfers between devices: 21.3 us -> 20.2 us
    ppermute x11, starting transfers between devices: 23 us -> 20.6 us  [exchange(): return lax.ppermute(block, 'chaos', [(i, i ^ step) for i in range(count)])]
    ppermute x11, waiting for transfers between devices: 21.3 us -> 20.2 us  [exchange(): return lax.ppermute(block, 'chaos', [(i, i ^ step) for i in range(count)])]
  transfers between devices with their start and end apart: 15 -> 15, of which waited for: 4 -> 4; matrix products, arithmetic and copies ran while one was open for 1% -> 1% of each run, Pallas kernels for 30% -> 31%
where the time goes in v7:
time: 83.6 us; the launch traced here: 82 us
  Pallas kernels  31.1 us (37%)
  starting transfers between devices  28.1 us (34%)
  waiting for transfers between devices  20.2 us (24%)
  local copies, waits for them, and re-layouts  1.4 us (2%)
  between operations  0.91 us (1%)
    pallas_call x11, Pallas kernels, call(): pl.pallas_call(kernel, out_shape=out_shape, in_specs=in_specs, out_specs=...  31.1 us
    ppermute x11, starting transfers between devices, exchange(): return lax.ppermute(block, 'chaos', [(i, i ^ step) for i in range(count)])  20.6 us
    ppermute x11, waiting for transfers between devices, exchange(): return lax.ppermute(block, 'chaos', [(i, i ^ step) for i in range(count)])  20.2 us
    ppermute x2, starting transfers between devices, neighbours(): after = lax.ppermute(last_plane, 'space', pairs)  5.8 us
    ppermute x2, starting transfers between devices, neighbours(): return (lax.ppermute(first_plane, 'space', others), after)  1.77 us
  transfers between devices with their start and end apart: 15, of which 4 were waited for; matrix products, arithmetic and copies ran while one was open for 1% of the time, Pallas kernels for 31%

profile of v7, /device:TPU:0, one launch (start us, length us, event | category | flops | bytes accessed | tf_op | source)
XLA Modules:
  0.0 82.0 jit_solution(14167500609593113713)
XLA Ops:
  0.7 0.0 copy-start
  0.7 1.1 %copy-done = bf16[53,3,2304]{2,0,1:T(8,128)(2,1)S(1)} copy-done((bf16[53,3,2304]{2,0,1:T(8,128)(2,1)S(1)}, bf16[53,3,2304]{2,0,1:T(8,128)(2,1)}, u32[]{:S(2)}) %copy-start) | copy-done | bytes 732696
  1.8 0.8 %cut.1 = (bf16[3,56,768]{2,1,0:T(8,128)(2,1)S(1)}, bf16[3,56,768]{2,1,0:T(8,128)(2,1)S(1)}, bf16[2,56,768]{2,1,0:T(8,128)(2,1)S(1)}, bf16[2,56,768]{2,1,0:T(8,12...) custom-call(s32[1]{0:T(128)} %bitcast.me_ref, bf16[3,53,2304]{2,1,0:T(8,128)(2,1)S(1)} %bitcast.10), custom_call_target="tpu_custom_call" | custom-call | flops 1100000000 | bytes 3600000 | tf_op jit(solution)/shard_map/cut/pallas_call | solution.py:30
  2.6 4.1 %collective-permute-start.1 = (bf16[2,56,768]{2,1,0:T(8,128)(2,1)S(1)}, bf16[2,56,768]{2,1,0:T(8,128)(2,1)S(1)}, u32[]{:S(2)}, u32[]{:S(2)}) collective-permute-start(bf16[2,56,768]{2,1,0:T(8,128)(2,1)S(1)} %get-tuple-element.38), channel_id=1, source_target_pairs={{0,16},{8,24},{16,0},{24,8},{1,17},{9,25},{17,1},{25,9},{2,18},{10... | collective-permute-start | bytes 516104 | tf_op jit(solution)/shard_map/ppermute | solution.py:441
  6.7 1.6 %collective-permute-start = (bf16[3,56,768]{2,1,0:T(8,128)(2,1)S(1)}, bf16[3,56,768]{2,1,0:T(8,128)(2,1)S(1)}, u32[]{:S(2)}, u32[]{:S(2)}) collective-permute-start(bf16[3,56,768]{2,1,0:T(8,128)(2,1)S(1)} %get-tuple-element.37), channel_id=1, source_target_pairs={{0,8},{8,0},{16,24},{24,16},{1,9},{9,1},{17,25},{25,17},{2,10},{10... | collective-permute-start | bytes 774152 | tf_op jit(solution)/shard_map/ppermute | solution.py:441
  8.3 0.0 collective-permute-start.2
  8.4 0.0 copy-done.4
  8.5 0.1 pad_maximum_fusion
  8.5 0.1 pad_dynamic-slice_fusion.1
  8.6 0.1 pad_dynamic-slice_fusion
  8.8 5.1 %tables.1.refs_2_.refs_4_.tables_ref.refs_7_.refs_5_ = bf16[1568,224]{1,0:T(8,128)(2,1)S(1)} custom-call(s32[1]{0:T(128)} %bitcast.me_ref, s32[3,1218]{1,0:T(4,128)S(1)} %bitcast.11, f32[1,1218]{1,0:T(1,128)S(1)} %broadcast_in_dim.15.products_ref, s32[1,210]{1,0:T(1,128)S(1)} %bitcast.12, bf16[3,56,768]{2,1,0:T(8,128)(2,1)S(1)} %get-tuple-element.36._.refs_0_), custom_call_target="tpu_custom_call" | custom-call | flops 5500000256 | bytes 18000000 | tf_op jit(solution)/shard_map/tables/pallas_call | solution.py:30
  14.0 0.1 pad_maximum_fusion.1.conduct_ref
  14.0 1.6 %collective-permute-done.1.refs_3_.refs_2_ = bf16[2,56,768]{2,1,0:T(8,128)(2,1)S(1)} collective-permute-done((bf16[2,56,768]{2,1,0:T(8,128)(2,1)S(1)}, bf16[2,56,768]{2,1,0:T(8,128)(2,1)S(1)}, u32[]{:S(2)}, u32[]{:S(2)}) %collective-permute-start.1) | collective-permute-done | bytes 172064 | tf_op jit(solution)/shard_map/ppermute | solution.py:441
  15.6 0.2 weights.1
  15.9 0.4 collective-permute-start.5
  16.3 2.6 %collective-permute-start.6 = (bf16[56,768]{1,0:T(8,128)(2,1)S(1)}, bf16[56,768]{1,0:T(8,128)(2,1)S(1)}, u32[]{:S(2)}, u32[]{:S(2)}) collective-permute-start(bf16[56,768]{1,0:T(8,128)(2,1)S(1)} %get-tuple-element.46), channel_id=1, source_target_pairs={{0,24},{8,16},{16,8},{24,0},{1,25},{9,17},{17,9},{25,1},{2,26},{10... | collective-permute-start | bytes 258056 | tf_op jit(solution)/shard_map/ppermute | solution.py:441
  18.9 3.8 %collective-permute-done.2.refs_3_ = bf16[2,56,768]{2,1,0:T(8,128)(2,1)S(1)} collective-permute-done((bf16[2,56,768]{2,1,0:T(8,128)(2,1)S(1)}, bf16[2,56,768]{2,1,0:T(8,128)(2,1)S(1)}, u32[]{:S(2)}, u32[]{:S(2)}) %collective-permute-start.2) | collective-permute-done | bytes 172064 | tf_op jit(solution)/shard_map/ppermute | solution.py:441
  22.6 0.0 collective-permute-done.refs_1_
  22.7 0.1 gather.1
  22.7 0.9 %collective-permute-start.3 = (bf16[256,768]{1,0:T(8,128)(2,1)S(1)}, bf16[256,768]{1,0:T(8,128)(2,1)S(1)}, u32[]{:S(2)}, u32[]{:S(2)}) collective-permute-start(bf16[256,768]{1,0:T(8,128)(2,1)S(1)} %get-tuple-element.43.low_ref.refs_2_), channel_id=1, source_target_pairs={{1,2},{2,1},{3,4},{4,3},{5,6},{6,5},{9,10},{10,9},{11,12},{12,11},... | collective-permute-start | bytes 1179656 | tf_op jit(solution)/shard_map/ppermute | solution.py:451
  23.6 2.9 %collective-permute-start.4 = (bf16[256,768]{1,0:T(8,128)(2,1)S(1)}, bf16[256,768]{1,0:T(8,128)(2,1)S(1)}, u32[]{:S(2)}, u32[]{:S(2)}) collective-permute-start(bf16[256,768]{1,0:T(8,128)(2,1)S(1)} %get-tuple-element.44.high_ref.refs_3_), channel_id=1, source_target_pairs={{0,1},{1,0},{2,3},{3,2},{4,5},{5,4},{6,7},{7,6},{8,9},{9,8},{10,11... | collective-permute-start | bytes 1179656 | tf_op jit(solution)/shard_map/ppermute | solution.py:450
  26.5 5.8 %outer.1 = (f32[6,224,128]{2,1,0:T(8,128)S(1)}, f32[6,224,128]{2,1,0:T(8,128)S(1)}, f32[6,224,128]{2,1,0:T(8,128)S(1)}) custom-call(bf16[256,768]{1,0:T(8,128)(2,1)S(1)} %get-tuple-element.43.low_ref.refs_2_, bf16[256,768]{1,0:T(8,128)(2,1)S(1)} %get-tuple-element.44.high_ref.refs_3_, bf16[1568,224]{1,0:T(8,128)(2,1)S(1)} %tables.1.refs_2_.refs_4_.tables_ref.refs_7_.refs_5_, ...), custom_call_target="tpu_custom_call" | custom-call | flops 6600000000 | bytes 21600000 | tf_op jit(solution)/shard_map/outer/pallas_call | solution.py:30
  32.3 0.0 collective-permute-done.5.refs_2_
  32.3 0.0 collective-permute-done.6.refs_3_
  32.4 3.3 %inner.1 = (f32[6,224,128]{2,1,0:T(8,128)S(1)}, f32[6,224,128]{2,1,0:T(8,128)S(1)}, f32[6,224,128]{2,1,0:T(8,128)S(1)}, bf16[224,768]{1,0:T(8,128)(2,1)S(1)}) custom-call(bf16[3,56,768]{2,1,0:T(8,128)(2,1)S(1)} %get-tuple-element.36._.refs_0_, bf16[3,56,768]{2,1,0:T(8,128)(2,1)S(1)} %collective-permute-done.refs_1_, ...), custom_call_target="tpu_custom_call" | custom-call | flops 3300000000 | bytes 10800000 | tf_op jit(solution)/shard_map/inner/pallas_call | solution.py:30
  35.7 0.0 collective-permute-done.3.refs_0_
  35.7 0.0 collective-permute-done.4.refs_1_
  35.7 3.6 %fix.1 = (bf16[224,768]{1,0:T(8,128)(2,1)S(1)}, bf16[224,768]{1,0:T(8,128)(2,1)S(1)}, bf16[224,640]{1,0:T(8,128)(2,1)S(1)}, bf16[224,640]{1,0:T(8,128)(2,1)S(1)}...) custom-call(s32[1]{0:T(128)} %bitcast.1.turn_ref, ...), custom_call_target="tpu_custom_call" | custom-call | flops 3300000000 | bytes 10800000 | tf_op jit(solution)/shard_map/fix/pallas_call | solution.py:30
  39.3 0.9 %collective-permute-start.10 = (bf16[224,640]{1,0:T(8,128)(2,1)S(1)}, bf16[224,640]{1,0:T(8,128)(2,1)S(1)}, u32[]{:S(2)}, u32[]{:S(2)}) collective-permute-start(bf16[224,640]{1,0:T(8,128)(2,1)S(1)} %get-tuple-element.57), channel_id=1, source_target_pairs={{1,2},{2,1},{3,4},{4,3},{5,6},{6,5},{9,10},{10,9},{11,12},{12,11},... | collective-permute-start | bytes 860168 | tf_op jit(solution)/shard_map/ppermute | solution.py:451
  40.2 2.9 %collective-permute-start.11 = (bf16[224,640]{1,0:T(8,128)(2,1)S(1)}, bf16[224,640]{1,0:T(8,128)(2,1)S(1)}, u32[]{:S(2)}, u32[]{:S(2)}) collective-permute-start(bf16[224,640]{1,0:T(8,128)(2,1)S(1)} %get-tuple-element.58), channel_id=1, source_target_pairs={{0,1},{1,0},{2,3},{3,2},{4,5},{5,4},{6,7},{7,6},{8,9},{9,8},{10,11... | collective-permute-start | bytes 860168 | tf_op jit(solution)/shard_map/ppermute | solution.py:450
  43.1 5.0 %collective-permute-start.7 = (bf16[736,128]{1,0:T(8,128)(2,1)S(1)}, bf16[736,128]{1,0:T(8,128)(2,1)S(1)}, u32[]{:S(2)}, u32[]{:S(2)}) collective-permute-start(bf16[736,128]{1,0:T(8,128)(2,1)S(1)} %get-tuple-element.54), channel_id=1, source_target_pairs={{0,8},{8,0},{16,24},{24,16},{1,9},{9,1},{17,25},{25,17},{2,10},{10... | collective-permute-start | bytes 565256 | tf_op jit(solution)/shard_map/ppermute | solution.py:441
  48.0 1.0 %collective-permute-start.8 = (bf16[736,128]{1,0:T(8,128)(2,1)S(1)}, bf16[736,128]{1,0:T(8,128)(2,1)S(1)}, u32[]{:S(2)}, u32[]{:S(2)}) collective-permute-start(bf16[736,128]{1,0:T(8,128)(2,1)S(1)} %get-tuple-element.55), channel_id=1, source_target_pairs={{0,16},{8,24},{16,0},{24,8},{1,17},{9,25},{17,1},{25,9},{2,18},{10... | collective-permute-start | bytes 565256 | tf_op jit(solution)/shard_map/ppermute | solution.py:441
  49.1 1.5 %collective-permute-start.9 = (bf16[736,128]{1,0:T(8,128)(2,1)S(1)}, bf16[736,128]{1,0:T(8,128)(2,1)S(1)}, u32[]{:S(2)}, u32[]{:S(2)}) collective-permute-start(bf16[736,128]{1,0:T(8,128)(2,1)S(1)} %get-tuple-element.56), channel_id=1, source_target_pairs={{0,24},{8,16},{16,8},{24,0},{1,25},{9,17},{17,9},{25,1},{2,26},{10... | collective-permute-start | bytes 565256 | tf_op jit(solution)/shard_map/ppermute | solution.py:441
  50.5 8.1 %second.1 = (f32[6,224,128]{2,1,0:T(8,128)S(1)}, f32[6,224,128]{2,1,0:T(8,128)S(1)}, f32[6,224,128]{2,1,0:T(8,128)S(1)}) custom-call(bf16[224,768]{1,0:T(8,128)(2,1)S(1)} %get-tuple-element.59.low_ref, bf16[224,768]{1,0:T(8,128)(2,1)S(1)} %get-tuple-element.60.values_ref, bf16[224,768]{1,0:T(8,128)(2,1)S(1)} %get-tuple-element.61.high_ref, ...), custom_call_target="tpu_custom_call" | custom-call | flops 8800000000 | bytes 28800000 | tf_op jit(solution)/shard_map/second/pallas_call | solution.py:30
  58.7 0.0 collective-permute-done.10.refs_0_
  58.7 0.0 collective-permute-done.11.refs_1_
  58.7 1.6 %last.1 = (bf16[736,128]{1,0:T(8,128)(2,1)S(1)}, bf16[736,128]{1,0:T(8,128)(2,1)S(1)}, bf16[736,128]{1,0:T(8,128)(2,1)S(1)}, bf16[736,128]{1,0:T(8,128)(2,1)S(1)}) custom-call(s32[1]{0:T(128)} %bitcast.1.turn_ref, bf16[224,640]{1,0:T(8,128)(2,1)S(1)} %collective-permute-done.10.refs_0_, bf16[224,640]{1,0:T(8,128)(2,1)S(1)} %collective-permute-done.11.refs_1_, ...), custom_call_target="tpu_custom_call" | custom-call | flops 3300000000 | bytes 10800000 | tf_op jit(solution)/shard_map/last/pallas_call | solution.py:30
  60.3 1.1 %collective-permute-start.12 = (bf16[736,128]{1,0:T(8,128)(2,1)S(1)}, bf16[736,128]{1,0:T(8,128)(2,1)S(1)}, u32[]{:S(2)}, u32[]{:S(2)}) collective-permute-start(bf16[736,128]{1,0:T(8,128)(2,1)S(1)} %get-tuple-element.67), channel_id=1, source_target_pairs={{0,8},{8,0},{16,24},{24,16},{1,9},{9,1},{17,25},{25,17},{2,10},{10... | collective-permute-start | bytes 565256 | tf_op jit(solution)/shard_map/ppermute | solution.py:441
  61.4 1.9 %collective-permute-start.13 = (bf16[736,128]{1,0:T(8,128)(2,1)S(1)}, bf16[736,128]{1,0:T(8,128)(2,1)S(1)}, u32[]{:S(2)}, u32[]{:S(2)}) collective-permute-start(bf16[736,128]{1,0:T(8,128)(2,1)S(1)} %get-tuple-element.68), channel_id=1, source_target_pairs={{0,16},{8,24},{16,0},{24,8},{1,17},{9,25},{17,1},{25,9},{2,18},{10... | collective-permute-start | bytes 565256 | tf_op jit(solution)/shard_map/ppermute | solution.py:441
  63.3 0.0 collective-permute-done.7.refs_1_
  63.3 1.5 %collective-permute-start.14 = (bf16[736,128]{1,0:T(8,128)(2,1)S(1)}, bf16[736,128]{1,0:T(8,128)(2,1)S(1)}, u32[]{:S(2)}, u32[]{:S(2)}) collective-permute-start(bf16[736,128]{1,0:T(8,128)(2,1)S(1)} %get-tuple-element.69), channel_id=1, source_target_pairs={{0,24},{8,16},{16,8},{24,0},{1,25},{9,17},{17,9},{25,1},{2,26},{10... | collective-permute-start | bytes 565256 | tf_op jit(solution)/shard_map/ppermute | solution.py:441
  64.8 0.0 collective-permute-done.8.refs_2_
  64.8 0.0 collective-permute-done.9.refs_3_
  64.8 1.2 %join.2 = bf16[3,53,2304]{2,1,0:T(8,128)(2,1)} custom-call(s32[1]{0:T(128)} %bitcast.me_ref, bf16[736,128]{1,0:T(8,128)(2,1)S(1)} %get-tuple-element.53.refs_0_, bf16[736,128]{1,0:T(8,128)(2,1)S(1)} %collective-permute-done.7.refs_1_, bf16[736,128]{1,0:T(8,128)(2,1)S(1)} %collective-permute-done.8.refs_2_, bf16[736,128]{1,0:T(8,128)(2,1)S(1)} %collective-permute-done.9.refs_3_), custom_call_target="tpu_custom_call" | custom-call | flops 1100000000 | bytes 3600000 | tf_op jit(solution)/shard_map/join/pallas_call | solution.py:30
  66.0 2.5 %collective-permute-done.12.refs_1_ = bf16[736,128]{1,0:T(8,128)(2,1)S(1)} collective-permute-done((bf16[736,128]{1,0:T(8,128)(2,1)S(1)}, bf16[736,128]{1,0:T(8,128)(2,1)S(1)}, u32[]{:S(2)}, u32[]{:S(2)}) %collective-permute-start.12) | collective-permute-done | bytes 188448 | tf_op jit(solution)/shard_map/ppermute | solution.py:441
  68.5 12.3 %collective-permute-done.13.refs_2_ = bf16[736,128]{1,0:T(8,128)(2,1)S(1)} collective-permute-done((bf16[736,128]{1,0:T(8,128)(2,1)S(1)}, bf16[736,128]{1,0:T(8,128)(2,1)S(1)}, u32[]{:S(2)}, u32[]{:S(2)}) %collective-permute-start.13) | collective-permute-done | bytes 188448 | tf_op jit(solution)/shard_map/ppermute | solution.py:441
  80.8 0.0 collective-permute-done.14.refs_3_
  80.8 1.2 %join.3 = bf16[3,53,2304]{2,1,0:T(8,128)(2,1)} custom-call(s32[1]{0:T(128)} %bitcast.me_ref, bf16[736,128]{1,0:T(8,128)(2,1)S(1)} %get-tuple-element.66.refs_0_, bf16[736,128]{1,0:T(8,128)(2,1)S(1)} %collective-permute-done.12.refs_1_, bf16[736,128]{1,0:T(8,128)(2,1)S(1)} %collective-permute-done.13.refs_2_, bf16[736,128]{1,0:T(8,128)(2,1)S(1)} %collective-permute-done.14.refs_3_), custom_call_target="tpu_custom_call" | custom-call | flops 1100000000 | bytes 3600000 | tf_op jit(solution)/shard_map/join/pallas_call | solution.py:30
  (17 shorter events, 0.2 us)
Async XLA Ops:
  0.6 8.1 %copy-start.5 = (f32[1218]{0:T(1024)S(1)}, f32[1218]{0:T(1024)}, u32[]{:S(2)}) copy-start(f32[1218]{0:T(1024)} %param.9) | copy-start | bytes 14620
  0.6 8.1 %copy-start.2 = (s32[210]{0:T(256)S(1)}, s32[210]{0:T(256)}, u32[]{:S(2)}) copy-start(s32[210]{0:T(256)} %param.11) | copy-start | bytes 2524
  0.7 1.1 %copy-start = (bf16[53,3,2304]{2,0,1:T(8,128)(2,1)S(1)}, bf16[53,3,2304]{2,0,1:T(8,128)(2,1)}, u32[]{:S(2)}) copy-start(bf16[53,3,2304]{2,0,1:T(8,128)(2,1)} %param.6) | copy-start | bytes 2198020
  1.8 6.6 %copy-start.3 = (f32[6,3,2304]{2,1,0:T(4,128)S(1)}, f32[6,3,2304]{2,1,0:T(4,128)}, u32[]{:S(2)}) copy-start(f32[6,3,2304]{2,1,0:T(4,128)} %param.8) | copy-start | bytes 497668
  1.8 6.6 %copy-start.4 = (f32[3,2304]{1,0:T(4,128)S(1)}, f32[3,2304]{1,0:T(4,128)}, u32[]{:S(2)}) copy-start(f32[3,2304]{1,0:T(4,128)} %param.7) | copy-start | bytes 82948
  1.8 7.0 %copy-start.1 = (s32[1218,3]{0,1:T(4,128)S(1)}, s32[1218,3]{0,1:T(4,128)}, u32[]{:S(2)}) copy-start(s32[1218,3]{0,1:T(4,128)} %param.10) | copy-start | bytes 43852
  2.6 13.0 %collective-permute-start.1 = (bf16[2,56,768]{2,1,0:T(8,128)(2,1)S(1)}, bf16[2,56,768]{2,1,0:T(8,128)(2,1)S(1)}, u32[]{:S(2)}, u32[]{:S(2)}) collective-permute-start(bf16[2,56,768]{2,1,0:T(8,128)(2,1)S(1)} %get-tuple-element.38), channel_id=1, source_target_pairs={{0,16},{8,24},{16,0},{24,8},{1,17},{9,25},{17,1},{25,9},{2,18},{10... | collective-permute-start | bytes 516104 | tf_op jit(solution)/shard_map/ppermute | solution.py:441
  6.7 15.9 %collective-permute-start = (bf16[3,56,768]{2,1,0:T(8,128)(2,1)S(1)}, bf16[3,56,768]{2,1,0:T(8,128)(2,1)S(1)}, u32[]{:S(2)}, u32[]{:S(2)}) collective-permute-start(bf16[3,56,768]{2,1,0:T(8,128)(2,1)S(1)} %get-tuple-element.37), channel_id=1, source_target_pairs={{0,8},{8,0},{16,24},{24,16},{1,9},{9,1},{17,25},{25,17},{2,10},{10... | collective-permute-start | bytes 774152 | tf_op jit(solution)/shard_map/ppermute | solution.py:441
  8.3 14.3 %collective-permute-start.2 = (bf16[2,56,768]{2,1,0:T(8,128)(2,1)S(1)}, bf16[2,56,768]{2,1,0:T(8,128)(2,1)S(1)}, u32[]{:S(2)}, u32[]{:S(2)}) collective-permute-start(bf16[2,56,768]{2,1,0:T(8,128)(2,1)S(1)} %get-tuple-element.39), channel_id=1, source_target_pairs={{0,24},{8,16},{16,8},{24,0},{1,25},{9,17},{17,9},{25,1},{2,26},{10... | collective-permute-start | bytes 516104 | tf_op jit(solution)/shard_map/ppermute | solution.py:441
  15.9 16.5 %collective-permute-start.5 = (bf16[56,768]{1,0:T(8,128)(2,1)S(1)}, bf16[56,768]{1,0:T(8,128)(2,1)S(1)}, u32[]{:S(2)}, u32[]{:S(2)}) collective-permute-start(bf16[56,768]{1,0:T(8,128)(2,1)S(1)} %get-tuple-element.45), channel_id=1, source_target_pairs={{0,16},{8,24},{16,0},{24,8},{1,17},{9,25},{17,1},{25,9},{2,18},{10... | collective-permute-start | bytes 258056 | tf_op jit(solution)/shard_map/ppermute | solution.py:441
  16.3 16.1 %collective-permute-start.6 = (bf16[56,768]{1,0:T(8,128)(2,1)S(1)}, bf16[56,768]{1,0:T(8,128)(2,1)S(1)}, u32[]{:S(2)}, u32[]{:S(2)}) collective-permute-start(bf16[56,768]{1,0:T(8,128)(2,1)S(1)} %get-tuple-element.46), channel_id=1, source_target_pairs={{0,24},{8,16},{16,8},{24,0},{1,25},{9,17},{17,9},{25,1},{2,26},{10... | collective-permute-start | bytes 258056 | tf_op jit(solution)/shard_map/ppermute | solution.py:441
  22.7 12.9 %collective-permute-start.3 = (bf16[256,768]{1,0:T(8,128)(2,1)S(1)}, bf16[256,768]{1,0:T(8,128)(2,1)S(1)}, u32[]{:S(2)}, u32[]{:S(2)}) collective-permute-start(bf16[256,768]{1,0:T(8,128)(2,1)S(1)} %get-tuple-element.43.low_ref.refs_2_), channel_id=1, source_target_pairs={{1,2},{2,1},{3,4},{4,3},{5,6},{6,5},{9,10},{10,9},{11,12},{12,11},... | collective-permute-start | bytes 1179656 | tf_op jit(solution)/shard_map/ppermute | solution.py:451
  23.6 12.1 %collective-permute-start.4 = (bf16[256,768]{1,0:T(8,128)(2,1)S(1)}, bf16[256,768]{1,0:T(8,128)(2,1)S(1)}, u32[]{:S(2)}, u32[]{:S(2)}) collective-permute-start(bf16[256,768]{1,0:T(8,128)(2,1)S(1)} %get-tuple-element.44.high_ref.refs_3_), channel_id=1, source_target_pairs={{0,1},{1,0},{2,3},{3,2},{4,5},{5,4},{6,7},{7,6},{8,9},{9,8},{10,11... | collective-permute-start | bytes 1179656 | tf_op jit(solution)/shard_map/ppermute | solution.py:450
  39.3 19.4 %collective-permute-start.10 = (bf16[224,640]{1,0:T(8,128)(2,1)S(1)}, bf16[224,640]{1,0:T(8,128)(2,1)S(1)}, u32[]{:S(2)}, u32[]{:S(2)}) collective-permute-start(bf16[224,640]{1,0:T(8,128)(2,1)S(1)} %get-tuple-element.57), channel_id=1, source_target_pairs={{1,2},{2,1},{3,4},{4,3},{5,6},{6,5},{9,10},{10,9},{11,12},{12,11},... | collective-permute-start | bytes 860168 | tf_op jit(solution)/shard_map/ppermute | solution.py:451
  40.2 18.5 %collective-permute-start.11 = (bf16[224,640]{1,0:T(8,128)(2,1)S(1)}, bf16[224,640]{1,0:T(8,128)(2,1)S(1)}, u32[]{:S(2)}, u32[]{:S(2)}) collective-permute-start(bf16[224,640]{1,0:T(8,128)(2,1)S(1)} %get-tuple-element.58), channel_id=1, source_target_pairs={{0,1},{1,0},{2,3},{3,2},{4,5},{5,4},{6,7},{7,6},{8,9},{9,8},{10,11... | collective-permute-start | bytes 860168 | tf_op jit(solution)/shard_map/ppermute | solution.py:450
  43.1 20.2 %collective-permute-start.7 = (bf16[736,128]{1,0:T(8,128)(2,1)S(1)}, bf16[736,128]{1,0:T(8,128)(2,1)S(1)}, u32[]{:S(2)}, u32[]{:S(2)}) collective-permute-start(bf16[736,128]{1,0:T(8,128)(2,1)S(1)} %get-tuple-element.54), channel_id=1, source_target_pairs={{0,8},{8,0},{16,24},{24,16},{1,9},{9,1},{17,25},{25,17},{2,10},{10... | collective-permute-start | bytes 565256 | tf_op jit(solution)/shard_map/ppermute | solution.py:441
  48.0 16.7 %collective-permute-start.8 = (bf16[736,128]{1,0:T(8,128)(2,1)S(1)}, bf16[736,128]{1,0:T(8,128)(2,1)S(1)}, u32[]{:S(2)}, u32[]{:S(2)}) collective-permute-start(bf16[736,128]{1,0:T(8,128)(2,1)S(1)} %get-tuple-element.55), channel_id=1, source_target_pairs={{0,16},{8,24},{16,0},{24,8},{1,17},{9,25},{17,1},{25,9},{2,18},{10... | collective-permute-start | bytes 565256 | tf_op jit(solution)/shard_map/ppermute | solution.py:441
  49.1 15.7 %collective-permute-start.9 = (bf16[736,128]{1,0:T(8,128)(2,1)S(1)}, bf16[736,128]{1,0:T(8,128)(2,1)S(1)}, u32[]{:S(2)}, u32[]{:S(2)}) collective-permute-start(bf16[736,128]{1,0:T(8,128)(2,1)S(1)} %get-tuple-element.56), channel_id=1, source_target_pairs={{0,24},{8,16},{16,8},{24,0},{1,25},{9,17},{17,9},{25,1},{2,26},{10... | collective-permute-start | bytes 565256 | tf_op jit(solution)/shard_map/ppermute | solution.py:441
  60.3 8.1 %collective-permute-start.12 = (bf16[736,128]{1,0:T(8,128)(2,1)S(1)}, bf16[736,128]{1,0:T(8,128)(2,1)S(1)}, u32[]{:S(2)}, u32[]{:S(2)}) collective-permute-start(bf16[736,128]{1,0:T(8,128)(2,1)S(1)} %get-tuple-element.67), channel_id=1, source_target_pairs={{0,8},{8,0},{16,24},{24,16},{1,9},{9,1},{17,25},{25,17},{2,10},{10... | collective-permute-start | bytes 565256 | tf_op jit(solution)/shard_map/ppermute | solution.py:441
  61.4 19.4 %collective-permute-start.13 = (bf16[736,128]{1,0:T(8,128)(2,1)S(1)}, bf16[736,128]{1,0:T(8,128)(2,1)S(1)}, u32[]{:S(2)}, u32[]{:S(2)}) collective-permute-start(bf16[736,128]{1,0:T(8,128)(2,1)S(1)} %get-tuple-element.68), channel_id=1, source_target_pairs={{0,16},{8,24},{16,0},{24,8},{1,17},{9,25},{17,1},{25,9},{2,18},{10... | collective-permute-start | bytes 565256 | tf_op jit(solution)/shard_map/ppermute | solution.py:441
  63.3 17.5 %collective-permute-start.14 = (bf16[736,128]{1,0:T(8,128)(2,1)S(1)}, bf16[736,128]{1,0:T(8,128)(2,1)S(1)}, u32[]{:S(2)}, u32[]{:S(2)}) collective-permute-start(bf16[736,128]{1,0:T(8,128)(2,1)S(1)} %get-tuple-element.69), channel_id=1, source_target_pairs={{0,24},{8,16},{16,8},{24,0},{1,25},{9,17},{17,9},{25,1},{2,26},{10... | collective-permute-start | bytes 565256 | tf_op jit(solution)/shard_map/ppermute | solution.py:441

commit v8 on v7

--- a/solution.py
+++ b/solution.py
@@ -356,22 +356,19 @@
 
 
 def first_fix_kernel(packing, turn_ref, *refs):
-    halo_refs, own_refs, share_refs, (middle_in, tables_ref, masks_ref), refs = (
+    halo_refs, (conduct_ref, own_ref), share_refs, (middle_in, tables_ref, masks_ref), refs = (
         refs[0:2], refs[2:4], refs[4:6], refs[6:9], refs[9:]
     )
     wholes, nears, faces_ref, pieces, (mixed, sums, ends, line) = refs[:2], refs[2:4], refs[4], refs[5:-4], refs[-4:]
     rows, (_, fields, tiles, _, _) = tables_ref.shape[1], faces_ref.shape
     for side in range(2):
-        coefficient = 0.0
-        for ref in (own_refs[side], halo_refs[side]):
-            parts = ref[rows : rows + EXTRA, :].astype(F32)
-            coefficient = coefficient + ((parts[16:24] + parts[8:16]) + parts[0:8])
-        spread_face(0.5 * coefficient, faces_ref.at[side])
-        for index, ref in enumerate((own_refs[side], halo_refs[side])):
-            mix(tables_ref, ref[0:rows, :], mixed.at[index])
+        parts = halo_refs[side][rows : rows + EXTRA, :].astype(F32)
+        coefficient = (parts[16:24] + parts[8:16]) + parts[0:8]
+        spread_face(0.5 * (conduct_ref[side * (conduct_ref.shape[0] - 1)] + coefficient), faces_ref.at[side])
+        mix(tables_ref, halo_refs[side][0:rows, :], mixed.at[side])
 
         def values_of(tile, here):
-            return mixed[0, tile, here, :].astype(F32) - mixed[1, tile, here, :].astype(F32)
+            return own_ref[side, tile, here, :].astype(F32) - mixed[side, tile, here, :].astype(F32)
 
         def face_of(way, field, tile):
             return faces_ref[side, field, tile]
@@ -405,12 +402,12 @@
     emit((ends.at[0], middle_in, ends.at[1]), packing, line, pieces)
 
 
-def join_kernel(count, packing, me_ref, *refs):
-    piece_refs, (out_ref, held) = refs[:count], refs[count:]
+def join_kernel(count, packing, order, me_ref, *refs):
+    out_ref, held = refs[count:]
     full, odd, beside = packing.full, packing.odd, packing.beside
     me = me_ref[0]
-    for step in range(count):
-        held[lax.bitwise_xor(me, step)] = piece_refs[step][...].astype(F32)
+    for step, piece_ref in zip(order, refs):
+        held[lax.bitwise_xor(me, step)] = piece_ref[...].astype(F32)
     pieces = [images_of(held.at[source], packing) for source in range(count)]
     for plane in range(packing.planes):
         parts = []
@@ -521,8 +518,14 @@
         unread=2,
     )
     halos = neighbours(low, high)
-    edges = (low, high)
-    low, high, middle = call(outer_kernel, "outer", 6, [share] * 3, (low, high, *common), scratch(tiles))
+    low, high, middle, mixed = call(
+        outer_kernel,
+        "outer",
+        6,
+        [share] * 3 + [shape(2, tiles, fields * rows, LANES)],
+        (low, high, *common),
+        scratch(tiles)[1:],
+    )
     low, high, middle, middle_whole = call(
         functools.partial(inner_kernel, count),
         "inner",
@@ -539,7 +542,7 @@
         + [shape(rows, near)] * 2
         + [shape(2, fields, tiles, 8, LANES, dtype=F32)]
         + pieces,
-        (turn_alone, *halos, *edges, low, high, middle, tables, masks),
+        (turn_alone, *halos, conduct, mixed, low, high, middle, tables, masks),
         scratch(tiles, 1) + [VMEM((2, tiles, rows, LANES), F32), line],
         scalars=1,
     )
@@ -564,19 +567,19 @@
     )
     second = exchanged(second)
 
-    def join(parts):
+    def join(parts, order):
         (result,) = call(
-            functools.partial(join_kernel, count, packing),
+            functools.partial(join_kernel, count, packing, order),
             "join",
             1,
             [shape(planes, own, cells)],
-            (me_alone, *parts),
+            (me_alone, *(parts[step] for step in order)),
             [VMEM((count,) + parts[0].shape, F32)],
             scalars=1,
         )
         return jnp.transpose(result, (1, 0, 2))
 
-    return join(sent), join(second)
+    return join(sent, tuple(range(count))), join(second, tuple(range(count - 1, -1, -1)))
 
 
 def solution(mesh):

time: 83.6 us -> 79.4 us (0.950); the launches traced: 82 us -> 79.1 us
  waiting for transfers between devices: 20.2 us -> 16.5 us
  local copies, waits for them, and re-layouts: 1.4 us -> 3.78 us
  Pallas kernels: 31.1 us -> 29.5 us
    ppermute x11, waiting for transfers between devices: 20.2 us -> 16.5 us  [exchange(): return lax.ppermute(block, 'chaos', [(i, i ^ step) for i in range(count)])]
    pallas_call x11, Pallas kernels: 31.1 us -> 29.5 us  [call(): pl.pallas_call(kernel, out_shape=out_shape, in_specs=in_specs, out_specs=...]
    unnamed x13 -> x7, local copies, waits for them, and re-layouts: 1.19 us -> 2.11 us
  transfers between devices with their start and end apart: 15 -> 15, of which waited for: 4 -> 3; matrix products, arithmetic and copies ran while one was open for 1% -> 4% of each run, Pallas kernels for 31% -> 32%
where the time goes in v8:
time: 79.4 us; the launch traced here: 79.1 us
  Pallas kernels  29.5 us (37%)
  starting transfers between devices  28.2 us (36%)
  waiting for transfers between devices  16.5 us (21%)
  local copies, waits for them, and re-layouts  3.78 us (5%)
  between operations  0.87 us (1%)
    pallas_call x11, Pallas kernels, call(): pl.pallas_call(kernel, out_shape=out_shape, in_specs=in_specs, out_specs=...  29.5 us
    ppermute x11, starting transfers between devices, exchange(): return lax.ppermute(block, 'chaos', [(i, i ^ step) for i in range(count)])  20.7 us
    ppermute x11, waiting for transfers between devices, exchange(): return lax.ppermute(block, 'chaos', [(i, i ^ step) for i in range(count)])  16.5 us
    ppermute x2, starting transfers between devices, neighbours(): after = lax.ppermute(last_plane, 'space', pairs)  5.79 us
    unnamed x7, local copies, waits for them, and re-layouts  2.11 us
    ppermute x2, starting transfers between devices, neighbours(): return (lax.ppermute(first_plane, 'space', others), after)  1.75 us
  transfers between devices with their start and end apart: 15, of which 3 were waited for; matrix products, arithmetic and copies ran while one was open for 4% of the time, Pallas kernels for 32%

profile of v8, /device:TPU:0, one launch (start us, length us, event | category | flops | bytes accessed | tf_op | source)
XLA Modules:
  0.0 79.1 jit_solution(16300322349801097816)
XLA Ops:
  0.7 1.1 %copy-done = bf16[53,3,2304]{2,0,1:T(8,128)(2,1)S(1)} copy-done((bf16[53,3,2304]{2,0,1:T(8,128)(2,1)S(1)}, bf16[53,3,2304]{2,0,1:T(8,128)(2,1)}, u32[]{:S(2)}) %copy-start) | copy-done | bytes 732696
  1.8 0.8 %cut.1 = (bf16[3,56,768]{2,1,0:T(8,128)(2,1)S(1)}, bf16[3,56,768]{2,1,0:T(8,128)(2,1)S(1)}, bf16[2,56,768]{2,1,0:T(8,128)(2,1)S(1)}, bf16[2,56,768]{2,1,0:T(8,12...) custom-call(s32[1]{0:T(128)} %bitcast.me_ref, bf16[3,53,2304]{2,1,0:T(8,128)(2,1)S(1)} %bitcast.10), custom_call_target="tpu_custom_call" | custom-call | flops 1100000000 | bytes 3600000 | tf_op jit(solution)/shard_map/cut/pallas_call | solution.py:30
  2.6 4.1 %collective-permute-start.1 = (bf16[2,56,768]{2,1,0:T(8,128)(2,1)S(1)}, bf16[2,56,768]{2,1,0:T(8,128)(2,1)S(1)}, u32[]{:S(2)}, u32[]{:S(2)}) collective-permute-start(bf16[2,56,768]{2,1,0:T(8,128)(2,1)S(1)} %get-tuple-element.39), channel_id=1, source_target_pairs={{0,16},{8,24},{16,0},{24,8},{1,17},{9,25},{17,1},{25,9},{2,18},{10... | collective-permute-start | bytes 516104 | tf_op jit(solution)/shard_map/ppermute | solution.py:438
  6.7 1.4 %collective-permute-start.2 = (bf16[2,56,768]{2,1,0:T(8,128)(2,1)S(1)}, bf16[2,56,768]{2,1,0:T(8,128)(2,1)S(1)}, u32[]{:S(2)}, u32[]{:S(2)}) collective-permute-start(bf16[2,56,768]{2,1,0:T(8,128)(2,1)S(1)} %get-tuple-element.40), channel_id=1, source_target_pairs={{0,24},{8,16},{16,8},{24,0},{1,25},{9,17},{17,9},{25,1},{2,26},{10... | collective-permute-start | bytes 516104 | tf_op jit(solution)/shard_map/ppermute | solution.py:438
  8.1 0.2 collective-permute-start
  8.4 0.7 broadcast_in_dim.15.products_ref
  9.1 0.8 broadcast_in_dim.14
  9.9 1.0 %copy.10 = f32[6,3,2304]{2,0,1:T(8,128)S(1)} copy(f32[6,3,2304]{2,1,0:T(4,128)} %param.8) | data formatting | bytes 331776 | tf_op args[2]
  10.8 0.1 pad_maximum_fusion
  10.9 0.1 pad_dynamic-slice_fusion.1
  11.0 0.1 pad_dynamic-slice_fusion
  11.1 5.1 %tables.1.refs_2_.refs_4_.tables_ref.refs_7_.refs_5_ = bf16[1568,224]{1,0:T(8,128)(2,1)S(1)} custom-call(s32[1]{0:T(128)} %bitcast.me_ref, s32[3,1218]{1,0:T(4,128)S(1)} %bitcast.11, f32[1,1218]{1,0:T(1,128)S(1)} %broadcast_in_dim.15.products_ref, s32[1,210]{1,0:T(1,128)S(1)} %bitcast.12, bf16[3,56,768]{2,1,0:T(8,128)(2,1)S(1)} %get-tuple-element.37._.refs_0_), custom_call_target="tpu_custom_call" | custom-call | flops 5500000256 | bytes 18000000 | tf_op jit(solution)/shard_map/tables/pallas_call | solution.py:30
  16.3 0.1 pad_maximum_fusion.1.conduct_ref.refs_2_
  16.4 3.0 %collective-permute-done.1.refs_3_.refs_2_ = bf16[2,56,768]{2,1,0:T(8,128)(2,1)S(1)} collective-permute-done((bf16[2,56,768]{2,1,0:T(8,128)(2,1)S(1)}, bf16[2,56,768]{2,1,0:T(8,128)(2,1)S(1)}, u32[]{:S(2)}, u32[]{:S(2)}) %collective-permute-start.1) | collective-permute-done | bytes 172064 | tf_op jit(solution)/shard_map/ppermute | solution.py:438
  19.4 0.2 weights.1
  19.6 0.1 collective-permute-start.5
  19.7 2.9 %collective-permute-start.6 = (bf16[56,768]{1,0:T(8,128)(2,1)S(1)}, bf16[56,768]{1,0:T(8,128)(2,1)S(1)}, u32[]{:S(2)}, u32[]{:S(2)}) collective-permute-start(bf16[56,768]{1,0:T(8,128)(2,1)S(1)} %get-tuple-element.48), channel_id=1, source_target_pairs={{0,24},{8,16},{16,8},{24,0},{1,25},{9,17},{17,9},{25,1},{2,26},{10... | collective-permute-start | bytes 258056 | tf_op jit(solution)/shard_map/ppermute | solution.py:438
  22.5 0.0 collective-permute-done.2.refs_3_
  22.6 0.0 collective-permute-done.refs_1_
  22.6 0.1 gather.1
  22.6 0.9 %collective-permute-start.3 = (bf16[256,768]{1,0:T(8,128)(2,1)S(1)}, bf16[256,768]{1,0:T(8,128)(2,1)S(1)}, u32[]{:S(2)}, u32[]{:S(2)}) collective-permute-start(bf16[256,768]{1,0:T(8,128)(2,1)S(1)} %get-tuple-element.44.low_ref), channel_id=1, source_target_pairs={{1,2},{2,1},{3,4},{4,3},{5,6},{6,5},{9,10},{10,9},{11,12},{12,11},... | collective-permute-start | bytes 1179656 | tf_op jit(solution)/shard_map/ppermute | solution.py:448
  23.5 2.9 %collective-permute-start.4 = (bf16[256,768]{1,0:T(8,128)(2,1)S(1)}, bf16[256,768]{1,0:T(8,128)(2,1)S(1)}, u32[]{:S(2)}, u32[]{:S(2)}) collective-permute-start(bf16[256,768]{1,0:T(8,128)(2,1)S(1)} %get-tuple-element.45.high_ref), channel_id=1, source_target_pairs={{0,1},{1,0},{2,3},{3,2},{4,5},{5,4},{6,7},{7,6},{8,9},{9,8},{10,11... | collective-permute-start | bytes 1179656 | tf_op jit(solution)/shard_map/ppermute | solution.py:447
  26.4 5.4 %outer.1 = (f32[6,224,128]{2,1,0:T(8,128)S(1)}, f32[6,224,128]{2,1,0:T(8,128)S(1)}, f32[6,224,128]{2,1,0:T(8,128)S(1)}, bf16[2,6,1568,128]{3,2,1,0:T(8,128)(2,1)S(1)}) custom-call(bf16[256,768]{1,0:T(8,128)(2,1)S(1)} %get-tuple-element.44.low_ref, bf16[256,768]{1,0:T(8,128)(2,1)S(1)} %get-tuple-element.45.high_ref, ...), custom_call_target="tpu_custom_call" | custom-call | flops 6600000000 | bytes 21600000 | tf_op jit(solution)/shard_map/outer/pallas_call | solution.py:30
  31.8 0.0 collective-permute-done.5.refs_2_
  31.8 0.0 collective-permute-done.6.refs_3_
  31.8 3.3 %inner.1 = (f32[6,224,128]{2,1,0:T(8,128)S(1)}, f32[6,224,128]{2,1,0:T(8,128)S(1)}, f32[6,224,128]{2,1,0:T(8,128)S(1)}, bf16[224,768]{1,0:T(8,128)(2,1)S(1)}) custom-call(bf16[3,56,768]{2,1,0:T(8,128)(2,1)S(1)} %get-tuple-element.37._.refs_0_, bf16[3,56,768]{2,1,0:T(8,128)(2,1)S(1)} %collective-permute-done.refs_1_, ...), custom_call_target="tpu_custom_call" | custom-call | flops 3300000000 | bytes 10800000 | tf_op jit(solution)/shard_map/inner/pallas_call | solution.py:30
  35.1 0.0 collective-permute-done.3.refs_0_
  35.1 0.0 collective-permute-done.4.refs_1_
  35.1 2.6 %fix.1 = (bf16[224,768]{1,0:T(8,128)(2,1)S(1)}, bf16[224,768]{1,0:T(8,128)(2,1)S(1)}, bf16[224,640]{1,0:T(8,128)(2,1)S(1)}, bf16[224,640]{1,0:T(8,128)(2,1)S(1)}...) custom-call(s32[1]{0:T(128)} %bitcast.1.turn_ref, ...), custom_call_target="tpu_custom_call" | custom-call | flops 3300000000 | bytes 10800000 | tf_op jit(solution)/shard_map/fix/pallas_call | solution.py:30
  37.7 4.2 %collective-permute-start.7 = (bf16[736,128]{1,0:T(8,128)(2,1)S(1)}, bf16[736,128]{1,0:T(8,128)(2,1)S(1)}, u32[]{:S(2)}, u32[]{:S(2)}) collective-permute-start(bf16[736,128]{1,0:T(8,128)(2,1)S(1)} %get-tuple-element.56), channel_id=1, source_target_pairs={{0,8},{8,0},{16,24},{24,16},{1,9},{9,1},{17,25},{25,17},{2,10},{10... | collective-permute-start | bytes 565256 | tf_op jit(solution)/shard_map/ppermute | solution.py:438
  41.9 2.1 %collective-permute-start.8 = (bf16[736,128]{1,0:T(8,128)(2,1)S(1)}, bf16[736,128]{1,0:T(8,128)(2,1)S(1)}, u32[]{:S(2)}, u32[]{:S(2)}) collective-permute-start(bf16[736,128]{1,0:T(8,128)(2,1)S(1)} %get-tuple-element.57), channel_id=1, source_target_pairs={{0,16},{8,24},{16,0},{24,8},{1,17},{9,25},{17,1},{25,9},{2,18},{10... | collective-permute-start | bytes 565256 | tf_op jit(solution)/shard_map/ppermute | solution.py:438
  43.9 1.4 %collective-permute-start.9 = (bf16[736,128]{1,0:T(8,128)(2,1)S(1)}, bf16[736,128]{1,0:T(8,128)(2,1)S(1)}, u32[]{:S(2)}, u32[]{:S(2)}) collective-permute-start(bf16[736,128]{1,0:T(8,128)(2,1)S(1)} %get-tuple-element.58), channel_id=1, source_target_pairs={{0,24},{8,16},{16,8},{24,0},{1,25},{9,17},{17,9},{25,1},{2,26},{10... | collective-permute-start | bytes 565256 | tf_op jit(solution)/shard_map/ppermute | solution.py:438
  45.3 0.9 %collective-permute-start.10 = (bf16[224,640]{1,0:T(8,128)(2,1)S(1)}, bf16[224,640]{1,0:T(8,128)(2,1)S(1)}, u32[]{:S(2)}, u32[]{:S(2)}) collective-permute-start(bf16[224,640]{1,0:T(8,128)(2,1)S(1)} %get-tuple-element.59), channel_id=1, source_target_pairs={{1,2},{2,1},{3,4},{4,3},{5,6},{6,5},{9,10},{10,9},{11,12},{12,11},... | collective-permute-start | bytes 860168 | tf_op jit(solution)/shard_map/ppermute | solution.py:448
  46.2 2.9 %collective-permute-start.11 = (bf16[224,640]{1,0:T(8,128)(2,1)S(1)}, bf16[224,640]{1,0:T(8,128)(2,1)S(1)}, u32[]{:S(2)}, u32[]{:S(2)}) collective-permute-start(bf16[224,640]{1,0:T(8,128)(2,1)S(1)} %get-tuple-element.60), channel_id=1, source_target_pairs={{0,1},{1,0},{2,3},{3,2},{4,5},{5,4},{6,7},{7,6},{8,9},{9,8},{10,11... | collective-permute-start | bytes 860168 | tf_op jit(solution)/shard_map/ppermute | solution.py:447
  49.1 8.1 %second.1 = (f32[6,224,128]{2,1,0:T(8,128)S(1)}, f32[6,224,128]{2,1,0:T(8,128)S(1)}, f32[6,224,128]{2,1,0:T(8,128)S(1)}) custom-call(bf16[224,768]{1,0:T(8,128)(2,1)S(1)} %get-tuple-element.61.low_ref, bf16[224,768]{1,0:T(8,128)(2,1)S(1)} %get-tuple-element.62.values_ref, bf16[224,768]{1,0:T(8,128)(2,1)S(1)} %get-tuple-element.63.high_ref, ...), custom_call_target="tpu_custom_call" | custom-call | flops 8800000000 | bytes 28800000 | tf_op jit(solution)/shard_map/second/pallas_call | solution.py:30
  57.2 0.0 collective-permute-done.10.refs_0_
  57.2 0.0 collective-permute-done.11.refs_1_
  57.2 1.6 %last.1 = (bf16[736,128]{1,0:T(8,128)(2,1)S(1)}, bf16[736,128]{1,0:T(8,128)(2,1)S(1)}, bf16[736,128]{1,0:T(8,128)(2,1)S(1)}, bf16[736,128]{1,0:T(8,128)(2,1)S(1)}) custom-call(s32[1]{0:T(128)} %bitcast.1.turn_ref, bf16[224,640]{1,0:T(8,128)(2,1)S(1)} %collective-permute-done.10.refs_0_, bf16[224,640]{1,0:T(8,128)(2,1)S(1)} %collective-permute-done.11.refs_1_, ...), custom_call_target="tpu_custom_call" | custom-call | flops 3300000000 | bytes 10800000 | tf_op jit(solution)/shard_map/last/pallas_call | solution.py:30
  58.8 2.5 %collective-permute-start.12 = (bf16[736,128]{1,0:T(8,128)(2,1)S(1)}, bf16[736,128]{1,0:T(8,128)(2,1)S(1)}, u32[]{:S(2)}, u32[]{:S(2)}) collective-permute-start(bf16[736,128]{1,0:T(8,128)(2,1)S(1)} %get-tuple-element.68), channel_id=1, source_target_pairs={{0,24},{8,16},{16,8},{24,0},{1,25},{9,17},{17,9},{25,1},{2,26},{10... | collective-permute-start | bytes 565256 | tf_op jit(solution)/shard_map/ppermute | solution.py:438
  61.3 0.0 collective-permute-start.13
  61.3 0.0 collective-permute-done.7.refs_1_
  61.3 2.0 %collective-permute-start.14 = (bf16[736,128]{1,0:T(8,128)(2,1)S(1)}, bf16[736,128]{1,0:T(8,128)(2,1)S(1)}, u32[]{:S(2)}, u32[]{:S(2)}) collective-permute-start(bf16[736,128]{1,0:T(8,128)(2,1)S(1)} %get-tuple-element.70), channel_id=1, source_target_pairs={{0,8},{8,0},{16,24},{24,16},{1,9},{9,1},{17,25},{25,17},{2,10},{10... | collective-permute-start | bytes 565256 | tf_op jit(solution)/shard_map/ppermute | solution.py:438
  63.3 0.0 collective-permute-done.8.refs_2_
  63.3 1.2 %join.2 = bf16[3,53,2304]{2,1,0:T(8,128)(2,1)} custom-call(s32[1]{0:T(128)} %bitcast.me_ref, bf16[736,128]{1,0:T(8,128)(2,1)S(1)} %get-tuple-element.55.refs_0_, bf16[736,128]{1,0:T(8,128)(2,1)S(1)} %collective-permute-done.7.refs_1_, bf16[736,128]{1,0:T(8,128)(2,1)S(1)} %collective-permute-done.8.refs_2_, bf16[736,128]{1,0:T(8,128)(2,1)S(1)} %collective-permute-done.9.refs_3_), custom_call_target="tpu_custom_call" | custom-call | flops 1100000000 | bytes 3600000 | tf_op jit(solution)/shard_map/join/pallas_call | solution.py:30
  64.5 4.0 %collective-permute-done.12.refs_0_ = bf16[736,128]{1,0:T(8,128)(2,1)S(1)} collective-permute-done((bf16[736,128]{1,0:T(8,128)(2,1)S(1)}, bf16[736,128]{1,0:T(8,128)(2,1)S(1)}, u32[]{:S(2)}, u32[]{:S(2)}) %collective-permute-start.12) | collective-permute-done | bytes 188448 | tf_op jit(solution)/shard_map/ppermute | solution.py:438
  68.4 9.5 %collective-permute-done.13.refs_1_ = bf16[736,128]{1,0:T(8,128)(2,1)S(1)} collective-permute-done((bf16[736,128]{1,0:T(8,128)(2,1)S(1)}, bf16[736,128]{1,0:T(8,128)(2,1)S(1)}, u32[]{:S(2)}, u32[]{:S(2)}) %collective-permute-start.13) | collective-permute-done | bytes 188448 | tf_op jit(solution)/shard_map/ppermute | solution.py:438
  77.9 0.0 collective-permute-done.14.refs_2_
  77.9 1.2 %join.3 = bf16[3,53,2304]{2,1,0:T(8,128)(2,1)} custom-call(s32[1]{0:T(128)} %bitcast.me_ref, bf16[736,128]{1,0:T(8,128)(2,1)S(1)} %collective-permute-done.12.refs_0_, bf16[736,128]{1,0:T(8,128)(2,1)S(1)} %collective-permute-done.13.refs_1_, bf16[736,128]{1,0:T(8,128)(2,1)S(1)} %collective-permute-done.14.refs_2_, bf16[736,128]{1,0:T(8,128)(2,1)S(1)} %get-tuple-element.71.refs_3_), custom_call_target="tpu_custom_call" | custom-call | flops 1100000000 | bytes 3600000 | tf_op jit(solution)/shard_map/join/pallas_call | solution.py:30
  (11 shorter events, 0.1 us)
Async XLA Ops:
  0.6 10.5 %copy-start.2 = (s32[210]{0:T(256)S(1)}, s32[210]{0:T(256)}, u32[]{:S(2)}) copy-start(s32[210]{0:T(256)} %param.11) | copy-start | bytes 2524
  0.6 1.1 %copy-start = (bf16[53,3,2304]{2,0,1:T(8,128)(2,1)S(1)}, bf16[53,3,2304]{2,0,1:T(8,128)(2,1)}, u32[]{:S(2)}) copy-start(bf16[53,3,2304]{2,0,1:T(8,128)(2,1)} %param.6) | copy-start | bytes 2198020
  1.8 9.3 %copy-start.1 = (s32[1218,3]{0,1:T(4,128)S(1)}, s32[1218,3]{0,1:T(4,128)}, u32[]{:S(2)}) copy-start(s32[1218,3]{0,1:T(4,128)} %param.10) | copy-start | bytes 43852
  2.6 16.7 %collective-permute-start.1 = (bf16[2,56,768]{2,1,0:T(8,128)(2,1)S(1)}, bf16[2,56,768]{2,1,0:T(8,128)(2,1)S(1)}, u32[]{:S(2)}, u32[]{:S(2)}) collective-permute-start(bf16[2,56,768]{2,1,0:T(8,128)(2,1)S(1)} %get-tuple-element.39), channel_id=1, source_target_pairs={{0,16},{8,24},{16,0},{24,8},{1,17},{9,25},{17,1},{25,9},{2,18},{10... | collective-permute-start | bytes 516104 | tf_op jit(solution)/shard_map/ppermute | solution.py:438
  6.7 15.8 %collective-permute-start.2 = (bf16[2,56,768]{2,1,0:T(8,128)(2,1)S(1)}, bf16[2,56,768]{2,1,0:T(8,128)(2,1)S(1)}, u32[]{:S(2)}, u32[]{:S(2)}) collective-permute-start(bf16[2,56,768]{2,1,0:T(8,128)(2,1)S(1)} %get-tuple-element.40), channel_id=1, source_target_pairs={{0,24},{8,16},{16,8},{24,0},{1,25},{9,17},{17,9},{25,1},{2,26},{10... | collective-permute-start | bytes 516104 | tf_op jit(solution)/shard_map/ppermute | solution.py:438
  8.1 14.5 %collective-permute-start = (bf16[3,56,768]{2,1,0:T(8,128)(2,1)S(1)}, bf16[3,56,768]{2,1,0:T(8,128)(2,1)S(1)}, u32[]{:S(2)}, u32[]{:S(2)}) collective-permute-start(bf16[3,56,768]{2,1,0:T(8,128)(2,1)S(1)} %get-tuple-element.38), channel_id=1, source_target_pairs={{0,8},{8,0},{16,24},{24,16},{1,9},{9,1},{17,25},{25,17},{2,10},{10... | collective-permute-start | bytes 774152 | tf_op jit(solution)/shard_map/ppermute | solution.py:438
  19.6 12.2 %collective-permute-start.5 = (bf16[56,768]{1,0:T(8,128)(2,1)S(1)}, bf16[56,768]{1,0:T(8,128)(2,1)S(1)}, u32[]{:S(2)}, u32[]{:S(2)}) collective-permute-start(bf16[56,768]{1,0:T(8,128)(2,1)S(1)} %get-tuple-element.47), channel_id=1, source_target_pairs={{0,16},{8,24},{16,0},{24,8},{1,17},{9,25},{17,1},{25,9},{2,18},{10... | collective-permute-start | bytes 258056 | tf_op jit(solution)/shard_map/ppermute | solution.py:438
  19.7 12.1 %collective-permute-start.6 = (bf16[56,768]{1,0:T(8,128)(2,1)S(1)}, bf16[56,768]{1,0:T(8,128)(2,1)S(1)}, u32[]{:S(2)}, u32[]{:S(2)}) collective-permute-start(bf16[56,768]{1,0:T(8,128)(2,1)S(1)} %get-tuple-element.48), channel_id=1, source_target_pairs={{0,24},{8,16},{16,8},{24,0},{1,25},{9,17},{17,9},{25,1},{2,26},{10... | collective-permute-start | bytes 258056 | tf_op jit(solution)/shard_map/ppermute | solution.py:438
  22.6 12.5 %collective-permute-start.3 = (bf16[256,768]{1,0:T(8,128)(2,1)S(1)}, bf16[256,768]{1,0:T(8,128)(2,1)S(1)}, u32[]{:S(2)}, u32[]{:S(2)}) collective-permute-start(bf16[256,768]{1,0:T(8,128)(2,1)S(1)} %get-tuple-element.44.low_ref), channel_id=1, source_target_pairs={{1,2},{2,1},{3,4},{4,3},{5,6},{6,5},{9,10},{10,9},{11,12},{12,11},... | collective-permute-start | bytes 1179656 | tf_op jit(solution)/shard_map/ppermute | solution.py:448
  23.5 11.6 %collective-permute-start.4 = (bf16[256,768]{1,0:T(8,128)(2,1)S(1)}, bf16[256,768]{1,0:T(8,128)(2,1)S(1)}, u32[]{:S(2)}, u32[]{:S(2)}) collective-permute-start(bf16[256,768]{1,0:T(8,128)(2,1)S(1)} %get-tuple-element.45.high_ref), channel_id=1, source_target_pairs={{0,1},{1,0},{2,3},{3,2},{4,5},{5,4},{6,7},{7,6},{8,9},{9,8},{10,11... | collective-permute-start | bytes 1179656 | tf_op jit(solution)/shard_map/ppermute | solution.py:447
  37.7 23.6 %collective-permute-start.7 = (bf16[736,128]{1,0:T(8,128)(2,1)S(1)}, bf16[736,128]{1,0:T(8,128)(2,1)S(1)}, u32[]{:S(2)}, u32[]{:S(2)}) collective-permute-start(bf16[736,128]{1,0:T(8,128)(2,1)S(1)} %get-tuple-element.56), channel_id=1, source_target_pairs={{0,8},{8,0},{16,24},{24,16},{1,9},{9,1},{17,25},{25,17},{2,10},{10... | collective-permute-start | bytes 565256 | tf_op jit(solution)/shard_map/ppermute | solution.py:438
  41.9 21.4 %collective-permute-start.8 = (bf16[736,128]{1,0:T(8,128)(2,1)S(1)}, bf16[736,128]{1,0:T(8,128)(2,1)S(1)}, u32[]{:S(2)}, u32[]{:S(2)}) collective-permute-start(bf16[736,128]{1,0:T(8,128)(2,1)S(1)} %get-tuple-element.57), channel_id=1, source_target_pairs={{0,16},{8,24},{16,0},{24,8},{1,17},{9,25},{17,1},{25,9},{2,18},{10... | collective-permute-start | bytes 565256 | tf_op jit(solution)/shard_map/ppermute | solution.py:438
  43.9 19.4 %collective-permute-start.9 = (bf16[736,128]{1,0:T(8,128)(2,1)S(1)}, bf16[736,128]{1,0:T(8,128)(2,1)S(1)}, u32[]{:S(2)}, u32[]{:S(2)}) collective-permute-start(bf16[736,128]{1,0:T(8,128)(2,1)S(1)} %get-tuple-element.58), channel_id=1, source_target_pairs={{0,24},{8,16},{16,8},{24,0},{1,25},{9,17},{17,9},{25,1},{2,26},{10... | collective-permute-start | bytes 565256 | tf_op jit(solution)/shard_map/ppermute | solution.py:438
  45.3 11.9 %collective-permute-start.10 = (bf16[224,640]{1,0:T(8,128)(2,1)S(1)}, bf16[224,640]{1,0:T(8,128)(2,1)S(1)}, u32[]{:S(2)}, u32[]{:S(2)}) collective-permute-start(bf16[224,640]{1,0:T(8,128)(2,1)S(1)} %get-tuple-element.59), channel_id=1, source_target_pairs={{1,2},{2,1},{3,4},{4,3},{5,6},{6,5},{9,10},{10,9},{11,12},{12,11},... | collective-permute-start | bytes 860168 | tf_op jit(solution)/shard_map/ppermute | solution.py:448
  46.2 11.0 %collective-permute-start.11 = (bf16[224,640]{1,0:T(8,128)(2,1)S(1)}, bf16[224,640]{1,0:T(8,128)(2,1)S(1)}, u32[]{:S(2)}, u32[]{:S(2)}) collective-permute-start(bf16[224,640]{1,0:T(8,128)(2,1)S(1)} %get-tuple-element.60), channel_id=1, source_target_pairs={{0,1},{1,0},{2,3},{3,2},{4,5},{5,4},{6,7},{7,6},{8,9},{9,8},{10,11... | collective-permute-start | bytes 860168 | tf_op jit(solution)/shard_map/ppermute | solution.py:447
  58.8 9.6 %collective-permute-start.12 = (bf16[736,128]{1,0:T(8,128)(2,1)S(1)}, bf16[736,128]{1,0:T(8,128)(2,1)S(1)}, u32[]{:S(2)}, u32[]{:S(2)}) collective-permute-start(bf16[736,128]{1,0:T(8,128)(2,1)S(1)} %get-tuple-element.68), channel_id=1, source_target_pairs={{0,24},{8,16},{16,8},{24,0},{1,25},{9,17},{17,9},{25,1},{2,26},{10... | collective-permute-start | bytes 565256 | tf_op jit(solution)/shard_map/ppermute | solution.py:438
  61.3 16.6 %collective-permute-start.13 = (bf16[736,128]{1,0:T(8,128)(2,1)S(1)}, bf16[736,128]{1,0:T(8,128)(2,1)S(1)}, u32[]{:S(2)}, u32[]{:S(2)}) collective-permute-start(bf16[736,128]{1,0:T(8,128)(2,1)S(1)} %get-tuple-element.69), channel_id=1, source_target_pairs={{0,16},{8,24},{16,0},{24,8},{1,17},{9,25},{17,1},{25,9},{2,18},{10... | collective-permute-start | bytes 565256 | tf_op jit(solution)/shard_map/ppermute | solution.py:438
  61.3 16.6 %collective-permute-start.14 = (bf16[736,128]{1,0:T(8,128)(2,1)S(1)}, bf16[736,128]{1,0:T(8,128)(2,1)S(1)}, u32[]{:S(2)}, u32[]{:S(2)}) collective-permute-start(bf16[736,128]{1,0:T(8,128)(2,1)S(1)} %get-tuple-element.70), channel_id=1, source_target_pairs={{0,8},{8,0},{16,24},{24,16},{1,9},{9,1},{17,25},{25,17},{2,10},{10... | collective-permute-start | bytes 565256 | tf_op jit(solution)/shard_map/ppermute | solution.py:438

commit v9 on v8

--- a/solution.py
+++ b/solution.py
@@ -194,6 +194,7 @@
                 sums[way, tile, here, :] = totals[i]
             if len(ways) > 1:
                 sums[ALL, tile, here, :] = functools.reduce(jnp.add, totals)
+            yield
 
 
 def settle(sums, masks_ref, tiles, write):
@@ -223,6 +224,16 @@
             value = sums[ALL, tile, here, :] - a - b
             value = value - spread(masks_ref[0, tile]) * c - spread(masks_ref[1, tile]) * d
             write(tile, here, value)
+        yield
+
+
+def run(steps, beside=()):
+    beside = iter(beside)
+    for index, _ in enumerate(steps):
+        if index % 5 == 4:
+            next(beside, None)
+    for _ in beside:
+        pass
 
 
 def measure_plane(values, plane, tables_ref, weights_ref, faces_ref, mixed, sums, tiles):
@@ -239,34 +250,32 @@
         return weights_ref[plane, way, field, tile]
 
     mix(tables_ref, values, mixed)
-    weigh(values_of, face_of, ways, fields, sums, range(tiles))
-    weigh(values_of, face_of, (NEXT_X,), fields, sums, range(tiles, sums.shape[1]))
-
-
-def outer(low, high, tables_ref, weights_ref, masks_ref, faces_ref, low_out, high_out, middle_out, mixed, sums, tiles):
-    last = weights_ref.shape[0] - 1
-    for plane, values, out_ref, way in ((0, low, low_out, NEXT_Z), (last, high, high_out, LAST_Z)):
-        measure_plane(values, plane, tables_ref, weights_ref, faces_ref, mixed.at[min(plane, 1)], sums, tiles)
-
-        def write(tile, here, value):
-            out_ref[tile, here, :] = value
-            given = sums[way, tile, here, :]
-            middle_out[tile, here, :] = -given if plane == 0 else middle_out[tile, here, :] - given
-
-        settle(sums, masks_ref, tiles, write)
-
-
-def inner(
+    yield from weigh(values_of, face_of, ways, fields, sums, range(tiles))
+    yield from weigh(values_of, face_of, (NEXT_X,), fields, sums, range(tiles, sums.shape[1]))
+
+
+def side_steps(values, side, tables_ref, weights_ref, masks_ref, faces_ref, out_ref, middle_out, mixed, sums, tiles):
+    plane, way = (0, NEXT_Z) if side == 0 else (weights_ref.shape[0] - 1, LAST_Z)
+
+    def write(tile, here, value):
+        out_ref[tile, here, :] = value
+        given = sums[way, tile, here, :]
+        middle_out[tile, here, :] = -given if side == 0 else middle_out[tile, here, :] - given
+
+    measured = measure_plane(values, plane, tables_ref, weights_ref, faces_ref, mixed, sums, tiles)
+    return measured, settle(sums, masks_ref, tiles, write)
+
+
+def middle_steps(
     values, low_in, high_in, middle_in, tables_ref, weights_ref, masks_ref, low_out, high_out, out, mixed, sums, tiles
 ):
-    measure_plane(values, 1, tables_ref, weights_ref, None, mixed.at[0], sums, tiles)
-
     def write(tile, here, value):
         out[tile, here, :] = SCALE * (value + middle_in[tile, here, :])
         low_out[tile, here, :] = low_in[tile, here, :] - sums[LAST_Z, tile, here, :]
         high_out[tile, here, :] = high_in[tile, here, :] - sums[NEXT_Z, tile, here, :]
 
-    settle(sums, masks_ref, tiles, write)
+    measured = measure_plane(values, 1, tables_ref, weights_ref, None, mixed, sums, tiles)
+    return measured, settle(sums, masks_ref, tiles, write)
 
 
 def fill(result, masks_ref, out_ref):
@@ -333,26 +342,38 @@
     return images
 
 
-def outer_kernel(low_ref, high_ref, tables_ref, weights_ref, masks_ref, *outs):
-    rows = tables_ref.shape[1]
+def outer_kernel(low_ref, high_ref, tables_ref, weights_ref, masks_ref, low_out, high_out, middle_out, mixed, sums):
+    rows, tiles = tables_ref.shape[1], weights_ref.shape[3]
     shared = (tables_ref, weights_ref, masks_ref, None)
-    outer(low_ref[0:rows, :], high_ref[0:rows, :], *shared, *outs, weights_ref.shape[3])
+    low = side_steps(low_ref[0:rows, :], 0, *shared, low_out, middle_out, mixed.at[0], sums.at[0], tiles)
+    high = side_steps(high_ref[0:rows, :], 1, *shared, high_out, middle_out, mixed.at[1], sums.at[1], tiles)
+    run(low[0])
+    run(high[0], low[1])
+    run(high[1])
 
 
 def inner_kernel(count, *refs):
     parts = [part[1] if len(part.shape) == 3 else part[...] for part in refs[:count]]
     low_in, high_in, middle_in, tables_ref, weights_ref, masks_ref, *outs = refs[count:]
     low_out, high_out, middle_out, whole_ref, mixed, sums = outs
-    shared = (tables_ref, weights_ref, masks_ref, low_out, high_out, middle_out, mixed, sums)
-    inner(joined(parts), low_in, high_in, middle_in, *shared, weights_ref.shape[3])
+    shared = (tables_ref, weights_ref, masks_ref, low_out, high_out, middle_out, mixed.at[0], sums)
+    middle = middle_steps(joined(parts), low_in, high_in, middle_in, *shared, weights_ref.shape[3])
+    run(middle[0])
+    run(middle[1])
     fill(middle_out, masks_ref, whole_ref)
 
 
 def own_kernel(tiles, low_ref, values_ref, high_ref, tables_ref, weights_ref, masks_ref, faces_ref, *refs):
-    low_out, high_out, middle_out, mixed, sums, low, high, middle = refs
+    low_out, high_out, middle_out, mixed, sums, low_share, high_share, given = refs
     shared = (tables_ref, weights_ref, masks_ref)
-    outer(low_ref[...], high_ref[...], *shared, faces_ref, low, high, middle, mixed, sums, tiles)
-    inner(values_ref[...], low, high, middle, *shared, low_out, high_out, middle_out, mixed, sums, tiles)
+    low = side_steps(low_ref[...], 0, *shared, faces_ref, low_share, given, mixed.at[0], sums.at[0], tiles)
+    high = side_steps(high_ref[...], 1, *shared, faces_ref, high_share, given, mixed.at[1], sums.at[1], tiles)
+    ins, outs = (low_share, high_share, given), (low_out, high_out, middle_out)
+    middle = middle_steps(values_ref[...], *ins, *shared, *outs, mixed.at[0], sums.at[0], tiles)
+    run(low[0])
+    run(high[0], low[1])
+    run(middle[0], high[1])
+    run(middle[1])
 
 
 def first_fix_kernel(packing, turn_ref, *refs):
@@ -373,7 +394,7 @@
         def face_of(way, field, tile):
             return faces_ref[side, field, tile]
 
-        weigh(values_of, face_of, (0,), fields, sums, range(tiles))
+        run(weigh(values_of, face_of, (0,), fields, sums, range(tiles)))
         result = ends.at[lax.bitwise_xor(turn_ref[0], side)]
         for tile in range(tiles):
             result[tile] = SCALE * (share_refs[side][tile] + sums[0, tile])
@@ -395,7 +416,7 @@
         def face_of(way, field, tile):
             return faces_ref[side, field, tile]
 
-        weigh(values_of, face_of, (0,), fields, sums, range(tiles))
+        run(weigh(values_of, face_of, (0,), fields, sums, range(tiles)))
         result = ends.at[lax.bitwise_xor(turn_ref[0], side)]
         for tile in range(tiles):
             result[tile] = SCALE * (share_refs[side][tile] - sums[0, tile])
@@ -524,7 +545,7 @@
         6,
         [share] * 3 + [shape(2, tiles, fields * rows, LANES)],
         (low, high, *common),
-        scratch(tiles)[1:],
+        [VMEM((2, 7, tiles, rows, LANES), F32)],
     )
     low, high, middle, middle_whole = call(
         functools.partial(inner_kernel, count),
@@ -554,7 +575,7 @@
         8,
         [share] * 3,
         (low, middle_whole, high, *common, faces),
-        scratch(tiles) + [VMEM((tiles, rows, LANES), F32)] * 3,
+        scratch(tiles)[:1] + [VMEM((2, 7, tiles, rows, LANES), F32)] + [VMEM((tiles, rows, LANES), F32)] * 3,
     )
     second = call(
         functools.partial(last_fix_kernel, packing),

time: 79.4 us -> 79.4 us (level)
  no operation moved by 1% of the time
where the time goes in v9:
time: 79.4 us; the launch traced here: 79.1 us
  Pallas kernels  29.6 us (37%)
  starting transfers between devices  28.2 us (36%)
  waiting for transfers between devices  16.5 us (21%)
  local copies, waits for them, and re-layouts  3.78 us (5%)
  between operations  0.87 us (1%)
    pallas_call x11, Pallas kernels, call(): pl.pallas_call(kernel, out_shape=out_shape, in_specs=in_specs, out_specs=...  29.6 us
    ppermute x11, starting transfers between devices, exchange(): return lax.ppermute(block, 'chaos', [(i, i ^ step) for i in range(count)])  20.7 us
    ppermute x11, waiting for transfers between devices, exchange(): return lax.ppermute(block, 'chaos', [(i, i ^ step) for i in range(count)])  16.5 us
    ppermute x2, starting transfers between devices, neighbours(): after = lax.ppermute(last_plane, 'space', pairs)  5.79 us
    unnamed x7, local copies, waits for them, and re-layouts  2.11 us
    ppermute x2, starting transfers between devices, neighbours(): return (lax.ppermute(first_plane, 'space', others), after)  1.75 us
  transfers between devices with their start and end apart: 15, of which 3 were waited for; matrix products, arithmetic and copies ran while one was open for 4% of the time, Pallas kernels for 32%

profile of v9, /device:TPU:0, one launch (start us, length us, event | category | flops | bytes accessed | tf_op | source)
XLA Modules:
  0.0 79.1 jit_solution(1674314200768353269)
XLA Ops:
  0.7 1.1 %copy-done = bf16[53,3,2304]{2,0,1:T(8,128)(2,1)S(1)} copy-done((bf16[53,3,2304]{2,0,1:T(8,128)(2,1)S(1)}, bf16[53,3,2304]{2,0,1:T(8,128)(2,1)}, u32[]{:S(2)}) %copy-start) | copy-done | bytes 732696
  1.8 0.8 %cut.1 = (bf16[3,56,768]{2,1,0:T(8,128)(2,1)S(1)}, bf16[3,56,768]{2,1,0:T(8,128)(2,1)S(1)}, bf16[2,56,768]{2,1,0:T(8,128)(2,1)S(1)}, bf16[2,56,768]{2,1,0:T(8,12...) custom-call(s32[1]{0:T(128)} %bitcast.me_ref, bf16[3,53,2304]{2,1,0:T(8,128)(2,1)S(1)} %bitcast.10), custom_call_target="tpu_custom_call" | custom-call | flops 1100000000 | bytes 3600000 | tf_op jit(solution)/shard_map/cut/pallas_call | solution.py:30
  2.6 4.1 %collective-permute-start.1 = (bf16[2,56,768]{2,1,0:T(8,128)(2,1)S(1)}, bf16[2,56,768]{2,1,0:T(8,128)(2,1)S(1)}, u32[]{:S(2)}, u32[]{:S(2)}) collective-permute-start(bf16[2,56,768]{2,1,0:T(8,128)(2,1)S(1)} %get-tuple-element.39), channel_id=1, source_target_pairs={{0,16},{8,24},{16,0},{24,8},{1,17},{9,25},{17,1},{25,9},{2,18},{10... | collective-permute-start | bytes 516104 | tf_op jit(solution)/shard_map/ppermute | solution.py:459
  6.7 1.4 %collective-permute-start.2 = (bf16[2,56,768]{2,1,0:T(8,128)(2,1)S(1)}, bf16[2,56,768]{2,1,0:T(8,128)(2,1)S(1)}, u32[]{:S(2)}, u32[]{:S(2)}) collective-permute-start(bf16[2,56,768]{2,1,0:T(8,128)(2,1)S(1)} %get-tuple-element.40), channel_id=1, source_target_pairs={{0,24},{8,16},{16,8},{24,0},{1,25},{9,17},{17,9},{25,1},{2,26},{10... | collective-permute-start | bytes 516104 | tf_op jit(solution)/shard_map/ppermute | solution.py:459
  8.1 0.2 collective-permute-start
  8.4 0.7 broadcast_in_dim.15.products_ref
  9.1 0.8 broadcast_in_dim.14
  9.9 1.0 %copy.10 = f32[6,3,2304]{2,0,1:T(8,128)S(1)} copy(f32[6,3,2304]{2,1,0:T(4,128)} %param.8) | data formatting | bytes 331776 | tf_op args[2]
  10.8 0.1 pad_maximum_fusion
  10.9 0.1 pad_dynamic-slice_fusion.1
  11.0 0.1 pad_dynamic-slice_fusion
  11.1 5.1 %tables.1.refs_2_.refs_4_.tables_ref.refs_7_.refs_5_ = bf16[1568,224]{1,0:T(8,128)(2,1)S(1)} custom-call(s32[1]{0:T(128)} %bitcast.me_ref, s32[3,1218]{1,0:T(4,128)S(1)} %bitcast.11, f32[1,1218]{1,0:T(1,128)S(1)} %broadcast_in_dim.15.products_ref, s32[1,210]{1,0:T(1,128)S(1)} %bitcast.12, bf16[3,56,768]{2,1,0:T(8,128)(2,1)S(1)} %get-tuple-element.37._.refs_0_), custom_call_target="tpu_custom_call" | custom-call | flops 5500000256 | bytes 18000000 | tf_op jit(solution)/shard_map/tables/pallas_call | solution.py:30
  16.3 0.1 pad_maximum_fusion.1.conduct_ref.refs_2_
  16.4 3.0 %collective-permute-done.1.refs_3_.refs_2_ = bf16[2,56,768]{2,1,0:T(8,128)(2,1)S(1)} collective-permute-done((bf16[2,56,768]{2,1,0:T(8,128)(2,1)S(1)}, bf16[2,56,768]{2,1,0:T(8,128)(2,1)S(1)}, u32[]{:S(2)}, u32[]{:S(2)}) %collective-permute-start.1) | collective-permute-done | bytes 172064 | tf_op jit(solution)/shard_map/ppermute | solution.py:459
  19.4 0.2 weights.1
  19.6 0.1 collective-permute-start.5
  19.7 2.9 %collective-permute-start.6 = (bf16[56,768]{1,0:T(8,128)(2,1)S(1)}, bf16[56,768]{1,0:T(8,128)(2,1)S(1)}, u32[]{:S(2)}, u32[]{:S(2)}) collective-permute-start(bf16[56,768]{1,0:T(8,128)(2,1)S(1)} %get-tuple-element.48), channel_id=1, source_target_pairs={{0,24},{8,16},{16,8},{24,0},{1,25},{9,17},{17,9},{25,1},{2,26},{10... | collective-permute-start | bytes 258056 | tf_op jit(solution)/shard_map/ppermute | solution.py:459
  22.5 0.0 collective-permute-done.2.refs_3_
  22.6 0.0 collective-permute-done.refs_1_
  22.6 0.1 gather.1
  22.6 0.9 %collective-permute-start.3 = (bf16[256,768]{1,0:T(8,128)(2,1)S(1)}, bf16[256,768]{1,0:T(8,128)(2,1)S(1)}, u32[]{:S(2)}, u32[]{:S(2)}) collective-permute-start(bf16[256,768]{1,0:T(8,128)(2,1)S(1)} %get-tuple-element.44.low_ref), channel_id=1, source_target_pairs={{1,2},{2,1},{3,4},{4,3},{5,6},{6,5},{9,10},{10,9},{11,12},{12,11},... | collective-permute-start | bytes 1179656 | tf_op jit(solution)/shard_map/ppermute | solution.py:469
  23.5 2.9 %collective-permute-start.4 = (bf16[256,768]{1,0:T(8,128)(2,1)S(1)}, bf16[256,768]{1,0:T(8,128)(2,1)S(1)}, u32[]{:S(2)}, u32[]{:S(2)}) collective-permute-start(bf16[256,768]{1,0:T(8,128)(2,1)S(1)} %get-tuple-element.45.high_ref), channel_id=1, source_target_pairs={{0,1},{1,0},{2,3},{3,2},{4,5},{5,4},{6,7},{7,6},{8,9},{9,8},{10,11... | collective-permute-start | bytes 1179656 | tf_op jit(solution)/shard_map/ppermute | solution.py:468
  26.4 5.4 %outer.1 = (f32[6,224,128]{2,1,0:T(8,128)S(1)}, f32[6,224,128]{2,1,0:T(8,128)S(1)}, f32[6,224,128]{2,1,0:T(8,128)S(1)}, bf16[2,6,1568,128]{3,2,1,0:T(8,128)(2,1)S(1)}) custom-call(bf16[256,768]{1,0:T(8,128)(2,1)S(1)} %get-tuple-element.44.low_ref, bf16[256,768]{1,0:T(8,128)(2,1)S(1)} %get-tuple-element.45.high_ref, ...), custom_call_target="tpu_custom_call" | custom-call | flops 6600000000 | bytes 21600000 | tf_op jit(solution)/shard_map/outer/pallas_call | solution.py:30
  31.8 0.0 collective-permute-done.5.refs_2_
  31.8 0.0 collective-permute-done.6.refs_3_
  31.8 3.3 %inner.1 = (f32[6,224,128]{2,1,0:T(8,128)S(1)}, f32[6,224,128]{2,1,0:T(8,128)S(1)}, f32[6,224,128]{2,1,0:T(8,128)S(1)}, bf16[224,768]{1,0:T(8,128)(2,1)S(1)}) custom-call(bf16[3,56,768]{2,1,0:T(8,128)(2,1)S(1)} %get-tuple-element.37._.refs_0_, bf16[3,56,768]{2,1,0:T(8,128)(2,1)S(1)} %collective-permute-done.refs_1_, ...), custom_call_target="tpu_custom_call" | custom-call | flops 3300000000 | bytes 10800000 | tf_op jit(solution)/shard_map/inner/pallas_call | solution.py:30
  35.1 0.0 collective-permute-done.3.refs_0_
  35.1 0.0 collective-permute-done.4.refs_1_
  35.1 2.6 %fix.1 = (bf16[224,768]{1,0:T(8,128)(2,1)S(1)}, bf16[224,768]{1,0:T(8,128)(2,1)S(1)}, bf16[224,640]{1,0:T(8,128)(2,1)S(1)}, bf16[224,640]{1,0:T(8,128)(2,1)S(1)}...) custom-call(s32[1]{0:T(128)} %bitcast.1.turn_ref, ...), custom_call_target="tpu_custom_call" | custom-call | flops 3300000000 | bytes 10800000 | tf_op jit(solution)/shard_map/fix/pallas_call | solution.py:30
  37.7 4.2 %collective-permute-start.7 = (bf16[736,128]{1,0:T(8,128)(2,1)S(1)}, bf16[736,128]{1,0:T(8,128)(2,1)S(1)}, u32[]{:S(2)}, u32[]{:S(2)}) collective-permute-start(bf16[736,128]{1,0:T(8,128)(2,1)S(1)} %get-tuple-element.56), channel_id=1, source_target_pairs={{0,8},{8,0},{16,24},{24,16},{1,9},{9,1},{17,25},{25,17},{2,10},{10... | collective-permute-start | bytes 565256 | tf_op jit(solution)/shard_map/ppermute | solution.py:459
  41.9 2.1 %collective-permute-start.8 = (bf16[736,128]{1,0:T(8,128)(2,1)S(1)}, bf16[736,128]{1,0:T(8,128)(2,1)S(1)}, u32[]{:S(2)}, u32[]{:S(2)}) collective-permute-start(bf16[736,128]{1,0:T(8,128)(2,1)S(1)} %get-tuple-element.57), channel_id=1, source_target_pairs={{0,16},{8,24},{16,0},{24,8},{1,17},{9,25},{17,1},{25,9},{2,18},{10... | collective-permute-start | bytes 565256 | tf_op jit(solution)/shard_map/ppermute | solution.py:459
  43.9 1.4 %collective-permute-start.9 = (bf16[736,128]{1,0:T(8,128)(2,1)S(1)}, bf16[736,128]{1,0:T(8,128)(2,1)S(1)}, u32[]{:S(2)}, u32[]{:S(2)}) collective-permute-start(bf16[736,128]{1,0:T(8,128)(2,1)S(1)} %get-tuple-element.58), channel_id=1, source_target_pairs={{0,24},{8,16},{16,8},{24,0},{1,25},{9,17},{17,9},{25,1},{2,26},{10... | collective-permute-start | bytes 565256 | tf_op jit(solution)/shard_map/ppermute | solution.py:459
  45.3 0.9 %collective-permute-start.10 = (bf16[224,640]{1,0:T(8,128)(2,1)S(1)}, bf16[224,640]{1,0:T(8,128)(2,1)S(1)}, u32[]{:S(2)}, u32[]{:S(2)}) collective-permute-start(bf16[224,640]{1,0:T(8,128)(2,1)S(1)} %get-tuple-element.59), channel_id=1, source_target_pairs={{1,2},{2,1},{3,4},{4,3},{5,6},{6,5},{9,10},{10,9},{11,12},{12,11},... | collective-permute-start | bytes 860168 | tf_op jit(solution)/shard_map/ppermute | solution.py:469
  46.2 2.9 %collective-permute-start.11 = (bf16[224,640]{1,0:T(8,128)(2,1)S(1)}, bf16[224,640]{1,0:T(8,128)(2,1)S(1)}, u32[]{:S(2)}, u32[]{:S(2)}) collective-permute-start(bf16[224,640]{1,0:T(8,128)(2,1)S(1)} %get-tuple-element.60), channel_id=1, source_target_pairs={{0,1},{1,0},{2,3},{3,2},{4,5},{5,4},{6,7},{7,6},{8,9},{9,8},{10,11... | collective-permute-start | bytes 860168 | tf_op jit(solution)/shard_map/ppermute | solution.py:468
  49.1 8.1 %second.1 = (f32[6,224,128]{2,1,0:T(8,128)S(1)}, f32[6,224,128]{2,1,0:T(8,128)S(1)}, f32[6,224,128]{2,1,0:T(8,128)S(1)}) custom-call(bf16[224,768]{1,0:T(8,128)(2,1)S(1)} %get-tuple-element.61.low_ref, bf16[224,768]{1,0:T(8,128)(2,1)S(1)} %get-tuple-element.62.values_ref, bf16[224,768]{1,0:T(8,128)(2,1)S(1)} %get-tuple-element.63.high_ref, ...), custom_call_target="tpu_custom_call" | custom-call | flops 8800000000 | bytes 28800000 | tf_op jit(solution)/shard_map/second/pallas_call | solution.py:30
  57.2 0.0 collective-permute-done.10.refs_0_
  57.3 0.0 collective-permute-done.11.refs_1_
  57.3 1.6 %last.1 = (bf16[736,128]{1,0:T(8,128)(2,1)S(1)}, bf16[736,128]{1,0:T(8,128)(2,1)S(1)}, bf16[736,128]{1,0:T(8,128)(2,1)S(1)}, bf16[736,128]{1,0:T(8,128)(2,1)S(1)}) custom-call(s32[1]{0:T(128)} %bitcast.1.turn_ref, bf16[224,640]{1,0:T(8,128)(2,1)S(1)} %collective-permute-done.10.refs_0_, bf16[224,640]{1,0:T(8,128)(2,1)S(1)} %collective-permute-done.11.refs_1_, ...), custom_call_target="tpu_custom_call" | custom-call | flops 3300000000 | bytes 10800000 | tf_op jit(solution)/shard_map/last/pallas_call | solution.py:30
  58.9 2.5 %collective-permute-start.12 = (bf16[736,128]{1,0:T(8,128)(2,1)S(1)}, bf16[736,128]{1,0:T(8,128)(2,1)S(1)}, u32[]{:S(2)}, u32[]{:S(2)}) collective-permute-start(bf16[736,128]{1,0:T(8,128)(2,1)S(1)} %get-tuple-element.68), channel_id=1, source_target_pairs={{0,24},{8,16},{16,8},{24,0},{1,25},{9,17},{17,9},{25,1},{2,26},{10... | collective-permute-start | bytes 565256 | tf_op jit(solution)/shard_map/ppermute | solution.py:459
  61.4 0.0 collective-permute-start.13
  61.4 0.0 collective-permute-done.7.refs_1_
  61.4 1.9 %collective-permute-start.14 = (bf16[736,128]{1,0:T(8,128)(2,1)S(1)}, bf16[736,128]{1,0:T(8,128)(2,1)S(1)}, u32[]{:S(2)}, u32[]{:S(2)}) collective-permute-start(bf16[736,128]{1,0:T(8,128)(2,1)S(1)} %get-tuple-element.70), channel_id=1, source_target_pairs={{0,8},{8,0},{16,24},{24,16},{1,9},{9,1},{17,25},{25,17},{2,10},{10... | collective-permute-start | bytes 565256 | tf_op jit(solution)/shard_map/ppermute | solution.py:459
  63.3 0.0 collective-permute-done.8.refs_2_
  63.3 1.2 %join.2 = bf16[3,53,2304]{2,1,0:T(8,128)(2,1)} custom-call(s32[1]{0:T(128)} %bitcast.me_ref, bf16[736,128]{1,0:T(8,128)(2,1)S(1)} %get-tuple-element.55.refs_0_, bf16[736,128]{1,0:T(8,128)(2,1)S(1)} %collective-permute-done.7.refs_1_, bf16[736,128]{1,0:T(8,128)(2,1)S(1)} %collective-permute-done.8.refs_2_, bf16[736,128]{1,0:T(8,128)(2,1)S(1)} %collective-permute-done.9.refs_3_), custom_call_target="tpu_custom_call" | custom-call | flops 1100000000 | bytes 3600000 | tf_op jit(solution)/shard_map/join/pallas_call | solution.py:30
  64.5 4.0 %collective-permute-done.12.refs_0_ = bf16[736,128]{1,0:T(8,128)(2,1)S(1)} collective-permute-done((bf16[736,128]{1,0:T(8,128)(2,1)S(1)}, bf16[736,128]{1,0:T(8,128)(2,1)S(1)}, u32[]{:S(2)}, u32[]{:S(2)}) %collective-permute-start.12) | collective-permute-done | bytes 188448 | tf_op jit(solution)/shard_map/ppermute | solution.py:459
  68.5 9.5 %collective-permute-done.13.refs_1_ = bf16[736,128]{1,0:T(8,128)(2,1)S(1)} collective-permute-done((bf16[736,128]{1,0:T(8,128)(2,1)S(1)}, bf16[736,128]{1,0:T(8,128)(2,1)S(1)}, u32[]{:S(2)}, u32[]{:S(2)}) %collective-permute-start.13) | collective-permute-done | bytes 188448 | tf_op jit(solution)/shard_map/ppermute | solution.py:459
  78.0 0.0 collective-permute-done.14.refs_2_
  78.0 1.2 %join.3 = bf16[3,53,2304]{2,1,0:T(8,128)(2,1)} custom-call(s32[1]{0:T(128)} %bitcast.me_ref, bf16[736,128]{1,0:T(8,128)(2,1)S(1)} %collective-permute-done.12.refs_0_, bf16[736,128]{1,0:T(8,128)(2,1)S(1)} %collective-permute-done.13.refs_1_, bf16[736,128]{1,0:T(8,128)(2,1)S(1)} %collective-permute-done.14.refs_2_, bf16[736,128]{1,0:T(8,128)(2,1)S(1)} %get-tuple-element.71.refs_3_), custom_call_target="tpu_custom_call" | custom-call | flops 1100000000 | bytes 3600000 | tf_op jit(solution)/shard_map/join/pallas_call | solution.py:30
  (11 shorter events, 0.1 us)
Async XLA Ops:
  0.6 10.5 %copy-start.2 = (s32[210]{0:T(256)S(1)}, s32[210]{0:T(256)}, u32[]{:S(2)}) copy-start(s32[210]{0:T(256)} %param.11) | copy-start | bytes 2524
  0.6 1.1 %copy-start = (bf16[53,3,2304]{2,0,1:T(8,128)(2,1)S(1)}, bf16[53,3,2304]{2,0,1:T(8,128)(2,1)}, u32[]{:S(2)}) copy-start(bf16[53,3,2304]{2,0,1:T(8,128)(2,1)} %param.6) | copy-start | bytes 2198020
  1.8 9.3 %copy-start.1 = (s32[1218,3]{0,1:T(4,128)S(1)}, s32[1218,3]{0,1:T(4,128)}, u32[]{:S(2)}) copy-start(s32[1218,3]{0,1:T(4,128)} %param.10) | copy-start | bytes 43852
  2.6 16.7 %collective-permute-start.1 = (bf16[2,56,768]{2,1,0:T(8,128)(2,1)S(1)}, bf16[2,56,768]{2,1,0:T(8,128)(2,1)S(1)}, u32[]{:S(2)}, u32[]{:S(2)}) collective-permute-start(bf16[2,56,768]{2,1,0:T(8,128)(2,1)S(1)} %get-tuple-element.39), channel_id=1, source_target_pairs={{0,16},{8,24},{16,0},{24,8},{1,17},{9,25},{17,1},{25,9},{2,18},{10... | collective-permute-start | bytes 516104 | tf_op jit(solution)/shard_map/ppermute | solution.py:459
  6.7 15.8 %collective-permute-start.2 = (bf16[2,56,768]{2,1,0:T(8,128)(2,1)S(1)}, bf16[2,56,768]{2,1,0:T(8,128)(2,1)S(1)}, u32[]{:S(2)}, u32[]{:S(2)}) collective-permute-start(bf16[2,56,768]{2,1,0:T(8,128)(2,1)S(1)} %get-tuple-element.40), channel_id=1, source_target_pairs={{0,24},{8,16},{16,8},{24,0},{1,25},{9,17},{17,9},{25,1},{2,26},{10... | collective-permute-start | bytes 516104 | tf_op jit(solution)/shard_map/ppermute | solution.py:459
  8.1 14.5 %collective-permute-start = (bf16[3,56,768]{2,1,0:T(8,128)(2,1)S(1)}, bf16[3,56,768]{2,1,0:T(8,128)(2,1)S(1)}, u32[]{:S(2)}, u32[]{:S(2)}) collective-permute-start(bf16[3,56,768]{2,1,0:T(8,128)(2,1)S(1)} %get-tuple-element.38), channel_id=1, source_target_pairs={{0,8},{8,0},{16,24},{24,16},{1,9},{9,1},{17,25},{25,17},{2,10},{10... | collective-permute-start | bytes 774152 | tf_op jit(solution)/shard_map/ppermute | solution.py:459
  19.6 12.2 %collective-permute-start.5 = (bf16[56,768]{1,0:T(8,128)(2,1)S(1)}, bf16[56,768]{1,0:T(8,128)(2,1)S(1)}, u32[]{:S(2)}, u32[]{:S(2)}) collective-permute-start(bf16[56,768]{1,0:T(8,128)(2,1)S(1)} %get-tuple-element.47), channel_id=1, source_target_pairs={{0,16},{8,24},{16,0},{24,8},{1,17},{9,25},{17,1},{25,9},{2,18},{10... | collective-permute-start | bytes 258056 | tf_op jit(solution)/shard_map/ppermute | solution.py:459
  19.7 12.1 %collective-permute-start.6 = (bf16[56,768]{1,0:T(8,128)(2,1)S(1)}, bf16[56,768]{1,0:T(8,128)(2,1)S(1)}, u32[]{:S(2)}, u32[]{:S(2)}) collective-permute-start(bf16[56,768]{1,0:T(8,128)(2,1)S(1)} %get-tuple-element.48), channel_id=1, source_target_pairs={{0,24},{8,16},{16,8},{24,0},{1,25},{9,17},{17,9},{25,1},{2,26},{10... | collective-permute-start | bytes 258056 | tf_op jit(solution)/shard_map/ppermute | solution.py:459
  22.6 12.5 %collective-permute-start.3 = (bf16[256,768]{1,0:T(8,128)(2,1)S(1)}, bf16[256,768]{1,0:T(8,128)(2,1)S(1)}, u32[]{:S(2)}, u32[]{:S(2)}) collective-permute-start(bf16[256,768]{1,0:T(8,128)(2,1)S(1)} %get-tuple-element.44.low_ref), channel_id=1, source_target_pairs={{1,2},{2,1},{3,4},{4,3},{5,6},{6,5},{9,10},{10,9},{11,12},{12,11},... | collective-permute-start | bytes 1179656 | tf_op jit(solution)/shard_map/ppermute | solution.py:469
  23.5 11.6 %collective-permute-start.4 = (bf16[256,768]{1,0:T(8,128)(2,1)S(1)}, bf16[256,768]{1,0:T(8,128)(2,1)S(1)}, u32[]{:S(2)}, u32[]{:S(2)}) collective-permute-start(bf16[256,768]{1,0:T(8,128)(2,1)S(1)} %get-tuple-element.45.high_ref), channel_id=1, source_target_pairs={{0,1},{1,0},{2,3},{3,2},{4,5},{5,4},{6,7},{7,6},{8,9},{9,8},{10,11... | collective-permute-start | bytes 1179656 | tf_op jit(solution)/shard_map/ppermute | solution.py:468
  37.7 23.7 %collective-permute-start.7 = (bf16[736,128]{1,0:T(8,128)(2,1)S(1)}, bf16[736,128]{1,0:T(8,128)(2,1)S(1)}, u32[]{:S(2)}, u32[]{:S(2)}) collective-permute-start(bf16[736,128]{1,0:T(8,128)(2,1)S(1)} %get-tuple-element.56), channel_id=1, source_target_pairs={{0,8},{8,0},{16,24},{24,16},{1,9},{9,1},{17,25},{25,17},{2,10},{10... | collective-permute-start | bytes 565256 | tf_op jit(solution)/shard_map/ppermute | solution.py:459
  41.9 21.5 %collective-permute-start.8 = (bf16[736,128]{1,0:T(8,128)(2,1)S(1)}, bf16[736,128]{1,0:T(8,128)(2,1)S(1)}, u32[]{:S(2)}, u32[]{:S(2)}) collective-permute-start(bf16[736,128]{1,0:T(8,128)(2,1)S(1)} %get-tuple-element.57), channel_id=1, source_target_pairs={{0,16},{8,24},{16,0},{24,8},{1,17},{9,25},{17,1},{25,9},{2,18},{10... | collective-permute-start | bytes 565256 | tf_op jit(solution)/shard_map/ppermute | solution.py:459
  43.9 19.4 %collective-permute-start.9 = (bf16[736,128]{1,0:T(8,128)(2,1)S(1)}, bf16[736,128]{1,0:T(8,128)(2,1)S(1)}, u32[]{:S(2)}, u32[]{:S(2)}) collective-permute-start(bf16[736,128]{1,0:T(8,128)(2,1)S(1)} %get-tuple-element.58), channel_id=1, source_target_pairs={{0,24},{8,16},{16,8},{24,0},{1,25},{9,17},{17,9},{25,1},{2,26},{10... | collective-permute-start | bytes 565256 | tf_op jit(solution)/shard_map/ppermute | solution.py:459
  45.3 11.9 %collective-permute-start.10 = (bf16[224,640]{1,0:T(8,128)(2,1)S(1)}, bf16[224,640]{1,0:T(8,128)(2,1)S(1)}, u32[]{:S(2)}, u32[]{:S(2)}) collective-permute-start(bf16[224,640]{1,0:T(8,128)(2,1)S(1)} %get-tuple-element.59), channel_id=1, source_target_pairs={{1,2},{2,1},{3,4},{4,3},{5,6},{6,5},{9,10},{10,9},{11,12},{12,11},... | collective-permute-start | bytes 860168 | tf_op jit(solution)/shard_map/ppermute | solution.py:469
  46.2 11.1 %collective-permute-start.11 = (bf16[224,640]{1,0:T(8,128)(2,1)S(1)}, bf16[224,640]{1,0:T(8,128)(2,1)S(1)}, u32[]{:S(2)}, u32[]{:S(2)}) collective-permute-start(bf16[224,640]{1,0:T(8,128)(2,1)S(1)} %get-tuple-element.60), channel_id=1, source_target_pairs={{0,1},{1,0},{2,3},{3,2},{4,5},{5,4},{6,7},{7,6},{8,9},{9,8},{10,11... | collective-permute-start | bytes 860168 | tf_op jit(solution)/shard_map/ppermute | solution.py:468
  58.9 9.6 %collective-permute-start.12 = (bf16[736,128]{1,0:T(8,128)(2,1)S(1)}, bf16[736,128]{1,0:T(8,128)(2,1)S(1)}, u32[]{:S(2)}, u32[]{:S(2)}) collective-permute-start(bf16[736,128]{1,0:T(8,128)(2,1)S(1)} %get-tuple-element.68), channel_id=1, source_target_pairs={{0,24},{8,16},{16,8},{24,0},{1,25},{9,17},{17,9},{25,1},{2,26},{10... | collective-permute-start | bytes 565256 | tf_op jit(solution)/shard_map/ppermute | solution.py:459
  61.4 16.6 %collective-permute-start.13 = (bf16[736,128]{1,0:T(8,128)(2,1)S(1)}, bf16[736,128]{1,0:T(8,128)(2,1)S(1)}, u32[]{:S(2)}, u32[]{:S(2)}) collective-permute-start(bf16[736,128]{1,0:T(8,128)(2,1)S(1)} %get-tuple-element.69), channel_id=1, source_target_pairs={{0,16},{8,24},{16,0},{24,8},{1,17},{9,25},{17,1},{25,9},{2,18},{10... | collective-permute-start | bytes 565256 | tf_op jit(solution)/shard_map/ppermute | solution.py:459
  61.4 16.6 %collective-permute-start.14 = (bf16[736,128]{1,0:T(8,128)(2,1)S(1)}, bf16[736,128]{1,0:T(8,128)(2,1)S(1)}, u32[]{:S(2)}, u32[]{:S(2)}) collective-permute-start(bf16[736,128]{1,0:T(8,128)(2,1)S(1)} %get-tuple-element.70), channel_id=1, source_target_pairs={{0,8},{8,0},{16,24},{24,16},{1,9},{9,1},{17,25},{25,17},{2,10},{10... | collective-permute-start | bytes 565256 | tf_op jit(solution)/shard_map/ppermute | solution.py:459

commit v10 on v9

--- a/solution.py
+++ b/solution.py
@@ -23,15 +23,15 @@
     return -(-value // step) * step
 
 
-def call(kernel, name, micros, out_shape, args, scratch=(), scalars=0, unread=0):
+def call(kernel, name, micros, out_shape, args, scratch=(), scalars=0, unread=0, space=pl.ANY, out_space=VMEM):
     in_specs = [pl.BlockSpec(memory_space=pltpu.SMEM)] * scalars
     in_specs += [pl.BlockSpec(memory_space=VMEM)] * (len(args) - scalars - unread)
-    in_specs += [pl.BlockSpec(memory_space=pl.ANY)] * unread
+    in_specs += [pl.BlockSpec(memory_space=space)] * unread
     return pl.pallas_call(
         kernel,
         out_shape=out_shape,
         in_specs=in_specs,
-        out_specs=[pl.BlockSpec(memory_space=VMEM)] * len(out_shape),
+        out_specs=[pl.BlockSpec(memory_space=out_space)] * len(out_shape),
         scratch_shapes=scratch,
         compiler_params=pltpu.CompilerParams(vmem_limit_bytes=40 << 20),
         cost_estimate=pl.CostEstimate(flops=int(micros * 1.1e9), bytes_accessed=int(micros * 3.6e6), transcendentals=0),
@@ -40,15 +40,19 @@
 
 
 def cut_kernel(count, chunk, me_ref, x_ref, *refs):
-    out_refs, middle_refs, held = refs[:count], refs[count:-1], refs[-1]
+    out_refs, middle_refs, (held, fetched, arrived) = refs[:count], refs[count:-3], refs[-3:]
     planes, own, cells = x_ref.shape
+    copies = [pltpu.make_async_copy(x_ref.at[i], fetched.at[i], arrived.at[i]) for i in range(planes)]
+    for copy in copies:
+        copy.start()
     _, padded, width = out_refs[0].shape
     halo = REACH * NXY
     me = me_ref[0]
     held[...] = jnp.zeros_like(held)
     lane = lax.broadcasted_iota(jnp.int32, (padded, LANES), 1)
     for plane in range(planes):
-        held[0:own, :] = x_ref[plane].astype(F32)
+        copies[plane].wait()
+        held[0:own, :] = fetched[plane].astype(F32)
         values = held[...]
         for target in range(count):
             turned = values if target == 0 else pltpu.roll(values, cells - target * chunk, 1)
@@ -424,7 +428,7 @@
 
 
 def join_kernel(count, packing, order, me_ref, *refs):
-    out_ref, held = refs[count:]
+    out_ref, held, ready, sent = refs[count:]
     full, odd, beside = packing.full, packing.odd, packing.beside
     me = me_ref[0]
     for step, piece_ref in zip(order, refs):
@@ -437,7 +441,10 @@
             if odd:
                 spot = plane % beside
                 parts.append(images[packing.planes * full + plane // beside][:, spot * odd : (spot + 1) * odd])
-        out_ref[plane] = jnp.concatenate(parts, axis=1)[: packing.own].astype(BF16)
+        ready[plane] = jnp.concatenate(parts, axis=1)[: packing.own].astype(BF16)
+        pltpu.make_async_copy(ready.at[plane], out_ref.at[plane], sent.at[plane]).start()
+    for plane in range(packing.planes):
+        pltpu.make_async_copy(ready.at[plane], out_ref.at[plane], sent.at[plane]).wait()
 
 
 def shards(panels, mean_field, fluctuations, products, triples, owner_slot):
@@ -478,9 +485,11 @@
         1,
         [shape(planes if step < joint else 2, padded, width) for step in range(count)]
         + [shape(padded, width)] * (count - joint),
-        (me_alone, jnp.transpose(panels, (1, 0, 2))),
-        [VMEM((padded, cells), F32)],
+        (me_alone, pltpu.with_memory_space_constraint(jnp.transpose(panels, (1, 0, 2)), pltpu.HBM)),
+        [VMEM((padded, cells), F32), VMEM((planes, own, cells), BF16), pltpu.SemaphoreType.DMA((planes,))],
         scalars=1,
+        unread=1,
+        space=pltpu.HBM,
     )
     parts = exchanged(cut[:count])
 
@@ -595,8 +604,13 @@
             1,
             [shape(planes, own, cells)],
             (me_alone, *(parts[step] for step in order)),
-            [VMEM((count,) + parts[0].shape, F32)],
+            [
+                VMEM((count,) + parts[0].shape, F32),
+                VMEM((planes, own, cells), BF16),
+                pltpu.SemaphoreType.DMA((planes,)),
+            ],
             scalars=1,
+            out_space=pl.ANY,
         )
         return jnp.transpose(result, (1, 0, 2))
 

time: 79.4 us -> 79.4 us (level)
  local copies, waits for them, and re-layouts: 3.78 us -> 2.66 us
  Pallas kernels: 29.6 us -> 30.5 us
    unnamed x7 -> x5, local copies, waits for them, and re-layouts: 2.11 us -> 0.99 us
    pallas_call x11, Pallas kernels: 29.6 us -> 30.5 us  [call(): pl.pallas_call(kernel, out_shape=out_shape, in_specs=in_specs, out_specs=...]
where the time goes in v10:
time: 79.4 us; the launch traced here: 79.1 us
  Pallas kernels  30.5 us (38%)
  starting transfers between devices  28.2 us (36%)
  waiting for transfers between devices  16.5 us (21%)
  local copies, waits for them, and re-layouts  2.66 us (3%)
  between operations  1.05 us (1%)
    pallas_call x11, Pallas kernels, call(): pl.pallas_call(kernel, out_shape=out_shape, in_specs=in_specs, out_specs=...  30.5 us
    ppermute x11, starting transfers between devices, exchange(): return lax.ppermute(block, 'chaos', [(i, i ^ step) for i in range(count)])  20.7 us
    ppermute x11, waiting for transfers between devices, exchange(): return lax.ppermute(block, 'chaos', [(i, i ^ step) for i in range(count)])  16.5 us
    ppermute x2, starting transfers between devices, neighbours(): after = lax.ppermute(last_plane, 'space', pairs)  5.79 us
    ppermute x2, starting transfers between devices, neighbours(): return (lax.ppermute(first_plane, 'space', others), after)  1.75 us
  transfers between devices with their start and end apart: 15, of which 3 were waited for; matrix products, arithmetic and copies ran while one was open for 4% of the time, Pallas kernels for 32%

profile of v10, /device:TPU:0, one launch (start us, length us, event | category | flops | bytes accessed | tf_op | source)
XLA Modules:
  0.0 79.1 jit_solution(523813074391146540)
XLA Ops:
  0.7 1.8 %cut.1 = (bf16[3,56,768]{2,1,0:T(8,128)(2,1)S(1)}, bf16[3,56,768]{2,1,0:T(8,128)(2,1)S(1)}, bf16[2,56,768]{2,1,0:T(8,128)(2,1)S(1)}, bf16[2,56,768]{2,1,0:T(8,12...) custom-call(s32[1]{0:T(128)} %bitcast.me_ref, bf16[3,53,2304]{2,1,0:T(8,128)(2,1)} %bitcast.13), custom_call_target="tpu_custom_call" | custom-call | flops 1100000000 | bytes 3600000 | tf_op jit(solution)/shard_map/cut/pallas_call | solution.py:30
  2.5 4.1 %collective-permute-start.1 = (bf16[2,56,768]{2,1,0:T(8,128)(2,1)S(1)}, bf16[2,56,768]{2,1,0:T(8,128)(2,1)S(1)}, u32[]{:S(2)}, u32[]{:S(2)}) collective-permute-start(bf16[2,56,768]{2,1,0:T(8,128)(2,1)S(1)} %get-tuple-element.39), channel_id=1, source_target_pairs={{0,16},{8,24},{16,0},{24,8},{1,17},{9,25},{17,1},{25,9},{2,18},{10... | collective-permute-start | bytes 516104 | tf_op jit(solution)/shard_map/ppermute | solution.py:466
  6.6 1.4 %collective-permute-start.2 = (bf16[2,56,768]{2,1,0:T(8,128)(2,1)S(1)}, bf16[2,56,768]{2,1,0:T(8,128)(2,1)S(1)}, u32[]{:S(2)}, u32[]{:S(2)}) collective-permute-start(bf16[2,56,768]{2,1,0:T(8,128)(2,1)S(1)} %get-tuple-element.40), channel_id=1, source_target_pairs={{0,24},{8,16},{16,8},{24,0},{1,25},{9,17},{17,9},{25,1},{2,26},{10... | collective-permute-start | bytes 516104 | tf_op jit(solution)/shard_map/ppermute | solution.py:466
  7.9 0.2 collective-permute-start
  8.2 0.7 broadcast_in_dim.15.products_ref
  8.9 0.8 broadcast_in_dim.14
  9.7 1.0 %copy.10 = f32[6,3,2304]{2,0,1:T(8,128)S(1)} copy(f32[6,3,2304]{2,1,0:T(4,128)} %param.8) | data formatting | bytes 331776 | tf_op args[2]
  10.7 0.1 pad_maximum_fusion
  10.8 0.1 pad_dynamic-slice_fusion.1
  10.9 0.1 pad_dynamic-slice_fusion
  11.0 5.1 %tables.1.refs_2_.refs_4_.tables_ref.refs_7_.refs_5_ = bf16[1568,224]{1,0:T(8,128)(2,1)S(1)} custom-call(s32[1]{0:T(128)} %bitcast.me_ref, s32[3,1218]{1,0:T(4,128)S(1)} %bitcast.10, f32[1,1218]{1,0:T(1,128)S(1)} %broadcast_in_dim.15.products_ref, s32[1,210]{1,0:T(1,128)S(1)} %bitcast.11, bf16[3,56,768]{2,1,0:T(8,128)(2,1)S(1)} %get-tuple-element.37._.refs_0_), custom_call_target="tpu_custom_call" | custom-call | flops 5500000256 | bytes 18000000 | tf_op jit(solution)/shard_map/tables/pallas_call | solution.py:30
  16.2 0.1 pad_maximum_fusion.1.conduct_ref.refs_2_
  16.2 3.0 %collective-permute-done.1.refs_3_.refs_2_ = bf16[2,56,768]{2,1,0:T(8,128)(2,1)S(1)} collective-permute-done((bf16[2,56,768]{2,1,0:T(8,128)(2,1)S(1)}, bf16[2,56,768]{2,1,0:T(8,128)(2,1)S(1)}, u32[]{:S(2)}, u32[]{:S(2)}) %collective-permute-start.1) | collective-permute-done | bytes 172064 | tf_op jit(solution)/shard_map/ppermute | solution.py:466
  19.2 0.2 weights.1
  19.5 0.1 collective-permute-start.5
  19.5 2.9 %collective-permute-start.6 = (bf16[56,768]{1,0:T(8,128)(2,1)S(1)}, bf16[56,768]{1,0:T(8,128)(2,1)S(1)}, u32[]{:S(2)}, u32[]{:S(2)}) collective-permute-start(bf16[56,768]{1,0:T(8,128)(2,1)S(1)} %get-tuple-element.48), channel_id=1, source_target_pairs={{0,24},{8,16},{16,8},{24,0},{1,25},{9,17},{17,9},{25,1},{2,26},{10... | collective-permute-start | bytes 258056 | tf_op jit(solution)/shard_map/ppermute | solution.py:466
  22.4 0.0 collective-permute-done.2.refs_3_
  22.4 0.0 collective-permute-done.refs_1_
  22.4 0.1 gather.1
  22.5 0.9 %collective-permute-start.3 = (bf16[256,768]{1,0:T(8,128)(2,1)S(1)}, bf16[256,768]{1,0:T(8,128)(2,1)S(1)}, u32[]{:S(2)}, u32[]{:S(2)}) collective-permute-start(bf16[256,768]{1,0:T(8,128)(2,1)S(1)} %get-tuple-element.44.low_ref), channel_id=1, source_target_pairs={{1,2},{2,1},{3,4},{4,3},{5,6},{6,5},{9,10},{10,9},{11,12},{12,11},... | collective-permute-start | bytes 1179656 | tf_op jit(solution)/shard_map/ppermute | solution.py:476
  23.4 2.9 %collective-permute-start.4 = (bf16[256,768]{1,0:T(8,128)(2,1)S(1)}, bf16[256,768]{1,0:T(8,128)(2,1)S(1)}, u32[]{:S(2)}, u32[]{:S(2)}) collective-permute-start(bf16[256,768]{1,0:T(8,128)(2,1)S(1)} %get-tuple-element.45.high_ref), channel_id=1, source_target_pairs={{0,1},{1,0},{2,3},{3,2},{4,5},{5,4},{6,7},{7,6},{8,9},{9,8},{10,11... | collective-permute-start | bytes 1179656 | tf_op jit(solution)/shard_map/ppermute | solution.py:475
  26.3 5.4 %outer.1 = (f32[6,224,128]{2,1,0:T(8,128)S(1)}, f32[6,224,128]{2,1,0:T(8,128)S(1)}, f32[6,224,128]{2,1,0:T(8,128)S(1)}, bf16[2,6,1568,128]{3,2,1,0:T(8,128)(2,1)S(1)}) custom-call(bf16[256,768]{1,0:T(8,128)(2,1)S(1)} %get-tuple-element.44.low_ref, bf16[256,768]{1,0:T(8,128)(2,1)S(1)} %get-tuple-element.45.high_ref, ...), custom_call_target="tpu_custom_call" | custom-call | flops 6600000000 | bytes 21600000 | tf_op jit(solution)/shard_map/outer/pallas_call | solution.py:30
  31.7 0.0 collective-permute-done.5.refs_2_
  31.7 0.0 collective-permute-done.6.refs_3_
  31.7 3.3 %inner.1 = (f32[6,224,128]{2,1,0:T(8,128)S(1)}, f32[6,224,128]{2,1,0:T(8,128)S(1)}, f32[6,224,128]{2,1,0:T(8,128)S(1)}, bf16[224,768]{1,0:T(8,128)(2,1)S(1)}) custom-call(bf16[3,56,768]{2,1,0:T(8,128)(2,1)S(1)} %get-tuple-element.37._.refs_0_, bf16[3,56,768]{2,1,0:T(8,128)(2,1)S(1)} %collective-permute-done.refs_1_, ...), custom_call_target="tpu_custom_call" | custom-call | flops 3300000000 | bytes 10800000 | tf_op jit(solution)/shard_map/inner/pallas_call | solution.py:30
  35.0 0.0 collective-permute-done.3.refs_0_
  35.0 0.0 collective-permute-done.4.refs_1_
  35.0 2.6 %fix.1 = (bf16[224,768]{1,0:T(8,128)(2,1)S(1)}, bf16[224,768]{1,0:T(8,128)(2,1)S(1)}, bf16[224,640]{1,0:T(8,128)(2,1)S(1)}, bf16[224,640]{1,0:T(8,128)(2,1)S(1)}...) custom-call(s32[1]{0:T(128)} %bitcast.1.turn_ref, ...), custom_call_target="tpu_custom_call" | custom-call | flops 3300000000 | bytes 10800000 | tf_op jit(solution)/shard_map/fix/pallas_call | solution.py:30
  37.6 4.2 %collective-permute-start.7 = (bf16[736,128]{1,0:T(8,128)(2,1)S(1)}, bf16[736,128]{1,0:T(8,128)(2,1)S(1)}, u32[]{:S(2)}, u32[]{:S(2)}) collective-permute-start(bf16[736,128]{1,0:T(8,128)(2,1)S(1)} %get-tuple-element.56), channel_id=1, source_target_pairs={{0,8},{8,0},{16,24},{24,16},{1,9},{9,1},{17,25},{25,17},{2,10},{10... | collective-permute-start | bytes 565256 | tf_op jit(solution)/shard_map/ppermute | solution.py:466
  41.7 2.1 %collective-permute-start.8 = (bf16[736,128]{1,0:T(8,128)(2,1)S(1)}, bf16[736,128]{1,0:T(8,128)(2,1)S(1)}, u32[]{:S(2)}, u32[]{:S(2)}) collective-permute-start(bf16[736,128]{1,0:T(8,128)(2,1)S(1)} %get-tuple-element.57), channel_id=1, source_target_pairs={{0,16},{8,24},{16,0},{24,8},{1,17},{9,25},{17,1},{25,9},{2,18},{10... | collective-permute-start | bytes 565256 | tf_op jit(solution)/shard_map/ppermute | solution.py:466
  43.8 1.4 %collective-permute-start.9 = (bf16[736,128]{1,0:T(8,128)(2,1)S(1)}, bf16[736,128]{1,0:T(8,128)(2,1)S(1)}, u32[]{:S(2)}, u32[]{:S(2)}) collective-permute-start(bf16[736,128]{1,0:T(8,128)(2,1)S(1)} %get-tuple-element.58), channel_id=1, source_target_pairs={{0,24},{8,16},{16,8},{24,0},{1,25},{9,17},{17,9},{25,1},{2,26},{10... | collective-permute-start | bytes 565256 | tf_op jit(solution)/shard_map/ppermute | solution.py:466
  45.2 0.9 %collective-permute-start.10 = (bf16[224,640]{1,0:T(8,128)(2,1)S(1)}, bf16[224,640]{1,0:T(8,128)(2,1)S(1)}, u32[]{:S(2)}, u32[]{:S(2)}) collective-permute-start(bf16[224,640]{1,0:T(8,128)(2,1)S(1)} %get-tuple-element.59), channel_id=1, source_target_pairs={{1,2},{2,1},{3,4},{4,3},{5,6},{6,5},{9,10},{10,9},{11,12},{12,11},... | collective-permute-start | bytes 860168 | tf_op jit(solution)/shard_map/ppermute | solution.py:476
  46.1 2.9 %collective-permute-start.11 = (bf16[224,640]{1,0:T(8,128)(2,1)S(1)}, bf16[224,640]{1,0:T(8,128)(2,1)S(1)}, u32[]{:S(2)}, u32[]{:S(2)}) collective-permute-start(bf16[224,640]{1,0:T(8,128)(2,1)S(1)} %get-tuple-element.60), channel_id=1, source_target_pairs={{0,1},{1,0},{2,3},{3,2},{4,5},{5,4},{6,7},{7,6},{8,9},{9,8},{10,11... | collective-permute-start | bytes 860168 | tf_op jit(solution)/shard_map/ppermute | solution.py:475
  49.0 8.1 %second.1 = (f32[6,224,128]{2,1,0:T(8,128)S(1)}, f32[6,224,128]{2,1,0:T(8,128)S(1)}, f32[6,224,128]{2,1,0:T(8,128)S(1)}) custom-call(bf16[224,768]{1,0:T(8,128)(2,1)S(1)} %get-tuple-element.61.low_ref, bf16[224,768]{1,0:T(8,128)(2,1)S(1)} %get-tuple-element.62.values_ref, bf16[224,768]{1,0:T(8,128)(2,1)S(1)} %get-tuple-element.63.high_ref, ...), custom_call_target="tpu_custom_call" | custom-call | flops 8800000000 | bytes 28800000 | tf_op jit(solution)/shard_map/second/pallas_call | solution.py:30
  57.1 0.0 collective-permute-done.10.refs_0_
  57.1 0.0 collective-permute-done.11.refs_1_
  57.1 1.6 %last.1 = (bf16[736,128]{1,0:T(8,128)(2,1)S(1)}, bf16[736,128]{1,0:T(8,128)(2,1)S(1)}, bf16[736,128]{1,0:T(8,128)(2,1)S(1)}, bf16[736,128]{1,0:T(8,128)(2,1)S(1)}) custom-call(s32[1]{0:T(128)} %bitcast.1.turn_ref, bf16[224,640]{1,0:T(8,128)(2,1)S(1)} %collective-permute-done.10.refs_0_, bf16[224,640]{1,0:T(8,128)(2,1)S(1)} %collective-permute-done.11.refs_1_, ...), custom_call_target="tpu_custom_call" | custom-call | flops 3300000000 | bytes 10800000 | tf_op jit(solution)/shard_map/last/pallas_call | solution.py:30
  58.7 2.5 %collective-permute-start.12 = (bf16[736,128]{1,0:T(8,128)(2,1)S(1)}, bf16[736,128]{1,0:T(8,128)(2,1)S(1)}, u32[]{:S(2)}, u32[]{:S(2)}) collective-permute-start(bf16[736,128]{1,0:T(8,128)(2,1)S(1)} %get-tuple-element.68), channel_id=1, source_target_pairs={{0,24},{8,16},{16,8},{24,0},{1,25},{9,17},{17,9},{25,1},{2,26},{10... | collective-permute-start | bytes 565256 | tf_op jit(solution)/shard_map/ppermute | solution.py:466
  61.2 0.0 collective-permute-start.13
  61.2 0.0 collective-permute-done.7.refs_1_
  61.3 1.9 %collective-permute-start.14 = (bf16[736,128]{1,0:T(8,128)(2,1)S(1)}, bf16[736,128]{1,0:T(8,128)(2,1)S(1)}, u32[]{:S(2)}, u32[]{:S(2)}) collective-permute-start(bf16[736,128]{1,0:T(8,128)(2,1)S(1)} %get-tuple-element.70), channel_id=1, source_target_pairs={{0,8},{8,0},{16,24},{24,16},{1,9},{9,1},{17,25},{25,17},{2,10},{10... | collective-permute-start | bytes 565256 | tf_op jit(solution)/shard_map/ppermute | solution.py:466
  63.2 0.0 collective-permute-done.8.refs_2_
  63.2 0.0 collective-permute-done.9.refs_3_
  63.2 1.1 %join.2 = bf16[3,53,2304]{2,1,0:T(8,128)(2,1)} custom-call(s32[1]{0:T(128)} %bitcast.me_ref, bf16[736,128]{1,0:T(8,128)(2,1)S(1)} %get-tuple-element.55.refs_0_, bf16[736,128]{1,0:T(8,128)(2,1)S(1)} %collective-permute-done.7.refs_1_, bf16[736,128]{1,0:T(8,128)(2,1)S(1)} %collective-permute-done.8.refs_2_, bf16[736,128]{1,0:T(8,128)(2,1)S(1)} %collective-permute-done.9.refs_3_), custom_call_target="tpu_custom_call" | custom-call | flops 1100000000 | bytes 3600000 | tf_op jit(solution)/shard_map/join/pallas_call | solution.py:30
  64.3 4.0 %collective-permute-done.12.refs_0_ = bf16[736,128]{1,0:T(8,128)(2,1)S(1)} collective-permute-done((bf16[736,128]{1,0:T(8,128)(2,1)S(1)}, bf16[736,128]{1,0:T(8,128)(2,1)S(1)}, u32[]{:S(2)}, u32[]{:S(2)}) %collective-permute-start.12) | collective-permute-done | bytes 188448 | tf_op jit(solution)/shard_map/ppermute | solution.py:466
  68.3 9.5 %collective-permute-done.13.refs_1_ = bf16[736,128]{1,0:T(8,128)(2,1)S(1)} collective-permute-done((bf16[736,128]{1,0:T(8,128)(2,1)S(1)}, bf16[736,128]{1,0:T(8,128)(2,1)S(1)}, u32[]{:S(2)}, u32[]{:S(2)}) %collective-permute-start.13) | collective-permute-done | bytes 188448 | tf_op jit(solution)/shard_map/ppermute | solution.py:466
  77.8 0.0 collective-permute-done.14.refs_2_
  77.8 1.1 %join.3 = bf16[3,53,2304]{2,1,0:T(8,128)(2,1)} custom-call(s32[1]{0:T(128)} %bitcast.me_ref, bf16[736,128]{1,0:T(8,128)(2,1)S(1)} %collective-permute-done.12.refs_0_, bf16[736,128]{1,0:T(8,128)(2,1)S(1)} %collective-permute-done.13.refs_1_, bf16[736,128]{1,0:T(8,128)(2,1)S(1)} %collective-permute-done.14.refs_2_, bf16[736,128]{1,0:T(8,128)(2,1)S(1)} %get-tuple-element.71.refs_3_), custom_call_target="tpu_custom_call" | custom-call | flops 1100000000 | bytes 3600000 | tf_op jit(solution)/shard_map/join/pallas_call | solution.py:30
  (9 shorter events, 0.1 us)
Async XLA Ops:
  0.6 10.3 %copy-start.1 = (s32[210]{0:T(256)S(1)}, s32[210]{0:T(256)}, u32[]{:S(2)}) copy-start(s32[210]{0:T(256)} %param.11) | copy-start | bytes 2524
  0.6 10.3 %copy-start = (s32[1218,3]{0,1:T(4,128)S(1)}, s32[1218,3]{0,1:T(4,128)}, u32[]{:S(2)}) copy-start(s32[1218,3]{0,1:T(4,128)} %param.10) | copy-start | bytes 43852
  2.5 16.7 %collective-permute-start.1 = (bf16[2,56,768]{2,1,0:T(8,128)(2,1)S(1)}, bf16[2,56,768]{2,1,0:T(8,128)(2,1)S(1)}, u32[]{:S(2)}, u32[]{:S(2)}) collective-permute-start(bf16[2,56,768]{2,1,0:T(8,128)(2,1)S(1)} %get-tuple-element.39), channel_id=1, source_target_pairs={{0,16},{8,24},{16,0},{24,8},{1,17},{9,25},{17,1},{25,9},{2,18},{10... | collective-permute-start | bytes 516104 | tf_op jit(solution)/shard_map/ppermute | solution.py:466
  6.6 15.8 %collective-permute-start.2 = (bf16[2,56,768]{2,1,0:T(8,128)(2,1)S(1)}, bf16[2,56,768]{2,1,0:T(8,128)(2,1)S(1)}, u32[]{:S(2)}, u32[]{:S(2)}) collective-permute-start(bf16[2,56,768]{2,1,0:T(8,128)(2,1)S(1)} %get-tuple-element.40), channel_id=1, source_target_pairs={{0,24},{8,16},{16,8},{24,0},{1,25},{9,17},{17,9},{25,1},{2,26},{10... | collective-permute-start | bytes 516104 | tf_op jit(solution)/shard_map/ppermute | solution.py:466
  7.9 14.5 %collective-permute-start = (bf16[3,56,768]{2,1,0:T(8,128)(2,1)S(1)}, bf16[3,56,768]{2,1,0:T(8,128)(2,1)S(1)}, u32[]{:S(2)}, u32[]{:S(2)}) collective-permute-start(bf16[3,56,768]{2,1,0:T(8,128)(2,1)S(1)} %get-tuple-element.38), channel_id=1, source_target_pairs={{0,8},{8,0},{16,24},{24,16},{1,9},{9,1},{17,25},{25,17},{2,10},{10... | collective-permute-start | bytes 774152 | tf_op jit(solution)/shard_map/ppermute | solution.py:466
  19.5 12.2 %collective-permute-start.5 = (bf16[56,768]{1,0:T(8,128)(2,1)S(1)}, bf16[56,768]{1,0:T(8,128)(2,1)S(1)}, u32[]{:S(2)}, u32[]{:S(2)}) collective-permute-start(bf16[56,768]{1,0:T(8,128)(2,1)S(1)} %get-tuple-element.47), channel_id=1, source_target_pairs={{0,16},{8,24},{16,0},{24,8},{1,17},{9,25},{17,1},{25,9},{2,18},{10... | collective-permute-start | bytes 258056 | tf_op jit(solution)/shard_map/ppermute | solution.py:466
  19.5 12.1 %collective-permute-start.6 = (bf16[56,768]{1,0:T(8,128)(2,1)S(1)}, bf16[56,768]{1,0:T(8,128)(2,1)S(1)}, u32[]{:S(2)}, u32[]{:S(2)}) collective-permute-start(bf16[56,768]{1,0:T(8,128)(2,1)S(1)} %get-tuple-element.48), channel_id=1, source_target_pairs={{0,24},{8,16},{16,8},{24,0},{1,25},{9,17},{17,9},{25,1},{2,26},{10... | collective-permute-start | bytes 258056 | tf_op jit(solution)/shard_map/ppermute | solution.py:466
  22.5 12.5 %collective-permute-start.3 = (bf16[256,768]{1,0:T(8,128)(2,1)S(1)}, bf16[256,768]{1,0:T(8,128)(2,1)S(1)}, u32[]{:S(2)}, u32[]{:S(2)}) collective-permute-start(bf16[256,768]{1,0:T(8,128)(2,1)S(1)} %get-tuple-element.44.low_ref), channel_id=1, source_target_pairs={{1,2},{2,1},{3,4},{4,3},{5,6},{6,5},{9,10},{10,9},{11,12},{12,11},... | collective-permute-start | bytes 1179656 | tf_op jit(solution)/shard_map/ppermute | solution.py:476
  23.4 11.6 %collective-permute-start.4 = (bf16[256,768]{1,0:T(8,128)(2,1)S(1)}, bf16[256,768]{1,0:T(8,128)(2,1)S(1)}, u32[]{:S(2)}, u32[]{:S(2)}) collective-permute-start(bf16[256,768]{1,0:T(8,128)(2,1)S(1)} %get-tuple-element.45.high_ref), channel_id=1, source_target_pairs={{0,1},{1,0},{2,3},{3,2},{4,5},{5,4},{6,7},{7,6},{8,9},{9,8},{10,11... | collective-permute-start | bytes 1179656 | tf_op jit(solution)/shard_map/ppermute | solution.py:475
  37.6 23.7 %collective-permute-start.7 = (bf16[736,128]{1,0:T(8,128)(2,1)S(1)}, bf16[736,128]{1,0:T(8,128)(2,1)S(1)}, u32[]{:S(2)}, u32[]{:S(2)}) collective-permute-start(bf16[736,128]{1,0:T(8,128)(2,1)S(1)} %get-tuple-element.56), channel_id=1, source_target_pairs={{0,8},{8,0},{16,24},{24,16},{1,9},{9,1},{17,25},{25,17},{2,10},{10... | collective-permute-start | bytes 565256 | tf_op jit(solution)/shard_map/ppermute | solution.py:466
  41.7 21.5 %collective-permute-start.8 = (bf16[736,128]{1,0:T(8,128)(2,1)S(1)}, bf16[736,128]{1,0:T(8,128)(2,1)S(1)}, u32[]{:S(2)}, u32[]{:S(2)}) collective-permute-start(bf16[736,128]{1,0:T(8,128)(2,1)S(1)} %get-tuple-element.57), channel_id=1, source_target_pairs={{0,16},{8,24},{16,0},{24,8},{1,17},{9,25},{17,1},{25,9},{2,18},{10... | collective-permute-start | bytes 565256 | tf_op jit(solution)/shard_map/ppermute | solution.py:466
  43.8 19.4 %collective-permute-start.9 = (bf16[736,128]{1,0:T(8,128)(2,1)S(1)}, bf16[736,128]{1,0:T(8,128)(2,1)S(1)}, u32[]{:S(2)}, u32[]{:S(2)}) collective-permute-start(bf16[736,128]{1,0:T(8,128)(2,1)S(1)} %get-tuple-element.58), channel_id=1, source_target_pairs={{0,24},{8,16},{16,8},{24,0},{1,25},{9,17},{17,9},{25,1},{2,26},{10... | collective-permute-start | bytes 565256 | tf_op jit(solution)/shard_map/ppermute | solution.py:466
  45.2 11.9 %collective-permute-start.10 = (bf16[224,640]{1,0:T(8,128)(2,1)S(1)}, bf16[224,640]{1,0:T(8,128)(2,1)S(1)}, u32[]{:S(2)}, u32[]{:S(2)}) collective-permute-start(bf16[224,640]{1,0:T(8,128)(2,1)S(1)} %get-tuple-element.59), channel_id=1, source_target_pairs={{1,2},{2,1},{3,4},{4,3},{5,6},{6,5},{9,10},{10,9},{11,12},{12,11},... | collective-permute-start | bytes 860168 | tf_op jit(solution)/shard_map/ppermute | solution.py:476
  46.1 11.1 %collective-permute-start.11 = (bf16[224,640]{1,0:T(8,128)(2,1)S(1)}, bf16[224,640]{1,0:T(8,128)(2,1)S(1)}, u32[]{:S(2)}, u32[]{:S(2)}) collective-permute-start(bf16[224,640]{1,0:T(8,128)(2,1)S(1)} %get-tuple-element.60), channel_id=1, source_target_pairs={{0,1},{1,0},{2,3},{3,2},{4,5},{5,4},{6,7},{7,6},{8,9},{9,8},{10,11... | collective-permute-start | bytes 860168 | tf_op jit(solution)/shard_map/ppermute | solution.py:475
  58.7 9.6 %collective-permute-start.12 = (bf16[736,128]{1,0:T(8,128)(2,1)S(1)}, bf16[736,128]{1,0:T(8,128)(2,1)S(1)}, u32[]{:S(2)}, u32[]{:S(2)}) collective-permute-start(bf16[736,128]{1,0:T(8,128)(2,1)S(1)} %get-tuple-element.68), channel_id=1, source_target_pairs={{0,24},{8,16},{16,8},{24,0},{1,25},{9,17},{17,9},{25,1},{2,26},{10... | collective-permute-start | bytes 565256 | tf_op jit(solution)/shard_map/ppermute | solution.py:466
  61.2 16.6 %collective-permute-start.13 = (bf16[736,128]{1,0:T(8,128)(2,1)S(1)}, bf16[736,128]{1,0:T(8,128)(2,1)S(1)}, u32[]{:S(2)}, u32[]{:S(2)}) collective-permute-start(bf16[736,128]{1,0:T(8,128)(2,1)S(1)} %get-tuple-element.69), channel_id=1, source_target_pairs={{0,16},{8,24},{16,0},{24,8},{1,17},{9,25},{17,1},{25,9},{2,18},{10... | collective-permute-start | bytes 565256 | tf_op jit(solution)/shard_map/ppermute | solution.py:466
  61.3 16.6 %collective-permute-start.14 = (bf16[736,128]{1,0:T(8,128)(2,1)S(1)}, bf16[736,128]{1,0:T(8,128)(2,1)S(1)}, u32[]{:S(2)}, u32[]{:S(2)}) collective-permute-start(bf16[736,128]{1,0:T(8,128)(2,1)S(1)} %get-tuple-element.70), channel_id=1, source_target_pairs={{0,8},{8,0},{16,24},{24,16},{1,9},{9,1},{17,25},{25,17},{2,10},{10... | collective-permute-start | bytes 565256 | tf_op jit(solution)/shard_map/ppermute | solution.py:466
